TPU v7x, 32 devices: a whole 2x2x4 slice. The times are simulated.
32 devices in a mesh: groups: 2 (over y), tok: 4 (over z), blk: 2 (over x), sub: 2 (over core).
Axes of the slice: x: 2, y: 2, z: 4, core: 2. Of those that a mesh axis runs over, the one named last changes fastest.
Arguments:
- features_in: bfloat16 [256, 4096], P(('groups', 'tok'), 'blk'), parts along dimension 0, may hold values from -6 to 6
- gate_tiles: bfloat16 [128, 2, 12, 128, 128], P(('tok', 'sub'), 'blk'), may hold values from -0.125 to 0.125
- up_tiles: bfloat16 [128, 2, 12, 128, 128], P(('tok', 'sub'), 'blk'), may hold values from -0.125 to 0.125
- block_rows: int32 [128, 2, 12], P(('tok', 'sub'), 'blk'), may hold values from 0 to 15, as said below
- block_counts: int32 [128, 2], P(('tok', 'sub'), 'blk'), may hold values from 4 to 12
- d_hidden: bfloat16 [256, 16384], P(('groups', 'blk'), ('tok', 'sub')), parts along dimension 0, may hold values from -6 to 6
Outputs:
- hidden: bfloat16 [256, 16384], P(('groups', 'blk'), ('tok', 'sub')), parts along dimension 0
- gate_tiles_grad: bfloat16 [256, 2, 12, 128, 128], P(('groups', 'tok', 'sub'), 'blk'), parts along dimension 0
- up_tiles_grad: bfloat16 [256, 2, 12, 128, 128], P(('groups', 'tok', 'sub'), 'blk'), parts along dimension 0
- features_grad: bfloat16 [256, 4096], P(('groups', 'tok'), 'blk'), parts along dimension 0
There are 2 independent parts, one for each index of `groups`. A program takes and returns all parts, laid end to end along the dimension named above; an argument that names none is the same for every part. Nothing has to cross between parts.
Inputs may be any that keep to these rules, and one draw needn't show every extreme that they name: `block_rows`: the 12 entries of one list are distinct local row-block indices; only the first block_counts of them are kept.
All inputs are finite; a program needn't handle non-finite values.
Results may differ from a plain program's by a relative error of at most 0.015.
Values may be sent and summed in bfloat16 or wider, within the bound.
No kernel may reach another device: no remote copies, remote signals or barrier semaphores. Data moves between devices by JAX's collectives and lax.ppermute only.
A program may use at most 128 MiB of HBM per device.

v0:
```python
import functools

import jax
import jax.numpy as jnp
from jax import lax
from jax.experimental import pallas as pl
from jax.experimental.pallas import tpu as pltpu
from jax.sharding import PartitionSpec as P

F32 = jnp.float32
BF16 = jnp.bfloat16
MIB = 1 << 20
VMEM_SPEC = pl.BlockSpec(memory_space=pltpu.VMEM)
SMEM_SPEC = pl.BlockSpec(memory_space=pltpu.SMEM)
ANY_SPEC = pl.BlockSpec(memory_space=pl.ANY)


def limit(mib):
    return pltpu.CompilerParams(vmem_limit_bytes=mib * MIB)


def lanes(index, width):
    return pl.ds(pl.multiple_of(index * width, width), width)


def weights_of(c, gate_ref, up_ref):
    slots, rows, cols = gate_ref.shape[2:]
    return jnp.concatenate(
        [gate_ref[c, 0].reshape(slots * rows, cols), up_ref[c, 0].reshape(slots * rows, cols)], axis=1
    )


def keep(k, count, block):
    return jnp.where(k < count, block, jnp.zeros_like(block))


def forward_column(c, first, lists, xs, gate_ref, up_ref):
    rows_ref, counts_ref = lists
    slots, tile = gate_ref.shape[2:4]
    count = counts_ref[0, first + c]
    picked = []
    for k in range(slots):
        where = lanes(rows_ref[k, 0, first + c], tile)
        picked.append(keep(k, count, jnp.concatenate([x[:, where] for x in xs], axis=0)))
    return jnp.dot(
        jnp.concatenate(picked, axis=1), weights_of(c, gate_ref, up_ref), preferred_element_type=F32
    ).astype(BF16)


def forward_kernel(members, first, rows_ref, counts_ref, *refs):
    xs = refs[:members]
    gate_ref, up_ref = refs[members : members + 2]
    part_ref = refs[-1]
    for c in range(gate_ref.shape[0]):
        part_ref[c] = forward_column(c, first, (rows_ref, counts_ref), xs, gate_ref, up_ref)


def forward_own_kernel(x_hbm, rows_hbm, counts_hbm, gate_hbm, up_hbm, part_ref, gate_ref, up_ref, *scratch):
    x_ref, rows_ref, counts_ref, sems, small_sems = scratch
    cols = gate_ref.shape[0]

    def copies(c):
        return (
            pltpu.make_async_copy(gate_hbm.at[c], gate_ref.at[c], sems.at[0, c]),
            pltpu.make_async_copy(up_hbm.at[c], up_ref.at[c], sems.at[1, c]),
        )

    small = [
        pltpu.make_async_copy(source, target, small_sems.at[i])
        for i, (source, target) in enumerate(((rows_hbm, rows_ref), (counts_hbm, counts_ref), (x_hbm, x_ref)))
    ]
    for copy in small:
        copy.start()
    for c in range(cols):
        for copy in copies(c):
            copy.start()
    for copy in small:
        copy.wait()
    for c in range(cols):
        for copy in copies(c):
            copy.wait()
        part_ref[c] = forward_column(c, 0, (rows_ref, counts_ref), [x_ref], gate_ref, up_ref)


def load_forward_kernel(members, groups, first, turn, rows_ref, counts_ref, *refs):
    xs = refs[:members]
    gate_hbm, up_hbm = refs[members : members + 2]
    outs = refs[-(len(groups) + 3 + turn) :]
    parts, gate_ref, up_ref, sems = outs[: len(groups)], outs[-3 - turn], outs[-2 - turn], outs[-1]
    cols, _, _, tile, _ = gate_ref.shape

    def copies(c):
        return (
            pltpu.make_async_copy(gate_hbm.at[first + c], gate_ref.at[c], sems.at[0, c]),
            pltpu.make_async_copy(up_hbm.at[first + c], up_ref.at[c], sems.at[1, c]),
        )

    for c in range(cols):
        for copy in copies(c):
            copy.start()
    if turn:
        turned_ref = outs[-2]
        for r in range(turned_ref.shape[0]):
            turned_ref[r] = jnp.concatenate([x[:, r * tile : (r + 1) * tile] for x in xs], axis=0).T
    for c in range(cols):
        for copy in copies(c):
            copy.wait()
        part = forward_column(c, first, (rows_ref, counts_ref), xs, gate_ref, up_ref)
        for (start, stop), part_ref in zip(groups, parts):
            part_ref[c] = part[start:stop]


def shard_of(member, meta_ref):
    if member < 2:
        return meta_ref[0] ^ member
    return meta_ref[0] ^ ((member & ~1) + ((member & 1) ^ meta_ref[2]))


def start_cots(members, first, meta_ref, cots, cot_ref, sems):
    count = len(members)
    shard_rows, width = cot_ref.shape[0] // count, cot_ref.shape[1]
    shards_each = cots[0].shape[0] // shard_rows

    def copy(i, cot, first_row):
        return pltpu.make_async_copy(
            cot.at[pl.ds(first_row, shard_rows), pl.ds(first, width)],
            cot_ref.at[pl.ds(i * shard_rows, shard_rows)],
            sems.at[i],
        )

    for i, member in enumerate(members):
        shard = shard_of(member, meta_ref)
        source = (shard // shards_each) ^ meta_ref[1]
        first_row = pl.multiple_of((shard % shards_each) * shard_rows, shard_rows)
        for j, cot in enumerate(cots):

            @pl.when(source == j)
            def _(i=i, cot=cot, first_row=first_row):
                copy(i, cot, first_row).start()

    return [copy(i, cots[0], 0) for i in range(count)]


def nonlinear(total, cotangent):
    tile = total.shape[1] // 2
    gate_value, up_value = total[:, :tile], total[:, tile:]
    sig_gate = jax.nn.sigmoid(gate_value)
    act_gate = gate_value * sig_gate
    hidden = (act_gate * up_value).astype(BF16)
    gate_grad = (cotangent * up_value * sig_gate * (1.0 + gate_value * (1.0 - sig_gate))).astype(BF16)
    up_grad = (cotangent * act_gate).astype(BF16)
    return hidden, jnp.concatenate([gate_grad, up_grad], axis=1)


def total_of(c, parts):
    total = parts[0][c].astype(F32)
    for part in parts[1:]:
        total = total + part[c].astype(F32)
    return total


def back_terms(c, grads, gate_ref, up_ref):
    return lax.dot_general(
        grads, weights_of(c, gate_ref, up_ref), (((1,), (1,)), ((), ())), preferred_element_type=F32
    )


def add_back(c, lists, back, accs, slots, tile):
    rows_ref, counts_ref = lists
    rows = [rows_ref[k, 0, c] for k in range(slots)]
    start = 0
    for acc in accs:
        stop = start + acc.shape[1]
        sums = [
            acc[rows[k]] + keep(k, counts_ref[0, c], back[start:stop, k * tile : (k + 1) * tile])
            for k in range(slots)
        ]
        for k in range(slots):
            acc[rows[k]] = sums[k]
        start = stop


def tile_grads(c, first, lists, turned_ref, grads, gate_ref, up_ref):
    rows_ref, counts_ref = lists
    slots, tile = gate_ref.shape[2:4]
    picked = jnp.concatenate([turned_ref[rows_ref[k, 0, first + c]] for k in range(slots)], axis=0)
    found = jnp.dot(picked, grads, preferred_element_type=F32)
    for k in range(slots):
        term = keep(k, counts_ref[0, first + c], found[k * tile : (k + 1) * tile]).astype(BF16)
        gate_ref[c, 0, k] = term[:, :tile]
        up_ref[c, 0, k] = term[:, tile:]


def start_hidden(members, first, meta_ref, source_of, hidden_hbm, shard_rows, sems):
    width = source_of(0).shape[1]
    shards_each = hidden_hbm.shape[0] // shard_rows

    def copy(i, member):
        return pltpu.make_async_copy(
            source_of(member), hidden_hbm.at[pl.ds(i * shard_rows, shard_rows), pl.ds(first, width)], sems.at[i]
        )

    for i in range(shards_each):
        wanted = meta_ref[1] * shards_each + i
        for member in members:

            @pl.when(shard_of(member, meta_ref) == wanted)
            def _(i=i, member=member):
                copy(i, member).start()

    return [copy(i, 0) for i in range(shards_each)]


def first_half_kernel(members, owners, meta_ref, rows_ref, counts_ref, gate_w, up_w, turned_ref, *refs):
    near, rest, cots = refs[:owners], refs[owners : 2 * owners], refs[2 * owners : 3 * owners]
    (gate_hbm, up_hbm, hidden_hbm, acc_near, acc_far, cot_ref, hidden_ref, gate_ref, up_ref, sems, cot_sems, hidden_sems) = refs[
        -12:
    ]
    cols, _, slots, tile, _ = gate_w.shape
    shard_rows = cot_ref.shape[0] // members
    lists = (rows_ref, counts_ref)
    waits = start_cots(range(members), 0, meta_ref, cots, cot_ref, cot_sems)
    acc_near[...] = jnp.zeros_like(acc_near)
    acc_far[...] = jnp.zeros_like(acc_far)
    for wait in waits:
        wait.wait()
    copies = []
    for c in range(cols):
        total = jnp.concatenate([total_of(c, near), total_of(c, rest)], axis=0)
        where = slice(c * tile, (c + 1) * tile)
        hidden, grads = nonlinear(total, cot_ref[:, where].astype(F32))
        hidden_ref[:, where] = hidden
        tile_grads(c, 0, lists, turned_ref, grads, gate_ref, up_ref)
        copies.append(pltpu.make_async_copy(gate_ref.at[c], gate_hbm.at[c], sems.at[0, c]))
        copies.append(pltpu.make_async_copy(up_ref.at[c], up_hbm.at[c], sems.at[1, c]))
        copies[-2].start()
        copies[-1].start()
        add_back(c, lists, back_terms(c, grads, gate_w, up_w), (acc_near, acc_far), slots, tile)
    waits = start_hidden(
        range(members),
        0,
        meta_ref,
        lambda m: hidden_ref.at[pl.ds(m * shard_rows, shard_rows)],
        hidden_hbm,
        shard_rows,
        hidden_sems,
    )
    for wait in copies + waits:
        wait.wait()


def second_half_kernel(members, owners, first, meta_ref, rows_ref, counts_ref, gate_w, up_w, acc_in, *refs):
    parts, cots = refs[:owners], refs[owners : 2 * owners]
    outs = refs[-(2 + len(members) + 3) :]
    grads_ref, hidden_ref = outs[:2]
    dxs = outs[2 : 2 + len(members)]
    cot_ref, acc_ref, cot_sems = outs[-3:]
    cols, _, slots, tile, _ = gate_w.shape
    shard_rows = cot_ref.shape[0] // len(members)
    waits = start_cots(members, first * tile, meta_ref, cots, cot_ref, cot_sems)
    acc_ref[...] = acc_in[...]
    for wait in waits:
        wait.wait()
    for c in range(cols):
        where = slice(c * tile, (c + 1) * tile)
        hidden, grads = nonlinear(total_of(c, parts), cot_ref[:, where].astype(F32))
        hidden_ref[:, where] = hidden
        grads_ref[c] = grads
        add_back(first + c, (rows_ref, counts_ref), back_terms(c, grads, gate_w, up_w), (acc_ref,), slots, tile)
    for r in range(acc_ref.shape[0]):
        block = acc_ref[r].astype(BF16)
        for m, dx in enumerate(dxs):
            dx[:, r * tile : (r + 1) * tile] = block[m * shard_rows : (m + 1) * shard_rows]


def last_grads_kernel(members, first, start, with_hidden, meta_ref, rows_ref, counts_ref, turned_ref, *refs):
    near_grads, far_grads, near_hidden, far_hidden = refs[:4]
    gate_hbm, up_hbm, hidden_hbm, token_ref, gate_ref, up_ref, sems, hidden_sems = refs[-8:]
    cols, _, _, tile, _ = gate_ref.shape
    shard_rows = near_hidden.shape[0] // 2
    token_ref[...] = jnp.zeros_like(token_ref)

    def hidden_of(m):
        if m < 2:
            return near_hidden.at[pl.ds(m * shard_rows, shard_rows)]
        return far_hidden.at[pl.ds((m - 2) * shard_rows, shard_rows)]

    waits = []
    if with_hidden:
        waits = start_hidden(
            range(members), first * tile, meta_ref, hidden_of, hidden_hbm, shard_rows, hidden_sems
        )
    for c in range(cols):
        grads = jnp.concatenate([near_grads[start + c], far_grads[start + c]], axis=0)
        at = first + start + c
        tile_grads(c, first + start, (rows_ref, counts_ref), turned_ref, grads, gate_ref, up_ref)
        waits.append(pltpu.make_async_copy(gate_ref.at[c], gate_hbm.at[at], sems.at[0, c]))
        waits.append(pltpu.make_async_copy(up_ref.at[c], up_hbm.at[at], sems.at[1, c]))
        waits[-2].start()
        waits[-1].start()
    for wait in waits:
        wait.wait()


def sum_kernel(count, *refs):
    total = sum(ref[...].astype(F32) for ref in refs[:count])
    refs[-2][...] = total
    refs[-1][...] = total.astype(BF16)


def swap(x, axis, step):
    return lax.ppermute(x, axis, [(i, i ^ step) for i in range(lax.axis_size(axis))])


def swap_far(x, base):
    shards, cores = lax.axis_size("tok"), lax.axis_size("sub")
    pairs = [(t * cores + s, (t ^ (base + s)) * cores + s) for t in range(shards) for s in range(cores)]
    return lax.ppermute(x, ("tok", "sub"), pairs)


def on_device(features_in, gate_tiles, up_tiles, block_rows, block_counts, d_hidden):
    shards, owners = lax.axis_size("tok"), lax.axis_size("blk")
    cols, _, slots, tile, _ = gate_tiles.shape
    shard_rows, width = features_in.shape
    row_blocks = width // tile
    row_total = shards * shard_rows
    near_rows = 2 * shard_rows
    half = cols // 2
    bases = range(2, shards, 2)
    meta = jnp.stack([lax.axis_index("tok"), lax.axis_index("blk"), lax.axis_index("sub")]).astype(jnp.int32)
    lists = (jnp.transpose(block_rows, (2, 1, 0)), jnp.transpose(block_counts, (1, 0)))

    def held(weights):
        return [pltpu.with_memory_space_constraint(w, pltpu.VMEM) for w in weights]

    def shape(*dims, dtype=BF16):
        return jax.ShapeDtypeStruct(dims, dtype)

    def cost(tokens, columns, products, tile_bytes):
        tiles = columns * slots
        return pl.CostEstimate(
            flops=4 * tokens * tiles * tile * tile * products,
            bytes_accessed=4 * tiles * tile * tile * tile_bytes,
            transcendentals=0,
        )

    def to_owners(part):
        return [part] + [swap(part, "blk", s) for s in range(1, owners)]

    fars = [swap_far(features_in, base) for base in bases]
    xs = [features_in, swap(features_in, "tok", 1)]
    cots = [d_hidden] + [swap(d_hidden, "blk", s) for s in range(1, owners)]

    def tile_shape(columns):
        return pltpu.VMEM((columns, 1, slots, tile, tile), BF16)

    def from_hbm(*arrays):
        return [pltpu.with_memory_space_constraint(array, pltpu.HBM) for array in arrays]

    near_a, *weights_a = pl.pallas_call(
        forward_own_kernel,
        out_shape=(shape(half, shard_rows, 2 * tile), tile_shape(half), tile_shape(half)),
        in_specs=[ANY_SPEC] * 5,
        out_specs=(VMEM_SPEC,) * 3,
        scratch_shapes=[
            pltpu.VMEM((shard_rows, width), BF16),
            pltpu.SMEM(lists[0].shape, jnp.int32),
            pltpu.SMEM(lists[1].shape, jnp.int32),
            pltpu.SemaphoreType.DMA((2, half)),
            pltpu.SemaphoreType.DMA((3,)),
        ],
        compiler_params=limit(8),
        cost_estimate=cost(shard_rows, half, 1, 1),
        name="forward_own_a",
    )(*from_hbm(features_in, *lists, gate_tiles, up_tiles))
    near_a = to_owners(near_a)

    for far in fars:
        xs += [far, swap(far, "sub", 1)]

    rest_a = pl.pallas_call(
        functools.partial(forward_kernel, shards - 1, 0),
        out_shape=shape(half, row_total - shard_rows, 2 * tile),
        in_specs=[SMEM_SPEC] * 2 + [VMEM_SPEC] * (shards + 1) + [ANY_SPEC] * 2,
        out_specs=VMEM_SPEC,
        compiler_params=limit(8),
        cost_estimate=cost(row_total, half, 1, 1),
        name="forward_rest_a",
    )(*lists, *xs[1:], *held(weights_a), cots[-1], near_a[-1])
    rest_a = to_owners(rest_a)

    rest = cols - half
    far_b, near_b, gate_b, up_b, turned = pl.pallas_call(
        functools.partial(load_forward_kernel, shards, ((near_rows, row_total), (0, near_rows)), half, 1),
        out_shape=(
            shape(rest, row_total - near_rows, 2 * tile),
            shape(rest, near_rows, 2 * tile),
            tile_shape(rest),
            tile_shape(rest),
            pltpu.VMEM((row_blocks, tile, row_total), BF16),
        ),
        in_specs=[SMEM_SPEC] * 2 + [VMEM_SPEC] * shards + [ANY_SPEC] * 3,
        out_specs=(VMEM_SPEC,) * 5,
        scratch_shapes=[pltpu.SemaphoreType.DMA((2, rest))],
        compiler_params=limit(8),
        cost_estimate=cost(row_total, rest, 1, 1),
        name="forward_b",
    )(*lists, *xs, *from_hbm(gate_tiles, up_tiles), rest_a[0])
    weights_b = [gate_b, up_b]
    far_b, near_b = to_owners(far_b), to_owners(near_b)

    out_tiles = shape(*gate_tiles.shape)
    gate_out, up_out, hidden_out, acc_near, acc_far = pl.pallas_call(
        functools.partial(first_half_kernel, shards, owners),
        out_shape=(
            out_tiles,
            out_tiles,
            shape(*d_hidden.shape),
            shape(row_blocks, near_rows, tile, dtype=F32),
            shape(row_blocks, row_total - near_rows, tile, dtype=F32),
        ),
        in_specs=[SMEM_SPEC] * 3 + [VMEM_SPEC] * (3 + 2 * owners) + [ANY_SPEC] * (owners + 2),
        out_specs=(ANY_SPEC,) * 3 + (VMEM_SPEC,) * 2,
        scratch_shapes=[
            pltpu.VMEM((row_total, half * tile), BF16),
            pltpu.VMEM((row_total, half * tile), BF16),
            pltpu.VMEM((half, 1, slots, tile, tile), BF16),
            pltpu.VMEM((half, 1, slots, tile, tile), BF16),
            pltpu.SemaphoreType.DMA((2, half)),
            pltpu.SemaphoreType.DMA((shards,)),
            pltpu.SemaphoreType.DMA((d_hidden.shape[0] // shard_rows,)),
        ],
        compiler_params=limit(16),
        cost_estimate=cost(row_total, half, 2, 1),
        name="first_half",
    )(meta, *lists, *held(weights_a), *held([turned]), *near_a, *rest_a, *cots, far_b[0], near_b[0])

    def second_half(members, acc, parts, after):
        rows_here = len(members) * shard_rows
        return pl.pallas_call(
            functools.partial(second_half_kernel, members, owners, half),
            out_shape=(
                shape(rest, rows_here, 2 * tile),
                shape(rows_here, rest * tile),
                *[shape(shard_rows, width) for _ in members],
            ),
            in_specs=[SMEM_SPEC] * 3 + [VMEM_SPEC] * (3 + owners) + [ANY_SPEC] * (owners + 1),
            out_specs=(VMEM_SPEC,) * (2 + len(members)),
            scratch_shapes=[
                pltpu.VMEM((rows_here, rest * tile), BF16),
                pltpu.VMEM((row_blocks, rows_here, tile), F32),
                pltpu.SemaphoreType.DMA((len(members),)),
            ],
            compiler_params=limit(8),
            cost_estimate=cost(rows_here, rest, 1, 1),
            name="second_half",
        )(meta, *lists, *held(weights_b), acc, *parts, *cots, after)

    far_grads, far_hidden, *far_dxs = second_half(range(2, shards), acc_far, far_b, acc_near)
    both_cores = []
    for mine, others in zip(far_dxs[::2], far_dxs[1::2]):
        other = swap(others, "sub", 1)
        both_cores.append((mine.astype(F32) + other.astype(F32)).astype(BF16))
    back_far = [swap_far(total, base) for total, base in zip(both_cores, bases)]

    near_grads, near_hidden, own_dx, next_dx = second_half(range(2), acc_near, near_b, far_grads)
    back_next = swap(next_dx, "tok", 1)

    def last_grads(start, stop, with_hidden, outs):
        count = stop - start
        return pl.pallas_call(
            functools.partial(last_grads_kernel, shards, half, start, with_hidden),
            out_shape=(out_tiles, out_tiles, shape(*d_hidden.shape), shape(8, tile, dtype=F32)),
            in_specs=[SMEM_SPEC] * 3 + [VMEM_SPEC] * 3 + [ANY_SPEC] * 5,
            out_specs=(ANY_SPEC,) * 3 + (VMEM_SPEC,),
            scratch_shapes=[
                pltpu.VMEM((count, 1, slots, tile, tile), BF16),
                pltpu.VMEM((count, 1, slots, tile, tile), BF16),
                pltpu.SemaphoreType.DMA((2, count)),
                pltpu.SemaphoreType.DMA((d_hidden.shape[0] // shard_rows,)),
            ],
            input_output_aliases={8: 0, 9: 1, 10: 2},
            compiler_params=limit(12),
            cost_estimate=cost(row_total, count, 1, 1),
            name="last_grads",
        )(meta, *lists, *held([turned]), near_grads, far_grads, near_hidden, far_hidden, *outs)

    middle = max(1, rest // 2)
    *outs, token = last_grads(0, middle, True, (gate_out, up_out, hidden_out))
    arrived = [own_dx, back_next, *back_far]
    mine, mine_sent = pl.pallas_call(
        functools.partial(sum_kernel, len(arrived)),
        out_shape=(shape(shard_rows, width, dtype=F32), shape(shard_rows, width)),
        in_specs=[VMEM_SPEC] * len(arrived) + [ANY_SPEC],
        out_specs=(VMEM_SPEC,) * 2,
        compiler_params=limit(8),
        name="sum_shards",
    )(*arrived, token)
    if middle < rest:
        *outs, _ = last_grads(middle, rest, False, outs)
    gate_out, up_out, hidden_out = outs
    features_grad = (mine + swap(mine_sent, "sub", 1).astype(F32)).astype(BF16)
    return (hidden_out, gate_out, up_out, features_grad)


def solution(mesh):
    return jax.shard_map(
        on_device,
        mesh=mesh,
        in_specs=(
            P(("groups", "tok"), "blk"),
            P(("tok", "sub"), "blk", None, None, None),
            P(("tok", "sub"), "blk", None, None, None),
            P(("tok", "sub"), "blk", None),
            P(("tok", "sub"), "blk"),
            P(("groups", "blk"), ("tok", "sub")),
        ),
        out_specs=(
            P(("groups", "blk"), ("tok", "sub")),
            P(("groups", "tok", "sub"), "blk", None, None, None),
            P(("groups", "tok", "sub"), "blk", None, None, None),
            P(("groups", "tok"), "blk"),
        ),
        check_vma=False,
    )
```

profile of v0, /device:TPU:0, one launch (start us, length us, event | category | flops | bytes accessed | tf_op | source)
XLA Modules:
  0.0 60.7 jit_solution(219282027415727617)
XLA Ops:
  0.6 4.1 %collective-permute-start.1 = (bf16[32,2048]{1,0:T(8,128)(2,1)}, bf16[32,2048]{1,0:T(8,128)(2,1)S(1)}, u32[]{:S(2)}, u32[]{:S(2)}) collective-permute-start(bf16[32,2048]{1,0:T(8,128)(2,1)} %refs_0_.1), channel_id=1, source_target_pairs={{0,8},{1,13},{4,12},{5,9},{8,0},{9,5},{12,4},{13,1},{2,10},{3,15},... | collective-permute-start | bytes 393224 | tf_op jit(solution)/shard_map/ppermute | solution.py:318
  4.7 1.5 %collective-permute-start.3 = (bf16[64,2048]{1,0:T(8,128)(2,1)}, bf16[64,2048]{1,0:T(8,128)(2,1)S(1)}, u32[]{:S(2)}, u32[]{:S(2)}) collective-permute-start(bf16[64,2048]{1,0:T(8,128)(2,1)} %refs_2_.3), channel_id=1, source_target_pairs={{0,2},{2,0},{1,3},{3,1},{4,6},{6,4},{5,7},{7,5},{8,10},{10,8},{9,1... | collective-permute-start | bytes 786440 | tf_op jit(solution)/shard_map/ppermute | solution.py:312
  6.2 1.6 %collective-permute-start = (bf16[32,2048]{1,0:T(8,128)(2,1)}, bf16[32,2048]{1,0:T(8,128)(2,1)S(1)}, u32[]{:S(2)}, u32[]{:S(2)}) collective-permute-start(bf16[32,2048]{1,0:T(8,128)(2,1)} %refs_0_.1), channel_id=1, source_target_pairs={{0,4},{4,0},{8,12},{12,8},{1,5},{5,1},{9,13},{13,9},{2,6},{6,2},{1... | collective-permute-start | bytes 393224 | tf_op jit(solution)/shard_map/ppermute | solution.py:312
  7.8 5.5 %forward_own_a.1 = (bf16[8,32,256]{2,1,0:T(8,128)(2,1)S(1)}, bf16[8,1,12,128,128]{4,3,2,1,0:T(8,128)(2,1)S(1)}, bf16[8,1,12,128,128]{4,3,2,1,0:T(8,128)(2,1)S(1)}) custom-call(bf16[32,2048]{1,0:T(8,128)(2,1)} %refs_0_.1, s32[12,1,16]{2,1,0:T(1,128)} %bitcast.5, s32[1,16]{1,0:T(1,128)} %bitcast.13, bf16[16,1,12,128,128]{4,3,2,1,0:T(8,128)(2,1)} %refs_4_.2, ...), custom_call_target="tpu_custom_call" | custom-call | flops 201326592 | bytes 6291456 | tf_op jit(solution)/shard_map/forward_own_a/pallas_call | solution.py:360
  13.3 0.6 collective-permute-start.4
  13.9 0.7 %copy-done.13 = bf16[8,32,256]{2,1,0:T(8,128)(2,1)} copy-done((bf16[8,32,256]{2,1,0:T(8,128)(2,1)}, bf16[8,32,256]{2,1,0:T(8,128)(2,1)S(1)}, u32[]{:S(2)}) %copy-start.13) | copy-done | bytes 131096
  14.6 3.7 %collective-permute-done.4.refs_6_.refs_1_ = bf16[8,32,256]{2,1,0:T(8,128)(2,1)S(1)} collective-permute-done((bf16[8,32,256]{2,1,0:T(8,128)(2,1)S(1)}, bf16[8,32,256]{2,1,0:T(8,128)(2,1)S(1)}, u32[]{:S(2)}, u32[]{:S(2)}) %collective-permute-start.4) | collective-permute-done | bytes 131104 | tf_op jit(solution)/shard_map/ppermute | solution.py:312
  18.4 2.5 %forward_rest_a.1.refs_6_.refs_2_ = bf16[8,96,256]{2,1,0:T(8,128)(2,1)} custom-call(s32[12,1,16]{2,1,0:T(1,128)S(1)} %bitcast.6, s32[1,16]{1,0:T(1,128)S(1)} %bitcast.14, bf16[32,2048]{1,0:T(8,128)(2,1)S(1)} %collective-permute-done.refs_0_.refs_1_, bf16[32,2048]{1,0:T(8,128)(2,1)S(1)} %collective-permute-done.1.refs_1_.refs_2_, ...), custom_call_target="tpu_custom_call" | custom-call | flops 805306368 | bytes 6291456 | tf_op jit(solution)/shard_map/forward_rest_a/pallas_call | solution.py:381
  20.9 1.7 %copy-done = bf16[8,1,12,128,128]{4,3,2,1,0:T(8,128)(2,1)} copy-done((bf16[8,1,12,128,128]{4,3,2,1,0:T(8,128)(2,1)}, bf16[8,1,12,128,128]{4,3,2,1,0:T(8,128)(2,1)S(1)}, u32[]{:S(2)}) %copy-start) | copy-done | bytes 3145752
  22.6 0.6 collective-permute-start.5
  23.2 0.9 %copy-done.7 = bf16[32,2048]{1,0:T(8,128)(2,1)S(1)} copy-done((bf16[32,2048]{1,0:T(8,128)(2,1)S(1)}, bf16[32,2048]{1,0:T(8,128)(2,1)}, u32[]{:S(2)}) %copy-start.7) | copy-done | bytes 131096
  24.1 0.9 %copy-done.9 = bf16[32,2048]{1,0:T(8,128)(2,1)S(1)} copy-done((bf16[32,2048]{1,0:T(8,128)(2,1)S(1)}, bf16[32,2048]{1,0:T(8,128)(2,1)}, u32[]{:S(2)}) %copy-start.9) | copy-done | bytes 131096
  25.0 0.9 %copy-done.11 = bf16[32,2048]{1,0:T(8,128)(2,1)S(1)} copy-done((bf16[32,2048]{1,0:T(8,128)(2,1)S(1)}, bf16[32,2048]{1,0:T(8,128)(2,1)}, u32[]{:S(2)}) %copy-start.11) | copy-done | bytes 131096
  25.9 5.1 %forward_b.1 = (bf16[8,64,256]{2,1,0:T(8,128)(2,1)S(1)}, bf16[8,64,256]{2,1,0:T(8,128)(2,1)S(1)}, bf16[8,1,12,128,128]{4,3,2,1,0:T(8,128)(2,1)S(1)}, bf16[8,1,12...) custom-call(s32[12,1,16]{2,1,0:T(1,128)S(1)} %bitcast.7, s32[1,16]{1,0:T(1,128)S(1)} %bitcast.15, ...), custom_call_target="tpu_custom_call" | custom-call | flops 805306368 | bytes 6291456 | tf_op jit(solution)/shard_map/forward_b/pallas_call | solution.py:393
  31.0 1.5 %collective-permute-start.7 = (bf16[8,64,256]{2,1,0:T(8,128)(2,1)S(1)}, bf16[8,64,256]{2,1,0:T(8,128)(2,1)S(1)}, u32[]{:S(2)}, u32[]{:S(2)}) collective-permute-start(bf16[8,64,256]{2,1,0:T(8,128)(2,1)S(1)} %get-tuple-element.40.refs_6_.refs_0_), channel_id=1, source_target_pairs={{0,2},{2,0},{1,3},{3,1},{4,6},{6,4},{5,7},{7,5},{8,10},{10,8},{9,1... | collective-permute-start | bytes 786440 | tf_op jit(solution)/shard_map/ppermute | solution.py:312
  32.6 0.1 pad_add_fusion.meta_ref
  32.6 0.6 collective-permute-start.6
  33.2 6.4 %first_half.1 = (bf16[16,1,12,128,128]{4,3,2,1,0:T(8,128)(2,1)}, bf16[16,1,12,128,128]{4,3,2,1,0:T(8,128)(2,1)}, bf16[64,2048]{1,0:T(8,128)(2,1)}, f32[16,64,128]{2,1,0:T(8,128)S(1)}, f32[16,64,128]{2,1,0:T(8,128)S(1)}) custom-call(s32[3]{0:T(128)S(1)} %pad_add_fusion.meta_ref, s32[12,1,16]{2,1,0:T(1,128)S(1)} %bitcast.8, s32[1,16]{1,0:T(1,128)S(1)} %bitcast.16, ...), custom_call_target="tpu_custom_call" | custom-call | flops 1610612736 | bytes 6291456 | tf_op jit(solution)/shard_map/first_half/pallas_call | solution.py:413
  39.6 0.7 %collective-permute-done.7.refs_1_ = bf16[8,64,256]{2,1,0:T(8,128)(2,1)S(1)} collective-permute-done((bf16[8,64,256]{2,1,0:T(8,128)(2,1)S(1)}, bf16[8,64,256]{2,1,0:T(8,128)(2,1)S(1)}, u32[]{:S(2)}, u32[]{:S(2)}) %collective-permute-start.7) | collective-permute-done | bytes 262176 | tf_op jit(solution)/shard_map/ppermute | solution.py:312
  40.3 2.9 %second_half.2 = (bf16[8,64,256]{2,1,0:T(8,128)(2,1)S(1)}, bf16[64,1024]{1,0:T(8,128)(2,1)S(1)}, bf16[32,2048]{1,0:T(8,128)(2,1)S(1)}, bf16[32,2048]{1,0:T(8,128)(2,1)S(1)}) custom-call(s32[3]{0:T(128)S(1)} %pad_add_fusion.meta_ref, s32[12,1,16]{2,1,0:T(1,128)S(1)} %bitcast.9, s32[1,16]{1,0:T(1,128)S(1)} %bitcast.17, ...), custom_call_target="tpu_custom_call" | custom-call | flops 402653184 | bytes 6291456 | tf_op jit(solution)/shard_map/second_half/pallas_call | solution.py:440
  43.2 0.1 collective-permute-start.9
  43.3 0.0 collective-permute-done.6.refs_1_
  43.3 3.0 %second_half.3 = (bf16[8,64,256]{2,1,0:T(8,128)(2,1)S(1)}, bf16[64,1024]{1,0:T(8,128)(2,1)S(1)}, bf16[32,2048]{1,0:T(8,128)(2,1)S(1)}, bf16[32,2048]{1,0:T(8,128)(2,1)S(1)}) custom-call(s32[3]{0:T(128)S(1)} %pad_add_fusion.meta_ref, s32[12,1,16]{2,1,0:T(1,128)S(1)} %bitcast.10, s32[1,16]{1,0:T(1,128)S(1)} %bitcast.18, ...), custom_call_target="tpu_custom_call" | custom-call | flops 402653184 | bytes 6291456 | tf_op jit(solution)/shard_map/second_half/pallas_call | solution.py:440
  46.3 1.9 %collective-permute-start.8 = (bf16[32,2048]{1,0:T(8,128)(2,1)S(1)}, bf16[32,2048]{1,0:T(8,128)(2,1)S(1)}, u32[]{:S(2)}, u32[]{:S(2)}) collective-permute-start(bf16[32,2048]{1,0:T(8,128)(2,1)S(1)} %get-tuple-element.58), channel_id=1, source_target_pairs={{0,4},{4,0},{8,12},{12,8},{1,5},{5,1},{9,13},{13,9},{2,6},{6,2},{1... | collective-permute-start | bytes 393224 | tf_op jit(solution)/shard_map/ppermute | solution.py:312
  48.2 0.1 collective-permute-start.10
  48.3 3.0 %last_grads.2 = (bf16[16,1,12,128,128]{4,3,2,1,0:T(8,128)(2,1)}, bf16[16,1,12,128,128]{4,3,2,1,0:T(8,128)(2,1)}, bf16[64,2048]{1,0:T(8,128)(2,1)}, f32[8,128]{1,0:T(8,128)S(1)}) custom-call(s32[3]{0:T(128)S(1)} %pad_add_fusion.meta_ref, s32[12,1,16]{2,1,0:T(1,128)S(1)} %bitcast.11, ...), custom_call_target="tpu_custom_call", output_to_operand_aliasing={{0}: (8, {}), {1}: (9, {}), {2}: (10, {})} | custom-call | flops 402653184 | bytes 3145728 | tf_op jit(solution)/shard_map/last_grads/pallas_call | solution.py:471
  51.3 1.4 %collective-permute-done.8.refs_1_ = bf16[32,2048]{1,0:T(8,128)(2,1)S(1)} collective-permute-done((bf16[32,2048]{1,0:T(8,128)(2,1)S(1)}, bf16[32,2048]{1,0:T(8,128)(2,1)S(1)}, u32[]{:S(2)}, u32[]{:S(2)}) %collective-permute-start.8) | collective-permute-done | bytes 131104 | tf_op jit(solution)/shard_map/ppermute | solution.py:312
  52.7 3.6 %collective-permute-done.10.refs_2_ = bf16[32,2048]{1,0:T(8,128)(2,1)S(1)} collective-permute-done((bf16[32,2048]{1,0:T(8,128)(2,1)S(1)}, bf16[32,2048]{1,0:T(8,128)(2,1)S(1)}, u32[]{:S(2)}, u32[]{:S(2)}) %collective-permute-start.10) | collective-permute-done | bytes 131104 | tf_op jit(solution)/shard_map/ppermute | solution.py:318
  56.4 0.1 sum_shards.1
  56.4 0.1 collective-permute-start.11
  56.5 3.5 %last_grads.3 = (bf16[16,1,12,128,128]{4,3,2,1,0:T(8,128)(2,1)}, bf16[16,1,12,128,128]{4,3,2,1,0:T(8,128)(2,1)}, bf16[64,2048]{1,0:T(8,128)(2,1)}, f32[8,128]{1,0:T(8,128)}) custom-call(s32[3]{0:T(128)S(1)} %pad_add_fusion.meta_ref, s32[12,1,16]{2,1,0:T(1,128)S(1)} %bitcast.12, ...), custom_call_target="tpu_custom_call", output_to_operand_aliasing={{0}: (8, {}), {1}: (9, {}), {2}: (10, {})} | custom-call | flops 402653184 | bytes 3145728 | tf_op jit(solution)/shard_map/last_grads/pallas_call | solution.py:471
  60.1 0.7 %add_convert_fusion = bf16[32,2048]{1,0:T(8,128)(2,1)} fusion(f32[32,2048]{1,0:T(8,128)S(1)} %get-tuple-element.62, bf16[32,2048]{1,0:T(8,128)(2,1)S(1)} %collective-permute-done.11), kind=kLoop, calls=%fused_computation | loop fusion | flops 196608 | bytes 524288 | tf_op jit(solution)/shard_map/convert_element_type | solution.py:502
  (36 shorter events, 0.1 us)
Async XLA Ops:
  0.6 13.9 %collective-permute-start.1 = (bf16[32,2048]{1,0:T(8,128)(2,1)}, bf16[32,2048]{1,0:T(8,128)(2,1)S(1)}, u32[]{:S(2)}, u32[]{:S(2)}) collective-permute-start(bf16[32,2048]{1,0:T(8,128)(2,1)} %refs_0_.1), channel_id=1, source_target_pairs={{0,8},{1,13},{4,12},{5,9},{8,0},{9,5},{12,4},{13,1},{2,10},{3,15},... | collective-permute-start | bytes 393224 | tf_op jit(solution)/shard_map/ppermute | solution.py:318
  4.7 13.6 %collective-permute-start.3 = (bf16[64,2048]{1,0:T(8,128)(2,1)}, bf16[64,2048]{1,0:T(8,128)(2,1)S(1)}, u32[]{:S(2)}, u32[]{:S(2)}) collective-permute-start(bf16[64,2048]{1,0:T(8,128)(2,1)} %refs_2_.3), channel_id=1, source_target_pairs={{0,2},{2,0},{1,3},{3,1},{4,6},{6,4},{5,7},{7,5},{8,10},{10,8},{9,1... | collective-permute-start | bytes 786440 | tf_op jit(solution)/shard_map/ppermute | solution.py:312
  6.2 8.4 %collective-permute-start = (bf16[32,2048]{1,0:T(8,128)(2,1)}, bf16[32,2048]{1,0:T(8,128)(2,1)S(1)}, u32[]{:S(2)}, u32[]{:S(2)}) collective-permute-start(bf16[32,2048]{1,0:T(8,128)(2,1)} %refs_0_.1), channel_id=1, source_target_pairs={{0,4},{4,0},{8,12},{12,8},{1,5},{5,1},{9,13},{13,9},{2,6},{6,2},{1... | collective-permute-start | bytes 393224 | tf_op jit(solution)/shard_map/ppermute | solution.py:312
  7.8 10.6 %copy-start.12 = (s32[16,1,12]{0,1,2:T(1,128)S(1)}, s32[16,1,12]{0,1,2:T(1,128)}, u32[]{:S(2)}) copy-start(s32[16,1,12]{0,1,2:T(1,128)} %param.9) | copy-start | bytes 2308
  7.8 10.6 %copy-start.15 = (s32[16,1]{0,1:T(1,128)S(1)}, s32[16,1]{0,1:T(1,128)}, u32[]{:S(2)}) copy-start(s32[16,1]{0,1:T(1,128)} %param.10) | copy-start | bytes 196
  13.3 9.8 %copy-start.3 = (bf16[32,2048]{1,0:T(8,128)(2,1)S(1)}, bf16[32,2048]{1,0:T(8,128)(2,1)}, u32[]{:S(2)}) copy-start(bf16[32,2048]{1,0:T(8,128)(2,1)} %refs_0_.1) | copy-start | bytes 393220
  13.3 5.0 %collective-permute-start.4 = (bf16[8,32,256]{2,1,0:T(8,128)(2,1)S(1)}, bf16[8,32,256]{2,1,0:T(8,128)(2,1)S(1)}, u32[]{:S(2)}, u32[]{:S(2)}) collective-permute-start(bf16[8,32,256]{2,1,0:T(8,128)(2,1)S(1)} %get-tuple-element.36.refs_0_), channel_id=1, source_target_pairs={{0,2},{2,0},{1,3},{3,1},{4,6},{6,4},{5,7},{7,5},{8,10},{10,8},{9,1... | collective-permute-start | bytes 393224 | tf_op jit(solution)/shard_map/ppermute | solution.py:312
  13.9 0.7 %copy-start.13 = (bf16[8,32,256]{2,1,0:T(8,128)(2,1)}, bf16[8,32,256]{2,1,0:T(8,128)(2,1)S(1)}, u32[]{:S(2)}) copy-start(bf16[8,32,256]{2,1,0:T(8,128)(2,1)S(1)} %get-tuple-element.36.refs_0_) | copy-start | bytes 393220
  14.6 8.6 %copy-start.6 = (bf16[32,2048]{1,0:T(8,128)(2,1)}, bf16[32,2048]{1,0:T(8,128)(2,1)S(1)}, u32[]{:S(2)}) copy-start(bf16[32,2048]{1,0:T(8,128)(2,1)S(1)} %collective-permute-done.1.refs_1_.refs_2_) | copy-start | bytes 393220
  14.6 3.8 %collective-permute-start.2 = (bf16[32,2048]{1,0:T(8,128)(2,1)S(1)}, bf16[32,2048]{1,0:T(8,128)(2,1)S(1)}, u32[]{:S(2)}, u32[]{:S(2)}) collective-permute-start(bf16[32,2048]{1,0:T(8,128)(2,1)S(1)} %collective-permute-done.1.refs_1_.refs_2_), channel_id=1, source_target_pairs={{0,1},{1,0},{2,3},{3,2},{4,5},{5,4},{6,7},{7,6},{8,9},{9,8},{10,11... | collective-permute-start | bytes 393224 | tf_op jit(solution)/shard_map/ppermute | solution.py:312
  14.6 8.6 %copy-start.8 = (bf16[32,2048]{1,0:T(8,128)(2,1)}, bf16[32,2048]{1,0:T(8,128)(2,1)S(1)}, u32[]{:S(2)}) copy-start(bf16[32,2048]{1,0:T(8,128)(2,1)S(1)} %collective-permute-done.refs_0_.refs_1_) | copy-start | bytes 393220
  18.3 2.6 %copy-start.4 = (bf16[8,32,256]{2,1,0:T(8,128)(2,1)}, bf16[8,32,256]{2,1,0:T(8,128)(2,1)S(1)}, u32[]{:S(2)}) copy-start(bf16[8,32,256]{2,1,0:T(8,128)(2,1)S(1)} %collective-permute-done.4.refs_6_.refs_1_) | copy-start | bytes 393220
  18.4 4.8 %copy-start.10 = (bf16[32,2048]{1,0:T(8,128)(2,1)}, bf16[32,2048]{1,0:T(8,128)(2,1)S(1)}, u32[]{:S(2)}) copy-start(bf16[32,2048]{1,0:T(8,128)(2,1)S(1)} %collective-permute-done.2.refs_2_.refs_3_) | copy-start | bytes 393220
  20.9 1.7 %copy-start = (bf16[8,1,12,128,128]{4,3,2,1,0:T(8,128)(2,1)}, bf16[8,1,12,128,128]{4,3,2,1,0:T(8,128)(2,1)S(1)}, u32[]{:S(2)}) copy-start(bf16[8,1,12,128,128]{4,3,2,1,0:T(8,128)(2,1)S(1)} %get-tuple-element.35.refs_4_.up_w) | copy-start | bytes 9437188
  22.6 10.6 %collective-permute-start.5 = (bf16[8,96,256]{2,1,0:T(8,128)(2,1)}, bf16[8,96,256]{2,1,0:T(8,128)(2,1)}, u32[]{:S(2)}, u32[]{:S(2)}) collective-permute-start(bf16[8,96,256]{2,1,0:T(8,128)(2,1)} %forward_rest_a.1.refs_6_.refs_2_), channel_id=1, source_target_pairs={{0,2},{2,0},{1,3},{3,1},{4,6},{6,4},{5,7},{7,5},{8,10},{10,8},{9,1... | collective-permute-start | bytes 1179656 | tf_op jit(solution)/shard_map/ppermute | solution.py:312
  23.2 0.9 %copy-start.7 = (bf16[32,2048]{1,0:T(8,128)(2,1)S(1)}, bf16[32,2048]{1,0:T(8,128)(2,1)}, u32[]{:S(2)}) copy-start(bf16[32,2048]{1,0:T(8,128)(2,1)} %copy-done.6) | copy-start | bytes 393220
  24.1 0.9 %copy-start.9 = (bf16[32,2048]{1,0:T(8,128)(2,1)S(1)}, bf16[32,2048]{1,0:T(8,128)(2,1)}, u32[]{:S(2)}) copy-start(bf16[32,2048]{1,0:T(8,128)(2,1)} %copy-done.8) | copy-start | bytes 393220
  25.0 0.9 %copy-start.11 = (bf16[32,2048]{1,0:T(8,128)(2,1)S(1)}, bf16[32,2048]{1,0:T(8,128)(2,1)}, u32[]{:S(2)}) copy-start(bf16[32,2048]{1,0:T(8,128)(2,1)} %copy-done.10) | copy-start | bytes 393220
  25.9 7.3 %copy-start.1 = (bf16[8,1,12,128,128]{4,3,2,1,0:T(8,128)(2,1)S(1)}, bf16[8,1,12,128,128]{4,3,2,1,0:T(8,128)(2,1)}, u32[]{:S(2)}) copy-start(bf16[8,1,12,128,128]{4,3,2,1,0:T(8,128)(2,1)} %copy-done) | copy-start | bytes 9437188
  25.9 7.3 %copy-start.2 = (bf16[64,2048]{1,0:T(8,128)(2,1)S(1)}, bf16[64,2048]{1,0:T(8,128)(2,1)}, u32[]{:S(2)}) copy-start(bf16[64,2048]{1,0:T(8,128)(2,1)} %refs_2_.3) | copy-start | bytes 786436
  25.9 7.3 %copy-start.5 = (bf16[8,32,256]{2,1,0:T(8,128)(2,1)S(1)}, bf16[8,32,256]{2,1,0:T(8,128)(2,1)}, u32[]{:S(2)}) copy-start(bf16[8,32,256]{2,1,0:T(8,128)(2,1)} %copy-done.4) | copy-start | bytes 393220
  25.9 7.3 %copy-start.14 = (bf16[8,32,256]{2,1,0:T(8,128)(2,1)S(1)}, bf16[8,32,256]{2,1,0:T(8,128)(2,1)}, u32[]{:S(2)}) copy-start(bf16[8,32,256]{2,1,0:T(8,128)(2,1)} %copy-done.13) | copy-start | bytes 393220
  31.0 9.3 %collective-permute-start.7 = (bf16[8,64,256]{2,1,0:T(8,128)(2,1)S(1)}, bf16[8,64,256]{2,1,0:T(8,128)(2,1)S(1)}, u32[]{:S(2)}, u32[]{:S(2)}) collective-permute-start(bf16[8,64,256]{2,1,0:T(8,128)(2,1)S(1)} %get-tuple-element.40.refs_6_.refs_0_), channel_id=1, source_target_pairs={{0,2},{2,0},{1,3},{3,1},{4,6},{6,4},{5,7},{7,5},{8,10},{10,8},{9,1... | collective-permute-start | bytes 786440 | tf_op jit(solution)/shard_map/ppermute | solution.py:312
  32.6 10.7 %collective-permute-start.6 = (bf16[8,64,256]{2,1,0:T(8,128)(2,1)S(1)}, bf16[8,64,256]{2,1,0:T(8,128)(2,1)S(1)}, u32[]{:S(2)}, u32[]{:S(2)}) collective-permute-start(bf16[8,64,256]{2,1,0:T(8,128)(2,1)S(1)} %get-tuple-element.41.refs_7_.refs_0_), channel_id=1, source_target_pairs={{0,2},{2,0},{1,3},{3,1},{4,6},{6,4},{5,7},{7,5},{8,10},{10,8},{9,1... | collective-permute-start | bytes 786440 | tf_op jit(solution)/shard_map/ppermute | solution.py:312
  43.2 5.0 %collective-permute-start.9 = (bf16[32,2048]{1,0:T(8,128)(2,1)S(1)}, bf16[32,2048]{1,0:T(8,128)(2,1)S(1)}, u32[]{:S(2)}, u32[]{:S(2)}) collective-permute-start(bf16[32,2048]{1,0:T(8,128)(2,1)S(1)} %get-tuple-element.60), channel_id=1, source_target_pairs={{0,1},{1,0},{2,3},{3,2},{4,5},{5,4},{6,7},{7,6},{8,9},{9,8},{10,11... | collective-permute-start | bytes 393224 | tf_op jit(solution)/shard_map/ppermute | solution.py:312
  46.3 6.4 %collective-permute-start.8 = (bf16[32,2048]{1,0:T(8,128)(2,1)S(1)}, bf16[32,2048]{1,0:T(8,128)(2,1)S(1)}, u32[]{:S(2)}, u32[]{:S(2)}) collective-permute-start(bf16[32,2048]{1,0:T(8,128)(2,1)S(1)} %get-tuple-element.58), channel_id=1, source_target_pairs={{0,4},{4,0},{8,12},{12,8},{1,5},{5,1},{9,13},{13,9},{2,6},{6,2},{1... | collective-permute-start | bytes 393224 | tf_op jit(solution)/shard_map/ppermute | solution.py:312
  48.2 8.1 %collective-permute-start.10 = (bf16[32,2048]{1,0:T(8,128)(2,1)S(1)}, bf16[32,2048]{1,0:T(8,128)(2,1)S(1)}, u32[]{:S(2)}, u32[]{:S(2)}) collective-permute-start(bf16[32,2048]{1,0:T(8,128)(2,1)S(1)} %add_convert_fusion.1), channel_id=1, source_target_pairs={{0,8},{1,13},{4,12},{5,9},{8,0},{9,5},{12,4},{13,1},{2,10},{3,15},... | collective-permute-start | bytes 393224 | tf_op jit(solution)/shard_map/ppermute | solution.py:318
  56.4 3.6 %collective-permute-start.11 = (bf16[32,2048]{1,0:T(8,128)(2,1)S(1)}, bf16[32,2048]{1,0:T(8,128)(2,1)S(1)}, u32[]{:S(2)}, u32[]{:S(2)}) collective-permute-start(bf16[32,2048]{1,0:T(8,128)(2,1)S(1)} %get-tuple-element.63), channel_id=1, source_target_pairs={{0,1},{1,0},{2,3},{3,2},{4,5},{5,4},{6,7},{7,6},{8,9},{9,8},{10,11... | collective-permute-start | bytes 393224 | tf_op jit(solution)/shard_map/ppermute | solution.py:312
where the time goes:
time: 61 us; the launch traced here: 60.7 us
  Pallas kernels  32 us (52%)
  starting transfers between devices  12.5 us (20%)
  waiting for transfers between devices  9.58 us (16%)
  local copies, waits for them, and re-layouts  5.07 us (8%)
  between operations  0.83 us (1%)
  other arithmetic  0.8 us (1%)
    ppermute x10, starting transfers between devices, swap(): lax.ppermute(x, axis, [(i, i ^ step) for i in range(lax.axis_size(axis))])  8.33 us
    pallas_call x2, Pallas kernels, last_grads(): pl.pallas_call(functools.partial(last_grads_kernel, shards, half, start,...  6.52 us
    pallas_call x1, Pallas kernels, on_device(): pl.pallas_call(functools.partial(first_half_kernel, shards, owners), out_...  6.37 us
    ppermute x10, waiting for transfers between devices, swap(): lax.ppermute(x, axis, [(i, i ^ step) for i in range(lax.axis_size(axis))])  5.95 us
    pallas_call x2, Pallas kernels, second_half(): pl.pallas_call(functools.partial(second_half_kernel, members, owners, hal...  5.88 us
    pallas_call x1, Pallas kernels, on_device(): pl.pallas_call(forward_own_kernel, out_shape=(shape(half, shard_rows, 2 *...  5.49 us
    pallas_call x1, Pallas kernels, on_device(): pl.pallas_call(functools.partial(load_forward_kernel, shards, ((near_rows...  5.13 us
    unnamed x32, local copies, waits for them, and re-layouts  5.07 us
  transfers between devices with their start and end apart: 12, of which 4 were waited for; matrix products, arithmetic and copies ran while one was open for 0% of the time, Pallas kernels for 48%

commit v1 on v0

--- a/solution.py
+++ b/solution.py
@@ -10,6 +10,7 @@
 F32 = jnp.float32
 BF16 = jnp.bfloat16
 MIB = 1 << 20
+WINDOW = 3
 VMEM_SPEC = pl.BlockSpec(memory_space=pltpu.VMEM)
 SMEM_SPEC = pl.BlockSpec(memory_space=pltpu.SMEM)
 ANY_SPEC = pl.BlockSpec(memory_space=pl.ANY)
@@ -55,6 +56,21 @@
         part_ref[c] = forward_column(c, first, (rows_ref, counts_ref), xs, gate_ref, up_ref)
 
 
+def windowed(copies, cols):
+    for c in range(min(WINDOW, cols)):
+        for copy in copies(c):
+            copy.start()
+
+    def arrive(c):
+        for copy in copies(c):
+            copy.wait()
+        if c + WINDOW < cols:
+            for copy in copies(c + WINDOW):
+                copy.start()
+
+    return arrive
+
+
 def forward_own_kernel(x_hbm, rows_hbm, counts_hbm, gate_hbm, up_hbm, part_ref, gate_ref, up_ref, *scratch):
     x_ref, rows_ref, counts_ref, sems, small_sems = scratch
     cols = gate_ref.shape[0]
@@ -71,14 +87,11 @@
     ]
     for copy in small:
         copy.start()
-    for c in range(cols):
-        for copy in copies(c):
-            copy.start()
+    arrive = windowed(copies, cols)
     for copy in small:
         copy.wait()
     for c in range(cols):
-        for copy in copies(c):
-            copy.wait()
+        arrive(c)
         part_ref[c] = forward_column(c, 0, (rows_ref, counts_ref), [x_ref], gate_ref, up_ref)
 
 
@@ -95,16 +108,13 @@
             pltpu.make_async_copy(up_hbm.at[first + c], up_ref.at[c], sems.at[1, c]),
         )
 
-    for c in range(cols):
-        for copy in copies(c):
-            copy.start()
+    arrive = windowed(copies, cols)
     if turn:
         turned_ref = outs[-2]
         for r in range(turned_ref.shape[0]):
             turned_ref[r] = jnp.concatenate([x[:, r * tile : (r + 1) * tile] for x in xs], axis=0).T
     for c in range(cols):
-        for copy in copies(c):
-            copy.wait()
+        arrive(c)
         part = forward_column(c, first, (rows_ref, counts_ref), xs, gate_ref, up_ref)
         for (start, stop), part_ref in zip(groups, parts):
             part_ref[c] = part[start:stop]
@@ -211,12 +221,20 @@
     return [copy(i, 0) for i in range(shards_each)]
 
 
-def first_half_kernel(members, owners, meta_ref, rows_ref, counts_ref, gate_w, up_w, turned_ref, *refs):
+def first_half_kernel(members, owners, meta_ref, rows_ref, counts_ref, gate_in, up_in, turned_ref, *refs):
     near, rest, cots = refs[:owners], refs[owners : 2 * owners], refs[2 * owners : 3 * owners]
-    (gate_hbm, up_hbm, hidden_hbm, acc_near, acc_far, cot_ref, hidden_ref, gate_ref, up_ref, sems, cot_sems, hidden_sems) = refs[
-        -12:
-    ]
-    cols, _, slots, tile, _ = gate_w.shape
+    gate_hbm, up_hbm, hidden_hbm, acc_near, acc_far = refs[-15:-10]
+    cot_ref, hidden_ref, gate_ref, up_ref, gate_w, up_w, sems, cot_sems, hidden_sems, load_sems = refs[-10:]
+    cols, _, slots, tile, _ = gate_ref.shape
+    ring = gate_w.shape[0]
+
+    def loads(c):
+        return (
+            pltpu.make_async_copy(gate_in.at[c], gate_w.at[c % ring], load_sems.at[0, c % ring]),
+            pltpu.make_async_copy(up_in.at[c], up_w.at[c % ring], load_sems.at[1, c % ring]),
+        )
+
+    arrive = windowed(loads, cols)
     shard_rows = cot_ref.shape[0] // members
     lists = (rows_ref, counts_ref)
     waits = start_cots(range(members), 0, meta_ref, cots, cot_ref, cot_sems)
@@ -235,7 +253,8 @@
         copies.append(pltpu.make_async_copy(up_ref.at[c], up_hbm.at[c], sems.at[1, c]))
         copies[-2].start()
         copies[-1].start()
-        add_back(c, lists, back_terms(c, grads, gate_w, up_w), (acc_near, acc_far), slots, tile)
+        arrive(c)
+        add_back(c, lists, back_terms(c % ring, grads, gate_w, up_w), (acc_near, acc_far), slots, tile)
     waits = start_hidden(
         range(members),
         0,
@@ -302,6 +321,14 @@
         wait.wait()
 
 
+def copy_kernel(x_ref, _, out_ref):
+    out_ref[...] = x_ref[...]
+
+
+def add_kernel(left_ref, right_ref, out_ref):
+    out_ref[...] = (left_ref[...].astype(F32) + right_ref[...].astype(F32)).astype(BF16)
+
+
 def sum_kernel(count, *refs):
     total = sum(ref[...].astype(F32) for ref in refs[:count])
     refs[-2][...] = total
@@ -336,8 +363,8 @@
     def shape(*dims, dtype=BF16):
         return jax.ShapeDtypeStruct(dims, dtype)
 
-    def cost(tokens, columns, products, tile_bytes):
-        tiles = columns * slots
+    def cost(tokens, columns, products, tile_bytes, weight=1):
+        tiles = weight * columns * slots
         return pl.CostEstimate(
             flops=4 * tokens * tiles * tile * tile * products,
             bytes_accessed=4 * tiles * tile * tile * tile_bytes,
@@ -376,17 +403,26 @@
     near_a = to_owners(near_a)
 
     for far in fars:
-        xs += [far, swap(far, "sub", 1)]
+        ready = pl.pallas_call(
+            copy_kernel,
+            out_shape=shape(shard_rows, width),
+            in_specs=[VMEM_SPEC, ANY_SPEC],
+            out_specs=VMEM_SPEC,
+            compiler_params=limit(8),
+            cost_estimate=pl.CostEstimate(flops=0, bytes_accessed=0, transcendentals=0),
+            name="after_own",
+        )(far, near_a[0])
+        xs += [far, swap(ready, "sub", 1)]
 
     rest_a = pl.pallas_call(
         functools.partial(forward_kernel, shards - 1, 0),
         out_shape=shape(half, row_total - shard_rows, 2 * tile),
-        in_specs=[SMEM_SPEC] * 2 + [VMEM_SPEC] * (shards + 1) + [ANY_SPEC] * 2,
+        in_specs=[SMEM_SPEC] * 2 + [VMEM_SPEC] * (shards + 1) + [ANY_SPEC],
         out_specs=VMEM_SPEC,
         compiler_params=limit(8),
         cost_estimate=cost(row_total, half, 1, 1),
         name="forward_rest_a",
-    )(*lists, *xs[1:], *held(weights_a), cots[-1], near_a[-1])
+    )(*lists, *xs[1:], *held(weights_a), cots[-1])
     rest_a = to_owners(rest_a)
 
     rest = cols - half
@@ -399,13 +435,13 @@
             tile_shape(rest),
             pltpu.VMEM((row_blocks, tile, row_total), BF16),
         ),
-        in_specs=[SMEM_SPEC] * 2 + [VMEM_SPEC] * shards + [ANY_SPEC] * 3,
+        in_specs=[SMEM_SPEC] * 2 + [VMEM_SPEC] * shards + [ANY_SPEC] * 4,
         out_specs=(VMEM_SPEC,) * 5,
         scratch_shapes=[pltpu.SemaphoreType.DMA((2, rest))],
         compiler_params=limit(8),
-        cost_estimate=cost(row_total, rest, 1, 1),
+        cost_estimate=cost(row_total, rest, 1, 1, 5),
         name="forward_b",
-    )(*lists, *xs, *from_hbm(gate_tiles, up_tiles), rest_a[0])
+    )(*lists, *xs, *from_hbm(gate_tiles, up_tiles), rest_a[0], near_a[-1])
     weights_b = [gate_b, up_b]
     far_b, near_b = to_owners(far_b), to_owners(near_b)
 
@@ -419,21 +455,27 @@
             shape(row_blocks, near_rows, tile, dtype=F32),
             shape(row_blocks, row_total - near_rows, tile, dtype=F32),
         ),
-        in_specs=[SMEM_SPEC] * 3 + [VMEM_SPEC] * (3 + 2 * owners) + [ANY_SPEC] * (owners + 2),
+        in_specs=[SMEM_SPEC] * 3
+        + [ANY_SPEC] * 2
+        + [VMEM_SPEC] * (1 + 2 * owners)
+        + [ANY_SPEC] * (owners + 2),
         out_specs=(ANY_SPEC,) * 3 + (VMEM_SPEC,) * 2,
         scratch_shapes=[
             pltpu.VMEM((row_total, half * tile), BF16),
             pltpu.VMEM((row_total, half * tile), BF16),
             pltpu.VMEM((half, 1, slots, tile, tile), BF16),
             pltpu.VMEM((half, 1, slots, tile, tile), BF16),
+            pltpu.VMEM((WINDOW + 1, 1, slots, tile, tile), BF16),
+            pltpu.VMEM((WINDOW + 1, 1, slots, tile, tile), BF16),
             pltpu.SemaphoreType.DMA((2, half)),
             pltpu.SemaphoreType.DMA((shards,)),
             pltpu.SemaphoreType.DMA((d_hidden.shape[0] // shard_rows,)),
+            pltpu.SemaphoreType.DMA((2, WINDOW + 1)),
         ],
         compiler_params=limit(16),
-        cost_estimate=cost(row_total, half, 2, 1),
+        cost_estimate=cost(row_total, half, 2, 1, 1),
         name="first_half",
-    )(meta, *lists, *held(weights_a), *held([turned]), *near_a, *rest_a, *cots, far_b[0], near_b[0])
+    )(meta, *lists, *from_hbm(gate_tiles, up_tiles), *held([turned]), *near_a, *rest_a, *cots, far_b[0], near_b[0])
 
     def second_half(members, acc, parts, after):
         rows_here = len(members) * shard_rows
@@ -452,7 +494,7 @@
                 pltpu.SemaphoreType.DMA((len(members),)),
             ],
             compiler_params=limit(8),
-            cost_estimate=cost(rows_here, rest, 1, 1),
+            cost_estimate=cost(rows_here, rest, 1, 1, 1 if members[0] == 0 else 1),
             name="second_half",
         )(meta, *lists, *held(weights_b), acc, *parts, *cots, after)
 
@@ -460,10 +502,20 @@
     both_cores = []
     for mine, others in zip(far_dxs[::2], far_dxs[1::2]):
         other = swap(others, "sub", 1)
-        both_cores.append((mine.astype(F32) + other.astype(F32)).astype(BF16))
+        both_cores.append(
+            pl.pallas_call(
+                add_kernel,
+                out_shape=shape(shard_rows, width),
+                in_specs=[VMEM_SPEC] * 2,
+                out_specs=VMEM_SPEC,
+                compiler_params=limit(8),
+                cost_estimate=pl.CostEstimate(flops=0, bytes_accessed=0, transcendentals=0),
+                name="add_cores",
+            )(mine, other)
+        )
     back_far = [swap_far(total, base) for total, base in zip(both_cores, bases)]
 
-    near_grads, near_hidden, own_dx, next_dx = second_half(range(2), acc_near, near_b, far_grads)
+    near_grads, near_hidden, own_dx, next_dx = second_half(range(2), acc_near, near_b, both_cores[-1])
     back_next = swap(next_dx, "tok", 1)
 
     def last_grads(start, stop, with_hidden, outs):
@@ -481,11 +533,11 @@
             ],
             input_output_aliases={8: 0, 9: 1, 10: 2},
             compiler_params=limit(12),
-            cost_estimate=cost(row_total, count, 1, 1),
+            cost_estimate=cost(row_total, count, 1, 1, 10),
             name="last_grads",
         )(meta, *lists, *held([turned]), near_grads, far_grads, near_hidden, far_hidden, *outs)
 
-    middle = max(1, rest // 2)
+    middle = rest
     *outs, token = last_grads(0, middle, True, (gate_out, up_out, hidden_out))
     arrived = [own_dx, back_next, *back_far]
     mine, mine_sent = pl.pallas_call(

time: 61 us -> 59.2 us (0.970)
  Pallas kernels: 32 us -> 30.8 us
  starting transfers between devices: 12.5 us -> 11.4 us
  waiting for transfers between devices: 9.58 us -> 10.5 us
    ppermute x10, waiting for transfers between devices: 5.95 us -> 10.5 us  [swap(): lax.ppermute(x, axis, [(i, i ^ step) for i in range(lax.axis_size(axis))])]
    ppermute x2, waiting for transfers between devices: 3.63 us -> 0.01 us  [swap_far(): return lax.ppermute(x, ('tok', 'sub'), pairs)]
    pallas_call x2 -> x1, Pallas kernels: 6.52 us -> 4.03 us  [last_grads(): pl.pallas_call(functools.partial(last_grads_kernel, shards, half, start,...]
    ppermute x10, starting transfers between devices: 8.33 us -> 6.94 us  [swap(): lax.ppermute(x, axis, [(i, i ^ step) for i in range(lax.axis_size(axis))])]
    pallas_call x1, Pallas kernels: 6.37 us -> 7.74 us  [on_device(): pl.pallas_call(functools.partial(first_half_kernel, shards, owners), out_...]
    pallas_call x1, Pallas kernels: 5.49 us -> 4.75 us  [on_device(): pl.pallas_call(forward_own_kernel, out_shape=(shape(half, shard_rows, 2 *...]
    pallas_call x0 -> x2, Pallas kernels: none -> 0.73 us  [the longest x1 0.7 us: on_device(): pl.pallas_call(copy_kernel, out_shape=shape(shard_rows, width), in_specs=...]
    unnamed x32 -> x16, local copies, waits for them, and re-layouts: 5.07 us -> 4.47 us
  transfers between devices with their start and end apart: 12 -> 12, of which waited for: 4 -> 5; matrix products, arithmetic and copies ran while one was open for 0% -> 0% of each run, Pallas kernels for 48% -> 52%
where the time goes in v1:
time: 59.2 us; the launch traced here: 58.8 us
  Pallas kernels  30.8 us (52%)
  starting transfers between devices  11.4 us (19%)
  waiting for transfers between devices  10.5 us (18%)
  local copies, waits for them, and re-layouts  4.47 us (8%)
  other arithmetic  0.76 us (1%)
  between operations  0.75 us (1%)
    ppermute x10, waiting for transfers between devices, swap(): lax.ppermute(x, axis, [(i, i ^ step) for i in range(lax.axis_size(axis))])  10.5 us
    pallas_call x1, Pallas kernels, on_device(): pl.pallas_call(functools.partial(first_half_kernel, shards, owners), out_...  7.74 us
    ppermute x10, starting transfers between devices, swap(): lax.ppermute(x, axis, [(i, i ^ step) for i in range(lax.axis_size(axis))])  6.94 us
    pallas_call x2, Pallas kernels, second_half(): pl.pallas_call(functools.partial(second_half_kernel, members, owners, hal...  5.88 us
    pallas_call x1, Pallas kernels, on_device(): pl.pallas_call(functools.partial(load_forward_kernel, shards, ((near_rows...  5.44 us
    pallas_call x1, Pallas kernels, on_device(): pl.pallas_call(forward_own_kernel, out_shape=(shape(half, shard_rows, 2 *...  4.75 us
    ppermute x2, starting transfers between devices, swap_far(): return lax.ppermute(x, ('tok', 'sub'), pairs)  4.5 us
    unnamed x16, local copies, waits for them, and re-layouts  4.47 us
  transfers between devices with their start and end apart: 12, of which 5 were waited for; matrix products, arithmetic and copies ran while one was open for 0% of the time, Pallas kernels for 52%

profile of v1, /device:TPU:0, one launch (start us, length us, event | category | flops | bytes accessed | tf_op | source)
XLA Modules:
  0.0 58.8 jit_solution(15556327158997782817)
XLA Ops:
  0.6 4.1 %collective-permute-start.1 = (bf16[32,2048]{1,0:T(8,128)(2,1)}, bf16[32,2048]{1,0:T(8,128)(2,1)S(1)}, u32[]{:S(2)}, u32[]{:S(2)}) collective-permute-start(bf16[32,2048]{1,0:T(8,128)(2,1)} %refs_0_.1), channel_id=1, source_target_pairs={{0,8},{1,13},{4,12},{5,9},{8,0},{9,5},{12,4},{13,1},{2,10},{3,15},... | collective-permute-start | bytes 393224 | tf_op jit(solution)/shard_map/ppermute | solution.py:345
  4.7 1.5 %collective-permute-start.3 = (bf16[64,2048]{1,0:T(8,128)(2,1)}, bf16[64,2048]{1,0:T(8,128)(2,1)S(1)}, u32[]{:S(2)}, u32[]{:S(2)}) collective-permute-start(bf16[64,2048]{1,0:T(8,128)(2,1)} %refs_2_.3), channel_id=1, source_target_pairs={{0,2},{2,0},{1,3},{3,1},{4,6},{6,4},{5,7},{7,5},{8,10},{10,8},{9,1... | collective-permute-start | bytes 786440 | tf_op jit(solution)/shard_map/ppermute | solution.py:339
  6.2 1.6 %collective-permute-start = (bf16[32,2048]{1,0:T(8,128)(2,1)}, bf16[32,2048]{1,0:T(8,128)(2,1)}, u32[]{:S(2)}, u32[]{:S(2)}) collective-permute-start(bf16[32,2048]{1,0:T(8,128)(2,1)} %refs_0_.1), channel_id=1, source_target_pairs={{0,4},{4,0},{8,12},{12,8},{1,5},{5,1},{9,13},{13,9},{2,6},{6,2},{1... | collective-permute-start | bytes 393224 | tf_op jit(solution)/shard_map/ppermute | solution.py:339
  7.8 4.7 %forward_own_a.1 = (bf16[8,32,256]{2,1,0:T(8,128)(2,1)S(1)}, bf16[8,1,12,128,128]{4,3,2,1,0:T(8,128)(2,1)S(1)}, bf16[8,1,12,128,128]{4,3,2,1,0:T(8,128)(2,1)S(1)}) custom-call(bf16[32,2048]{1,0:T(8,128)(2,1)} %refs_0_.1, s32[12,1,16]{2,1,0:T(1,128)} %bitcast.5, s32[1,16]{1,0:T(1,128)} %bitcast.12, bf16[16,1,12,128,128]{4,3,2,1,0:T(8,128)(2,1)} %gate_in.1, ...), custom_call_target="tpu_custom_call" | custom-call | flops 201326592 | bytes 6291456 | tf_op jit(solution)/shard_map/forward_own_a/pallas_call | solution.py:387
  12.6 0.0 copy-start
  12.6 1.7 %copy-done = bf16[8,1,12,128,128]{4,3,2,1,0:T(8,128)(2,1)} copy-done((bf16[8,1,12,128,128]{4,3,2,1,0:T(8,128)(2,1)}, bf16[8,1,12,128,128]{4,3,2,1,0:T(8,128)(2,1)S(1)}, u32[]{:S(2)}) %copy-start) | copy-done | bytes 3145752
  14.2 0.7 %after_own.1 = bf16[32,2048]{1,0:T(8,128)(2,1)} custom-call(bf16[32,2048]{1,0:T(8,128)(2,1)S(1)} %collective-permute-done.1.x_ref.refs_1_.refs_2_, bf16[8,32,256]{2,1,0:T(8,128)(2,1)S(1)} %get-tuple-element.31._.refs_0_), custom_call_target="tpu_custom_call" | custom-call | tf_op jit(solution)/shard_map/after_own/pallas_call | solution.py:406
  14.9 0.5 collective-permute-start.4
  15.5 1.1 %collective-permute-done.2.refs_2_.refs_3_ = bf16[32,2048]{1,0:T(8,128)(2,1)} collective-permute-done((bf16[32,2048]{1,0:T(8,128)(2,1)}, bf16[32,2048]{1,0:T(8,128)(2,1)}, u32[]{:S(2)}, u32[]{:S(2)}) %collective-permute-start.2) | collective-permute-done | bytes 131104 | tf_op jit(solution)/shard_map/ppermute | solution.py:339
  16.6 1.9 %copy-done.1 = bf16[8,1,12,128,128]{4,3,2,1,0:T(8,128)(2,1)S(1)} copy-done((bf16[8,1,12,128,128]{4,3,2,1,0:T(8,128)(2,1)S(1)}, bf16[8,1,12,128,128]{4,3,2,1,0:T(8,128)(2,1)}, u32[]{:S(2)}) %copy-start.1) | copy-done | bytes 3145752
  18.5 0.9 %copy-done.4 = bf16[32,2048]{1,0:T(8,128)(2,1)S(1)} copy-done((bf16[32,2048]{1,0:T(8,128)(2,1)S(1)}, bf16[32,2048]{1,0:T(8,128)(2,1)}, u32[]{:S(2)}) %copy-start.4) | copy-done | bytes 131096
  19.4 2.2 %forward_rest_a.1.refs_6_.refs_2_ = bf16[8,96,256]{2,1,0:T(8,128)(2,1)S(1)} custom-call(s32[12,1,16]{2,1,0:T(1,128)S(1)} %bitcast.6, s32[1,16]{1,0:T(1,128)S(1)} %bitcast.13, bf16[32,2048]{1,0:T(8,128)(2,1)} %collective-permute-done.refs_0_.refs_1_, bf16[32,2048]{1,0:T(8,128)(2,1)S(1)} %copy-done.4, bf16[32,2048]{1,0:T(8,128)(2,1)} %collective-permute-done.2.refs_2_.refs_3_, ...), custom_call_target="tpu_custom_call" | custom-call | flops 805306368 | bytes 6291456 | tf_op jit(solution)/shard_map/forward_rest_a/pallas_call | solution.py:417
  21.7 0.0 copy-start.2
  21.7 0.6 %collective-permute-start.5 = (bf16[8,96,256]{2,1,0:T(8,128)(2,1)S(1)}, bf16[8,96,256]{2,1,0:T(8,128)(2,1)S(1)}, u32[]{:S(2)}, u32[]{:S(2)}) collective-permute-start(bf16[8,96,256]{2,1,0:T(8,128)(2,1)S(1)} %forward_rest_a.1.refs_6_.refs_2_), channel_id=1, source_target_pairs={{0,2},{2,0},{1,3},{3,1},{4,6},{6,4},{5,7},{7,5},{8,10},{10,8},{9,1... | collective-permute-start | bytes 1179656 | tf_op jit(solution)/shard_map/ppermute | solution.py:339
  22.3 5.4 %forward_b.1 = (bf16[8,64,256]{2,1,0:T(8,128)(2,1)S(1)}, bf16[8,64,256]{2,1,0:T(8,128)(2,1)S(1)}, bf16[8,1,12,128,128]{4,3,2,1,0:T(8,128)(2,1)S(1)}, bf16[8,1,12...) custom-call(s32[12,1,16]{2,1,0:T(1,128)S(1)} %bitcast.7, s32[1,16]{1,0:T(1,128)S(1)} %bitcast.14, ...), custom_call_target="tpu_custom_call" | custom-call | flops 4026531840 | bytes 31457280 | tf_op jit(solution)/shard_map/forward_b/pallas_call | solution.py:429
  27.7 1.6 %collective-permute-start.7 = (bf16[8,64,256]{2,1,0:T(8,128)(2,1)S(1)}, bf16[8,64,256]{2,1,0:T(8,128)(2,1)S(1)}, u32[]{:S(2)}, u32[]{:S(2)}) collective-permute-start(bf16[8,64,256]{2,1,0:T(8,128)(2,1)S(1)} %get-tuple-element.37.refs_6_.refs_0_), channel_id=1, source_target_pairs={{0,2},{2,0},{1,3},{3,1},{4,6},{6,4},{5,7},{7,5},{8,10},{10,8},{9,1... | collective-permute-start | bytes 786440 | tf_op jit(solution)/shard_map/ppermute | solution.py:339
  29.3 0.1 pad_add_fusion.meta_ref
  29.4 0.5 collective-permute-start.6
  29.9 3.8 %collective-permute-done.5.refs_3_ = bf16[8,96,256]{2,1,0:T(8,128)(2,1)S(1)} collective-permute-done((bf16[8,96,256]{2,1,0:T(8,128)(2,1)S(1)}, bf16[8,96,256]{2,1,0:T(8,128)(2,1)S(1)}, u32[]{:S(2)}, u32[]{:S(2)}) %collective-permute-start.5) | collective-permute-done | bytes 393248 | tf_op jit(solution)/shard_map/ppermute | solution.py:339
  33.7 7.7 %first_half.1 = (bf16[16,1,12,128,128]{4,3,2,1,0:T(8,128)(2,1)}, bf16[16,1,12,128,128]{4,3,2,1,0:T(8,128)(2,1)}, bf16[64,2048]{1,0:T(8,128)(2,1)}, f32[16,64,128]{2,1,0:T(8,128)S(1)}, f32[16,64,128]{2,1,0:T(8,128)S(1)}) custom-call(s32[3]{0:T(128)S(1)} %pad_add_fusion.meta_ref, s32[12,1,16]{2,1,0:T(1,128)S(1)} %bitcast.8, s32[1,16]{1,0:T(1,128)S(1)} %bitcast.15, ...), custom_call_target="tpu_custom_call" | custom-call | flops 1610612736 | bytes 6291456 | tf_op jit(solution)/shard_map/first_half/pallas_call | solution.py:449
  41.5 2.9 %second_half.2 = (bf16[8,64,256]{2,1,0:T(8,128)(2,1)S(1)}, bf16[64,1024]{1,0:T(8,128)(2,1)S(1)}, bf16[32,2048]{1,0:T(8,128)(2,1)S(1)}, bf16[32,2048]{1,0:T(8,128)(2,1)S(1)}) custom-call(s32[3]{0:T(128)S(1)} %pad_add_fusion.meta_ref, s32[12,1,16]{2,1,0:T(1,128)S(1)} %bitcast.9, s32[1,16]{1,0:T(1,128)S(1)} %bitcast.16, ...), custom_call_target="tpu_custom_call" | custom-call | flops 402653184 | bytes 6291456 | tf_op jit(solution)/shard_map/second_half/pallas_call | solution.py:482
  44.3 0.1 collective-permute-start.8
  44.4 1.3 %collective-permute-done.8.right_ref = bf16[32,2048]{1,0:T(8,128)(2,1)S(1)} collective-permute-done((bf16[32,2048]{1,0:T(8,128)(2,1)S(1)}, bf16[32,2048]{1,0:T(8,128)(2,1)S(1)}, u32[]{:S(2)}, u32[]{:S(2)}) %collective-permute-start.8) | collective-permute-done | bytes 131104 | tf_op jit(solution)/shard_map/ppermute | solution.py:339
  45.8 0.4 collective-permute-start.10
  46.2 3.0 %second_half.3 = (bf16[8,64,256]{2,1,0:T(8,128)(2,1)S(1)}, bf16[64,1024]{1,0:T(8,128)(2,1)S(1)}, bf16[32,2048]{1,0:T(8,128)(2,1)S(1)}, bf16[32,2048]{1,0:T(8,128)(2,1)S(1)}) custom-call(s32[3]{0:T(128)S(1)} %pad_add_fusion.meta_ref, s32[12,1,16]{2,1,0:T(1,128)S(1)} %bitcast.10, s32[1,16]{1,0:T(1,128)S(1)} %bitcast.17, ...), custom_call_target="tpu_custom_call" | custom-call | flops 402653184 | bytes 6291456 | tf_op jit(solution)/shard_map/second_half/pallas_call | solution.py:482
  49.2 0.5 collective-permute-start.9
  49.7 4.0 %last_grads.1 = (bf16[16,1,12,128,128]{4,3,2,1,0:T(8,128)(2,1)}, bf16[16,1,12,128,128]{4,3,2,1,0:T(8,128)(2,1)}, bf16[64,2048]{1,0:T(8,128)(2,1)}, f32[8,128]{1,0:T(8,128)S(1)}) custom-call(s32[3]{0:T(128)S(1)} %pad_add_fusion.meta_ref, s32[12,1,16]{2,1,0:T(1,128)S(1)} %bitcast.11, ...), custom_call_target="tpu_custom_call", output_to_operand_aliasing={{0}: (8, {}), {1}: (9, {}), {2}: (10, {})} | custom-call | flops 8053063680 | bytes 62914560 | tf_op jit(solution)/shard_map/last_grads/pallas_call | solution.py:523
  53.8 2.9 %collective-permute-done.9.refs_1_ = bf16[32,2048]{1,0:T(8,128)(2,1)S(1)} collective-permute-done((bf16[32,2048]{1,0:T(8,128)(2,1)S(1)}, bf16[32,2048]{1,0:T(8,128)(2,1)S(1)}, u32[]{:S(2)}, u32[]{:S(2)}) %collective-permute-start.9) | collective-permute-done | bytes 131104 | tf_op jit(solution)/shard_map/ppermute | solution.py:339
  56.6 0.1 sum_shards.1
  56.7 0.1 collective-permute-start.11
  56.8 1.3 %collective-permute-done.11 = bf16[32,2048]{1,0:T(8,128)(2,1)S(1)} collective-permute-done((bf16[32,2048]{1,0:T(8,128)(2,1)S(1)}, bf16[32,2048]{1,0:T(8,128)(2,1)S(1)}, u32[]{:S(2)}, u32[]{:S(2)}) %collective-permute-start.11) | collective-permute-done | bytes 131104 | tf_op jit(solution)/shard_map/ppermute | solution.py:339
  58.1 0.7 %add_convert_fusion = bf16[32,2048]{1,0:T(8,128)(2,1)} fusion(f32[32,2048]{1,0:T(8,128)S(1)} %get-tuple-element.56, bf16[32,2048]{1,0:T(8,128)(2,1)S(1)} %collective-permute-done.11), kind=kLoop, calls=%fused_computation | loop fusion | flops 196608 | bytes 524288 | tf_op jit(solution)/shard_map/convert_element_type | solution.py:554
  (20 shorter events, 0.1 us)
Async XLA Ops:
  0.6 13.6 %collective-permute-start.1 = (bf16[32,2048]{1,0:T(8,128)(2,1)}, bf16[32,2048]{1,0:T(8,128)(2,1)S(1)}, u32[]{:S(2)}, u32[]{:S(2)}) collective-permute-start(bf16[32,2048]{1,0:T(8,128)(2,1)} %refs_0_.1), channel_id=1, source_target_pairs={{0,8},{1,13},{4,12},{5,9},{8,0},{9,5},{12,4},{13,1},{2,10},{3,15},... | collective-permute-start | bytes 393224 | tf_op jit(solution)/shard_map/ppermute | solution.py:345
  4.7 10.7 %collective-permute-start.3 = (bf16[64,2048]{1,0:T(8,128)(2,1)}, bf16[64,2048]{1,0:T(8,128)(2,1)S(1)}, u32[]{:S(2)}, u32[]{:S(2)}) collective-permute-start(bf16[64,2048]{1,0:T(8,128)(2,1)} %refs_2_.3), channel_id=1, source_target_pairs={{0,2},{2,0},{1,3},{3,1},{4,6},{6,4},{5,7},{7,5},{8,10},{10,8},{9,1... | collective-permute-start | bytes 786440 | tf_op jit(solution)/shard_map/ppermute | solution.py:339
  6.2 9.3 %collective-permute-start = (bf16[32,2048]{1,0:T(8,128)(2,1)}, bf16[32,2048]{1,0:T(8,128)(2,1)}, u32[]{:S(2)}, u32[]{:S(2)}) collective-permute-start(bf16[32,2048]{1,0:T(8,128)(2,1)} %refs_0_.1), channel_id=1, source_target_pairs={{0,4},{4,0},{8,12},{12,8},{1,5},{5,1},{9,13},{13,9},{2,6},{6,2},{1... | collective-permute-start | bytes 393224 | tf_op jit(solution)/shard_map/ppermute | solution.py:339
  7.8 8.8 %copy-start.5 = (s32[16,1,12]{0,1,2:T(1,128)S(1)}, s32[16,1,12]{0,1,2:T(1,128)}, u32[]{:S(2)}) copy-start(s32[16,1,12]{0,1,2:T(1,128)} %param.9) | copy-start | bytes 2308
  7.8 8.8 %copy-start.7 = (s32[16,1]{0,1:T(1,128)S(1)}, s32[16,1]{0,1:T(1,128)}, u32[]{:S(2)}) copy-start(s32[16,1]{0,1:T(1,128)} %param.10) | copy-start | bytes 196
  12.6 1.7 %copy-start = (bf16[8,1,12,128,128]{4,3,2,1,0:T(8,128)(2,1)}, bf16[8,1,12,128,128]{4,3,2,1,0:T(8,128)(2,1)S(1)}, u32[]{:S(2)}) copy-start(bf16[8,1,12,128,128]{4,3,2,1,0:T(8,128)(2,1)S(1)} %get-tuple-element.33.refs_4_) | copy-start | bytes 9437188
  14.2 0.7 %copy-start.3 = (bf16[32,2048]{1,0:T(8,128)(2,1)}, bf16[32,2048]{1,0:T(8,128)(2,1)S(1)}, u32[]{:S(2)}) copy-start(bf16[32,2048]{1,0:T(8,128)(2,1)S(1)} %collective-permute-done.1.x_ref.refs_1_.refs_2_) | copy-start | bytes 393220
  14.9 1.7 %collective-permute-start.2 = (bf16[32,2048]{1,0:T(8,128)(2,1)}, bf16[32,2048]{1,0:T(8,128)(2,1)}, u32[]{:S(2)}, u32[]{:S(2)}) collective-permute-start(bf16[32,2048]{1,0:T(8,128)(2,1)} %after_own.1), channel_id=1, source_target_pairs={{0,1},{1,0},{2,3},{3,2},{4,5},{5,4},{6,7},{7,6},{8,9},{9,8},{10,11... | collective-permute-start | bytes 393224 | tf_op jit(solution)/shard_map/ppermute | solution.py:339
  14.9 7.3 %collective-permute-start.4 = (bf16[8,32,256]{2,1,0:T(8,128)(2,1)S(1)}, bf16[8,32,256]{2,1,0:T(8,128)(2,1)}, u32[]{:S(2)}, u32[]{:S(2)}) collective-permute-start(bf16[8,32,256]{2,1,0:T(8,128)(2,1)S(1)} %get-tuple-element.31._.refs_0_), channel_id=1, source_target_pairs={{0,2},{2,0},{1,3},{3,1},{4,6},{6,4},{5,7},{7,5},{8,10},{10,8},{9,1... | collective-permute-start | bytes 393224 | tf_op jit(solution)/shard_map/ppermute | solution.py:339
  16.6 1.9 %copy-start.1 = (bf16[8,1,12,128,128]{4,3,2,1,0:T(8,128)(2,1)S(1)}, bf16[8,1,12,128,128]{4,3,2,1,0:T(8,128)(2,1)}, u32[]{:S(2)}) copy-start(bf16[8,1,12,128,128]{4,3,2,1,0:T(8,128)(2,1)} %copy-done) | copy-start | bytes 9437188
  18.5 0.9 %copy-start.4 = (bf16[32,2048]{1,0:T(8,128)(2,1)S(1)}, bf16[32,2048]{1,0:T(8,128)(2,1)}, u32[]{:S(2)}) copy-start(bf16[32,2048]{1,0:T(8,128)(2,1)} %copy-done.3) | copy-start | bytes 393220
  19.4 2.8 %copy-start.6 = (bf16[32,2048]{1,0:T(8,128)(2,1)S(1)}, bf16[32,2048]{1,0:T(8,128)(2,1)}, u32[]{:S(2)}) copy-start(bf16[32,2048]{1,0:T(8,128)(2,1)} %refs_0_.1) | copy-start | bytes 393220
  21.7 12.0 %copy-start.2 = (bf16[64,2048]{1,0:T(8,128)(2,1)S(1)}, bf16[64,2048]{1,0:T(8,128)(2,1)}, u32[]{:S(2)}) copy-start(bf16[64,2048]{1,0:T(8,128)(2,1)} %refs_2_.3) | copy-start | bytes 786436
  21.7 12.0 %collective-permute-start.5 = (bf16[8,96,256]{2,1,0:T(8,128)(2,1)S(1)}, bf16[8,96,256]{2,1,0:T(8,128)(2,1)S(1)}, u32[]{:S(2)}, u32[]{:S(2)}) collective-permute-start(bf16[8,96,256]{2,1,0:T(8,128)(2,1)S(1)} %forward_rest_a.1.refs_6_.refs_2_), channel_id=1, source_target_pairs={{0,2},{2,0},{1,3},{3,1},{4,6},{6,4},{5,7},{7,5},{8,10},{10,8},{9,1... | collective-permute-start | bytes 1179656 | tf_op jit(solution)/shard_map/ppermute | solution.py:339
  27.7 13.7 %collective-permute-start.7 = (bf16[8,64,256]{2,1,0:T(8,128)(2,1)S(1)}, bf16[8,64,256]{2,1,0:T(8,128)(2,1)S(1)}, u32[]{:S(2)}, u32[]{:S(2)}) collective-permute-start(bf16[8,64,256]{2,1,0:T(8,128)(2,1)S(1)} %get-tuple-element.37.refs_6_.refs_0_), channel_id=1, source_target_pairs={{0,2},{2,0},{1,3},{3,1},{4,6},{6,4},{5,7},{7,5},{8,10},{10,8},{9,1... | collective-permute-start | bytes 786440 | tf_op jit(solution)/shard_map/ppermute | solution.py:339
  29.4 16.8 %collective-permute-start.6 = (bf16[8,64,256]{2,1,0:T(8,128)(2,1)S(1)}, bf16[8,64,256]{2,1,0:T(8,128)(2,1)S(1)}, u32[]{:S(2)}, u32[]{:S(2)}) collective-permute-start(bf16[8,64,256]{2,1,0:T(8,128)(2,1)S(1)} %get-tuple-element.38.refs_7_.refs_0_), channel_id=1, source_target_pairs={{0,2},{2,0},{1,3},{3,1},{4,6},{6,4},{5,7},{7,5},{8,10},{10,8},{9,1... | collective-permute-start | bytes 786440 | tf_op jit(solution)/shard_map/ppermute | solution.py:339
  44.3 1.4 %collective-permute-start.8 = (bf16[32,2048]{1,0:T(8,128)(2,1)S(1)}, bf16[32,2048]{1,0:T(8,128)(2,1)S(1)}, u32[]{:S(2)}, u32[]{:S(2)}) collective-permute-start(bf16[32,2048]{1,0:T(8,128)(2,1)S(1)} %get-tuple-element.42), channel_id=1, source_target_pairs={{0,1},{1,0},{2,3},{3,2},{4,5},{5,4},{6,7},{7,6},{8,9},{9,8},{10,11... | collective-permute-start | bytes 393224 | tf_op jit(solution)/shard_map/ppermute | solution.py:339
  45.8 10.8 %collective-permute-start.10 = (bf16[32,2048]{1,0:T(8,128)(2,1)S(1)}, bf16[32,2048]{1,0:T(8,128)(2,1)S(1)}, u32[]{:S(2)}, u32[]{:S(2)}) collective-permute-start(bf16[32,2048]{1,0:T(8,128)(2,1)S(1)} %add_cores.1.refs_4_), channel_id=1, source_target_pairs={{0,8},{1,13},{4,12},{5,9},{8,0},{9,5},{12,4},{13,1},{2,10},{3,15},... | collective-permute-start | bytes 393224 | tf_op jit(solution)/shard_map/ppermute | solution.py:345
  49.2 7.4 %collective-permute-start.9 = (bf16[32,2048]{1,0:T(8,128)(2,1)S(1)}, bf16[32,2048]{1,0:T(8,128)(2,1)S(1)}, u32[]{:S(2)}, u32[]{:S(2)}) collective-permute-start(bf16[32,2048]{1,0:T(8,128)(2,1)S(1)} %get-tuple-element.54), channel_id=1, source_target_pairs={{0,4},{4,0},{8,12},{12,8},{1,5},{5,1},{9,13},{13,9},{2,6},{6,2},{1... | collective-permute-start | bytes 393224 | tf_op jit(solution)/shard_map/ppermute | solution.py:339
  56.7 1.4 %collective-permute-start.11 = (bf16[32,2048]{1,0:T(8,128)(2,1)S(1)}, bf16[32,2048]{1,0:T(8,128)(2,1)S(1)}, u32[]{:S(2)}, u32[]{:S(2)}) collective-permute-start(bf16[32,2048]{1,0:T(8,128)(2,1)S(1)} %get-tuple-element.57), channel_id=1, source_target_pairs={{0,1},{1,0},{2,3},{3,2},{4,5},{5,4},{6,7},{7,6},{8,9},{9,8},{10,11... | collective-permute-start | bytes 393224 | tf_op jit(solution)/shard_map/ppermute | solution.py:339

commit v2 on v1

--- a/solution.py
+++ b/solution.py
@@ -10,7 +10,7 @@
 F32 = jnp.float32
 BF16 = jnp.bfloat16
 MIB = 1 << 20
-WINDOW = 3
+WINDOW = 5
 VMEM_SPEC = pl.BlockSpec(memory_space=pltpu.VMEM)
 SMEM_SPEC = pl.BlockSpec(memory_space=pltpu.SMEM)
 ANY_SPEC = pl.BlockSpec(memory_space=pl.ANY)
@@ -48,14 +48,6 @@
     ).astype(BF16)
 
 
-def forward_kernel(members, first, rows_ref, counts_ref, *refs):
-    xs = refs[:members]
-    gate_ref, up_ref = refs[members : members + 2]
-    part_ref = refs[-1]
-    for c in range(gate_ref.shape[0]):
-        part_ref[c] = forward_column(c, first, (rows_ref, counts_ref), xs, gate_ref, up_ref)
-
-
 def windowed(copies, cols):
     for c in range(min(WINDOW, cols)):
         for copy in copies(c):
@@ -71,8 +63,8 @@
     return arrive
 
 
-def forward_own_kernel(x_hbm, rows_hbm, counts_hbm, gate_hbm, up_hbm, part_ref, gate_ref, up_ref, *scratch):
-    x_ref, rows_ref, counts_ref, sems, small_sems = scratch
+def forward_own_kernel(x_hbm, rows_hbm, counts_hbm, gate_hbm, up_hbm, part_ref, *scratch):
+    x_ref, rows_ref, counts_ref, gate_ref, up_ref, sems, small_sems = scratch
     cols = gate_ref.shape[0]
 
     def copies(c):
@@ -95,6 +87,24 @@
         part_ref[c] = forward_column(c, 0, (rows_ref, counts_ref), [x_ref], gate_ref, up_ref)
 
 
+def forward_kernel(members, rows_ref, counts_ref, *refs):
+    xs = refs[:members]
+    gate_hbm, up_hbm = refs[members : members + 2]
+    part_ref, gate_ref, up_ref, sems = refs[-4:]
+
+    def copies(c):
+        return (
+            pltpu.make_async_copy(gate_hbm.at[c], gate_ref.at[c], sems.at[0, c]),
+            pltpu.make_async_copy(up_hbm.at[c], up_ref.at[c], sems.at[1, c]),
+        )
+
+    cols = gate_ref.shape[0]
+    arrive = windowed(copies, cols)
+    for c in range(cols):
+        arrive(c)
+        part_ref[c] = forward_column(c, 0, (rows_ref, counts_ref), xs, gate_ref, up_ref)
+
+
 def load_forward_kernel(members, groups, first, turn, rows_ref, counts_ref, *refs):
     xs = refs[:members]
     gate_hbm, up_hbm = refs[members : members + 2]
@@ -111,8 +121,14 @@
     arrive = windowed(copies, cols)
     if turn:
         turned_ref = outs[-2]
+        identity = (
+            lax.broadcasted_iota(jnp.int32, (tile, tile), 0) == lax.broadcasted_iota(jnp.int32, (tile, tile), 1)
+        ).astype(F32).astype(BF16)
         for r in range(turned_ref.shape[0]):
-            turned_ref[r] = jnp.concatenate([x[:, r * tile : (r + 1) * tile] for x in xs], axis=0).T
+            block = jnp.concatenate([x[:, r * tile : (r + 1) * tile] for x in xs], axis=0)
+            turned_ref[r] = lax.dot_general(
+                identity, block, (((1,), (1,)), ((), ())), preferred_element_type=F32
+            ).astype(BF16)
     for c in range(cols):
         arrive(c)
         part = forward_column(c, first, (rows_ref, counts_ref), xs, gate_ref, up_ref)
@@ -384,19 +400,21 @@
     def from_hbm(*arrays):
         return [pltpu.with_memory_space_constraint(array, pltpu.HBM) for array in arrays]
 
-    near_a, *weights_a = pl.pallas_call(
+    near_a = pl.pallas_call(
         forward_own_kernel,
-        out_shape=(shape(half, shard_rows, 2 * tile), tile_shape(half), tile_shape(half)),
+        out_shape=shape(half, shard_rows, 2 * tile),
         in_specs=[ANY_SPEC] * 5,
-        out_specs=(VMEM_SPEC,) * 3,
+        out_specs=VMEM_SPEC,
         scratch_shapes=[
             pltpu.VMEM((shard_rows, width), BF16),
             pltpu.SMEM(lists[0].shape, jnp.int32),
             pltpu.SMEM(lists[1].shape, jnp.int32),
+            tile_shape(half),
+            tile_shape(half),
             pltpu.SemaphoreType.DMA((2, half)),
             pltpu.SemaphoreType.DMA((3,)),
         ],
-        compiler_params=limit(8),
+        compiler_params=limit(12),
         cost_estimate=cost(shard_rows, half, 1, 1),
         name="forward_own_a",
     )(*from_hbm(features_in, *lists, gate_tiles, up_tiles))
@@ -415,14 +433,15 @@
         xs += [far, swap(ready, "sub", 1)]
 
     rest_a = pl.pallas_call(
-        functools.partial(forward_kernel, shards - 1, 0),
+        functools.partial(forward_kernel, shards - 1),
         out_shape=shape(half, row_total - shard_rows, 2 * tile),
-        in_specs=[SMEM_SPEC] * 2 + [VMEM_SPEC] * (shards + 1) + [ANY_SPEC],
+        in_specs=[SMEM_SPEC] * 2 + [VMEM_SPEC] * (shards - 1) + [ANY_SPEC] * 3,
         out_specs=VMEM_SPEC,
-        compiler_params=limit(8),
+        scratch_shapes=[tile_shape(half), tile_shape(half), pltpu.SemaphoreType.DMA((2, half))],
+        compiler_params=limit(12),
         cost_estimate=cost(row_total, half, 1, 1),
         name="forward_rest_a",
-    )(*lists, *xs[1:], *held(weights_a), cots[-1])
+    )(*lists, *xs[1:], *from_hbm(gate_tiles, up_tiles), cots[-1])
     rest_a = to_owners(rest_a)
 
     rest = cols - half
@@ -465,12 +484,12 @@
             pltpu.VMEM((row_total, half * tile), BF16),
             pltpu.VMEM((half, 1, slots, tile, tile), BF16),
             pltpu.VMEM((half, 1, slots, tile, tile), BF16),
-            pltpu.VMEM((WINDOW + 1, 1, slots, tile, tile), BF16),
-            pltpu.VMEM((WINDOW + 1, 1, slots, tile, tile), BF16),
+            tile_shape(min(WINDOW + 1, half)),
+            tile_shape(min(WINDOW + 1, half)),
             pltpu.SemaphoreType.DMA((2, half)),
             pltpu.SemaphoreType.DMA((shards,)),
             pltpu.SemaphoreType.DMA((d_hidden.shape[0] // shard_rows,)),
-            pltpu.SemaphoreType.DMA((2, WINDOW + 1)),
+            pltpu.SemaphoreType.DMA((2, min(WINDOW + 1, half))),
         ],
         compiler_params=limit(16),
         cost_estimate=cost(row_total, half, 2, 1, 1),

time: 59.2 us -> 56.5 us (0.954)
  local copies, waits for them, and re-layouts: 4.47 us -> 0.02 us
  starting transfers between devices: 11.4 us -> 14.2 us
  waiting for transfers between devices: 10.5 us -> 8.85 us
  Pallas kernels: 30.8 us -> 31.8 us
    unnamed x16 -> x8, local copies, waits for them, and re-layouts: 4.47 us -> 0.02 us
    ppermute x10, starting transfers between devices: 6.94 us -> 9.67 us  [swap(): lax.ppermute(x, axis, [(i, i ^ step) for i in range(lax.axis_size(axis))])]
    pallas_call x2, Pallas kernels: 6.98 us -> 9.48 us  [the longest x1 4.79 us: on_device(): pl.pallas_call(forward_own_kernel, out_shape=shape(half, shard_rows, 2 *...]
    ppermute x10, waiting for transfers between devices: 10.5 us -> 8.85 us  [swap(): lax.ppermute(x, axis, [(i, i ^ step) for i in range(lax.axis_size(axis))])]
    pallas_call x1, Pallas kernels: 0.7 us -> 0.01 us  [on_device(): pl.pallas_call(copy_kernel, out_shape=shape(shard_rows, width), in_specs=...]
    pallas_call x1, Pallas kernels: 5.44 us -> 4.8 us  [on_device(): pl.pallas_call(functools.partial(load_forward_kernel, shards, ((near_rows...]
  transfers between devices with their start and end apart: 12 -> 12, of which waited for: 5 -> 5; matrix products, arithmetic and copies ran while one was open for 0% -> 0% of each run, Pallas kernels for 52% -> 56%
where the time goes in v2:
time: 56.5 us; the launch traced here: 56.4 us
  Pallas kernels  31.8 us (56%)
  starting transfers between devices  14.2 us (25%)
  waiting for transfers between devices  8.85 us (16%)
  other arithmetic  0.76 us (1%)
  between operations  0.76 us (1%)
    ppermute x10, starting transfers between devices, swap(): lax.ppermute(x, axis, [(i, i ^ step) for i in range(lax.axis_size(axis))])  9.67 us
    ppermute x10, waiting for transfers between devices, swap(): lax.ppermute(x, axis, [(i, i ^ step) for i in range(lax.axis_size(axis))])  8.85 us
    pallas_call x1, Pallas kernels, on_device(): pl.pallas_call(functools.partial(first_half_kernel, shards, owners), out_...  7.51 us
    pallas_call x2, Pallas kernels, second_half(): pl.pallas_call(functools.partial(second_half_kernel, members, owners, hal...  5.88 us
    pallas_call x1, Pallas kernels, on_device(): pl.pallas_call(functools.partial(load_forward_kernel, shards, ((near_rows...  4.8 us
    pallas_call x1, Pallas kernels, on_device(): pl.pallas_call(forward_own_kernel, out_shape=shape(half, shard_rows, 2 *...  4.79 us
    pallas_call x1, Pallas kernels, on_device(): pl.pallas_call(functools.partial(forward_kernel, shards - 1), out_shape=s...  4.69 us
    ppermute x2, starting transfers between devices, swap_far(): return lax.ppermute(x, ('tok', 'sub'), pairs)  4.53 us
  transfers between devices with their start and end apart: 12, of which 5 were waited for; matrix products, arithmetic and copies ran while one was open for 0% of the time, Pallas kernels for 56%

profile of v2, /device:TPU:0, one launch (start us, length us, event | category | flops | bytes accessed | tf_op | source)
XLA Modules:
  0.0 56.4 jit_solution(783216874321761907)
XLA Ops:
  0.6 4.1 %collective-permute-start.1 = (bf16[32,2048]{1,0:T(8,128)(2,1)}, bf16[32,2048]{1,0:T(8,128)(2,1)S(1)}, u32[]{:S(2)}, u32[]{:S(2)}) collective-permute-start(bf16[32,2048]{1,0:T(8,128)(2,1)} %refs_0_.1), channel_id=1, source_target_pairs={{0,8},{1,13},{4,12},{5,9},{8,0},{9,5},{12,4},{13,1},{2,10},{3,15},... | collective-permute-start | bytes 393224 | tf_op jit(solution)/shard_map/ppermute | solution.py:361
  4.7 1.5 %collective-permute-start.3 = (bf16[64,2048]{1,0:T(8,128)(2,1)}, bf16[64,2048]{1,0:T(8,128)(2,1)S(1)}, u32[]{:S(2)}, u32[]{:S(2)}) collective-permute-start(bf16[64,2048]{1,0:T(8,128)(2,1)} %refs_2_.3), channel_id=1, source_target_pairs={{0,2},{2,0},{1,3},{3,1},{4,6},{6,4},{5,7},{7,5},{8,10},{10,8},{9,1... | collective-permute-start | bytes 786440 | tf_op jit(solution)/shard_map/ppermute | solution.py:355
  6.2 1.6 %collective-permute-start = (bf16[32,2048]{1,0:T(8,128)(2,1)}, bf16[32,2048]{1,0:T(8,128)(2,1)S(1)}, u32[]{:S(2)}, u32[]{:S(2)}) collective-permute-start(bf16[32,2048]{1,0:T(8,128)(2,1)} %refs_0_.1), channel_id=1, source_target_pairs={{0,4},{4,0},{8,12},{12,8},{1,5},{5,1},{9,13},{13,9},{2,6},{6,2},{1... | collective-permute-start | bytes 393224 | tf_op jit(solution)/shard_map/ppermute | solution.py:355
  7.8 4.8 %forward_own_a.1._.refs_0_ = bf16[8,32,256]{2,1,0:T(8,128)(2,1)S(1)} custom-call(bf16[32,2048]{1,0:T(8,128)(2,1)} %refs_0_.1, s32[12,1,16]{2,1,0:T(1,128)} %bitcast.5, s32[1,16]{1,0:T(1,128)} %bitcast.12, bf16[16,1,12,128,128]{4,3,2,1,0:T(8,128)(2,1)} %gate_in.1, bf16[16,1,12,128,128]{4,3,2,1,0:T(8,128)(2,1)} %up_in.1), custom_call_target="tpu_custom_call" | custom-call | flops 201326592 | bytes 6291456 | tf_op jit(solution)/shard_map/forward_own_a/pallas_call | solution.py:403
  12.6 0.0 collective-permute-done.1.x_ref.refs_1_.refs_2_
  12.6 0.1 collective-permute-start.2
  12.7 0.6 %collective-permute-start.4 = (bf16[8,32,256]{2,1,0:T(8,128)(2,1)S(1)}, bf16[8,32,256]{2,1,0:T(8,128)(2,1)S(1)}, u32[]{:S(2)}, u32[]{:S(2)}) collective-permute-start(bf16[8,32,256]{2,1,0:T(8,128)(2,1)S(1)} %forward_own_a.1._.refs_0_), channel_id=1, source_target_pairs={{0,2},{2,0},{1,3},{3,1},{4,6},{6,4},{5,7},{7,5},{8,10},{10,8},{9,1... | collective-permute-start | bytes 393224 | tf_op jit(solution)/shard_map/ppermute | solution.py:355
  13.3 0.0 collective-permute-done.refs_0_.refs_1_
  13.3 0.7 %collective-permute-done.2.refs_2_.refs_3_ = bf16[32,2048]{1,0:T(8,128)(2,1)S(1)} collective-permute-done((bf16[32,2048]{1,0:T(8,128)(2,1)S(1)}, bf16[32,2048]{1,0:T(8,128)(2,1)S(1)}, u32[]{:S(2)}, u32[]{:S(2)}) %collective-permute-start.2) | collective-permute-done | bytes 131104 | tf_op jit(solution)/shard_map/ppermute | solution.py:355
  14.1 4.7 %forward_rest_a.1.refs_6_.refs_2_ = bf16[8,96,256]{2,1,0:T(8,128)(2,1)S(1)} custom-call(s32[12,1,16]{2,1,0:T(1,128)S(1)} %bitcast.6, s32[1,16]{1,0:T(1,128)S(1)} %bitcast.13, bf16[32,2048]{1,0:T(8,128)(2,1)S(1)} %collective-permute-done.refs_0_.refs_1_, bf16[32,2048]{1,0:T(8,128)(2,1)S(1)} %collective-permute-done.1.x_ref.refs_1_.refs_2_, ...), custom_call_target="tpu_custom_call" | custom-call | flops 805306368 | bytes 6291456 | tf_op jit(solution)/shard_map/forward_rest_a/pallas_call | solution.py:435
  18.8 0.0 copy-start
  18.8 1.2 %collective-permute-start.5 = (bf16[8,96,256]{2,1,0:T(8,128)(2,1)S(1)}, bf16[8,96,256]{2,1,0:T(8,128)(2,1)S(1)}, u32[]{:S(2)}, u32[]{:S(2)}) collective-permute-start(bf16[8,96,256]{2,1,0:T(8,128)(2,1)S(1)} %forward_rest_a.1.refs_6_.refs_2_), channel_id=1, source_target_pairs={{0,2},{2,0},{1,3},{3,1},{4,6},{6,4},{5,7},{7,5},{8,10},{10,8},{9,1... | collective-permute-start | bytes 1179656 | tf_op jit(solution)/shard_map/ppermute | solution.py:355
  20.0 4.8 %forward_b.1 = (bf16[8,64,256]{2,1,0:T(8,128)(2,1)S(1)}, bf16[8,64,256]{2,1,0:T(8,128)(2,1)S(1)}, bf16[8,1,12,128,128]{4,3,2,1,0:T(8,128)(2,1)S(1)}, bf16[8,1,12...) custom-call(s32[12,1,16]{2,1,0:T(1,128)S(1)} %bitcast.7, s32[1,16]{1,0:T(1,128)S(1)} %bitcast.14, ...), custom_call_target="tpu_custom_call" | custom-call | flops 4026531840 | bytes 31457280 | tf_op jit(solution)/shard_map/forward_b/pallas_call | solution.py:448
  24.8 0.9 %collective-permute-start.7 = (bf16[8,64,256]{2,1,0:T(8,128)(2,1)S(1)}, bf16[8,64,256]{2,1,0:T(8,128)(2,1)S(1)}, u32[]{:S(2)}, u32[]{:S(2)}) collective-permute-start(bf16[8,64,256]{2,1,0:T(8,128)(2,1)S(1)} %get-tuple-element.31.refs_6_.refs_0_), channel_id=1, source_target_pairs={{0,2},{2,0},{1,3},{3,1},{4,6},{6,4},{5,7},{7,5},{8,10},{10,8},{9,1... | collective-permute-start | bytes 786440 | tf_op jit(solution)/shard_map/ppermute | solution.py:355
  25.7 0.1 pad_add_fusion.meta_ref
  25.8 1.2 %collective-permute-start.6 = (bf16[8,64,256]{2,1,0:T(8,128)(2,1)S(1)}, bf16[8,64,256]{2,1,0:T(8,128)(2,1)S(1)}, u32[]{:S(2)}, u32[]{:S(2)}) collective-permute-start(bf16[8,64,256]{2,1,0:T(8,128)(2,1)S(1)} %get-tuple-element.32.refs_7_.refs_0_), channel_id=1, source_target_pairs={{0,2},{2,0},{1,3},{3,1},{4,6},{6,4},{5,7},{7,5},{8,10},{10,8},{9,1... | collective-permute-start | bytes 786440 | tf_op jit(solution)/shard_map/ppermute | solution.py:355
  27.0 3.8 %collective-permute-done.5.refs_3_ = bf16[8,96,256]{2,1,0:T(8,128)(2,1)S(1)} collective-permute-done((bf16[8,96,256]{2,1,0:T(8,128)(2,1)S(1)}, bf16[8,96,256]{2,1,0:T(8,128)(2,1)S(1)}, u32[]{:S(2)}, u32[]{:S(2)}) %collective-permute-start.5) | collective-permute-done | bytes 393248 | tf_op jit(solution)/shard_map/ppermute | solution.py:355
  30.8 7.5 %first_half.1 = (bf16[16,1,12,128,128]{4,3,2,1,0:T(8,128)(2,1)}, bf16[16,1,12,128,128]{4,3,2,1,0:T(8,128)(2,1)}, bf16[64,2048]{1,0:T(8,128)(2,1)}, f32[16,64,128]{2,1,0:T(8,128)S(1)}, f32[16,64,128]{2,1,0:T(8,128)S(1)}) custom-call(s32[3]{0:T(128)S(1)} %pad_add_fusion.meta_ref, s32[12,1,16]{2,1,0:T(1,128)S(1)} %bitcast.8, s32[1,16]{1,0:T(1,128)S(1)} %bitcast.15, ...), custom_call_target="tpu_custom_call" | custom-call | flops 1610612736 | bytes 6291456 | tf_op jit(solution)/shard_map/first_half/pallas_call | solution.py:468
  38.3 0.0 collective-permute-done.7.refs_1_
  38.3 3.0 %second_half.2 = (bf16[8,64,256]{2,1,0:T(8,128)(2,1)S(1)}, bf16[64,1024]{1,0:T(8,128)(2,1)S(1)}, bf16[32,2048]{1,0:T(8,128)(2,1)S(1)}, bf16[32,2048]{1,0:T(8,128)(2,1)S(1)}) custom-call(s32[3]{0:T(128)S(1)} %pad_add_fusion.meta_ref, s32[12,1,16]{2,1,0:T(1,128)S(1)} %bitcast.9, s32[1,16]{1,0:T(1,128)S(1)} %bitcast.16, ...), custom_call_target="tpu_custom_call" | custom-call | flops 402653184 | bytes 6291456 | tf_op jit(solution)/shard_map/second_half/pallas_call | solution.py:501
  41.4 0.1 collective-permute-start.8
  41.4 1.3 %collective-permute-done.8.right_ref = bf16[32,2048]{1,0:T(8,128)(2,1)S(1)} collective-permute-done((bf16[32,2048]{1,0:T(8,128)(2,1)S(1)}, bf16[32,2048]{1,0:T(8,128)(2,1)S(1)}, u32[]{:S(2)}, u32[]{:S(2)}) %collective-permute-start.8) | collective-permute-done | bytes 131104 | tf_op jit(solution)/shard_map/ppermute | solution.py:355
  42.8 0.4 collective-permute-start.10
  43.2 0.0 collective-permute-done.6.refs_1_
  43.2 2.8 %second_half.3 = (bf16[8,64,256]{2,1,0:T(8,128)(2,1)S(1)}, bf16[64,1024]{1,0:T(8,128)(2,1)S(1)}, bf16[32,2048]{1,0:T(8,128)(2,1)S(1)}, bf16[32,2048]{1,0:T(8,128)(2,1)S(1)}) custom-call(s32[3]{0:T(128)S(1)} %pad_add_fusion.meta_ref, s32[12,1,16]{2,1,0:T(1,128)S(1)} %bitcast.10, s32[1,16]{1,0:T(1,128)S(1)} %bitcast.17, ...), custom_call_target="tpu_custom_call" | custom-call | flops 402653184 | bytes 6291456 | tf_op jit(solution)/shard_map/second_half/pallas_call | solution.py:501
  46.1 2.4 %collective-permute-start.9 = (bf16[32,2048]{1,0:T(8,128)(2,1)S(1)}, bf16[32,2048]{1,0:T(8,128)(2,1)S(1)}, u32[]{:S(2)}, u32[]{:S(2)}) collective-permute-start(bf16[32,2048]{1,0:T(8,128)(2,1)S(1)} %get-tuple-element.48), channel_id=1, source_target_pairs={{0,4},{4,0},{8,12},{12,8},{1,5},{5,1},{9,13},{13,9},{2,6},{6,2},{1... | collective-permute-start | bytes 393224 | tf_op jit(solution)/shard_map/ppermute | solution.py:355
  48.5 4.0 %last_grads.1 = (bf16[16,1,12,128,128]{4,3,2,1,0:T(8,128)(2,1)}, bf16[16,1,12,128,128]{4,3,2,1,0:T(8,128)(2,1)}, bf16[64,2048]{1,0:T(8,128)(2,1)}, f32[8,128]{1,0:T(8,128)S(1)}) custom-call(s32[3]{0:T(128)S(1)} %pad_add_fusion.meta_ref, s32[12,1,16]{2,1,0:T(1,128)S(1)} %bitcast.11, ...), custom_call_target="tpu_custom_call", output_to_operand_aliasing={{0}: (8, {}), {1}: (9, {}), {2}: (10, {})} | custom-call | flops 8053063680 | bytes 62914560 | tf_op jit(solution)/shard_map/last_grads/pallas_call | solution.py:542
  52.5 1.7 %collective-permute-done.9.refs_1_ = bf16[32,2048]{1,0:T(8,128)(2,1)S(1)} collective-permute-done((bf16[32,2048]{1,0:T(8,128)(2,1)S(1)}, bf16[32,2048]{1,0:T(8,128)(2,1)S(1)}, u32[]{:S(2)}, u32[]{:S(2)}) %collective-permute-start.9) | collective-permute-done | bytes 131104 | tf_op jit(solution)/shard_map/ppermute | solution.py:355
  54.2 0.1 sum_shards.1
  54.3 0.2 collective-permute-start.11
  54.5 1.2 %collective-permute-done.11 = bf16[32,2048]{1,0:T(8,128)(2,1)S(1)} collective-permute-done((bf16[32,2048]{1,0:T(8,128)(2,1)S(1)}, bf16[32,2048]{1,0:T(8,128)(2,1)S(1)}, u32[]{:S(2)}, u32[]{:S(2)}) %collective-permute-start.11) | collective-permute-done | bytes 131104 | tf_op jit(solution)/shard_map/ppermute | solution.py:355
  55.7 0.7 %add_convert_fusion = bf16[32,2048]{1,0:T(8,128)(2,1)} fusion(f32[32,2048]{1,0:T(8,128)S(1)} %get-tuple-element.50, bf16[32,2048]{1,0:T(8,128)(2,1)S(1)} %collective-permute-done.11), kind=kLoop, calls=%fused_computation | loop fusion | flops 196608 | bytes 524288 | tf_op jit(solution)/shard_map/convert_element_type | solution.py:573
  (12 shorter events, 0.1 us)
Async XLA Ops:
  0.6 12.0 %collective-permute-start.1 = (bf16[32,2048]{1,0:T(8,128)(2,1)}, bf16[32,2048]{1,0:T(8,128)(2,1)S(1)}, u32[]{:S(2)}, u32[]{:S(2)}) collective-permute-start(bf16[32,2048]{1,0:T(8,128)(2,1)} %refs_0_.1), channel_id=1, source_target_pairs={{0,8},{1,13},{4,12},{5,9},{8,0},{9,5},{12,4},{13,1},{2,10},{3,15},... | collective-permute-start | bytes 393224 | tf_op jit(solution)/shard_map/ppermute | solution.py:361
  4.7 9.3 %collective-permute-start.3 = (bf16[64,2048]{1,0:T(8,128)(2,1)}, bf16[64,2048]{1,0:T(8,128)(2,1)S(1)}, u32[]{:S(2)}, u32[]{:S(2)}) collective-permute-start(bf16[64,2048]{1,0:T(8,128)(2,1)} %refs_2_.3), channel_id=1, source_target_pairs={{0,2},{2,0},{1,3},{3,1},{4,6},{6,4},{5,7},{7,5},{8,10},{10,8},{9,1... | collective-permute-start | bytes 786440 | tf_op jit(solution)/shard_map/ppermute | solution.py:355
  6.2 7.1 %collective-permute-start = (bf16[32,2048]{1,0:T(8,128)(2,1)}, bf16[32,2048]{1,0:T(8,128)(2,1)S(1)}, u32[]{:S(2)}, u32[]{:S(2)}) collective-permute-start(bf16[32,2048]{1,0:T(8,128)(2,1)} %refs_0_.1), channel_id=1, source_target_pairs={{0,4},{4,0},{8,12},{12,8},{1,5},{5,1},{9,13},{13,9},{2,6},{6,2},{1... | collective-permute-start | bytes 393224 | tf_op jit(solution)/shard_map/ppermute | solution.py:355
  7.8 6.3 %copy-start.1 = (s32[16,1,12]{0,1,2:T(1,128)S(1)}, s32[16,1,12]{0,1,2:T(1,128)}, u32[]{:S(2)}) copy-start(s32[16,1,12]{0,1,2:T(1,128)} %param.9) | copy-start | bytes 2308
  7.8 6.3 %copy-start.3 = (s32[16,1]{0,1:T(1,128)S(1)}, s32[16,1]{0,1:T(1,128)}, u32[]{:S(2)}) copy-start(s32[16,1]{0,1:T(1,128)} %param.10) | copy-start | bytes 196
  12.6 1.4 %collective-permute-start.2 = (bf16[32,2048]{1,0:T(8,128)(2,1)S(1)}, bf16[32,2048]{1,0:T(8,128)(2,1)S(1)}, u32[]{:S(2)}, u32[]{:S(2)}) collective-permute-start(bf16[32,2048]{1,0:T(8,128)(2,1)S(1)} %after_own.1), channel_id=1, source_target_pairs={{0,1},{1,0},{2,3},{3,2},{4,5},{5,4},{6,7},{7,6},{8,9},{9,8},{10,11... | collective-permute-start | bytes 393224 | tf_op jit(solution)/shard_map/ppermute | solution.py:355
  12.7 7.3 %collective-permute-start.4 = (bf16[8,32,256]{2,1,0:T(8,128)(2,1)S(1)}, bf16[8,32,256]{2,1,0:T(8,128)(2,1)S(1)}, u32[]{:S(2)}, u32[]{:S(2)}) collective-permute-start(bf16[8,32,256]{2,1,0:T(8,128)(2,1)S(1)} %forward_own_a.1._.refs_0_), channel_id=1, source_target_pairs={{0,2},{2,0},{1,3},{3,1},{4,6},{6,4},{5,7},{7,5},{8,10},{10,8},{9,1... | collective-permute-start | bytes 393224 | tf_op jit(solution)/shard_map/ppermute | solution.py:355
  13.3 6.7 %copy-start.2 = (bf16[32,2048]{1,0:T(8,128)(2,1)S(1)}, bf16[32,2048]{1,0:T(8,128)(2,1)}, u32[]{:S(2)}) copy-start(bf16[32,2048]{1,0:T(8,128)(2,1)} %refs_0_.1) | copy-start | bytes 393220
  18.8 12.0 %copy-start = (bf16[64,2048]{1,0:T(8,128)(2,1)S(1)}, bf16[64,2048]{1,0:T(8,128)(2,1)}, u32[]{:S(2)}) copy-start(bf16[64,2048]{1,0:T(8,128)(2,1)} %refs_2_.3) | copy-start | bytes 786436
  18.8 12.0 %collective-permute-start.5 = (bf16[8,96,256]{2,1,0:T(8,128)(2,1)S(1)}, bf16[8,96,256]{2,1,0:T(8,128)(2,1)S(1)}, u32[]{:S(2)}, u32[]{:S(2)}) collective-permute-start(bf16[8,96,256]{2,1,0:T(8,128)(2,1)S(1)} %forward_rest_a.1.refs_6_.refs_2_), channel_id=1, source_target_pairs={{0,2},{2,0},{1,3},{3,1},{4,6},{6,4},{5,7},{7,5},{8,10},{10,8},{9,1... | collective-permute-start | bytes 1179656 | tf_op jit(solution)/shard_map/ppermute | solution.py:355
  24.8 13.5 %collective-permute-start.7 = (bf16[8,64,256]{2,1,0:T(8,128)(2,1)S(1)}, bf16[8,64,256]{2,1,0:T(8,128)(2,1)S(1)}, u32[]{:S(2)}, u32[]{:S(2)}) collective-permute-start(bf16[8,64,256]{2,1,0:T(8,128)(2,1)S(1)} %get-tuple-element.31.refs_6_.refs_0_), channel_id=1, source_target_pairs={{0,2},{2,0},{1,3},{3,1},{4,6},{6,4},{5,7},{7,5},{8,10},{10,8},{9,1... | collective-permute-start | bytes 786440 | tf_op jit(solution)/shard_map/ppermute | solution.py:355
  25.8 17.4 %collective-permute-start.6 = (bf16[8,64,256]{2,1,0:T(8,128)(2,1)S(1)}, bf16[8,64,256]{2,1,0:T(8,128)(2,1)S(1)}, u32[]{:S(2)}, u32[]{:S(2)}) collective-permute-start(bf16[8,64,256]{2,1,0:T(8,128)(2,1)S(1)} %get-tuple-element.32.refs_7_.refs_0_), channel_id=1, source_target_pairs={{0,2},{2,0},{1,3},{3,1},{4,6},{6,4},{5,7},{7,5},{8,10},{10,8},{9,1... | collective-permute-start | bytes 786440 | tf_op jit(solution)/shard_map/ppermute | solution.py:355
  41.4 1.4 %collective-permute-start.8 = (bf16[32,2048]{1,0:T(8,128)(2,1)S(1)}, bf16[32,2048]{1,0:T(8,128)(2,1)S(1)}, u32[]{:S(2)}, u32[]{:S(2)}) collective-permute-start(bf16[32,2048]{1,0:T(8,128)(2,1)S(1)} %get-tuple-element.36), channel_id=1, source_target_pairs={{0,1},{1,0},{2,3},{3,2},{4,5},{5,4},{6,7},{7,6},{8,9},{9,8},{10,11... | collective-permute-start | bytes 393224 | tf_op jit(solution)/shard_map/ppermute | solution.py:355
  42.8 11.4 %collective-permute-start.10 = (bf16[32,2048]{1,0:T(8,128)(2,1)S(1)}, bf16[32,2048]{1,0:T(8,128)(2,1)S(1)}, u32[]{:S(2)}, u32[]{:S(2)}) collective-permute-start(bf16[32,2048]{1,0:T(8,128)(2,1)S(1)} %add_cores.1.refs_4_), channel_id=1, source_target_pairs={{0,8},{1,13},{4,12},{5,9},{8,0},{9,5},{12,4},{13,1},{2,10},{3,15},... | collective-permute-start | bytes 393224 | tf_op jit(solution)/shard_map/ppermute | solution.py:361
  46.1 8.1 %collective-permute-start.9 = (bf16[32,2048]{1,0:T(8,128)(2,1)S(1)}, bf16[32,2048]{1,0:T(8,128)(2,1)S(1)}, u32[]{:S(2)}, u32[]{:S(2)}) collective-permute-start(bf16[32,2048]{1,0:T(8,128)(2,1)S(1)} %get-tuple-element.48), channel_id=1, source_target_pairs={{0,4},{4,0},{8,12},{12,8},{1,5},{5,1},{9,13},{13,9},{2,6},{6,2},{1... | collective-permute-start | bytes 393224 | tf_op jit(solution)/shard_map/ppermute | solution.py:355
  54.3 1.4 %collective-permute-start.11 = (bf16[32,2048]{1,0:T(8,128)(2,1)S(1)}, bf16[32,2048]{1,0:T(8,128)(2,1)S(1)}, u32[]{:S(2)}, u32[]{:S(2)}) collective-permute-start(bf16[32,2048]{1,0:T(8,128)(2,1)S(1)} %get-tuple-element.51), channel_id=1, source_target_pairs={{0,1},{1,0},{2,3},{3,2},{4,5},{5,4},{6,7},{7,6},{8,9},{9,8},{10,11... | collective-permute-start | bytes 393224 | tf_op jit(solution)/shard_map/ppermute | solution.py:355

commit v3 on v2

--- a/solution.py
+++ b/solution.py
@@ -10,7 +10,6 @@
 F32 = jnp.float32
 BF16 = jnp.bfloat16
 MIB = 1 << 20
-WINDOW = 5
 VMEM_SPEC = pl.BlockSpec(memory_space=pltpu.VMEM)
 SMEM_SPEC = pl.BlockSpec(memory_space=pltpu.SMEM)
 ANY_SPEC = pl.BlockSpec(memory_space=pl.ANY)
@@ -48,38 +47,54 @@
     ).astype(BF16)
 
 
-def windowed(copies, cols):
-    for c in range(min(WINDOW, cols)):
-        for copy in copies(c):
+def groups_of(cols):
+    edges = [0, -(-cols * 3 // 8), -(-cols * 6 // 8), cols]
+    return [(start, stop) for start, stop in zip(edges, edges[1:]) if start < stop]
+
+
+def load_tiles(first, cols, gate_hbm, up_hbm, gate_ref, up_ref, sems):
+    def copies(i, start, stop):
+        return [
+            pltpu.make_async_copy(
+                source.at[pl.ds(first + start, stop - start)], target.at[pl.ds(start, stop - start)], sems.at[j, i]
+            )
+            for j, (source, target) in enumerate(((gate_hbm, gate_ref), (up_hbm, up_ref)))
+        ]
+
+    started = {start: copies(i, start, stop) for i, (start, stop) in enumerate(groups_of(cols))}
+    for group in started.values():
+        for copy in group:
             copy.start()
 
     def arrive(c):
-        for copy in copies(c):
+        for copy in started.get(c, ()):
             copy.wait()
-        if c + WINDOW < cols:
-            for copy in copies(c + WINDOW):
-                copy.start()
 
     return arrive
+
+
+def store_tiles(first, start, stop, i, gate_ref, up_ref, gate_hbm, up_hbm, sems):
+    copies = [
+        pltpu.make_async_copy(
+            source.at[pl.ds(start, stop - start)], target.at[pl.ds(first + start, stop - start)], sems.at[j, i]
+        )
+        for j, (source, target) in enumerate(((gate_ref, gate_hbm), (up_ref, up_hbm)))
+    ]
+    for copy in copies:
+        copy.start()
+    return copies
 
 
 def forward_own_kernel(x_hbm, rows_hbm, counts_hbm, gate_hbm, up_hbm, part_ref, *scratch):
     x_ref, rows_ref, counts_ref, gate_ref, up_ref, sems, small_sems = scratch
     cols = gate_ref.shape[0]
-
-    def copies(c):
-        return (
-            pltpu.make_async_copy(gate_hbm.at[c], gate_ref.at[c], sems.at[0, c]),
-            pltpu.make_async_copy(up_hbm.at[c], up_ref.at[c], sems.at[1, c]),
-        )
-
     small = [
         pltpu.make_async_copy(source, target, small_sems.at[i])
         for i, (source, target) in enumerate(((rows_hbm, rows_ref), (counts_hbm, counts_ref), (x_hbm, x_ref)))
     ]
     for copy in small:
         copy.start()
-    arrive = windowed(copies, cols)
+    arrive = load_tiles(0, cols, gate_hbm, up_hbm, gate_ref, up_ref, sems)
     for copy in small:
         copy.wait()
     for c in range(cols):
@@ -91,15 +106,8 @@
     xs = refs[:members]
     gate_hbm, up_hbm = refs[members : members + 2]
     part_ref, gate_ref, up_ref, sems = refs[-4:]
-
-    def copies(c):
-        return (
-            pltpu.make_async_copy(gate_hbm.at[c], gate_ref.at[c], sems.at[0, c]),
-            pltpu.make_async_copy(up_hbm.at[c], up_ref.at[c], sems.at[1, c]),
-        )
-
     cols = gate_ref.shape[0]
-    arrive = windowed(copies, cols)
+    arrive = load_tiles(0, cols, gate_hbm, up_hbm, gate_ref, up_ref, sems)
     for c in range(cols):
         arrive(c)
         part_ref[c] = forward_column(c, 0, (rows_ref, counts_ref), xs, gate_ref, up_ref)
@@ -111,14 +119,7 @@
     outs = refs[-(len(groups) + 3 + turn) :]
     parts, gate_ref, up_ref, sems = outs[: len(groups)], outs[-3 - turn], outs[-2 - turn], outs[-1]
     cols, _, _, tile, _ = gate_ref.shape
-
-    def copies(c):
-        return (
-            pltpu.make_async_copy(gate_hbm.at[first + c], gate_ref.at[c], sems.at[0, c]),
-            pltpu.make_async_copy(up_hbm.at[first + c], up_ref.at[c], sems.at[1, c]),
-        )
-
-    arrive = windowed(copies, cols)
+    arrive = load_tiles(first, cols, gate_hbm, up_hbm, gate_ref, up_ref, sems)
     if turn:
         turned_ref = outs[-2]
         identity = (
@@ -242,15 +243,7 @@
     gate_hbm, up_hbm, hidden_hbm, acc_near, acc_far = refs[-15:-10]
     cot_ref, hidden_ref, gate_ref, up_ref, gate_w, up_w, sems, cot_sems, hidden_sems, load_sems = refs[-10:]
     cols, _, slots, tile, _ = gate_ref.shape
-    ring = gate_w.shape[0]
-
-    def loads(c):
-        return (
-            pltpu.make_async_copy(gate_in.at[c], gate_w.at[c % ring], load_sems.at[0, c % ring]),
-            pltpu.make_async_copy(up_in.at[c], up_w.at[c % ring], load_sems.at[1, c % ring]),
-        )
-
-    arrive = windowed(loads, cols)
+    arrive = load_tiles(0, cols, gate_in, up_in, gate_w, up_w, load_sems)
     shard_rows = cot_ref.shape[0] // members
     lists = (rows_ref, counts_ref)
     waits = start_cots(range(members), 0, meta_ref, cots, cot_ref, cot_sems)
@@ -259,18 +252,16 @@
     for wait in waits:
         wait.wait()
     copies = []
-    for c in range(cols):
-        total = jnp.concatenate([total_of(c, near), total_of(c, rest)], axis=0)
-        where = slice(c * tile, (c + 1) * tile)
-        hidden, grads = nonlinear(total, cot_ref[:, where].astype(F32))
-        hidden_ref[:, where] = hidden
-        tile_grads(c, 0, lists, turned_ref, grads, gate_ref, up_ref)
-        copies.append(pltpu.make_async_copy(gate_ref.at[c], gate_hbm.at[c], sems.at[0, c]))
-        copies.append(pltpu.make_async_copy(up_ref.at[c], up_hbm.at[c], sems.at[1, c]))
-        copies[-2].start()
-        copies[-1].start()
-        arrive(c)
-        add_back(c, lists, back_terms(c % ring, grads, gate_w, up_w), (acc_near, acc_far), slots, tile)
+    for i, (start, stop) in enumerate(groups_of(cols)):
+        arrive(start)
+        for c in range(start, stop):
+            total = jnp.concatenate([total_of(c, near), total_of(c, rest)], axis=0)
+            where = slice(c * tile, (c + 1) * tile)
+            hidden, grads = nonlinear(total, cot_ref[:, where].astype(F32))
+            hidden_ref[:, where] = hidden
+            tile_grads(c, 0, lists, turned_ref, grads, gate_ref, up_ref)
+            add_back(c, lists, back_terms(c, grads, gate_w, up_w), (acc_near, acc_far), slots, tile)
+        copies += store_tiles(0, start, stop, i, gate_ref, up_ref, gate_hbm, up_hbm, sems)
     waits = start_hidden(
         range(members),
         0,
@@ -325,14 +316,11 @@
         waits = start_hidden(
             range(members), first * tile, meta_ref, hidden_of, hidden_hbm, shard_rows, hidden_sems
         )
-    for c in range(cols):
-        grads = jnp.concatenate([near_grads[start + c], far_grads[start + c]], axis=0)
-        at = first + start + c
-        tile_grads(c, first + start, (rows_ref, counts_ref), turned_ref, grads, gate_ref, up_ref)
-        waits.append(pltpu.make_async_copy(gate_ref.at[c], gate_hbm.at[at], sems.at[0, c]))
-        waits.append(pltpu.make_async_copy(up_ref.at[c], up_hbm.at[at], sems.at[1, c]))
-        waits[-2].start()
-        waits[-1].start()
+    for i, (begin, end) in enumerate(groups_of(cols)):
+        for c in range(begin, end):
+            grads = jnp.concatenate([near_grads[start + c], far_grads[start + c]], axis=0)
+            tile_grads(c, first + start, (rows_ref, counts_ref), turned_ref, grads, gate_ref, up_ref)
+        waits += store_tiles(first + start, begin, end, i, gate_ref, up_ref, gate_hbm, up_hbm, sems)
     for wait in waits:
         wait.wait()
 
@@ -411,7 +399,7 @@
             pltpu.SMEM(lists[1].shape, jnp.int32),
             tile_shape(half),
             tile_shape(half),
-            pltpu.SemaphoreType.DMA((2, half)),
+            pltpu.SemaphoreType.DMA((2, 3)),
             pltpu.SemaphoreType.DMA((3,)),
         ],
         compiler_params=limit(12),
@@ -437,7 +425,7 @@
         out_shape=shape(half, row_total - shard_rows, 2 * tile),
         in_specs=[SMEM_SPEC] * 2 + [VMEM_SPEC] * (shards - 1) + [ANY_SPEC] * 3,
         out_specs=VMEM_SPEC,
-        scratch_shapes=[tile_shape(half), tile_shape(half), pltpu.SemaphoreType.DMA((2, half))],
+        scratch_shapes=[tile_shape(half), tile_shape(half), pltpu.SemaphoreType.DMA((2, 3))],
         compiler_params=limit(12),
         cost_estimate=cost(row_total, half, 1, 1),
         name="forward_rest_a",
@@ -456,7 +444,7 @@
         ),
         in_specs=[SMEM_SPEC] * 2 + [VMEM_SPEC] * shards + [ANY_SPEC] * 4,
         out_specs=(VMEM_SPEC,) * 5,
-        scratch_shapes=[pltpu.SemaphoreType.DMA((2, rest))],
+        scratch_shapes=[pltpu.SemaphoreType.DMA((2, 3))],
         compiler_params=limit(8),
         cost_estimate=cost(row_total, rest, 1, 1, 5),
         name="forward_b",
@@ -484,14 +472,14 @@
             pltpu.VMEM((row_total, half * tile), BF16),
             pltpu.VMEM((half, 1, slots, tile, tile), BF16),
             pltpu.VMEM((half, 1, slots, tile, tile), BF16),
-            tile_shape(min(WINDOW + 1, half)),
-            tile_shape(min(WINDOW + 1, half)),
-            pltpu.SemaphoreType.DMA((2, half)),
+            tile_shape(half),
+            tile_shape(half),
+            pltpu.SemaphoreType.DMA((2, 3)),
             pltpu.SemaphoreType.DMA((shards,)),
             pltpu.SemaphoreType.DMA((d_hidden.shape[0] // shard_rows,)),
-            pltpu.SemaphoreType.DMA((2, min(WINDOW + 1, half))),
+            pltpu.SemaphoreType.DMA((2, 3)),
         ],
-        compiler_params=limit(16),
+        compiler_params=limit(20),
         cost_estimate=cost(row_total, half, 2, 1, 1),
         name="first_half",
     )(meta, *lists, *from_hbm(gate_tiles, up_tiles), *held([turned]), *near_a, *rest_a, *cots, far_b[0], near_b[0])
@@ -547,7 +535,7 @@
             scratch_shapes=[
                 pltpu.VMEM((count, 1, slots, tile, tile), BF16),
                 pltpu.VMEM((count, 1, slots, tile, tile), BF16),
-                pltpu.SemaphoreType.DMA((2, count)),
+                pltpu.SemaphoreType.DMA((2, 3)),
                 pltpu.SemaphoreType.DMA((d_hidden.shape[0] // shard_rows,)),
             ],
             input_output_aliases={8: 0, 9: 1, 10: 2},

time: 56.5 us -> 55.5 us (0.982)
  Pallas kernels: 31.8 us -> 30.3 us
  starting transfers between devices: 14.2 us -> 15.3 us
  waiting for transfers between devices: 8.85 us -> 8.17 us
    ppermute x10, starting transfers between devices: 9.67 us -> 11 us  [swap(): lax.ppermute(x, axis, [(i, i ^ step) for i in range(lax.axis_size(axis))])]
    pallas_call x1, Pallas kernels: 4.8 us -> 4.08 us  [on_device(): pl.pallas_call(functools.partial(load_forward_kernel, shards, ((near_rows...]
    pallas_call x1, Pallas kernels: 4.79 us -> 4.11 us  [on_device(): pl.pallas_call(forward_own_kernel, out_shape=shape(half, shard_rows, 2 *...]
    ppermute x10, waiting for transfers between devices: 8.85 us -> 8.17 us  [swap(): lax.ppermute(x, axis, [(i, i ^ step) for i in range(lax.axis_size(axis))])]
    pallas_call x1, Pallas kernels: 4.69 us -> 4.04 us  [on_device(): pl.pallas_call(functools.partial(forward_kernel, shards - 1), out_shape=s...]
  transfers between devices with their start and end apart: 12 -> 12, of which waited for: 5 -> 6; matrix products, arithmetic and copies ran while one was open for 0% -> 0% of each run, Pallas kernels for 56% -> 55%
where the time goes in v3:
time: 55.5 us; the launch traced here: 55.4 us
  Pallas kernels  30.3 us (55%)
  starting transfers between devices  15.3 us (28%)
  waiting for transfers between devices  8.17 us (15%)
  other arithmetic  0.76 us (1%)
  between operations  0.76 us (1%)
    ppermute x10, starting transfers between devices, swap(): lax.ppermute(x, axis, [(i, i ^ step) for i in range(lax.axis_size(axis))])  11 us
    ppermute x10, waiting for transfers between devices, swap(): lax.ppermute(x, axis, [(i, i ^ step) for i in range(lax.axis_size(axis))])  8.17 us
    pallas_call x1, Pallas kernels, on_device(): pl.pallas_call(functools.partial(first_half_kernel, shards, owners), out_...  7.76 us
    pallas_call x2, Pallas kernels, second_half(): pl.pallas_call(functools.partial(second_half_kernel, members, owners, hal...  5.88 us
    pallas_call x1, Pallas kernels, last_grads(): pl.pallas_call(functools.partial(last_grads_kernel, shards, half, start,...  4.38 us
    ppermute x2, starting transfers between devices, swap_far(): return lax.ppermute(x, ('tok', 'sub'), pairs)  4.35 us
    pallas_call x1, Pallas kernels, on_device(): pl.pallas_call(forward_own_kernel, out_shape=shape(half, shard_rows, 2 *...  4.11 us
    pallas_call x1, Pallas kernels, on_device(): pl.pallas_call(functools.partial(load_forward_kernel, shards, ((near_rows...  4.08 us
  transfers between devices with their start and end apart: 12, of which 6 were waited for; matrix products, arithmetic and copies ran while one was open for 0% of the time, Pallas kernels for 55%

profile of v3, /device:TPU:0, one launch (start us, length us, event | category | flops | bytes accessed | tf_op | source)
XLA Modules:
  0.0 55.4 jit_solution(9008395497458010049)
XLA Ops:
  0.6 4.1 %collective-permute-start.1 = (bf16[32,2048]{1,0:T(8,128)(2,1)}, bf16[32,2048]{1,0:T(8,128)(2,1)S(1)}, u32[]{:S(2)}, u32[]{:S(2)}) collective-permute-start(bf16[32,2048]{1,0:T(8,128)(2,1)} %refs_0_.1), channel_id=1, source_target_pairs={{0,8},{1,13},{4,12},{5,9},{8,0},{9,5},{12,4},{13,1},{2,10},{3,15},... | collective-permute-start | bytes 393224 | tf_op jit(solution)/shard_map/ppermute | solution.py:349
  4.7 1.5 %collective-permute-start.3 = (bf16[64,2048]{1,0:T(8,128)(2,1)}, bf16[64,2048]{1,0:T(8,128)(2,1)S(1)}, u32[]{:S(2)}, u32[]{:S(2)}) collective-permute-start(bf16[64,2048]{1,0:T(8,128)(2,1)} %refs_2_.3), channel_id=1, source_target_pairs={{0,2},{2,0},{1,3},{3,1},{4,6},{6,4},{5,7},{7,5},{8,10},{10,8},{9,1... | collective-permute-start | bytes 786440 | tf_op jit(solution)/shard_map/ppermute | solution.py:343
  6.2 1.6 %collective-permute-start = (bf16[32,2048]{1,0:T(8,128)(2,1)}, bf16[32,2048]{1,0:T(8,128)(2,1)S(1)}, u32[]{:S(2)}, u32[]{:S(2)}) collective-permute-start(bf16[32,2048]{1,0:T(8,128)(2,1)} %refs_0_.1), channel_id=1, source_target_pairs={{0,4},{4,0},{8,12},{12,8},{1,5},{5,1},{9,13},{13,9},{2,6},{6,2},{1... | collective-permute-start | bytes 393224 | tf_op jit(solution)/shard_map/ppermute | solution.py:343
  7.8 4.1 %forward_own_a.1._.refs_0_ = bf16[8,32,256]{2,1,0:T(8,128)(2,1)S(1)} custom-call(bf16[32,2048]{1,0:T(8,128)(2,1)} %refs_0_.1, s32[12,1,16]{2,1,0:T(1,128)} %bitcast.5, s32[1,16]{1,0:T(1,128)} %bitcast.12, bf16[16,1,12,128,128]{4,3,2,1,0:T(8,128)(2,1)} %gate_in.1, bf16[16,1,12,128,128]{4,3,2,1,0:T(8,128)(2,1)} %up_in.1), custom_call_target="tpu_custom_call" | custom-call | flops 201326592 | bytes 6291456 | tf_op jit(solution)/shard_map/forward_own_a/pallas_call | solution.py:391
  11.9 0.0 collective-permute-done.1.x_ref.refs_1_.refs_2_
  11.9 0.1 collective-permute-start.2
  12.0 1.1 %collective-permute-start.4 = (bf16[8,32,256]{2,1,0:T(8,128)(2,1)S(1)}, bf16[8,32,256]{2,1,0:T(8,128)(2,1)S(1)}, u32[]{:S(2)}, u32[]{:S(2)}) collective-permute-start(bf16[8,32,256]{2,1,0:T(8,128)(2,1)S(1)} %forward_own_a.1._.refs_0_), channel_id=1, source_target_pairs={{0,2},{2,0},{1,3},{3,1},{4,6},{6,4},{5,7},{7,5},{8,10},{10,8},{9,1... | collective-permute-start | bytes 393224 | tf_op jit(solution)/shard_map/ppermute | solution.py:343
  13.2 0.0 collective-permute-done.refs_0_.refs_1_
  13.2 0.2 collective-permute-done.2.refs_2_.refs_3_
  13.4 0.4 collective-permute-done.3.refs_5_.refs_3_
  13.7 4.0 %forward_rest_a.1.refs_6_.refs_2_ = bf16[8,96,256]{2,1,0:T(8,128)(2,1)S(1)} custom-call(s32[12,1,16]{2,1,0:T(1,128)S(1)} %bitcast.6, s32[1,16]{1,0:T(1,128)S(1)} %bitcast.13, bf16[32,2048]{1,0:T(8,128)(2,1)S(1)} %collective-permute-done.refs_0_.refs_1_, bf16[32,2048]{1,0:T(8,128)(2,1)S(1)} %collective-permute-done.1.x_ref.refs_1_.refs_2_, ...), custom_call_target="tpu_custom_call" | custom-call | flops 805306368 | bytes 6291456 | tf_op jit(solution)/shard_map/forward_rest_a/pallas_call | solution.py:423
  17.8 0.0 copy-start
  17.8 1.6 %collective-permute-start.5 = (bf16[8,96,256]{2,1,0:T(8,128)(2,1)S(1)}, bf16[8,96,256]{2,1,0:T(8,128)(2,1)S(1)}, u32[]{:S(2)}, u32[]{:S(2)}) collective-permute-start(bf16[8,96,256]{2,1,0:T(8,128)(2,1)S(1)} %forward_rest_a.1.refs_6_.refs_2_), channel_id=1, source_target_pairs={{0,2},{2,0},{1,3},{3,1},{4,6},{6,4},{5,7},{7,5},{8,10},{10,8},{9,1... | collective-permute-start | bytes 1179656 | tf_op jit(solution)/shard_map/ppermute | solution.py:343
  19.4 4.1 %forward_b.1 = (bf16[8,64,256]{2,1,0:T(8,128)(2,1)S(1)}, bf16[8,64,256]{2,1,0:T(8,128)(2,1)S(1)}, bf16[8,1,12,128,128]{4,3,2,1,0:T(8,128)(2,1)S(1)}, bf16[8,1,12...) custom-call(s32[12,1,16]{2,1,0:T(1,128)S(1)} %bitcast.7, s32[1,16]{1,0:T(1,128)S(1)} %bitcast.14, ...), custom_call_target="tpu_custom_call" | custom-call | flops 4026531840 | bytes 31457280 | tf_op jit(solution)/shard_map/forward_b/pallas_call | solution.py:436
  23.5 0.6 %collective-permute-start.7 = (bf16[8,64,256]{2,1,0:T(8,128)(2,1)S(1)}, bf16[8,64,256]{2,1,0:T(8,128)(2,1)S(1)}, u32[]{:S(2)}, u32[]{:S(2)}) collective-permute-start(bf16[8,64,256]{2,1,0:T(8,128)(2,1)S(1)} %get-tuple-element.31.refs_6_.refs_0_), channel_id=1, source_target_pairs={{0,2},{2,0},{1,3},{3,1},{4,6},{6,4},{5,7},{7,5},{8,10},{10,8},{9,1... | collective-permute-start | bytes 786440 | tf_op jit(solution)/shard_map/ppermute | solution.py:343
  24.0 0.1 pad_add_fusion.meta_ref
  24.1 1.5 %collective-permute-start.6 = (bf16[8,64,256]{2,1,0:T(8,128)(2,1)S(1)}, bf16[8,64,256]{2,1,0:T(8,128)(2,1)S(1)}, u32[]{:S(2)}, u32[]{:S(2)}) collective-permute-start(bf16[8,64,256]{2,1,0:T(8,128)(2,1)S(1)} %get-tuple-element.32.refs_7_.refs_0_), channel_id=1, source_target_pairs={{0,2},{2,0},{1,3},{3,1},{4,6},{6,4},{5,7},{7,5},{8,10},{10,8},{9,1... | collective-permute-start | bytes 786440 | tf_op jit(solution)/shard_map/ppermute | solution.py:343
  25.6 4.2 %collective-permute-done.5.refs_3_ = bf16[8,96,256]{2,1,0:T(8,128)(2,1)S(1)} collective-permute-done((bf16[8,96,256]{2,1,0:T(8,128)(2,1)S(1)}, bf16[8,96,256]{2,1,0:T(8,128)(2,1)S(1)}, u32[]{:S(2)}, u32[]{:S(2)}) %collective-permute-start.5) | collective-permute-done | bytes 393248 | tf_op jit(solution)/shard_map/ppermute | solution.py:343
  29.9 7.8 %first_half.1 = (bf16[16,1,12,128,128]{4,3,2,1,0:T(8,128)(2,1)}, bf16[16,1,12,128,128]{4,3,2,1,0:T(8,128)(2,1)}, bf16[64,2048]{1,0:T(8,128)(2,1)}, f32[16,64,128]{2,1,0:T(8,128)S(1)}, f32[16,64,128]{2,1,0:T(8,128)S(1)}) custom-call(s32[3]{0:T(128)S(1)} %pad_add_fusion.meta_ref, s32[12,1,16]{2,1,0:T(1,128)S(1)} %bitcast.8, s32[1,16]{1,0:T(1,128)S(1)} %bitcast.15, ...), custom_call_target="tpu_custom_call" | custom-call | flops 1610612736 | bytes 6291456 | tf_op jit(solution)/shard_map/first_half/pallas_call | solution.py:456
  37.6 2.9 %second_half.2 = (bf16[8,64,256]{2,1,0:T(8,128)(2,1)S(1)}, bf16[64,1024]{1,0:T(8,128)(2,1)S(1)}, bf16[32,2048]{1,0:T(8,128)(2,1)S(1)}, bf16[32,2048]{1,0:T(8,128)(2,1)S(1)}) custom-call(s32[3]{0:T(128)S(1)} %pad_add_fusion.meta_ref, s32[12,1,16]{2,1,0:T(1,128)S(1)} %bitcast.9, s32[1,16]{1,0:T(1,128)S(1)} %bitcast.16, ...), custom_call_target="tpu_custom_call" | custom-call | flops 402653184 | bytes 6291456 | tf_op jit(solution)/shard_map/second_half/pallas_call | solution.py:489
  40.5 0.1 collective-permute-start.8
  40.6 1.3 %collective-permute-done.8.right_ref = bf16[32,2048]{1,0:T(8,128)(2,1)S(1)} collective-permute-done((bf16[32,2048]{1,0:T(8,128)(2,1)S(1)}, bf16[32,2048]{1,0:T(8,128)(2,1)S(1)}, u32[]{:S(2)}, u32[]{:S(2)}) %collective-permute-start.8) | collective-permute-done | bytes 131104 | tf_op jit(solution)/shard_map/ppermute | solution.py:343
  42.0 0.3 collective-permute-start.10
  42.2 3.0 %second_half.3 = (bf16[8,64,256]{2,1,0:T(8,128)(2,1)S(1)}, bf16[64,1024]{1,0:T(8,128)(2,1)S(1)}, bf16[32,2048]{1,0:T(8,128)(2,1)S(1)}, bf16[32,2048]{1,0:T(8,128)(2,1)S(1)}) custom-call(s32[3]{0:T(128)S(1)} %pad_add_fusion.meta_ref, s32[12,1,16]{2,1,0:T(1,128)S(1)} %bitcast.10, s32[1,16]{1,0:T(1,128)S(1)} %bitcast.17, ...), custom_call_target="tpu_custom_call" | custom-call | flops 402653184 | bytes 6291456 | tf_op jit(solution)/shard_map/second_half/pallas_call | solution.py:489
  45.2 2.8 %collective-permute-start.9 = (bf16[32,2048]{1,0:T(8,128)(2,1)S(1)}, bf16[32,2048]{1,0:T(8,128)(2,1)S(1)}, u32[]{:S(2)}, u32[]{:S(2)}) collective-permute-start(bf16[32,2048]{1,0:T(8,128)(2,1)S(1)} %get-tuple-element.48), channel_id=1, source_target_pairs={{0,4},{4,0},{8,12},{12,8},{1,5},{5,1},{9,13},{13,9},{2,6},{6,2},{1... | collective-permute-start | bytes 393224 | tf_op jit(solution)/shard_map/ppermute | solution.py:343
  48.0 4.4 %last_grads.1 = (bf16[16,1,12,128,128]{4,3,2,1,0:T(8,128)(2,1)}, bf16[16,1,12,128,128]{4,3,2,1,0:T(8,128)(2,1)}, bf16[64,2048]{1,0:T(8,128)(2,1)}, f32[8,128]{1,0:T(8,128)S(1)}) custom-call(s32[3]{0:T(128)S(1)} %pad_add_fusion.meta_ref, s32[12,1,16]{2,1,0:T(1,128)S(1)} %bitcast.11, ...), custom_call_target="tpu_custom_call", output_to_operand_aliasing={{0}: (8, {}), {1}: (9, {}), {2}: (10, {})} | custom-call | flops 8053063680 | bytes 62914560 | tf_op jit(solution)/shard_map/last_grads/pallas_call | solution.py:530
  52.4 0.8 %collective-permute-done.9.refs_1_ = bf16[32,2048]{1,0:T(8,128)(2,1)S(1)} collective-permute-done((bf16[32,2048]{1,0:T(8,128)(2,1)S(1)}, bf16[32,2048]{1,0:T(8,128)(2,1)S(1)}, u32[]{:S(2)}, u32[]{:S(2)}) %collective-permute-start.9) | collective-permute-done | bytes 131104 | tf_op jit(solution)/shard_map/ppermute | solution.py:343
  53.2 0.0 collective-permute-done.10.refs_2_
  53.2 0.1 sum_shards.1
  53.3 0.2 collective-permute-start.11
  53.5 1.2 %collective-permute-done.11 = bf16[32,2048]{1,0:T(8,128)(2,1)S(1)} collective-permute-done((bf16[32,2048]{1,0:T(8,128)(2,1)S(1)}, bf16[32,2048]{1,0:T(8,128)(2,1)S(1)}, u32[]{:S(2)}, u32[]{:S(2)}) %collective-permute-start.11) | collective-permute-done | bytes 131104 | tf_op jit(solution)/shard_map/ppermute | solution.py:343
  54.7 0.7 %add_convert_fusion = bf16[32,2048]{1,0:T(8,128)(2,1)} fusion(f32[32,2048]{1,0:T(8,128)S(1)} %get-tuple-element.50, bf16[32,2048]{1,0:T(8,128)(2,1)S(1)} %collective-permute-done.11), kind=kLoop, calls=%fused_computation | loop fusion | flops 196608 | bytes 524288 | tf_op jit(solution)/shard_map/convert_element_type | solution.py:561
  (12 shorter events, 0.1 us)
Async XLA Ops:
  0.6 11.3 %collective-permute-start.1 = (bf16[32,2048]{1,0:T(8,128)(2,1)}, bf16[32,2048]{1,0:T(8,128)(2,1)S(1)}, u32[]{:S(2)}, u32[]{:S(2)}) collective-permute-start(bf16[32,2048]{1,0:T(8,128)(2,1)} %refs_0_.1), channel_id=1, source_target_pairs={{0,8},{1,13},{4,12},{5,9},{8,0},{9,5},{12,4},{13,1},{2,10},{3,15},... | collective-permute-start | bytes 393224 | tf_op jit(solution)/shard_map/ppermute | solution.py:349
  4.7 9.0 %collective-permute-start.3 = (bf16[64,2048]{1,0:T(8,128)(2,1)}, bf16[64,2048]{1,0:T(8,128)(2,1)S(1)}, u32[]{:S(2)}, u32[]{:S(2)}) collective-permute-start(bf16[64,2048]{1,0:T(8,128)(2,1)} %refs_2_.3), channel_id=1, source_target_pairs={{0,2},{2,0},{1,3},{3,1},{4,6},{6,4},{5,7},{7,5},{8,10},{10,8},{9,1... | collective-permute-start | bytes 786440 | tf_op jit(solution)/shard_map/ppermute | solution.py:343
  6.2 6.9 %collective-permute-start = (bf16[32,2048]{1,0:T(8,128)(2,1)}, bf16[32,2048]{1,0:T(8,128)(2,1)S(1)}, u32[]{:S(2)}, u32[]{:S(2)}) collective-permute-start(bf16[32,2048]{1,0:T(8,128)(2,1)} %refs_0_.1), channel_id=1, source_target_pairs={{0,4},{4,0},{8,12},{12,8},{1,5},{5,1},{9,13},{13,9},{2,6},{6,2},{1... | collective-permute-start | bytes 393224 | tf_op jit(solution)/shard_map/ppermute | solution.py:343
  7.8 5.9 %copy-start.1 = (s32[16,1,12]{0,1,2:T(1,128)S(1)}, s32[16,1,12]{0,1,2:T(1,128)}, u32[]{:S(2)}) copy-start(s32[16,1,12]{0,1,2:T(1,128)} %param.9) | copy-start | bytes 2308
  7.8 5.9 %copy-start.3 = (s32[16,1]{0,1:T(1,128)S(1)}, s32[16,1]{0,1:T(1,128)}, u32[]{:S(2)}) copy-start(s32[16,1]{0,1:T(1,128)} %param.10) | copy-start | bytes 196
  11.9 1.4 %collective-permute-start.2 = (bf16[32,2048]{1,0:T(8,128)(2,1)S(1)}, bf16[32,2048]{1,0:T(8,128)(2,1)S(1)}, u32[]{:S(2)}, u32[]{:S(2)}) collective-permute-start(bf16[32,2048]{1,0:T(8,128)(2,1)S(1)} %after_own.1), channel_id=1, source_target_pairs={{0,1},{1,0},{2,3},{3,2},{4,5},{5,4},{6,7},{7,6},{8,9},{9,8},{10,11... | collective-permute-start | bytes 393224 | tf_op jit(solution)/shard_map/ppermute | solution.py:343
  12.0 7.3 %collective-permute-start.4 = (bf16[8,32,256]{2,1,0:T(8,128)(2,1)S(1)}, bf16[8,32,256]{2,1,0:T(8,128)(2,1)S(1)}, u32[]{:S(2)}, u32[]{:S(2)}) collective-permute-start(bf16[8,32,256]{2,1,0:T(8,128)(2,1)S(1)} %forward_own_a.1._.refs_0_), channel_id=1, source_target_pairs={{0,2},{2,0},{1,3},{3,1},{4,6},{6,4},{5,7},{7,5},{8,10},{10,8},{9,1... | collective-permute-start | bytes 393224 | tf_op jit(solution)/shard_map/ppermute | solution.py:343
  13.2 6.2 %copy-start.2 = (bf16[32,2048]{1,0:T(8,128)(2,1)S(1)}, bf16[32,2048]{1,0:T(8,128)(2,1)}, u32[]{:S(2)}) copy-start(bf16[32,2048]{1,0:T(8,128)(2,1)} %refs_0_.1) | copy-start | bytes 393220
  17.8 12.1 %copy-start = (bf16[64,2048]{1,0:T(8,128)(2,1)S(1)}, bf16[64,2048]{1,0:T(8,128)(2,1)}, u32[]{:S(2)}) copy-start(bf16[64,2048]{1,0:T(8,128)(2,1)} %refs_2_.3) | copy-start | bytes 786436
  17.8 12.1 %collective-permute-start.5 = (bf16[8,96,256]{2,1,0:T(8,128)(2,1)S(1)}, bf16[8,96,256]{2,1,0:T(8,128)(2,1)S(1)}, u32[]{:S(2)}, u32[]{:S(2)}) collective-permute-start(bf16[8,96,256]{2,1,0:T(8,128)(2,1)S(1)} %forward_rest_a.1.refs_6_.refs_2_), channel_id=1, source_target_pairs={{0,2},{2,0},{1,3},{3,1},{4,6},{6,4},{5,7},{7,5},{8,10},{10,8},{9,1... | collective-permute-start | bytes 1179656 | tf_op jit(solution)/shard_map/ppermute | solution.py:343
  23.5 14.2 %collective-permute-start.7 = (bf16[8,64,256]{2,1,0:T(8,128)(2,1)S(1)}, bf16[8,64,256]{2,1,0:T(8,128)(2,1)S(1)}, u32[]{:S(2)}, u32[]{:S(2)}) collective-permute-start(bf16[8,64,256]{2,1,0:T(8,128)(2,1)S(1)} %get-tuple-element.31.refs_6_.refs_0_), channel_id=1, source_target_pairs={{0,2},{2,0},{1,3},{3,1},{4,6},{6,4},{5,7},{7,5},{8,10},{10,8},{9,1... | collective-permute-start | bytes 786440 | tf_op jit(solution)/shard_map/ppermute | solution.py:343
  24.1 18.1 %collective-permute-start.6 = (bf16[8,64,256]{2,1,0:T(8,128)(2,1)S(1)}, bf16[8,64,256]{2,1,0:T(8,128)(2,1)S(1)}, u32[]{:S(2)}, u32[]{:S(2)}) collective-permute-start(bf16[8,64,256]{2,1,0:T(8,128)(2,1)S(1)} %get-tuple-element.32.refs_7_.refs_0_), channel_id=1, source_target_pairs={{0,2},{2,0},{1,3},{3,1},{4,6},{6,4},{5,7},{7,5},{8,10},{10,8},{9,1... | collective-permute-start | bytes 786440 | tf_op jit(solution)/shard_map/ppermute | solution.py:343
  40.5 1.4 %collective-permute-start.8 = (bf16[32,2048]{1,0:T(8,128)(2,1)S(1)}, bf16[32,2048]{1,0:T(8,128)(2,1)S(1)}, u32[]{:S(2)}, u32[]{:S(2)}) collective-permute-start(bf16[32,2048]{1,0:T(8,128)(2,1)S(1)} %get-tuple-element.36), channel_id=1, source_target_pairs={{0,1},{1,0},{2,3},{3,2},{4,5},{5,4},{6,7},{7,6},{8,9},{9,8},{10,11... | collective-permute-start | bytes 393224 | tf_op jit(solution)/shard_map/ppermute | solution.py:343
  42.0 11.3 %collective-permute-start.10 = (bf16[32,2048]{1,0:T(8,128)(2,1)S(1)}, bf16[32,2048]{1,0:T(8,128)(2,1)S(1)}, u32[]{:S(2)}, u32[]{:S(2)}) collective-permute-start(bf16[32,2048]{1,0:T(8,128)(2,1)S(1)} %add_cores.1.refs_4_), channel_id=1, source_target_pairs={{0,8},{1,13},{4,12},{5,9},{8,0},{9,5},{12,4},{13,1},{2,10},{3,15},... | collective-permute-start | bytes 393224 | tf_op jit(solution)/shard_map/ppermute | solution.py:349
  45.2 8.0 %collective-permute-start.9 = (bf16[32,2048]{1,0:T(8,128)(2,1)S(1)}, bf16[32,2048]{1,0:T(8,128)(2,1)S(1)}, u32[]{:S(2)}, u32[]{:S(2)}) collective-permute-start(bf16[32,2048]{1,0:T(8,128)(2,1)S(1)} %get-tuple-element.48), channel_id=1, source_target_pairs={{0,4},{4,0},{8,12},{12,8},{1,5},{5,1},{9,13},{13,9},{2,6},{6,2},{1... | collective-permute-start | bytes 393224 | tf_op jit(solution)/shard_map/ppermute | solution.py:343
  53.3 1.4 %collective-permute-start.11 = (bf16[32,2048]{1,0:T(8,128)(2,1)S(1)}, bf16[32,2048]{1,0:T(8,128)(2,1)S(1)}, u32[]{:S(2)}, u32[]{:S(2)}) collective-permute-start(bf16[32,2048]{1,0:T(8,128)(2,1)S(1)} %get-tuple-element.51), channel_id=1, source_target_pairs={{0,1},{1,0},{2,3},{3,2},{4,5},{5,4},{6,7},{7,6},{8,9},{9,8},{10,11... | collective-permute-start | bytes 393224 | tf_op jit(solution)/shard_map/ppermute | solution.py:343

commit v4 on v3

--- a/solution.py
+++ b/solution.py
@@ -73,20 +73,18 @@
     return arrive
 
 
-def store_tiles(first, start, stop, i, gate_ref, up_ref, gate_hbm, up_hbm, sems):
+def store_tiles(first, c, gate_ref, up_ref, gate_hbm, up_hbm, sems):
     copies = [
-        pltpu.make_async_copy(
-            source.at[pl.ds(start, stop - start)], target.at[pl.ds(first + start, stop - start)], sems.at[j, i]
-        )
-        for j, (source, target) in enumerate(((gate_ref, gate_hbm), (up_ref, up_hbm)))
+        pltpu.make_async_copy(gate_ref.at[c], gate_hbm.at[first + c], sems.at[0, c]),
+        pltpu.make_async_copy(up_ref.at[c], up_hbm.at[first + c], sems.at[1, c]),
     ]
     for copy in copies:
         copy.start()
     return copies
 
 
-def forward_own_kernel(x_hbm, rows_hbm, counts_hbm, gate_hbm, up_hbm, part_ref, *scratch):
-    x_ref, rows_ref, counts_ref, gate_ref, up_ref, sems, small_sems = scratch
+def forward_own_kernel(x_hbm, rows_hbm, counts_hbm, gate_hbm, up_hbm, part_ref, gate_ref, up_ref, *scratch):
+    x_ref, rows_ref, counts_ref, sems, small_sems = scratch
     cols = gate_ref.shape[0]
     small = [
         pltpu.make_async_copy(source, target, small_sems.at[i])
@@ -104,12 +102,9 @@
 
 def forward_kernel(members, rows_ref, counts_ref, *refs):
     xs = refs[:members]
-    gate_hbm, up_hbm = refs[members : members + 2]
-    part_ref, gate_ref, up_ref, sems = refs[-4:]
-    cols = gate_ref.shape[0]
-    arrive = load_tiles(0, cols, gate_hbm, up_hbm, gate_ref, up_ref, sems)
-    for c in range(cols):
-        arrive(c)
+    gate_ref, up_ref = refs[members : members + 2]
+    part_ref = refs[-1]
+    for c in range(gate_ref.shape[0]):
         part_ref[c] = forward_column(c, 0, (rows_ref, counts_ref), xs, gate_ref, up_ref)
 
 
@@ -137,13 +132,13 @@
             part_ref[c] = part[start:stop]
 
 
-def shard_of(member, meta_ref):
+def shard_of(member):
     if member < 2:
-        return meta_ref[0] ^ member
-    return meta_ref[0] ^ ((member & ~1) + ((member & 1) ^ meta_ref[2]))
-
-
-def start_cots(members, first, meta_ref, cots, cot_ref, sems):
+        return lax.axis_index("tok") ^ member
+    return lax.axis_index("tok") ^ ((member & ~1) + ((member & 1) ^ lax.axis_index("sub")))
+
+
+def start_cots(members, first, cots, cot_ref, sems):
     count = len(members)
     shard_rows, width = cot_ref.shape[0] // count, cot_ref.shape[1]
     shards_each = cots[0].shape[0] // shard_rows
@@ -156,8 +151,8 @@
         )
 
     for i, member in enumerate(members):
-        shard = shard_of(member, meta_ref)
-        source = (shard // shards_each) ^ meta_ref[1]
+        shard = shard_of(member)
+        source = (shard // shards_each) ^ lax.axis_index("blk")
         first_row = pl.multiple_of((shard % shards_each) * shard_rows, shard_rows)
         for j, cot in enumerate(cots):
 
@@ -218,7 +213,7 @@
         up_ref[c, 0, k] = term[:, tile:]
 
 
-def start_hidden(members, first, meta_ref, source_of, hidden_hbm, shard_rows, sems):
+def start_hidden(members, first, source_of, hidden_hbm, shard_rows, sems):
     width = source_of(0).shape[1]
     shards_each = hidden_hbm.shape[0] // shard_rows
 
@@ -228,44 +223,40 @@
         )
 
     for i in range(shards_each):
-        wanted = meta_ref[1] * shards_each + i
+        wanted = lax.axis_index("blk") * shards_each + i
         for member in members:
 
-            @pl.when(shard_of(member, meta_ref) == wanted)
+            @pl.when(shard_of(member) == wanted)
             def _(i=i, member=member):
                 copy(i, member).start()
 
     return [copy(i, 0) for i in range(shards_each)]
 
 
-def first_half_kernel(members, owners, meta_ref, rows_ref, counts_ref, gate_in, up_in, turned_ref, *refs):
+def first_half_kernel(members, owners, rows_ref, counts_ref, gate_w, up_w, turned_ref, *refs):
     near, rest, cots = refs[:owners], refs[owners : 2 * owners], refs[2 * owners : 3 * owners]
-    gate_hbm, up_hbm, hidden_hbm, acc_near, acc_far = refs[-15:-10]
-    cot_ref, hidden_ref, gate_ref, up_ref, gate_w, up_w, sems, cot_sems, hidden_sems, load_sems = refs[-10:]
+    gate_hbm, up_hbm, hidden_hbm, acc_near, acc_far = refs[-12:-7]
+    cot_ref, hidden_ref, gate_ref, up_ref, sems, cot_sems, hidden_sems = refs[-7:]
     cols, _, slots, tile, _ = gate_ref.shape
-    arrive = load_tiles(0, cols, gate_in, up_in, gate_w, up_w, load_sems)
     shard_rows = cot_ref.shape[0] // members
     lists = (rows_ref, counts_ref)
-    waits = start_cots(range(members), 0, meta_ref, cots, cot_ref, cot_sems)
+    waits = start_cots(range(members), 0, cots, cot_ref, cot_sems)
     acc_near[...] = jnp.zeros_like(acc_near)
     acc_far[...] = jnp.zeros_like(acc_far)
     for wait in waits:
         wait.wait()
     copies = []
-    for i, (start, stop) in enumerate(groups_of(cols)):
-        arrive(start)
-        for c in range(start, stop):
-            total = jnp.concatenate([total_of(c, near), total_of(c, rest)], axis=0)
-            where = slice(c * tile, (c + 1) * tile)
-            hidden, grads = nonlinear(total, cot_ref[:, where].astype(F32))
-            hidden_ref[:, where] = hidden
-            tile_grads(c, 0, lists, turned_ref, grads, gate_ref, up_ref)
-            add_back(c, lists, back_terms(c, grads, gate_w, up_w), (acc_near, acc_far), slots, tile)
-        copies += store_tiles(0, start, stop, i, gate_ref, up_ref, gate_hbm, up_hbm, sems)
+    for c in range(cols):
+        total = jnp.concatenate([total_of(c, near), total_of(c, rest)], axis=0)
+        where = slice(c * tile, (c + 1) * tile)
+        hidden, grads = nonlinear(total, cot_ref[:, where].astype(F32))
+        hidden_ref[:, where] = hidden
+        tile_grads(c, 0, lists, turned_ref, grads, gate_ref, up_ref)
+        copies += store_tiles(0, c, gate_ref, up_ref, gate_hbm, up_hbm, sems)
+        add_back(c, lists, back_terms(c, grads, gate_w, up_w), (acc_near, acc_far), slots, tile)
     waits = start_hidden(
         range(members),
         0,
-        meta_ref,
         lambda m: hidden_ref.at[pl.ds(m * shard_rows, shard_rows)],
         hidden_hbm,
         shard_rows,
@@ -275,7 +266,7 @@
         wait.wait()
 
 
-def second_half_kernel(members, owners, first, meta_ref, rows_ref, counts_ref, gate_w, up_w, acc_in, *refs):
+def second_half_kernel(members, owners, first, rows_ref, counts_ref, gate_w, up_w, acc_in, *refs):
     parts, cots = refs[:owners], refs[owners : 2 * owners]
     outs = refs[-(2 + len(members) + 3) :]
     grads_ref, hidden_ref = outs[:2]
@@ -283,7 +274,7 @@
     cot_ref, acc_ref, cot_sems = outs[-3:]
     cols, _, slots, tile, _ = gate_w.shape
     shard_rows = cot_ref.shape[0] // len(members)
-    waits = start_cots(members, first * tile, meta_ref, cots, cot_ref, cot_sems)
+    waits = start_cots(members, first * tile, cots, cot_ref, cot_sems)
     acc_ref[...] = acc_in[...]
     for wait in waits:
         wait.wait()
@@ -299,7 +290,7 @@
             dx[:, r * tile : (r + 1) * tile] = block[m * shard_rows : (m + 1) * shard_rows]
 
 
-def last_grads_kernel(members, first, start, with_hidden, meta_ref, rows_ref, counts_ref, turned_ref, *refs):
+def last_grads_kernel(members, first, start, with_hidden, rows_ref, counts_ref, turned_ref, *refs):
     near_grads, far_grads, near_hidden, far_hidden = refs[:4]
     gate_hbm, up_hbm, hidden_hbm, token_ref, gate_ref, up_ref, sems, hidden_sems = refs[-8:]
     cols, _, _, tile, _ = gate_ref.shape
@@ -314,13 +305,12 @@
     waits = []
     if with_hidden:
         waits = start_hidden(
-            range(members), first * tile, meta_ref, hidden_of, hidden_hbm, shard_rows, hidden_sems
+            range(members), first * tile, hidden_of, hidden_hbm, shard_rows, hidden_sems
         )
-    for i, (begin, end) in enumerate(groups_of(cols)):
-        for c in range(begin, end):
-            grads = jnp.concatenate([near_grads[start + c], far_grads[start + c]], axis=0)
-            tile_grads(c, first + start, (rows_ref, counts_ref), turned_ref, grads, gate_ref, up_ref)
-        waits += store_tiles(first + start, begin, end, i, gate_ref, up_ref, gate_hbm, up_hbm, sems)
+    for c in range(cols):
+        grads = jnp.concatenate([near_grads[start + c], far_grads[start + c]], axis=0)
+        tile_grads(c, first + start, (rows_ref, counts_ref), turned_ref, grads, gate_ref, up_ref)
+        waits += store_tiles(first + start, c, gate_ref, up_ref, gate_hbm, up_hbm, sems)
     for wait in waits:
         wait.wait()
 
@@ -356,13 +346,9 @@
     row_blocks = width // tile
     row_total = shards * shard_rows
     near_rows = 2 * shard_rows
-    half = cols // 2
+    half = max(1, cols * 3 // 8)
     bases = range(2, shards, 2)
-    meta = jnp.stack([lax.axis_index("tok"), lax.axis_index("blk"), lax.axis_index("sub")]).astype(jnp.int32)
     lists = (jnp.transpose(block_rows, (2, 1, 0)), jnp.transpose(block_counts, (1, 0)))
-
-    def held(weights):
-        return [pltpu.with_memory_space_constraint(w, pltpu.VMEM) for w in weights]
 
     def shape(*dims, dtype=BF16):
         return jax.ShapeDtypeStruct(dims, dtype)
@@ -388,21 +374,19 @@
     def from_hbm(*arrays):
         return [pltpu.with_memory_space_constraint(array, pltpu.HBM) for array in arrays]
 
-    near_a = pl.pallas_call(
+    near_a, *weights_a = pl.pallas_call(
         forward_own_kernel,
-        out_shape=shape(half, shard_rows, 2 * tile),
+        out_shape=(shape(half, shard_rows, 2 * tile), tile_shape(half), tile_shape(half)),
         in_specs=[ANY_SPEC] * 5,
-        out_specs=VMEM_SPEC,
+        out_specs=(VMEM_SPEC,) * 3,
         scratch_shapes=[
             pltpu.VMEM((shard_rows, width), BF16),
             pltpu.SMEM(lists[0].shape, jnp.int32),
             pltpu.SMEM(lists[1].shape, jnp.int32),
-            tile_shape(half),
-            tile_shape(half),
             pltpu.SemaphoreType.DMA((2, 3)),
             pltpu.SemaphoreType.DMA((3,)),
         ],
-        compiler_params=limit(12),
+        compiler_params=limit(8),
         cost_estimate=cost(shard_rows, half, 1, 1),
         name="forward_own_a",
     )(*from_hbm(features_in, *lists, gate_tiles, up_tiles))
@@ -423,13 +407,12 @@
     rest_a = pl.pallas_call(
         functools.partial(forward_kernel, shards - 1),
         out_shape=shape(half, row_total - shard_rows, 2 * tile),
-        in_specs=[SMEM_SPEC] * 2 + [VMEM_SPEC] * (shards - 1) + [ANY_SPEC] * 3,
+        in_specs=[SMEM_SPEC] * 2 + [VMEM_SPEC] * (shards + 1) + [ANY_SPEC],
         out_specs=VMEM_SPEC,
-        scratch_shapes=[tile_shape(half), tile_shape(half), pltpu.SemaphoreType.DMA((2, 3))],
-        compiler_params=limit(12),
+        compiler_params=limit(8),
         cost_estimate=cost(row_total, half, 1, 1),
         name="forward_rest_a",
-    )(*lists, *xs[1:], *from_hbm(gate_tiles, up_tiles), cots[-1])
+    )(*lists, *xs[1:], *weights_a, cots[-1])
     rest_a = to_owners(rest_a)
 
     rest = cols - half
@@ -462,27 +445,21 @@
             shape(row_blocks, near_rows, tile, dtype=F32),
             shape(row_blocks, row_total - near_rows, tile, dtype=F32),
         ),
-        in_specs=[SMEM_SPEC] * 3
-        + [ANY_SPEC] * 2
-        + [VMEM_SPEC] * (1 + 2 * owners)
-        + [ANY_SPEC] * (owners + 2),
+        in_specs=[SMEM_SPEC] * 2 + [VMEM_SPEC] * (3 + 2 * owners) + [ANY_SPEC] * (owners + 2),
         out_specs=(ANY_SPEC,) * 3 + (VMEM_SPEC,) * 2,
         scratch_shapes=[
             pltpu.VMEM((row_total, half * tile), BF16),
             pltpu.VMEM((row_total, half * tile), BF16),
-            pltpu.VMEM((half, 1, slots, tile, tile), BF16),
-            pltpu.VMEM((half, 1, slots, tile, tile), BF16),
             tile_shape(half),
             tile_shape(half),
-            pltpu.SemaphoreType.DMA((2, 3)),
+            pltpu.SemaphoreType.DMA((2, half)),
             pltpu.SemaphoreType.DMA((shards,)),
             pltpu.SemaphoreType.DMA((d_hidden.shape[0] // shard_rows,)),
-            pltpu.SemaphoreType.DMA((2, 3)),
         ],
-        compiler_params=limit(20),
+        compiler_params=limit(8 + 2 * half * slots * tile * tile * 2 // MIB),
         cost_estimate=cost(row_total, half, 2, 1, 1),
         name="first_half",
-    )(meta, *lists, *from_hbm(gate_tiles, up_tiles), *held([turned]), *near_a, *rest_a, *cots, far_b[0], near_b[0])
+    )(*lists, *weights_a, turned, *near_a, *rest_a, *cots, far_b[0], near_b[0])
 
     def second_half(members, acc, parts, after):
         rows_here = len(members) * shard_rows
@@ -493,7 +470,7 @@
                 shape(rows_here, rest * tile),
                 *[shape(shard_rows, width) for _ in members],
             ),
-            in_specs=[SMEM_SPEC] * 3 + [VMEM_SPEC] * (3 + owners) + [ANY_SPEC] * (owners + 1),
+            in_specs=[SMEM_SPEC] * 2 + [VMEM_SPEC] * (3 + owners) + [ANY_SPEC] * (owners + 1),
             out_specs=(VMEM_SPEC,) * (2 + len(members)),
             scratch_shapes=[
                 pltpu.VMEM((rows_here, rest * tile), BF16),
@@ -503,7 +480,7 @@
             compiler_params=limit(8),
             cost_estimate=cost(rows_here, rest, 1, 1, 1 if members[0] == 0 else 1),
             name="second_half",
-        )(meta, *lists, *held(weights_b), acc, *parts, *cots, after)
+        )(*lists, *weights_b, acc, *parts, *cots, after)
 
     far_grads, far_hidden, *far_dxs = second_half(range(2, shards), acc_far, far_b, acc_near)
     both_cores = []
@@ -530,19 +507,19 @@
         return pl.pallas_call(
             functools.partial(last_grads_kernel, shards, half, start, with_hidden),
             out_shape=(out_tiles, out_tiles, shape(*d_hidden.shape), shape(8, tile, dtype=F32)),
-            in_specs=[SMEM_SPEC] * 3 + [VMEM_SPEC] * 3 + [ANY_SPEC] * 5,
+            in_specs=[SMEM_SPEC] * 2 + [VMEM_SPEC] * 3 + [ANY_SPEC] * 5,
             out_specs=(ANY_SPEC,) * 3 + (VMEM_SPEC,),
             scratch_shapes=[
                 pltpu.VMEM((count, 1, slots, tile, tile), BF16),
                 pltpu.VMEM((count, 1, slots, tile, tile), BF16),
-                pltpu.SemaphoreType.DMA((2, 3)),
+                pltpu.SemaphoreType.DMA((2, count)),
                 pltpu.SemaphoreType.DMA((d_hidden.shape[0] // shard_rows,)),
             ],
-            input_output_aliases={8: 0, 9: 1, 10: 2},
-            compiler_params=limit(12),
+            input_output_aliases={7: 0, 8: 1, 9: 2},
+            compiler_params=limit(8 + 2 * count * slots * tile * tile * 2 // MIB),
             cost_estimate=cost(row_total, count, 1, 1, 10),
             name="last_grads",
-        )(meta, *lists, *held([turned]), near_grads, far_grads, near_hidden, far_hidden, *outs)
+        )(*lists, turned, near_grads, far_grads, near_hidden, far_hidden, *outs)
 
     middle = rest
     *outs, token = last_grads(0, middle, True, (gate_out, up_out, hidden_out))

time: 55.5 us -> 51.1 us (0.921)
  Pallas kernels: 30.3 us -> 26.3 us
  waiting for transfers between devices: 8.17 us -> 7.35 us
  starting transfers between devices: 15.3 us -> 15.9 us
    pallas_call x1, Pallas kernels: 7.76 us -> 4.89 us  [on_device(): pl.pallas_call(functools.partial(first_half_kernel, shards, owners), out_...]
    pallas_call x1, Pallas kernels: 4.04 us -> 1.55 us  [on_device(): pl.pallas_call(functools.partial(forward_kernel, shards - 1), out_shape=s...]
    pallas_call x2, Pallas kernels: 5.88 us -> 6.95 us  [second_half(): pl.pallas_call(functools.partial(second_half_kernel, members, owners, hal...]
    ppermute x10, waiting for transfers between devices: 8.17 us -> 7.2 us  [swap(): lax.ppermute(x, axis, [(i, i ^ step) for i in range(lax.axis_size(axis))])]
    pallas_call x1, Pallas kernels: 4.08 us -> 4.67 us  [on_device(): pl.pallas_call(functools.partial(load_forward_kernel, shards, ((near_rows...]
  transfers between devices with their start and end apart: 12 -> 12, of which waited for: 6 -> 7; matrix products, arithmetic and copies ran while one was open for 0% -> 0% of each run, Pallas kernels for 55% -> 51%
where the time goes in v4:
time: 51.1 us; the launch traced here: 51 us
  Pallas kernels  26.3 us (51%)
  starting transfers between devices  15.9 us (31%)
  waiting for transfers between devices  7.35 us (14%)
  between operations  0.76 us (1%)
  other arithmetic  0.68 us (1%)
    ppermute x10, starting transfers between devices, swap(): lax.ppermute(x, axis, [(i, i ^ step) for i in range(lax.axis_size(axis))])  11.1 us
    ppermute x10, waiting for transfers between devices, swap(): lax.ppermute(x, axis, [(i, i ^ step) for i in range(lax.axis_size(axis))])  7.2 us
    pallas_call x2, Pallas kernels, second_half(): pl.pallas_call(functools.partial(second_half_kernel, members, owners, hal...  6.95 us
    pallas_call x1, Pallas kernels, on_device(): pl.pallas_call(functools.partial(first_half_kernel, shards, owners), out_...  4.89 us
    ppermute x2, starting transfers between devices, swap_far(): return lax.ppermute(x, ('tok', 'sub'), pairs)  4.87 us
    pallas_call x1, Pallas kernels, on_device(): pl.pallas_call(functools.partial(load_forward_kernel, shards, ((near_rows...  4.67 us
    pallas_call x1, Pallas kernels, last_grads(): pl.pallas_call(functools.partial(last_grads_kernel, shards, half, start,...  4.54 us
    pallas_call x1, Pallas kernels, on_device(): pl.pallas_call(forward_own_kernel, out_shape=(shape(half, shard_rows, 2 *...  3.56 us
  transfers between devices with their start and end apart: 12, of which 7 were waited for; matrix products, arithmetic and copies ran while one was open for 0% of the time, Pallas kernels for 51%

profile of v4, /device:TPU:0, one launch (start us, length us, event | category | flops | bytes accessed | tf_op | source)
XLA Modules:
  0.0 51.0 jit_solution(6028858293119987617)
XLA Ops:
  0.6 4.1 %collective-permute-start.1 = (bf16[32,2048]{1,0:T(8,128)(2,1)}, bf16[32,2048]{1,0:T(8,128)(2,1)S(1)}, u32[]{:S(2)}, u32[]{:S(2)}) collective-permute-start(bf16[32,2048]{1,0:T(8,128)(2,1)} %refs_0_.1), channel_id=1, source_target_pairs={{0,8},{1,13},{4,12},{5,9},{8,0},{9,5},{12,4},{13,1},{2,10},{3,15},... | collective-permute-start | bytes 393224 | tf_op jit(solution)/shard_map/ppermute | solution.py:339
  4.7 1.5 %collective-permute-start.3 = (bf16[64,2048]{1,0:T(8,128)(2,1)}, bf16[64,2048]{1,0:T(8,128)(2,1)S(1)}, u32[]{:S(2)}, u32[]{:S(2)}) collective-permute-start(bf16[64,2048]{1,0:T(8,128)(2,1)} %refs_2_.3), channel_id=1, source_target_pairs={{0,2},{2,0},{1,3},{3,1},{4,6},{6,4},{5,7},{7,5},{8,10},{10,8},{9,1... | collective-permute-start | bytes 786440 | tf_op jit(solution)/shard_map/ppermute | solution.py:333
  6.2 1.6 %collective-permute-start = (bf16[32,2048]{1,0:T(8,128)(2,1)}, bf16[32,2048]{1,0:T(8,128)(2,1)S(1)}, u32[]{:S(2)}, u32[]{:S(2)}) collective-permute-start(bf16[32,2048]{1,0:T(8,128)(2,1)} %refs_0_.1), channel_id=1, source_target_pairs={{0,4},{4,0},{8,12},{12,8},{1,5},{5,1},{9,13},{13,9},{2,6},{6,2},{1... | collective-permute-start | bytes 393224 | tf_op jit(solution)/shard_map/ppermute | solution.py:333
  7.8 3.6 %forward_own_a.1 = (bf16[6,32,256]{2,1,0:T(8,128)(2,1)S(1)}, bf16[6,1,12,128,128]{4,3,2,1,0:T(8,128)(2,1)S(1)}, bf16[6,1,12,128,128]{4,3,2,1,0:T(8,128)(2,1)S(1)}) custom-call(bf16[32,2048]{1,0:T(8,128)(2,1)} %refs_0_.1, s32[12,1,16]{2,1,0:T(1,128)} %bitcast.2, s32[1,16]{1,0:T(1,128)} %bitcast.9, bf16[16,1,12,128,128]{4,3,2,1,0:T(8,128)(2,1)} %refs_4_.2, ...), custom_call_target="tpu_custom_call" | custom-call | flops 150994944 | bytes 4718592 | tf_op jit(solution)/shard_map/forward_own_a/pallas_call | solution.py:377
  11.4 0.1 collective-permute-done.1.x_ref.refs_1_.refs_2_
  11.5 0.1 collective-permute-start.2
  11.6 1.6 %collective-permute-start.4 = (bf16[6,32,256]{2,1,0:T(8,128)(2,1)S(1)}, bf16[6,32,256]{2,1,0:T(8,128)(2,1)S(1)}, u32[]{:S(2)}, u32[]{:S(2)}) collective-permute-start(bf16[6,32,256]{2,1,0:T(8,128)(2,1)S(1)} %get-tuple-element.31._.refs_0_), channel_id=1, source_target_pairs={{0,2},{2,0},{1,3},{3,1},{4,6},{6,4},{5,7},{7,5},{8,10},{10,8},{9,1... | collective-permute-start | bytes 294920 | tf_op jit(solution)/shard_map/ppermute | solution.py:333
  13.2 0.0 collective-permute-done.refs_0_.refs_1_
  13.2 0.5 %collective-permute-done.3.refs_5_.refs_3_ = bf16[64,2048]{1,0:T(8,128)(2,1)S(1)} collective-permute-done((bf16[64,2048]{1,0:T(8,128)(2,1)}, bf16[64,2048]{1,0:T(8,128)(2,1)S(1)}, u32[]{:S(2)}, u32[]{:S(2)}) %collective-permute-start.3) | collective-permute-done | bytes 262176 | tf_op jit(solution)/shard_map/ppermute | solution.py:333
  13.7 1.5 %forward_rest_a.1.refs_6_.refs_2_ = bf16[6,96,256]{2,1,0:T(8,128)(2,1)S(1)} custom-call(s32[12,1,16]{2,1,0:T(1,128)S(1)} %bitcast.3, s32[1,16]{1,0:T(1,128)S(1)} %bitcast.10, bf16[32,2048]{1,0:T(8,128)(2,1)S(1)} %collective-permute-done.refs_0_.refs_1_, bf16[32,2048]{1,0:T(8,128)(2,1)S(1)} %collective-permute-done.1.x_ref.refs_1_.refs_2_, ...), custom_call_target="tpu_custom_call" | custom-call | flops 603979776 | bytes 4718592 | tf_op jit(solution)/shard_map/forward_rest_a/pallas_call | solution.py:407
  15.3 0.0 copy-start
  15.3 1.6 %collective-permute-start.5 = (bf16[6,96,256]{2,1,0:T(8,128)(2,1)S(1)}, bf16[6,96,256]{2,1,0:T(8,128)(2,1)S(1)}, u32[]{:S(2)}, u32[]{:S(2)}) collective-permute-start(bf16[6,96,256]{2,1,0:T(8,128)(2,1)S(1)} %forward_rest_a.1.refs_6_.refs_2_), channel_id=1, source_target_pairs={{0,2},{2,0},{1,3},{3,1},{4,6},{6,4},{5,7},{7,5},{8,10},{10,8},{9,1... | collective-permute-start | bytes 884744 | tf_op jit(solution)/shard_map/ppermute | solution.py:333
  16.9 0.0 collective-permute-done.4.refs_7_.refs_1_
  16.9 4.7 %forward_b.1 = (bf16[10,64,256]{2,1,0:T(8,128)(2,1)S(1)}, bf16[10,64,256]{2,1,0:T(8,128)(2,1)S(1)}, bf16[10,1,12,128,128]{4,3,2,1,0:T(8,128)(2,1)S(1)}, bf16[10,...) custom-call(s32[12,1,16]{2,1,0:T(1,128)S(1)} %bitcast.4, s32[1,16]{1,0:T(1,128)S(1)} %bitcast.11, ...), custom_call_target="tpu_custom_call" | custom-call | flops 5033164800 | bytes 39321600 | tf_op jit(solution)/shard_map/forward_b/pallas_call | solution.py:419
  21.5 1.5 %collective-permute-start.7 = (bf16[10,64,256]{2,1,0:T(8,128)(2,1)S(1)}, bf16[10,64,256]{2,1,0:T(8,128)(2,1)S(1)}, u32[]{:S(2)}, u32[]{:S(2)}) collective-permute-start(bf16[10,64,256]{2,1,0:T(8,128)(2,1)S(1)} %get-tuple-element.37.refs_6_.refs_0_), channel_id=1, source_target_pairs={{0,2},{2,0},{1,3},{3,1},{4,6},{6,4},{5,7},{7,5},{8,10},{10,8},{9,1... | collective-permute-start | bytes 983048 | tf_op jit(solution)/shard_map/ppermute | solution.py:333
  23.1 0.6 %collective-permute-start.6 = (bf16[10,64,256]{2,1,0:T(8,128)(2,1)S(1)}, bf16[10,64,256]{2,1,0:T(8,128)(2,1)S(1)}, u32[]{:S(2)}, u32[]{:S(2)}) collective-permute-start(bf16[10,64,256]{2,1,0:T(8,128)(2,1)S(1)} %get-tuple-element.38.refs_7_.refs_0_), channel_id=1, source_target_pairs={{0,2},{2,0},{1,3},{3,1},{4,6},{6,4},{5,7},{7,5},{8,10},{10,8},{9,1... | collective-permute-start | bytes 983048 | tf_op jit(solution)/shard_map/ppermute | solution.py:333
  23.6 0.6 %collective-permute-done.5.refs_3_ = bf16[6,96,256]{2,1,0:T(8,128)(2,1)S(1)} collective-permute-done((bf16[6,96,256]{2,1,0:T(8,128)(2,1)S(1)}, bf16[6,96,256]{2,1,0:T(8,128)(2,1)S(1)}, u32[]{:S(2)}, u32[]{:S(2)}) %collective-permute-start.5) | collective-permute-done | bytes 294944 | tf_op jit(solution)/shard_map/ppermute | solution.py:333
  24.2 4.9 %first_half.1 = (bf16[16,1,12,128,128]{4,3,2,1,0:T(8,128)(2,1)}, bf16[16,1,12,128,128]{4,3,2,1,0:T(8,128)(2,1)}, bf16[64,2048]{1,0:T(8,128)(2,1)}, f32[16,64,128]{2,1,0:T(8,128)S(1)}, f32[16,64,128]{2,1,0:T(8,128)S(1)}) custom-call(s32[12,1,16]{2,1,0:T(1,128)S(1)} %bitcast.5, s32[1,16]{1,0:T(1,128)S(1)} %bitcast.12, ...), custom_call_target="tpu_custom_call" | custom-call | flops 1207959552 | bytes 4718592 | tf_op jit(solution)/shard_map/first_half/pallas_call | solution.py:439
  29.2 3.1 %collective-permute-done.7.refs_1_ = bf16[10,64,256]{2,1,0:T(8,128)(2,1)S(1)} collective-permute-done((bf16[10,64,256]{2,1,0:T(8,128)(2,1)S(1)}, bf16[10,64,256]{2,1,0:T(8,128)(2,1)S(1)}, u32[]{:S(2)}, u32[]{:S(2)}) %collective-permute-start.7) | collective-permute-done | bytes 327712 | tf_op jit(solution)/shard_map/ppermute | solution.py:333
  32.2 3.4 %second_half.2 = (bf16[10,64,256]{2,1,0:T(8,128)(2,1)S(1)}, bf16[64,1280]{1,0:T(8,128)(2,1)S(1)}, bf16[32,2048]{1,0:T(8,128)(2,1)S(1)}, bf16[32,2048]{1,0:T(8,128)(2,1)S(1)}) custom-call(s32[12,1,16]{2,1,0:T(1,128)S(1)} %bitcast.6, s32[1,16]{1,0:T(1,128)S(1)} %bitcast.13, bf16[10,1,12,128,128]{4,3,2,1,0:T(8,128)(2,1)S(1)} %get-tuple-element.35.gate_w, ...), custom_call_target="tpu_custom_call" | custom-call | flops 503316480 | bytes 7864320 | tf_op jit(solution)/shard_map/second_half/pallas_call | solution.py:466
  35.6 0.1 collective-permute-start.8
  35.7 1.3 %collective-permute-done.8.right_ref = bf16[32,2048]{1,0:T(8,128)(2,1)S(1)} collective-permute-done((bf16[32,2048]{1,0:T(8,128)(2,1)S(1)}, bf16[32,2048]{1,0:T(8,128)(2,1)S(1)}, u32[]{:S(2)}, u32[]{:S(2)}) %collective-permute-start.8) | collective-permute-done | bytes 131104 | tf_op jit(solution)/shard_map/ppermute | solution.py:333
  37.1 0.8 %collective-permute-start.10 = (bf16[32,2048]{1,0:T(8,128)(2,1)S(1)}, bf16[32,2048]{1,0:T(8,128)(2,1)S(1)}, u32[]{:S(2)}, u32[]{:S(2)}) collective-permute-start(bf16[32,2048]{1,0:T(8,128)(2,1)S(1)} %add_cores.1.refs_4_), channel_id=1, source_target_pairs={{0,8},{1,13},{4,12},{5,9},{8,0},{9,5},{12,4},{13,1},{2,10},{3,15},... | collective-permute-start | bytes 393224 | tf_op jit(solution)/shard_map/ppermute | solution.py:339
  37.8 0.3 collective-permute-done.6.refs_1_
  38.1 3.6 %second_half.3 = (bf16[10,64,256]{2,1,0:T(8,128)(2,1)S(1)}, bf16[64,1280]{1,0:T(8,128)(2,1)S(1)}, bf16[32,2048]{1,0:T(8,128)(2,1)S(1)}, bf16[32,2048]{1,0:T(8,128)(2,1)S(1)}) custom-call(s32[12,1,16]{2,1,0:T(1,128)S(1)} %bitcast.7, s32[1,16]{1,0:T(1,128)S(1)} %bitcast.14, bf16[10,1,12,128,128]{4,3,2,1,0:T(8,128)(2,1)S(1)} %get-tuple-element.35.gate_w, ...), custom_call_target="tpu_custom_call" | custom-call | flops 503316480 | bytes 7864320 | tf_op jit(solution)/shard_map/second_half/pallas_call | solution.py:466
  41.7 2.6 %collective-permute-start.9 = (bf16[32,2048]{1,0:T(8,128)(2,1)S(1)}, bf16[32,2048]{1,0:T(8,128)(2,1)S(1)}, u32[]{:S(2)}, u32[]{:S(2)}) collective-permute-start(bf16[32,2048]{1,0:T(8,128)(2,1)S(1)} %get-tuple-element.54), channel_id=1, source_target_pairs={{0,4},{4,0},{8,12},{12,8},{1,5},{5,1},{9,13},{13,9},{2,6},{6,2},{1... | collective-permute-start | bytes 393224 | tf_op jit(solution)/shard_map/ppermute | solution.py:333
  44.3 4.5 %last_grads.1 = (bf16[16,1,12,128,128]{4,3,2,1,0:T(8,128)(2,1)}, bf16[16,1,12,128,128]{4,3,2,1,0:T(8,128)(2,1)}, bf16[64,2048]{1,0:T(8,128)(2,1)}, f32[8,128]{1,0:T(8,128)S(1)}) custom-call(s32[12,1,16]{2,1,0:T(1,128)S(1)} %bitcast.8, s32[1,16]{1,0:T(1,128)S(1)} %bitcast.15, ...), custom_call_target="tpu_custom_call", output_to_operand_aliasing={{0}: (7, {}), {1}: (8, {}), {2}: (9, {})} | custom-call | flops 10066329600 | bytes 78643200 | tf_op jit(solution)/shard_map/last_grads/pallas_call | solution.py:507
  48.8 0.0 collective-permute-done.9.refs_1_
  48.8 0.1 sum_shards.1
  48.9 0.1 collective-permute-start.11
  49.0 1.3 %collective-permute-done.11 = bf16[32,2048]{1,0:T(8,128)(2,1)S(1)} collective-permute-done((bf16[32,2048]{1,0:T(8,128)(2,1)S(1)}, bf16[32,2048]{1,0:T(8,128)(2,1)S(1)}, u32[]{:S(2)}, u32[]{:S(2)}) %collective-permute-start.11) | collective-permute-done | bytes 131104 | tf_op jit(solution)/shard_map/ppermute | solution.py:333
  50.3 0.7 %add_convert_fusion = bf16[32,2048]{1,0:T(8,128)(2,1)} fusion(f32[32,2048]{1,0:T(8,128)S(1)} %get-tuple-element.56, bf16[32,2048]{1,0:T(8,128)(2,1)S(1)} %collective-permute-done.11), kind=kLoop, calls=%fused_computation | loop fusion | flops 196608 | bytes 524288 | tf_op jit(solution)/shard_map/convert_element_type | solution.py:538
  (11 shorter events, 0.1 us)
Async XLA Ops:
  0.6 10.9 %collective-permute-start.1 = (bf16[32,2048]{1,0:T(8,128)(2,1)}, bf16[32,2048]{1,0:T(8,128)(2,1)S(1)}, u32[]{:S(2)}, u32[]{:S(2)}) collective-permute-start(bf16[32,2048]{1,0:T(8,128)(2,1)} %refs_0_.1), channel_id=1, source_target_pairs={{0,8},{1,13},{4,12},{5,9},{8,0},{9,5},{12,4},{13,1},{2,10},{3,15},... | collective-permute-start | bytes 393224 | tf_op jit(solution)/shard_map/ppermute | solution.py:339
  4.7 9.0 %collective-permute-start.3 = (bf16[64,2048]{1,0:T(8,128)(2,1)}, bf16[64,2048]{1,0:T(8,128)(2,1)S(1)}, u32[]{:S(2)}, u32[]{:S(2)}) collective-permute-start(bf16[64,2048]{1,0:T(8,128)(2,1)} %refs_2_.3), channel_id=1, source_target_pairs={{0,2},{2,0},{1,3},{3,1},{4,6},{6,4},{5,7},{7,5},{8,10},{10,8},{9,1... | collective-permute-start | bytes 786440 | tf_op jit(solution)/shard_map/ppermute | solution.py:333
  6.2 6.9 %collective-permute-start = (bf16[32,2048]{1,0:T(8,128)(2,1)}, bf16[32,2048]{1,0:T(8,128)(2,1)S(1)}, u32[]{:S(2)}, u32[]{:S(2)}) collective-permute-start(bf16[32,2048]{1,0:T(8,128)(2,1)} %refs_0_.1), channel_id=1, source_target_pairs={{0,4},{4,0},{8,12},{12,8},{1,5},{5,1},{9,13},{13,9},{2,6},{6,2},{1... | collective-permute-start | bytes 393224 | tf_op jit(solution)/shard_map/ppermute | solution.py:333
  7.8 5.9 %copy-start.1 = (s32[16,1,12]{0,1,2:T(1,128)S(1)}, s32[16,1,12]{0,1,2:T(1,128)}, u32[]{:S(2)}) copy-start(s32[16,1,12]{0,1,2:T(1,128)} %param.9) | copy-start | bytes 2308
  7.8 5.9 %copy-start.3 = (s32[16,1]{0,1:T(1,128)S(1)}, s32[16,1]{0,1:T(1,128)}, u32[]{:S(2)}) copy-start(s32[16,1]{0,1:T(1,128)} %param.10) | copy-start | bytes 196
  7.8 9.1 %copy-start.2 = (bf16[32,2048]{1,0:T(8,128)(2,1)S(1)}, bf16[32,2048]{1,0:T(8,128)(2,1)}, u32[]{:S(2)}) copy-start(bf16[32,2048]{1,0:T(8,128)(2,1)} %refs_0_.1) | copy-start | bytes 393220
  11.5 1.6 %collective-permute-start.2 = (bf16[32,2048]{1,0:T(8,128)(2,1)S(1)}, bf16[32,2048]{1,0:T(8,128)(2,1)S(1)}, u32[]{:S(2)}, u32[]{:S(2)}) collective-permute-start(bf16[32,2048]{1,0:T(8,128)(2,1)S(1)} %after_own.1), channel_id=1, source_target_pairs={{0,1},{1,0},{2,3},{3,2},{4,5},{5,4},{6,7},{7,6},{8,9},{9,8},{10,11... | collective-permute-start | bytes 393224 | tf_op jit(solution)/shard_map/ppermute | solution.py:333
  11.6 5.2 %collective-permute-start.4 = (bf16[6,32,256]{2,1,0:T(8,128)(2,1)S(1)}, bf16[6,32,256]{2,1,0:T(8,128)(2,1)S(1)}, u32[]{:S(2)}, u32[]{:S(2)}) collective-permute-start(bf16[6,32,256]{2,1,0:T(8,128)(2,1)S(1)} %get-tuple-element.31._.refs_0_), channel_id=1, source_target_pairs={{0,2},{2,0},{1,3},{3,1},{4,6},{6,4},{5,7},{7,5},{8,10},{10,8},{9,1... | collective-permute-start | bytes 294920 | tf_op jit(solution)/shard_map/ppermute | solution.py:333
  15.3 9.0 %copy-start = (bf16[64,2048]{1,0:T(8,128)(2,1)S(1)}, bf16[64,2048]{1,0:T(8,128)(2,1)}, u32[]{:S(2)}) copy-start(bf16[64,2048]{1,0:T(8,128)(2,1)} %refs_2_.3) | copy-start | bytes 786436
  15.3 9.0 %collective-permute-start.5 = (bf16[6,96,256]{2,1,0:T(8,128)(2,1)S(1)}, bf16[6,96,256]{2,1,0:T(8,128)(2,1)S(1)}, u32[]{:S(2)}, u32[]{:S(2)}) collective-permute-start(bf16[6,96,256]{2,1,0:T(8,128)(2,1)S(1)} %forward_rest_a.1.refs_6_.refs_2_), channel_id=1, source_target_pairs={{0,2},{2,0},{1,3},{3,1},{4,6},{6,4},{5,7},{7,5},{8,10},{10,8},{9,1... | collective-permute-start | bytes 884744 | tf_op jit(solution)/shard_map/ppermute | solution.py:333
  21.5 10.7 %collective-permute-start.7 = (bf16[10,64,256]{2,1,0:T(8,128)(2,1)S(1)}, bf16[10,64,256]{2,1,0:T(8,128)(2,1)S(1)}, u32[]{:S(2)}, u32[]{:S(2)}) collective-permute-start(bf16[10,64,256]{2,1,0:T(8,128)(2,1)S(1)} %get-tuple-element.37.refs_6_.refs_0_), channel_id=1, source_target_pairs={{0,2},{2,0},{1,3},{3,1},{4,6},{6,4},{5,7},{7,5},{8,10},{10,8},{9,1... | collective-permute-start | bytes 983048 | tf_op jit(solution)/shard_map/ppermute | solution.py:333
  23.1 15.1 %collective-permute-start.6 = (bf16[10,64,256]{2,1,0:T(8,128)(2,1)S(1)}, bf16[10,64,256]{2,1,0:T(8,128)(2,1)S(1)}, u32[]{:S(2)}, u32[]{:S(2)}) collective-permute-start(bf16[10,64,256]{2,1,0:T(8,128)(2,1)S(1)} %get-tuple-element.38.refs_7_.refs_0_), channel_id=1, source_target_pairs={{0,2},{2,0},{1,3},{3,1},{4,6},{6,4},{5,7},{7,5},{8,10},{10,8},{9,1... | collective-permute-start | bytes 983048 | tf_op jit(solution)/shard_map/ppermute | solution.py:333
  35.6 1.4 %collective-permute-start.8 = (bf16[32,2048]{1,0:T(8,128)(2,1)S(1)}, bf16[32,2048]{1,0:T(8,128)(2,1)S(1)}, u32[]{:S(2)}, u32[]{:S(2)}) collective-permute-start(bf16[32,2048]{1,0:T(8,128)(2,1)S(1)} %get-tuple-element.42), channel_id=1, source_target_pairs={{0,1},{1,0},{2,3},{3,2},{4,5},{5,4},{6,7},{7,6},{8,9},{9,8},{10,11... | collective-permute-start | bytes 393224 | tf_op jit(solution)/shard_map/ppermute | solution.py:333
  37.1 11.8 %collective-permute-start.10 = (bf16[32,2048]{1,0:T(8,128)(2,1)S(1)}, bf16[32,2048]{1,0:T(8,128)(2,1)S(1)}, u32[]{:S(2)}, u32[]{:S(2)}) collective-permute-start(bf16[32,2048]{1,0:T(8,128)(2,1)S(1)} %add_cores.1.refs_4_), channel_id=1, source_target_pairs={{0,8},{1,13},{4,12},{5,9},{8,0},{9,5},{12,4},{13,1},{2,10},{3,15},... | collective-permute-start | bytes 393224 | tf_op jit(solution)/shard_map/ppermute | solution.py:339
  41.7 7.1 %collective-permute-start.9 = (bf16[32,2048]{1,0:T(8,128)(2,1)S(1)}, bf16[32,2048]{1,0:T(8,128)(2,1)S(1)}, u32[]{:S(2)}, u32[]{:S(2)}) collective-permute-start(bf16[32,2048]{1,0:T(8,128)(2,1)S(1)} %get-tuple-element.54), channel_id=1, source_target_pairs={{0,4},{4,0},{8,12},{12,8},{1,5},{5,1},{9,13},{13,9},{2,6},{6,2},{1... | collective-permute-start | bytes 393224 | tf_op jit(solution)/shard_map/ppermute | solution.py:333
  48.9 1.4 %collective-permute-start.11 = (bf16[32,2048]{1,0:T(8,128)(2,1)S(1)}, bf16[32,2048]{1,0:T(8,128)(2,1)S(1)}, u32[]{:S(2)}, u32[]{:S(2)}) collective-permute-start(bf16[32,2048]{1,0:T(8,128)(2,1)S(1)} %get-tuple-element.57), channel_id=1, source_target_pairs={{0,1},{1,0},{2,3},{3,2},{4,5},{5,4},{6,7},{7,6},{8,9},{9,8},{10,11... | collective-permute-start | bytes 393224 | tf_op jit(solution)/shard_map/ppermute | solution.py:333

commit v5 on v4

--- a/solution.py
+++ b/solution.py
@@ -83,8 +83,8 @@
     return copies
 
 
-def forward_own_kernel(x_hbm, rows_hbm, counts_hbm, gate_hbm, up_hbm, part_ref, gate_ref, up_ref, *scratch):
-    x_ref, rows_ref, counts_ref, sems, small_sems = scratch
+def forward_own_kernel(x_hbm, rows_hbm, counts_hbm, gate_hbm, up_hbm, part_ref, gate_ref, up_ref, rows_ref, counts_ref, *scratch):
+    x_ref, sems, small_sems = scratch
     cols = gate_ref.shape[0]
     small = [
         pltpu.make_async_copy(source, target, small_sems.at[i])
@@ -138,29 +138,18 @@
     return lax.axis_index("tok") ^ ((member & ~1) + ((member & 1) ^ lax.axis_index("sub")))
 
 
-def start_cots(members, first, cots, cot_ref, sems):
-    count = len(members)
-    shard_rows, width = cot_ref.shape[0] // count, cot_ref.shape[1]
+def cotangent_of(members, cots, shard_rows, where):
     shards_each = cots[0].shape[0] // shard_rows
-
-    def copy(i, cot, first_row):
-        return pltpu.make_async_copy(
-            cot.at[pl.ds(first_row, shard_rows), pl.ds(first, width)],
-            cot_ref.at[pl.ds(i * shard_rows, shard_rows)],
-            sems.at[i],
-        )
-
-    for i, member in enumerate(members):
+    blocks = []
+    for member in members:
         shard = shard_of(member)
         source = (shard // shards_each) ^ lax.axis_index("blk")
-        first_row = pl.multiple_of((shard % shards_each) * shard_rows, shard_rows)
-        for j, cot in enumerate(cots):
-
-            @pl.when(source == j)
-            def _(i=i, cot=cot, first_row=first_row):
-                copy(i, cot, first_row).start()
-
-    return [copy(i, cots[0], 0) for i in range(count)]
+        rows = pl.ds(pl.multiple_of((shard % shards_each) * shard_rows, shard_rows), shard_rows)
+        block = cots[0][rows, where]
+        for j, cot in enumerate(cots[1:], 1):
+            block = jnp.where(source == j, cot[rows, where], block)
+        blocks.append(block.astype(F32))
+    return jnp.concatenate(blocks, axis=0)
 
 
 def nonlinear(total, cotangent):
@@ -213,14 +202,17 @@
         up_ref[c, 0, k] = term[:, tile:]
 
 
-def start_hidden(members, first, source_of, hidden_hbm, shard_rows, sems):
-    width = source_of(0).shape[1]
+def start_hidden(members, parts, hidden_hbm, shard_rows, sems):
     shards_each = hidden_hbm.shape[0] // shard_rows
 
-    def copy(i, member):
-        return pltpu.make_async_copy(
-            source_of(member), hidden_hbm.at[pl.ds(i * shard_rows, shard_rows), pl.ds(first, width)], sems.at[i]
-        )
+    def copies(i, member):
+        rows = pl.ds(i * shard_rows, shard_rows)
+        return [
+            pltpu.make_async_copy(
+                array.at[pl.ds(row, shard_rows)], hidden_hbm.at[rows, pl.ds(first, array.shape[1])], sems.at[j, i]
+            )
+            for j, (array, row, first) in enumerate(parts(member))
+        ]
 
     for i in range(shards_each):
         wanted = lax.axis_index("blk") * shards_each + i
@@ -228,60 +220,47 @@
 
             @pl.when(shard_of(member) == wanted)
             def _(i=i, member=member):
-                copy(i, member).start()
-
-    return [copy(i, 0) for i in range(shards_each)]
+                for copy in copies(i, member):
+                    copy.start()
+
+    return [copy for i in range(shards_each) for copy in copies(i, 0)]
 
 
 def first_half_kernel(members, owners, rows_ref, counts_ref, gate_w, up_w, turned_ref, *refs):
     near, rest, cots = refs[:owners], refs[owners : 2 * owners], refs[2 * owners : 3 * owners]
-    gate_hbm, up_hbm, hidden_hbm, acc_near, acc_far = refs[-12:-7]
-    cot_ref, hidden_ref, gate_ref, up_ref, sems, cot_sems, hidden_sems = refs[-7:]
+    gate_hbm, up_hbm, hidden_ref, acc_near, acc_far, grads_ref, gate_ref, up_ref, sems = refs[-9:]
     cols, _, slots, tile, _ = gate_ref.shape
-    shard_rows = cot_ref.shape[0] // members
+    shard_rows = hidden_ref.shape[0] // members
     lists = (rows_ref, counts_ref)
-    waits = start_cots(range(members), 0, cots, cot_ref, cot_sems)
     acc_near[...] = jnp.zeros_like(acc_near)
     acc_far[...] = jnp.zeros_like(acc_far)
-    for wait in waits:
-        wait.wait()
     copies = []
     for c in range(cols):
         total = jnp.concatenate([total_of(c, near), total_of(c, rest)], axis=0)
         where = slice(c * tile, (c + 1) * tile)
-        hidden, grads = nonlinear(total, cot_ref[:, where].astype(F32))
+        hidden, grads = nonlinear(total, cotangent_of(range(members), cots, shard_rows, where))
         hidden_ref[:, where] = hidden
+        grads_ref[c] = grads
         tile_grads(c, 0, lists, turned_ref, grads, gate_ref, up_ref)
         copies += store_tiles(0, c, gate_ref, up_ref, gate_hbm, up_hbm, sems)
-        add_back(c, lists, back_terms(c, grads, gate_w, up_w), (acc_near, acc_far), slots, tile)
-    waits = start_hidden(
-        range(members),
-        0,
-        lambda m: hidden_ref.at[pl.ds(m * shard_rows, shard_rows)],
-        hidden_hbm,
-        shard_rows,
-        hidden_sems,
-    )
-    for wait in copies + waits:
-        wait.wait()
+    for c in range(cols):
+        add_back(c, lists, back_terms(c, grads_ref[c], gate_w, up_w), (acc_near, acc_far), slots, tile)
+    for copy in copies:
+        copy.wait()
 
 
 def second_half_kernel(members, owners, first, rows_ref, counts_ref, gate_w, up_w, acc_in, *refs):
     parts, cots = refs[:owners], refs[owners : 2 * owners]
-    outs = refs[-(2 + len(members) + 3) :]
+    outs = refs[-(2 + len(members) + 1) :]
     grads_ref, hidden_ref = outs[:2]
-    dxs = outs[2 : 2 + len(members)]
-    cot_ref, acc_ref, cot_sems = outs[-3:]
+    dxs, acc_ref = outs[2:-1], outs[-1]
     cols, _, slots, tile, _ = gate_w.shape
-    shard_rows = cot_ref.shape[0] // len(members)
-    waits = start_cots(members, first * tile, cots, cot_ref, cot_sems)
+    shard_rows = hidden_ref.shape[0] // len(members)
     acc_ref[...] = acc_in[...]
-    for wait in waits:
-        wait.wait()
     for c in range(cols):
-        where = slice(c * tile, (c + 1) * tile)
-        hidden, grads = nonlinear(total_of(c, parts), cot_ref[:, where].astype(F32))
-        hidden_ref[:, where] = hidden
+        where = slice((first + c) * tile, (first + c + 1) * tile)
+        hidden, grads = nonlinear(total_of(c, parts), cotangent_of(members, cots, shard_rows, where))
+        hidden_ref[:, c * tile : (c + 1) * tile] = hidden
         grads_ref[c] = grads
         add_back(first + c, (rows_ref, counts_ref), back_terms(c, grads, gate_w, up_w), (acc_ref,), slots, tile)
     for r in range(acc_ref.shape[0]):
@@ -290,29 +269,24 @@
             dx[:, r * tile : (r + 1) * tile] = block[m * shard_rows : (m + 1) * shard_rows]
 
 
-def last_grads_kernel(members, first, start, with_hidden, rows_ref, counts_ref, turned_ref, *refs):
-    near_grads, far_grads, near_hidden, far_hidden = refs[:4]
+def last_grads_kernel(members, first, rows_ref, counts_ref, turned_ref, *refs):
+    near_grads, far_grads, hidden_a, near_hidden, far_hidden = refs[:5]
     gate_hbm, up_hbm, hidden_hbm, token_ref, gate_ref, up_ref, sems, hidden_sems = refs[-8:]
     cols, _, _, tile, _ = gate_ref.shape
     shard_rows = near_hidden.shape[0] // 2
     token_ref[...] = jnp.zeros_like(token_ref)
 
-    def hidden_of(m):
-        if m < 2:
-            return near_hidden.at[pl.ds(m * shard_rows, shard_rows)]
-        return far_hidden.at[pl.ds((m - 2) * shard_rows, shard_rows)]
-
-    waits = []
-    if with_hidden:
-        waits = start_hidden(
-            range(members), first * tile, hidden_of, hidden_hbm, shard_rows, hidden_sems
-        )
+    def parts(m):
+        mine = (near_hidden, m * shard_rows) if m < 2 else (far_hidden, (m - 2) * shard_rows)
+        return (hidden_a, m * shard_rows, 0), (*mine, first * tile)
+
+    copies = start_hidden(range(members), parts, hidden_hbm, shard_rows, hidden_sems)
     for c in range(cols):
-        grads = jnp.concatenate([near_grads[start + c], far_grads[start + c]], axis=0)
-        tile_grads(c, first + start, (rows_ref, counts_ref), turned_ref, grads, gate_ref, up_ref)
-        waits += store_tiles(first + start, c, gate_ref, up_ref, gate_hbm, up_hbm, sems)
-    for wait in waits:
-        wait.wait()
+        grads = jnp.concatenate([near_grads[c], far_grads[c]], axis=0)
+        tile_grads(c, first, (rows_ref, counts_ref), turned_ref, grads, gate_ref, up_ref)
+        copies += store_tiles(first, c, gate_ref, up_ref, gate_hbm, up_hbm, sems)
+    for copy in copies:
+        copy.wait()
 
 
 def copy_kernel(x_ref, _, out_ref):
@@ -346,7 +320,7 @@
     row_blocks = width // tile
     row_total = shards * shard_rows
     near_rows = 2 * shard_rows
-    half = max(1, cols * 3 // 8)
+    half = max(1, cols // 2)
     bases = range(2, shards, 2)
     lists = (jnp.transpose(block_rows, (2, 1, 0)), jnp.transpose(block_counts, (1, 0)))
 
@@ -374,15 +348,19 @@
     def from_hbm(*arrays):
         return [pltpu.with_memory_space_constraint(array, pltpu.HBM) for array in arrays]
 
-    near_a, *weights_a = pl.pallas_call(
+    near_a, *weights_a, rows_held, counts_held = pl.pallas_call(
         forward_own_kernel,
-        out_shape=(shape(half, shard_rows, 2 * tile), tile_shape(half), tile_shape(half)),
+        out_shape=(
+            shape(half, shard_rows, 2 * tile),
+            tile_shape(half),
+            tile_shape(half),
+            pltpu.SMEM(lists[0].shape, jnp.int32),
+            pltpu.SMEM(lists[1].shape, jnp.int32),
+        ),
         in_specs=[ANY_SPEC] * 5,
-        out_specs=(VMEM_SPEC,) * 3,
+        out_specs=(VMEM_SPEC,) * 3 + (SMEM_SPEC,) * 2,
         scratch_shapes=[
             pltpu.VMEM((shard_rows, width), BF16),
-            pltpu.SMEM(lists[0].shape, jnp.int32),
-            pltpu.SMEM(lists[1].shape, jnp.int32),
             pltpu.SemaphoreType.DMA((2, 3)),
             pltpu.SemaphoreType.DMA((3,)),
         ],
@@ -391,6 +369,7 @@
         name="forward_own_a",
     )(*from_hbm(features_in, *lists, gate_tiles, up_tiles))
     near_a = to_owners(near_a)
+    lists = (rows_held, counts_held)
 
     for far in fars:
         ready = pl.pallas_call(
@@ -436,32 +415,30 @@
     far_b, near_b = to_owners(far_b), to_owners(near_b)
 
     out_tiles = shape(*gate_tiles.shape)
-    gate_out, up_out, hidden_out, acc_near, acc_far = pl.pallas_call(
+    tile_bytes = slots * tile * tile * 2
+    gate_out, up_out, hidden_a, acc_near, acc_far = pl.pallas_call(
         functools.partial(first_half_kernel, shards, owners),
         out_shape=(
             out_tiles,
             out_tiles,
-            shape(*d_hidden.shape),
+            shape(row_total, half * tile),
             shape(row_blocks, near_rows, tile, dtype=F32),
             shape(row_blocks, row_total - near_rows, tile, dtype=F32),
         ),
-        in_specs=[SMEM_SPEC] * 2 + [VMEM_SPEC] * (3 + 2 * owners) + [ANY_SPEC] * (owners + 2),
-        out_specs=(ANY_SPEC,) * 3 + (VMEM_SPEC,) * 2,
+        in_specs=[SMEM_SPEC] * 2 + [VMEM_SPEC] * (3 + 3 * owners) + [ANY_SPEC] * 2,
+        out_specs=(ANY_SPEC,) * 2 + (VMEM_SPEC,) * 3,
         scratch_shapes=[
-            pltpu.VMEM((row_total, half * tile), BF16),
-            pltpu.VMEM((row_total, half * tile), BF16),
+            pltpu.VMEM((half, row_total, 2 * tile), BF16),
             tile_shape(half),
             tile_shape(half),
             pltpu.SemaphoreType.DMA((2, half)),
-            pltpu.SemaphoreType.DMA((shards,)),
-            pltpu.SemaphoreType.DMA((d_hidden.shape[0] // shard_rows,)),
         ],
-        compiler_params=limit(8 + 2 * half * slots * tile * tile * 2 // MIB),
+        compiler_params=limit(8 + 2 * half * tile_bytes // MIB),
         cost_estimate=cost(row_total, half, 2, 1, 1),
         name="first_half",
     )(*lists, *weights_a, turned, *near_a, *rest_a, *cots, far_b[0], near_b[0])
 
-    def second_half(members, acc, parts, after):
+    def second_half(members, acc, parts, after, weight):
         rows_here = len(members) * shard_rows
         return pl.pallas_call(
             functools.partial(second_half_kernel, members, owners, half),
@@ -470,19 +447,15 @@
                 shape(rows_here, rest * tile),
                 *[shape(shard_rows, width) for _ in members],
             ),
-            in_specs=[SMEM_SPEC] * 2 + [VMEM_SPEC] * (3 + owners) + [ANY_SPEC] * (owners + 1),
+            in_specs=[SMEM_SPEC] * 2 + [VMEM_SPEC] * (3 + 2 * owners) + [ANY_SPEC],
             out_specs=(VMEM_SPEC,) * (2 + len(members)),
-            scratch_shapes=[
-                pltpu.VMEM((rows_here, rest * tile), BF16),
-                pltpu.VMEM((row_blocks, rows_here, tile), F32),
-                pltpu.SemaphoreType.DMA((len(members),)),
-            ],
+            scratch_shapes=[pltpu.VMEM((row_blocks, rows_here, tile), F32)],
             compiler_params=limit(8),
-            cost_estimate=cost(rows_here, rest, 1, 1, 1 if members[0] == 0 else 1),
+            cost_estimate=cost(rows_here, rest, 1, 1, weight),
             name="second_half",
         )(*lists, *weights_b, acc, *parts, *cots, after)
 
-    far_grads, far_hidden, *far_dxs = second_half(range(2, shards), acc_far, far_b, acc_near)
+    far_grads, far_hidden, *far_dxs = second_half(range(2, shards), acc_far, far_b, acc_near, 1)
     both_cores = []
     for mine, others in zip(far_dxs[::2], far_dxs[1::2]):
         other = swap(others, "sub", 1)
@@ -499,30 +472,25 @@
         )
     back_far = [swap_far(total, base) for total, base in zip(both_cores, bases)]
 
-    near_grads, near_hidden, own_dx, next_dx = second_half(range(2), acc_near, near_b, both_cores[-1])
+    near_grads, near_hidden, own_dx, next_dx = second_half(range(2), acc_near, near_b, both_cores[-1], 1)
     back_next = swap(next_dx, "tok", 1)
 
-    def last_grads(start, stop, with_hidden, outs):
-        count = stop - start
-        return pl.pallas_call(
-            functools.partial(last_grads_kernel, shards, half, start, with_hidden),
-            out_shape=(out_tiles, out_tiles, shape(*d_hidden.shape), shape(8, tile, dtype=F32)),
-            in_specs=[SMEM_SPEC] * 2 + [VMEM_SPEC] * 3 + [ANY_SPEC] * 5,
-            out_specs=(ANY_SPEC,) * 3 + (VMEM_SPEC,),
-            scratch_shapes=[
-                pltpu.VMEM((count, 1, slots, tile, tile), BF16),
-                pltpu.VMEM((count, 1, slots, tile, tile), BF16),
-                pltpu.SemaphoreType.DMA((2, count)),
-                pltpu.SemaphoreType.DMA((d_hidden.shape[0] // shard_rows,)),
-            ],
-            input_output_aliases={7: 0, 8: 1, 9: 2},
-            compiler_params=limit(8 + 2 * count * slots * tile * tile * 2 // MIB),
-            cost_estimate=cost(row_total, count, 1, 1, 10),
-            name="last_grads",
-        )(*lists, turned, near_grads, far_grads, near_hidden, far_hidden, *outs)
-
-    middle = rest
-    *outs, token = last_grads(0, middle, True, (gate_out, up_out, hidden_out))
+    gate_out, up_out, hidden_out, token = pl.pallas_call(
+        functools.partial(last_grads_kernel, shards, half),
+        out_shape=(out_tiles, out_tiles, shape(*d_hidden.shape), shape(8, tile, dtype=F32)),
+        in_specs=[SMEM_SPEC] * 2 + [VMEM_SPEC] * 6 + [ANY_SPEC] * 2,
+        out_specs=(ANY_SPEC,) * 3 + (VMEM_SPEC,),
+        scratch_shapes=[
+            tile_shape(rest),
+            tile_shape(rest),
+            pltpu.SemaphoreType.DMA((2, rest)),
+            pltpu.SemaphoreType.DMA((2, d_hidden.shape[0] // shard_rows)),
+        ],
+        input_output_aliases={8: 0, 9: 1},
+        compiler_params=limit(8 + 2 * rest * tile_bytes // MIB),
+        cost_estimate=cost(row_total, rest, 1, 1, 10),
+        name="last_grads",
+    )(*lists, turned, near_grads, far_grads, hidden_a, near_hidden, far_hidden, gate_out, up_out)
     arrived = [own_dx, back_next, *back_far]
     mine, mine_sent = pl.pallas_call(
         functools.partial(sum_kernel, len(arrived)),
@@ -532,9 +500,6 @@
         compiler_params=limit(8),
         name="sum_shards",
     )(*arrived, token)
-    if middle < rest:
-        *outs, _ = last_grads(middle, rest, False, outs)
-    gate_out, up_out, hidden_out = outs
     features_grad = (mine + swap(mine_sent, "sub", 1).astype(F32)).astype(BF16)
     return (hidden_out, gate_out, up_out, features_grad)
 

time: 51.1 us -> 49.8 us (0.975)
  waiting for transfers between devices: 7.35 us -> 12.7 us
  Pallas kernels: 26.3 us -> 21.5 us
  starting transfers between devices: 15.9 us -> 14 us
    ppermute x10, waiting for transfers between devices: 7.2 us -> 12.7 us  [swap(): lax.ppermute(x, axis, [(i, i ^ step) for i in range(lax.axis_size(axis))])]
    pallas_call x2, Pallas kernels: 6.95 us -> 4.15 us  [second_half(): pl.pallas_call(functools.partial(second_half_kernel, members, owners, hal...]
    ppermute x10, starting transfers between devices: 11.1 us -> 9.72 us  [swap(): lax.ppermute(x, axis, [(i, i ^ step) for i in range(lax.axis_size(axis))])]
    pallas_call x1, Pallas kernels: 4.67 us -> 3.45 us  [on_device(): pl.pallas_call(functools.partial(load_forward_kernel, shards, ((near_rows...]
    pallas_call x1, Pallas kernels: 4.54 us -> 3.44 us  [on_device(): pl.pallas_call(functools.partial(last_grads_kernel, shards, half), out_sh...]
    ppermute x2, starting transfers between devices: 4.87 us -> 4.29 us  [swap_far(): return lax.ppermute(x, ('tok', 'sub'), pairs)]
    pallas_call x1, Pallas kernels: 3.56 us -> 4.07 us  [on_device(): pl.pallas_call(forward_own_kernel, out_shape=(shape(half, shard_rows, 2 *...]
  transfers between devices with their start and end apart: 12 -> 12, of which waited for: 7 -> 9; matrix products, arithmetic and copies ran while one was open for 0% -> 0% of each run, Pallas kernels for 51% -> 43%
where the time goes in v5:
time: 49.8 us; the launch traced here: 49.6 us
  Pallas kernels  21.5 us (43%)
  starting transfers between devices  14 us (28%)
  waiting for transfers between devices  12.7 us (26%)
  between operations  0.75 us (2%)
  other arithmetic  0.68 us (1%)
    ppermute x10, waiting for transfers between devices, swap(): lax.ppermute(x, axis, [(i, i ^ step) for i in range(lax.axis_size(axis))])  12.7 us
    ppermute x10, starting transfers between devices, swap(): lax.ppermute(x, axis, [(i, i ^ step) for i in range(lax.axis_size(axis))])  9.72 us
    pallas_call x1, Pallas kernels, on_device(): pl.pallas_call(functools.partial(first_half_kernel, shards, owners), out_...  5.14 us
    ppermute x2, starting transfers between devices, swap_far(): return lax.ppermute(x, ('tok', 'sub'), pairs)  4.29 us
    pallas_call x2, Pallas kernels, second_half(): pl.pallas_call(functools.partial(second_half_kernel, members, owners, hal...  4.15 us
    pallas_call x1, Pallas kernels, on_device(): pl.pallas_call(forward_own_kernel, out_shape=(shape(half, shard_rows, 2 *...  4.07 us
    pallas_call x1, Pallas kernels, on_device(): pl.pallas_call(functools.partial(load_forward_kernel, shards, ((near_rows...  3.45 us
    pallas_call x1, Pallas kernels, on_device(): pl.pallas_call(functools.partial(last_grads_kernel, shards, half), out_sh...  3.44 us
  transfers between devices with their start and end apart: 12, of which 9 were waited for; matrix products, arithmetic and copies ran while one was open for 0% of the time, Pallas kernels for 43%

profile of v5, /device:TPU:0, one launch (start us, length us, event | category | flops | bytes accessed | tf_op | source)
XLA Modules:
  0.0 49.6 jit_solution(5818827801540724774)
XLA Ops:
  0.6 4.1 %collective-permute-start.1 = (bf16[32,2048]{1,0:T(8,128)(2,1)}, bf16[32,2048]{1,0:T(8,128)(2,1)S(1)}, u32[]{:S(2)}, u32[]{:S(2)}) collective-permute-start(bf16[32,2048]{1,0:T(8,128)(2,1)} %refs_0_.1), channel_id=1, source_target_pairs={{0,8},{1,13},{4,12},{5,9},{8,0},{9,5},{12,4},{13,1},{2,10},{3,15},... | collective-permute-start | bytes 393224 | tf_op jit(solution)/shard_map/ppermute | solution.py:313
  4.7 1.5 %collective-permute-start.3 = (bf16[64,2048]{1,0:T(8,128)(2,1)}, bf16[64,2048]{1,0:T(8,128)(2,1)S(1)}, u32[]{:S(2)}, u32[]{:S(2)}) collective-permute-start(bf16[64,2048]{1,0:T(8,128)(2,1)} %refs_2_.3), channel_id=1, source_target_pairs={{0,2},{2,0},{1,3},{3,1},{4,6},{6,4},{5,7},{7,5},{8,10},{10,8},{9,1... | collective-permute-start | bytes 786440 | tf_op jit(solution)/shard_map/ppermute | solution.py:307
  6.2 1.6 %collective-permute-start = (bf16[32,2048]{1,0:T(8,128)(2,1)}, bf16[32,2048]{1,0:T(8,128)(2,1)S(1)}, u32[]{:S(2)}, u32[]{:S(2)}) collective-permute-start(bf16[32,2048]{1,0:T(8,128)(2,1)} %refs_0_.1), channel_id=1, source_target_pairs={{0,4},{4,0},{8,12},{12,8},{1,5},{5,1},{9,13},{13,9},{2,6},{6,2},{1... | collective-permute-start | bytes 393224 | tf_op jit(solution)/shard_map/ppermute | solution.py:307
  7.8 4.1 %forward_own_a.1 = (bf16[8,32,256]{2,1,0:T(8,128)(2,1)S(1)}, bf16[8,1,12,128,128]{4,3,2,1,0:T(8,128)(2,1)S(1)}, bf16[8,1,12,128,128]{4,3,2,1,0:T(8,128)(2,1)S(1)}, s32[12,1,16]{2,1,0:T(1,128)S(4)}, s32[1,16]{1,0:T(1,128)S(4)}) custom-call(bf16[32,2048]{1,0:T(8,128)(2,1)} %refs_0_.1, s32[12,1,16]{2,1,0:T(1,128)} %bitcast.2, s32[1,16]{1,0:T(1,128)} %bitcast.3, ...), custom_call_target="tpu_custom_call" | custom-call | flops 201326592 | bytes 6291456 | tf_op jit(solution)/shard_map/forward_own_a/pallas_call | solution.py:351
  11.9 0.0 copy-start.1
  11.9 0.1 collective-permute-start.2
  12.0 1.2 %collective-permute-start.4 = (bf16[8,32,256]{2,1,0:T(8,128)(2,1)S(1)}, bf16[8,32,256]{2,1,0:T(8,128)(2,1)S(1)}, u32[]{:S(2)}, u32[]{:S(2)}) collective-permute-start(bf16[8,32,256]{2,1,0:T(8,128)(2,1)S(1)} %get-tuple-element.35._.refs_0_), channel_id=1, source_target_pairs={{0,2},{2,0},{1,3},{3,1},{4,6},{6,4},{5,7},{7,5},{8,10},{10,8},{9,1... | collective-permute-start | bytes 393224 | tf_op jit(solution)/shard_map/ppermute | solution.py:307
  13.2 0.2 collective-permute-done.2.refs_2_.refs_3_
  13.3 0.4 collective-permute-done.3.refs_5_.refs_3_
  13.7 1.1 %forward_rest_a.1.refs_6_.refs_2_ = bf16[8,96,256]{2,1,0:T(8,128)(2,1)S(1)} custom-call(s32[12,1,16]{2,1,0:T(1,128)S(4)} %get-tuple-element.33.rows_ref, s32[1,16]{1,0:T(1,128)S(4)} %get-tuple-element.34.counts_ref, bf16[32,2048]{1,0:T(8,128)(2,1)S(1)} %collective-permute-done.refs_0_.refs_1_, ...), custom_call_target="tpu_custom_call" | custom-call | flops 805306368 | bytes 6291456 | tf_op jit(solution)/shard_map/forward_rest_a/pallas_call | solution.py:386
  14.9 0.0 copy-start
  14.9 1.5 %collective-permute-start.5 = (bf16[8,96,256]{2,1,0:T(8,128)(2,1)S(1)}, bf16[8,96,256]{2,1,0:T(8,128)(2,1)S(1)}, u32[]{:S(2)}, u32[]{:S(2)}) collective-permute-start(bf16[8,96,256]{2,1,0:T(8,128)(2,1)S(1)} %forward_rest_a.1.refs_6_.refs_2_), channel_id=1, source_target_pairs={{0,2},{2,0},{1,3},{3,1},{4,6},{6,4},{5,7},{7,5},{8,10},{10,8},{9,1... | collective-permute-start | bytes 1179656 | tf_op jit(solution)/shard_map/ppermute | solution.py:307
  16.4 1.9 %collective-permute-done.4.refs_7_.refs_1_ = bf16[8,32,256]{2,1,0:T(8,128)(2,1)S(1)} collective-permute-done((bf16[8,32,256]{2,1,0:T(8,128)(2,1)S(1)}, bf16[8,32,256]{2,1,0:T(8,128)(2,1)S(1)}, u32[]{:S(2)}, u32[]{:S(2)}) %collective-permute-start.4) | collective-permute-done | bytes 131104 | tf_op jit(solution)/shard_map/ppermute | solution.py:307
  18.4 3.4 %forward_b.1 = (bf16[8,64,256]{2,1,0:T(8,128)(2,1)S(1)}, bf16[8,64,256]{2,1,0:T(8,128)(2,1)S(1)}, bf16[8,1,12,128,128]{4,3,2,1,0:T(8,128)(2,1)S(1)}, bf16[8,1,12...) custom-call(s32[12,1,16]{2,1,0:T(1,128)S(4)} %get-tuple-element.33.rows_ref, ...), custom_call_target="tpu_custom_call" | custom-call | flops 4026531840 | bytes 31457280 | tf_op jit(solution)/shard_map/forward_b/pallas_call | solution.py:398
  21.8 0.8 %collective-permute-start.7 = (bf16[8,64,256]{2,1,0:T(8,128)(2,1)S(1)}, bf16[8,64,256]{2,1,0:T(8,128)(2,1)S(1)}, u32[]{:S(2)}, u32[]{:S(2)}) collective-permute-start(bf16[8,64,256]{2,1,0:T(8,128)(2,1)S(1)} %get-tuple-element.41.refs_6_.refs_0_), channel_id=1, source_target_pairs={{0,2},{2,0},{1,3},{3,1},{4,6},{6,4},{5,7},{7,5},{8,10},{10,8},{9,1... | collective-permute-start | bytes 786440 | tf_op jit(solution)/shard_map/ppermute | solution.py:307
  22.6 1.3 %collective-permute-start.6 = (bf16[8,64,256]{2,1,0:T(8,128)(2,1)S(1)}, bf16[8,64,256]{2,1,0:T(8,128)(2,1)S(1)}, u32[]{:S(2)}, u32[]{:S(2)}) collective-permute-start(bf16[8,64,256]{2,1,0:T(8,128)(2,1)S(1)} %get-tuple-element.42.refs_7_.refs_0_), channel_id=1, source_target_pairs={{0,2},{2,0},{1,3},{3,1},{4,6},{6,4},{5,7},{7,5},{8,10},{10,8},{9,1... | collective-permute-start | bytes 786440 | tf_op jit(solution)/shard_map/ppermute | solution.py:307
  23.9 3.1 %collective-permute-done.5.refs_3_ = bf16[8,96,256]{2,1,0:T(8,128)(2,1)S(1)} collective-permute-done((bf16[8,96,256]{2,1,0:T(8,128)(2,1)S(1)}, bf16[8,96,256]{2,1,0:T(8,128)(2,1)S(1)}, u32[]{:S(2)}, u32[]{:S(2)}) %collective-permute-start.5) | collective-permute-done | bytes 393248 | tf_op jit(solution)/shard_map/ppermute | solution.py:307
  27.0 5.1 %first_half.1 = (bf16[16,1,12,128,128]{4,3,2,1,0:T(8,128)(2,1)}, bf16[16,1,12,128,128]{4,3,2,1,0:T(8,128)(2,1)}, bf16[128,1024]{1,0:T(8,128)(2,1)S(1)}, f32[16,64,128]{2,1,0:T(8,128)S(1)}, f32[16,64,128]{2,1,0:T(8,128)S(1)}) custom-call(s32[12,1,16]{2,1,0:T(1,128)S(4)} %get-tuple-element.33.rows_ref, s32[1,16]{1,0:T(1,128)S(4)} %get-tuple-element.34.counts_ref, ...), custom_call_target="tpu_custom_call" | custom-call | flops 1610612736 | bytes 6291456 | tf_op jit(solution)/shard_map/first_half/pallas_call | solution.py:419
  32.2 0.5 collective-permute-done.7.refs_1_
  32.6 2.1 %second_half.2 = (bf16[8,64,256]{2,1,0:T(8,128)(2,1)S(1)}, bf16[64,1024]{1,0:T(8,128)(2,1)S(1)}, bf16[32,2048]{1,0:T(8,128)(2,1)S(1)}, bf16[32,2048]{1,0:T(8,128)(2,1)S(1)}) custom-call(s32[12,1,16]{2,1,0:T(1,128)S(4)} %get-tuple-element.33.rows_ref, s32[1,16]{1,0:T(1,128)S(4)} %get-tuple-element.34.counts_ref, ...), custom_call_target="tpu_custom_call" | custom-call | flops 402653184 | bytes 6291456 | tf_op jit(solution)/shard_map/second_half/pallas_call | solution.py:443
  34.7 0.1 collective-permute-start.8
  34.8 1.3 %collective-permute-done.8.right_ref = bf16[32,2048]{1,0:T(8,128)(2,1)S(1)} collective-permute-done((bf16[32,2048]{1,0:T(8,128)(2,1)S(1)}, bf16[32,2048]{1,0:T(8,128)(2,1)S(1)}, u32[]{:S(2)}, u32[]{:S(2)}) %collective-permute-start.8) | collective-permute-done | bytes 131104 | tf_op jit(solution)/shard_map/ppermute | solution.py:307
  36.2 0.2 collective-permute-start.10
  36.3 1.2 %collective-permute-done.6.refs_1_ = bf16[8,64,256]{2,1,0:T(8,128)(2,1)S(1)} collective-permute-done((bf16[8,64,256]{2,1,0:T(8,128)(2,1)S(1)}, bf16[8,64,256]{2,1,0:T(8,128)(2,1)S(1)}, u32[]{:S(2)}, u32[]{:S(2)}) %collective-permute-start.6) | collective-permute-done | bytes 262176 | tf_op jit(solution)/shard_map/ppermute | solution.py:307
  37.6 2.1 %second_half.3 = (bf16[8,64,256]{2,1,0:T(8,128)(2,1)S(1)}, bf16[64,1024]{1,0:T(8,128)(2,1)S(1)}, bf16[32,2048]{1,0:T(8,128)(2,1)S(1)}, bf16[32,2048]{1,0:T(8,128)(2,1)S(1)}) custom-call(s32[12,1,16]{2,1,0:T(1,128)S(4)} %get-tuple-element.33.rows_ref, s32[1,16]{1,0:T(1,128)S(4)} %get-tuple-element.34.counts_ref, ...), custom_call_target="tpu_custom_call" | custom-call | flops 402653184 | bytes 6291456 | tf_op jit(solution)/shard_map/second_half/pallas_call | solution.py:443
  39.7 1.5 %collective-permute-start.9 = (bf16[32,2048]{1,0:T(8,128)(2,1)S(1)}, bf16[32,2048]{1,0:T(8,128)(2,1)S(1)}, u32[]{:S(2)}, u32[]{:S(2)}) collective-permute-start(bf16[32,2048]{1,0:T(8,128)(2,1)S(1)} %get-tuple-element.58), channel_id=1, source_target_pairs={{0,4},{4,0},{8,12},{12,8},{1,5},{5,1},{9,13},{13,9},{2,6},{6,2},{1... | collective-permute-start | bytes 393224 | tf_op jit(solution)/shard_map/ppermute | solution.py:307
  41.2 3.4 %last_grads.1 = (bf16[16,1,12,128,128]{4,3,2,1,0:T(8,128)(2,1)}, bf16[16,1,12,128,128]{4,3,2,1,0:T(8,128)(2,1)}, bf16[64,2048]{1,0:T(8,128)(2,1)}, f32[8,128]{1,0:T(8,128)S(1)}) custom-call(s32[12,1,16]{2,1,0:T(1,128)S(4)} %get-tuple-element.33.rows_ref, s32[1,16]{1,0:T(1,128)S(4)} %get-tuple-element.34.counts_ref, ...), custom_call_target="tpu_custom_call", output_to_operand_aliasing={{0}: (8, {}), {1}: (9, {})} | custom-call | flops 8053063680 | bytes 62914560 | tf_op jit(solution)/shard_map/last_grads/pallas_call | solution.py:478
  44.7 2.8 %collective-permute-done.9.refs_1_ = bf16[32,2048]{1,0:T(8,128)(2,1)S(1)} collective-permute-done((bf16[32,2048]{1,0:T(8,128)(2,1)S(1)}, bf16[32,2048]{1,0:T(8,128)(2,1)S(1)}, u32[]{:S(2)}, u32[]{:S(2)}) %collective-permute-start.9) | collective-permute-done | bytes 131104 | tf_op jit(solution)/shard_map/ppermute | solution.py:307
  47.5 0.1 sum_shards.1
  47.5 0.2 collective-permute-start.11
  47.7 1.2 %collective-permute-done.11 = bf16[32,2048]{1,0:T(8,128)(2,1)S(1)} collective-permute-done((bf16[32,2048]{1,0:T(8,128)(2,1)S(1)}, bf16[32,2048]{1,0:T(8,128)(2,1)S(1)}, u32[]{:S(2)}, u32[]{:S(2)}) %collective-permute-start.11) | collective-permute-done | bytes 131104 | tf_op jit(solution)/shard_map/ppermute | solution.py:307
  48.9 0.7 %add_convert_fusion = bf16[32,2048]{1,0:T(8,128)(2,1)} fusion(f32[32,2048]{1,0:T(8,128)S(1)} %get-tuple-element.60, bf16[32,2048]{1,0:T(8,128)(2,1)S(1)} %collective-permute-done.11), kind=kLoop, calls=%fused_computation | loop fusion | flops 196608 | bytes 524288 | tf_op jit(solution)/shard_map/convert_element_type | solution.py:503
  (7 shorter events, 0.1 us)
Async XLA Ops:
  0.6 11.3 %collective-permute-start.1 = (bf16[32,2048]{1,0:T(8,128)(2,1)}, bf16[32,2048]{1,0:T(8,128)(2,1)S(1)}, u32[]{:S(2)}, u32[]{:S(2)}) collective-permute-start(bf16[32,2048]{1,0:T(8,128)(2,1)} %refs_0_.1), channel_id=1, source_target_pairs={{0,8},{1,13},{4,12},{5,9},{8,0},{9,5},{12,4},{13,1},{2,10},{3,15},... | collective-permute-start | bytes 393224 | tf_op jit(solution)/shard_map/ppermute | solution.py:313
  4.7 9.0 %collective-permute-start.3 = (bf16[64,2048]{1,0:T(8,128)(2,1)}, bf16[64,2048]{1,0:T(8,128)(2,1)S(1)}, u32[]{:S(2)}, u32[]{:S(2)}) collective-permute-start(bf16[64,2048]{1,0:T(8,128)(2,1)} %refs_2_.3), channel_id=1, source_target_pairs={{0,2},{2,0},{1,3},{3,1},{4,6},{6,4},{5,7},{7,5},{8,10},{10,8},{9,1... | collective-permute-start | bytes 786440 | tf_op jit(solution)/shard_map/ppermute | solution.py:307
  6.2 6.9 %collective-permute-start = (bf16[32,2048]{1,0:T(8,128)(2,1)}, bf16[32,2048]{1,0:T(8,128)(2,1)S(1)}, u32[]{:S(2)}, u32[]{:S(2)}) collective-permute-start(bf16[32,2048]{1,0:T(8,128)(2,1)} %refs_0_.1), channel_id=1, source_target_pairs={{0,4},{4,0},{8,12},{12,8},{1,5},{5,1},{9,13},{13,9},{2,6},{6,2},{1... | collective-permute-start | bytes 393224 | tf_op jit(solution)/shard_map/ppermute | solution.py:307
  11.9 6.5 %copy-start.1 = (bf16[32,2048]{1,0:T(8,128)(2,1)S(1)}, bf16[32,2048]{1,0:T(8,128)(2,1)}, u32[]{:S(2)}) copy-start(bf16[32,2048]{1,0:T(8,128)(2,1)} %refs_0_.1) | copy-start | bytes 393220
  11.9 1.4 %collective-permute-start.2 = (bf16[32,2048]{1,0:T(8,128)(2,1)S(1)}, bf16[32,2048]{1,0:T(8,128)(2,1)S(1)}, u32[]{:S(2)}, u32[]{:S(2)}) collective-permute-start(bf16[32,2048]{1,0:T(8,128)(2,1)S(1)} %after_own.1), channel_id=1, source_target_pairs={{0,1},{1,0},{2,3},{3,2},{4,5},{5,4},{6,7},{7,6},{8,9},{9,8},{10,11... | collective-permute-start | bytes 393224 | tf_op jit(solution)/shard_map/ppermute | solution.py:307
  12.0 6.4 %collective-permute-start.4 = (bf16[8,32,256]{2,1,0:T(8,128)(2,1)S(1)}, bf16[8,32,256]{2,1,0:T(8,128)(2,1)S(1)}, u32[]{:S(2)}, u32[]{:S(2)}) collective-permute-start(bf16[8,32,256]{2,1,0:T(8,128)(2,1)S(1)} %get-tuple-element.35._.refs_0_), channel_id=1, source_target_pairs={{0,2},{2,0},{1,3},{3,1},{4,6},{6,4},{5,7},{7,5},{8,10},{10,8},{9,1... | collective-permute-start | bytes 393224 | tf_op jit(solution)/shard_map/ppermute | solution.py:307
  14.9 12.1 %copy-start = (bf16[64,2048]{1,0:T(8,128)(2,1)S(1)}, bf16[64,2048]{1,0:T(8,128)(2,1)}, u32[]{:S(2)}) copy-start(bf16[64,2048]{1,0:T(8,128)(2,1)} %refs_2_.3) | copy-start | bytes 786436
  14.9 12.1 %collective-permute-start.5 = (bf16[8,96,256]{2,1,0:T(8,128)(2,1)S(1)}, bf16[8,96,256]{2,1,0:T(8,128)(2,1)S(1)}, u32[]{:S(2)}, u32[]{:S(2)}) collective-permute-start(bf16[8,96,256]{2,1,0:T(8,128)(2,1)S(1)} %forward_rest_a.1.refs_6_.refs_2_), channel_id=1, source_target_pairs={{0,2},{2,0},{1,3},{3,1},{4,6},{6,4},{5,7},{7,5},{8,10},{10,8},{9,1... | collective-permute-start | bytes 1179656 | tf_op jit(solution)/shard_map/ppermute | solution.py:307
  21.8 10.8 %collective-permute-start.7 = (bf16[8,64,256]{2,1,0:T(8,128)(2,1)S(1)}, bf16[8,64,256]{2,1,0:T(8,128)(2,1)S(1)}, u32[]{:S(2)}, u32[]{:S(2)}) collective-permute-start(bf16[8,64,256]{2,1,0:T(8,128)(2,1)S(1)} %get-tuple-element.41.refs_6_.refs_0_), channel_id=1, source_target_pairs={{0,2},{2,0},{1,3},{3,1},{4,6},{6,4},{5,7},{7,5},{8,10},{10,8},{9,1... | collective-permute-start | bytes 786440 | tf_op jit(solution)/shard_map/ppermute | solution.py:307
  22.6 14.9 %collective-permute-start.6 = (bf16[8,64,256]{2,1,0:T(8,128)(2,1)S(1)}, bf16[8,64,256]{2,1,0:T(8,128)(2,1)S(1)}, u32[]{:S(2)}, u32[]{:S(2)}) collective-permute-start(bf16[8,64,256]{2,1,0:T(8,128)(2,1)S(1)} %get-tuple-element.42.refs_7_.refs_0_), channel_id=1, source_target_pairs={{0,2},{2,0},{1,3},{3,1},{4,6},{6,4},{5,7},{7,5},{8,10},{10,8},{9,1... | collective-permute-start | bytes 786440 | tf_op jit(solution)/shard_map/ppermute | solution.py:307
  34.7 1.4 %collective-permute-start.8 = (bf16[32,2048]{1,0:T(8,128)(2,1)S(1)}, bf16[32,2048]{1,0:T(8,128)(2,1)S(1)}, u32[]{:S(2)}, u32[]{:S(2)}) collective-permute-start(bf16[32,2048]{1,0:T(8,128)(2,1)S(1)} %get-tuple-element.46), channel_id=1, source_target_pairs={{0,1},{1,0},{2,3},{3,2},{4,5},{5,4},{6,7},{7,6},{8,9},{9,8},{10,11... | collective-permute-start | bytes 393224 | tf_op jit(solution)/shard_map/ppermute | solution.py:307
  36.2 11.3 %collective-permute-start.10 = (bf16[32,2048]{1,0:T(8,128)(2,1)S(1)}, bf16[32,2048]{1,0:T(8,128)(2,1)S(1)}, u32[]{:S(2)}, u32[]{:S(2)}) collective-permute-start(bf16[32,2048]{1,0:T(8,128)(2,1)S(1)} %add_cores.1.refs_4_), channel_id=1, source_target_pairs={{0,8},{1,13},{4,12},{5,9},{8,0},{9,5},{12,4},{13,1},{2,10},{3,15},... | collective-permute-start | bytes 393224 | tf_op jit(solution)/shard_map/ppermute | solution.py:313
  39.7 7.8 %collective-permute-start.9 = (bf16[32,2048]{1,0:T(8,128)(2,1)S(1)}, bf16[32,2048]{1,0:T(8,128)(2,1)S(1)}, u32[]{:S(2)}, u32[]{:S(2)}) collective-permute-start(bf16[32,2048]{1,0:T(8,128)(2,1)S(1)} %get-tuple-element.58), channel_id=1, source_target_pairs={{0,4},{4,0},{8,12},{12,8},{1,5},{5,1},{9,13},{13,9},{2,6},{6,2},{1... | collective-permute-start | bytes 393224 | tf_op jit(solution)/shard_map/ppermute | solution.py:307
  47.5 1.4 %collective-permute-start.11 = (bf16[32,2048]{1,0:T(8,128)(2,1)S(1)}, bf16[32,2048]{1,0:T(8,128)(2,1)S(1)}, u32[]{:S(2)}, u32[]{:S(2)}) collective-permute-start(bf16[32,2048]{1,0:T(8,128)(2,1)S(1)} %get-tuple-element.61), channel_id=1, source_target_pairs={{0,1},{1,0},{2,3},{3,2},{4,5},{5,4},{6,7},{7,6},{8,9},{9,8},{10,11... | collective-permute-start | bytes 393224 | tf_op jit(solution)/shard_map/ppermute | solution.py:307

commit v6 on v5

--- a/solution.py
+++ b/solution.py
@@ -227,24 +227,27 @@
 
 
 def first_half_kernel(members, owners, rows_ref, counts_ref, gate_w, up_w, turned_ref, *refs):
-    near, rest, cots = refs[:owners], refs[owners : 2 * owners], refs[2 * owners : 3 * owners]
-    gate_hbm, up_hbm, hidden_ref, acc_near, acc_far, grads_ref, gate_ref, up_ref, sems = refs[-9:]
+    groups = [refs[start : start + owners] for start in range(0, 3 * owners, owners)]
+    cots = refs[3 * owners : 4 * owners]
+    gate_hbm, up_hbm, hidden_ref = refs[-10:-7]
+    accs = refs[-7:-4]
+    grads_ref, gate_ref, up_ref, sems = refs[-4:]
     cols, _, slots, tile, _ = gate_ref.shape
-    shard_rows = hidden_ref.shape[0] // members
+    shard_rows = hidden_ref.shape[0] // len(members)
     lists = (rows_ref, counts_ref)
-    acc_near[...] = jnp.zeros_like(acc_near)
-    acc_far[...] = jnp.zeros_like(acc_far)
+    for acc in accs:
+        acc[...] = jnp.zeros_like(acc)
     copies = []
     for c in range(cols):
-        total = jnp.concatenate([total_of(c, near), total_of(c, rest)], axis=0)
+        total = jnp.concatenate([total_of(c, parts) for parts in groups], axis=0)
         where = slice(c * tile, (c + 1) * tile)
-        hidden, grads = nonlinear(total, cotangent_of(range(members), cots, shard_rows, where))
+        hidden, grads = nonlinear(total, cotangent_of(members, cots, shard_rows, where))
         hidden_ref[:, where] = hidden
         grads_ref[c] = grads
         tile_grads(c, 0, lists, turned_ref, grads, gate_ref, up_ref)
         copies += store_tiles(0, c, gate_ref, up_ref, gate_hbm, up_hbm, sems)
     for c in range(cols):
-        add_back(c, lists, back_terms(c, grads_ref[c], gate_w, up_w), (acc_near, acc_far), slots, tile)
+        add_back(c, lists, back_terms(c, grads_ref[c], gate_w, up_w), accs, slots, tile)
     for copy in copies:
         copy.wait()
 
@@ -270,19 +273,20 @@
 
 
 def last_grads_kernel(members, first, rows_ref, counts_ref, turned_ref, *refs):
-    near_grads, far_grads, hidden_a, near_hidden, far_hidden = refs[:5]
+    all_grads, hidden_a, hiddens = refs[:3], refs[3], refs[4:7]
     gate_hbm, up_hbm, hidden_hbm, token_ref, gate_ref, up_ref, sems, hidden_sems = refs[-8:]
     cols, _, _, tile, _ = gate_ref.shape
-    shard_rows = near_hidden.shape[0] // 2
+    shard_rows = hiddens[0].shape[0]
     token_ref[...] = jnp.zeros_like(token_ref)
 
-    def parts(m):
-        mine = (near_hidden, m * shard_rows) if m < 2 else (far_hidden, (m - 2) * shard_rows)
-        return (hidden_a, m * shard_rows, 0), (*mine, first * tile)
-
-    copies = start_hidden(range(members), parts, hidden_hbm, shard_rows, hidden_sems)
+    def parts(member):
+        at = members.index(member)
+        mine = (hiddens[at], 0) if at < 2 else (hiddens[2], (at - 2) * shard_rows)
+        return (hidden_a, at * shard_rows, 0), (*mine, first * tile)
+
+    copies = start_hidden(members, parts, hidden_hbm, shard_rows, hidden_sems)
     for c in range(cols):
-        grads = jnp.concatenate([near_grads[c], far_grads[c]], axis=0)
+        grads = jnp.concatenate([part[c] for part in all_grads], axis=0)
         tile_grads(c, first, (rows_ref, counts_ref), turned_ref, grads, gate_ref, up_ref)
         copies += store_tiles(first, c, gate_ref, up_ref, gate_hbm, up_hbm, sems)
     for copy in copies:
@@ -293,7 +297,8 @@
     out_ref[...] = x_ref[...]
 
 
-def add_kernel(left_ref, right_ref, out_ref):
+def add_kernel(left_ref, right_ref, *refs):
+    out_ref = refs[-1]
     out_ref[...] = (left_ref[...].astype(F32) + right_ref[...].astype(F32)).astype(BF16)
 
 
@@ -339,7 +344,7 @@
         return [part] + [swap(part, "blk", s) for s in range(1, owners)]
 
     fars = [swap_far(features_in, base) for base in bases]
-    xs = [features_in, swap(features_in, "tok", 1)]
+    features_next = swap(features_in, "tok", 1)
     cots = [d_hidden] + [swap(d_hidden, "blk", s) for s in range(1, owners)]
 
     def tile_shape(columns):
@@ -371,8 +376,11 @@
     near_a = to_owners(near_a)
     lists = (rows_held, counts_held)
 
-    for far in fars:
-        ready = pl.pallas_call(
+    members = [0, 1, *range(2, shards, 2), *range(3, shards, 2)]
+    far_members = members[2:]
+    own_rows, far_rows = shard_rows, row_total - near_rows
+    before_swap = [
+        pl.pallas_call(
             copy_kernel,
             out_shape=shape(shard_rows, width),
             in_specs=[VMEM_SPEC, ANY_SPEC],
@@ -381,52 +389,61 @@
             cost_estimate=pl.CostEstimate(flops=0, bytes_accessed=0, transcendentals=0),
             name="after_own",
         )(far, near_a[0])
-        xs += [far, swap(ready, "sub", 1)]
-
-    rest_a = pl.pallas_call(
-        functools.partial(forward_kernel, shards - 1),
-        out_shape=shape(half, row_total - shard_rows, 2 * tile),
-        in_specs=[SMEM_SPEC] * 2 + [VMEM_SPEC] * (shards + 1) + [ANY_SPEC],
-        out_specs=VMEM_SPEC,
-        compiler_params=limit(8),
-        cost_estimate=cost(row_total, half, 1, 1),
-        name="forward_rest_a",
-    )(*lists, *xs[1:], *weights_a, cots[-1])
-    rest_a = to_owners(rest_a)
+        for far in fars
+    ]
+    fetched = [features_next, *fars]
+    swapped = [swap(far, "sub", 1) for far in before_swap]
+    xs = [features_in, *fetched, *swapped]
+
+    def forward_a(name, shard_xs, after):
+        tokens = len(shard_xs) * shard_rows
+        return to_owners(
+            pl.pallas_call(
+                functools.partial(forward_kernel, len(shard_xs)),
+                out_shape=shape(half, tokens, 2 * tile),
+                in_specs=[SMEM_SPEC] * 2 + [VMEM_SPEC] * (len(shard_xs) + 2) + [ANY_SPEC] * len(after),
+                out_specs=VMEM_SPEC,
+                compiler_params=limit(8),
+                cost_estimate=cost(tokens, half, 1, 1),
+                name=name,
+            )(*lists, *shard_xs, *weights_a, *after)
+        )
+
+    fetched_a = forward_a("forward_fetched_a", fetched, [cots[-1], before_swap[-1]])
+    swapped_a = forward_a("forward_swapped_a", swapped, [fetched_a[0]])
 
     rest = cols - half
-    far_b, near_b, gate_b, up_b, turned = pl.pallas_call(
-        functools.partial(load_forward_kernel, shards, ((near_rows, row_total), (0, near_rows)), half, 1),
+    groups = ((near_rows, row_total), (own_rows, near_rows), (0, own_rows))
+    far_b, next_b, own_b, gate_b, up_b, turned = pl.pallas_call(
+        functools.partial(load_forward_kernel, shards, groups, half, 1),
         out_shape=(
-            shape(rest, row_total - near_rows, 2 * tile),
-            shape(rest, near_rows, 2 * tile),
+            *[shape(rest, stop - start, 2 * tile) for start, stop in groups],
             tile_shape(rest),
             tile_shape(rest),
             pltpu.VMEM((row_blocks, tile, row_total), BF16),
         ),
         in_specs=[SMEM_SPEC] * 2 + [VMEM_SPEC] * shards + [ANY_SPEC] * 4,
-        out_specs=(VMEM_SPEC,) * 5,
+        out_specs=(VMEM_SPEC,) * 6,
         scratch_shapes=[pltpu.SemaphoreType.DMA((2, 3))],
         compiler_params=limit(8),
         cost_estimate=cost(row_total, rest, 1, 1, 5),
         name="forward_b",
-    )(*lists, *xs, *from_hbm(gate_tiles, up_tiles), rest_a[0], near_a[-1])
+    )(*lists, *xs, *from_hbm(gate_tiles, up_tiles), swapped_a[0], near_a[-1])
     weights_b = [gate_b, up_b]
-    far_b, near_b = to_owners(far_b), to_owners(near_b)
+    far_b, next_b, own_b = to_owners(far_b), to_owners(next_b), to_owners(own_b)
 
     out_tiles = shape(*gate_tiles.shape)
     tile_bytes = slots * tile * tile * 2
-    gate_out, up_out, hidden_a, acc_near, acc_far = pl.pallas_call(
-        functools.partial(first_half_kernel, shards, owners),
+    gate_out, up_out, hidden_a, acc_own, acc_next, acc_far = pl.pallas_call(
+        functools.partial(first_half_kernel, members, owners),
         out_shape=(
             out_tiles,
             out_tiles,
             shape(row_total, half * tile),
-            shape(row_blocks, near_rows, tile, dtype=F32),
-            shape(row_blocks, row_total - near_rows, tile, dtype=F32),
+            *[shape(row_blocks, rows, tile, dtype=F32) for rows in (own_rows, own_rows, far_rows)],
         ),
-        in_specs=[SMEM_SPEC] * 2 + [VMEM_SPEC] * (3 + 3 * owners) + [ANY_SPEC] * 2,
-        out_specs=(ANY_SPEC,) * 2 + (VMEM_SPEC,) * 3,
+        in_specs=[SMEM_SPEC] * 2 + [VMEM_SPEC] * (3 + 4 * owners) + [ANY_SPEC] * 3,
+        out_specs=(ANY_SPEC,) * 2 + (VMEM_SPEC,) * 4,
         scratch_shapes=[
             pltpu.VMEM((half, row_total, 2 * tile), BF16),
             tile_shape(half),
@@ -436,49 +453,50 @@
         compiler_params=limit(8 + 2 * half * tile_bytes // MIB),
         cost_estimate=cost(row_total, half, 2, 1, 1),
         name="first_half",
-    )(*lists, *weights_a, turned, *near_a, *rest_a, *cots, far_b[0], near_b[0])
-
-    def second_half(members, acc, parts, after, weight):
-        rows_here = len(members) * shard_rows
+    )(
+        *lists, *weights_a, turned, *near_a, *fetched_a, *swapped_a, *cots, far_b[0], next_b[0], own_b[0]
+    )
+
+    def second_half(name, chunk, acc, parts, after, weight):
+        rows_here = len(chunk) * shard_rows
         return pl.pallas_call(
-            functools.partial(second_half_kernel, members, owners, half),
+            functools.partial(second_half_kernel, chunk, owners, half),
             out_shape=(
                 shape(rest, rows_here, 2 * tile),
                 shape(rows_here, rest * tile),
-                *[shape(shard_rows, width) for _ in members],
+                *[shape(shard_rows, width) for _ in chunk],
             ),
             in_specs=[SMEM_SPEC] * 2 + [VMEM_SPEC] * (3 + 2 * owners) + [ANY_SPEC],
-            out_specs=(VMEM_SPEC,) * (2 + len(members)),
+            out_specs=(VMEM_SPEC,) * (2 + len(chunk)),
             scratch_shapes=[pltpu.VMEM((row_blocks, rows_here, tile), F32)],
             compiler_params=limit(8),
             cost_estimate=cost(rows_here, rest, 1, 1, weight),
-            name="second_half",
+            name=name,
         )(*lists, *weights_b, acc, *parts, *cots, after)
 
-    far_grads, far_hidden, *far_dxs = second_half(range(2, shards), acc_far, far_b, acc_near, 1)
+    far_grads, far_hidden, *far_dxs = second_half("far_b", far_members, acc_far, far_b, acc_own, 1)
+    next_grads, next_hidden, next_dx = second_half("next_b", [1], acc_next, next_b, far_grads, 1)
     both_cores = []
-    for mine, others in zip(far_dxs[::2], far_dxs[1::2]):
-        other = swap(others, "sub", 1)
+    for mine, others in zip(far_dxs[: len(bases)], far_dxs[len(bases) :]):
         both_cores.append(
             pl.pallas_call(
                 add_kernel,
                 out_shape=shape(shard_rows, width),
-                in_specs=[VMEM_SPEC] * 2,
+                in_specs=[VMEM_SPEC] * 2 + [ANY_SPEC] * 2,
                 out_specs=VMEM_SPEC,
                 compiler_params=limit(8),
                 cost_estimate=pl.CostEstimate(flops=0, bytes_accessed=0, transcendentals=0),
                 name="add_cores",
-            )(mine, other)
+            )(mine, swap(others, "sub", 1), next_grads, own_b[-1])
         )
     back_far = [swap_far(total, base) for total, base in zip(both_cores, bases)]
-
-    near_grads, near_hidden, own_dx, next_dx = second_half(range(2), acc_near, near_b, both_cores[-1], 1)
     back_next = swap(next_dx, "tok", 1)
+    own_grads, own_hidden, own_dx = second_half("own_b", [0], acc_own, own_b, both_cores[-1], 1)
 
     gate_out, up_out, hidden_out, token = pl.pallas_call(
-        functools.partial(last_grads_kernel, shards, half),
+        functools.partial(last_grads_kernel, members, half),
         out_shape=(out_tiles, out_tiles, shape(*d_hidden.shape), shape(8, tile, dtype=F32)),
-        in_specs=[SMEM_SPEC] * 2 + [VMEM_SPEC] * 6 + [ANY_SPEC] * 2,
+        in_specs=[SMEM_SPEC] * 2 + [VMEM_SPEC] * 8 + [ANY_SPEC] * 2,
         out_specs=(ANY_SPEC,) * 3 + (VMEM_SPEC,),
         scratch_shapes=[
             tile_shape(rest),
@@ -486,11 +504,23 @@
             pltpu.SemaphoreType.DMA((2, rest)),
             pltpu.SemaphoreType.DMA((2, d_hidden.shape[0] // shard_rows)),
         ],
-        input_output_aliases={8: 0, 9: 1},
+        input_output_aliases={10: 0, 11: 1},
         compiler_params=limit(8 + 2 * rest * tile_bytes // MIB),
         cost_estimate=cost(row_total, rest, 1, 1, 10),
         name="last_grads",
-    )(*lists, turned, near_grads, far_grads, hidden_a, near_hidden, far_hidden, gate_out, up_out)
+    )(
+        *lists,
+        turned,
+        own_grads,
+        next_grads,
+        far_grads,
+        hidden_a,
+        own_hidden,
+        next_hidden,
+        far_hidden,
+        gate_out,
+        up_out,
+    )
     arrived = [own_dx, back_next, *back_far]
     mine, mine_sent = pl.pallas_call(
         functools.partial(sum_kernel, len(arrived)),

time: 49.8 us -> 52.1 us (1.046)
  Pallas kernels: 21.5 us -> 24.7 us
  waiting for transfers between devices: 12.7 us -> 9.64 us
  starting transfers between devices: 14 us -> 16.2 us
    ppermute x10 -> x12, waiting for transfers between devices: 12.7 us -> 8.61 us  [swap(): lax.ppermute(x, axis, [(i, i ^ step) for i in range(lax.axis_size(axis))])]
    pallas_call x6 -> x8, Pallas kernels: 17.3 us -> 20.6 us  [the longest x3 6.17 us: second_half(): pl.pallas_call(functools.partial(second_half_kernel, chunk, owners, half)...]
    ppermute x2, starting transfers between devices: 4.29 us -> 5.93 us  [swap_far(): return lax.ppermute(x, ('tok', 'sub'), pairs)]
    ppermute x2, waiting for transfers between devices: 0.01 us -> 1.03 us  [swap_far(): return lax.ppermute(x, ('tok', 'sub'), pairs)]
    ppermute x10 -> x12, starting transfers between devices: 9.72 us -> 10.3 us  [swap(): lax.ppermute(x, axis, [(i, i ^ step) for i in range(lax.axis_size(axis))])]
  transfers between devices with their start and end apart: 12 -> 14, of which waited for: 9 -> 8; matrix products, arithmetic and copies ran while one was open for 0% -> 0% of each run, Pallas kernels for 43% -> 47%
where the time goes in v6:
time: 52.1 us; the launch traced here: 52 us
  Pallas kernels  24.7 us (47%)
  starting transfers between devices  16.2 us (31%)
  waiting for transfers between devices  9.64 us (19%)
  between operations  0.76 us (1%)
  other arithmetic  0.68 us (1%)
    ppermute x12, starting transfers between devices, swap(): lax.ppermute(x, axis, [(i, i ^ step) for i in range(lax.axis_size(axis))])  10.3 us
    ppermute x12, waiting for transfers between devices, swap(): lax.ppermute(x, axis, [(i, i ^ step) for i in range(lax.axis_size(axis))])  8.61 us
    pallas_call x3, Pallas kernels, second_half(): pl.pallas_call(functools.partial(second_half_kernel, chunk, owners, half)...  6.17 us
    ppermute x2, starting transfers between devices, swap_far(): return lax.ppermute(x, ('tok', 'sub'), pairs)  5.93 us
    pallas_call x1, Pallas kernels, on_device(): pl.pallas_call(functools.partial(first_half_kernel, members, owners), out...  5.23 us
    pallas_call x1, Pallas kernels, on_device(): pl.pallas_call(forward_own_kernel, out_shape=(shape(half, shard_rows, 2 *...  4.07 us
    pallas_call x1, Pallas kernels, on_device(): pl.pallas_call(functools.partial(last_grads_kernel, members, half), out_s...  3.46 us
    pallas_call x1, Pallas kernels, on_device(): pl.pallas_call(functools.partial(load_forward_kernel, shards, groups, hal...  3.43 us
  transfers between devices with their start and end apart: 14, of which 8 were waited for; matrix products, arithmetic and copies ran while one was open for 0% of the time, Pallas kernels for 47%

profile of v6, /device:TPU:0, one launch (start us, length us, event | category | flops | bytes accessed | tf_op | source)
XLA Modules:
  0.0 52.0 jit_solution(11215980170280864209)
XLA Ops:
  0.6 3.0 %collective-permute-start.3 = (bf16[64,2048]{1,0:T(8,128)(2,1)}, bf16[64,2048]{1,0:T(8,128)(2,1)S(1)}, u32[]{:S(2)}, u32[]{:S(2)}) collective-permute-start(bf16[64,2048]{1,0:T(8,128)(2,1)} %refs_2_.5), channel_id=1, source_target_pairs={{0,2},{2,0},{1,3},{3,1},{4,6},{6,4},{5,7},{7,5},{8,10},{10,8},{9,1... | collective-permute-start | bytes 786440 | tf_op jit(solution)/shard_map/ppermute | solution.py:312
  3.6 2.6 %collective-permute-start.1 = (bf16[32,2048]{1,0:T(8,128)(2,1)}, bf16[32,2048]{1,0:T(8,128)(2,1)S(1)}, u32[]{:S(2)}, u32[]{:S(2)}) collective-permute-start(bf16[32,2048]{1,0:T(8,128)(2,1)} %refs_0_.1), channel_id=1, source_target_pairs={{0,8},{1,13},{4,12},{5,9},{8,0},{9,5},{12,4},{13,1},{2,10},{3,15},... | collective-permute-start | bytes 393224 | tf_op jit(solution)/shard_map/ppermute | solution.py:318
  6.2 1.6 %collective-permute-start = (bf16[32,2048]{1,0:T(8,128)(2,1)}, bf16[32,2048]{1,0:T(8,128)(2,1)S(1)}, u32[]{:S(2)}, u32[]{:S(2)}) collective-permute-start(bf16[32,2048]{1,0:T(8,128)(2,1)} %refs_0_.1), channel_id=1, source_target_pairs={{0,4},{4,0},{8,12},{12,8},{1,5},{5,1},{9,13},{13,9},{2,6},{6,2},{1... | collective-permute-start | bytes 393224 | tf_op jit(solution)/shard_map/ppermute | solution.py:312
  7.8 4.1 %forward_own_a.1 = (bf16[8,32,256]{2,1,0:T(8,128)(2,1)S(1)}, bf16[8,1,12,128,128]{4,3,2,1,0:T(8,128)(2,1)S(1)}, bf16[8,1,12,128,128]{4,3,2,1,0:T(8,128)(2,1)S(1)}, s32[12,1,16]{2,1,0:T(1,128)S(4)}, s32[1,16]{1,0:T(1,128)S(4)}) custom-call(bf16[32,2048]{1,0:T(8,128)(2,1)} %refs_0_.1, s32[12,1,16]{2,1,0:T(1,128)} %bitcast.2, s32[1,16]{1,0:T(1,128)} %bitcast.3, ...), custom_call_target="tpu_custom_call" | custom-call | flops 201326592 | bytes 6291456 | tf_op jit(solution)/shard_map/forward_own_a/pallas_call | solution.py:356
  11.9 0.8 %collective-permute-done.1.x_ref.refs_1_.refs_2_ = bf16[32,2048]{1,0:T(8,128)(2,1)S(1)} collective-permute-done((bf16[32,2048]{1,0:T(8,128)(2,1)}, bf16[32,2048]{1,0:T(8,128)(2,1)S(1)}, u32[]{:S(2)}, u32[]{:S(2)}) %collective-permute-start.1) | collective-permute-done | bytes 131104 | tf_op jit(solution)/shard_map/ppermute | solution.py:318
  12.7 0.1 collective-permute-start.2
  12.8 0.6 %collective-permute-start.4 = (bf16[8,32,256]{2,1,0:T(8,128)(2,1)S(1)}, bf16[8,32,256]{2,1,0:T(8,128)(2,1)S(1)}, u32[]{:S(2)}, u32[]{:S(2)}) collective-permute-start(bf16[8,32,256]{2,1,0:T(8,128)(2,1)S(1)} %get-tuple-element.39._.refs_0_), channel_id=1, source_target_pairs={{0,2},{2,0},{1,3},{3,1},{4,6},{6,4},{5,7},{7,5},{8,10},{10,8},{9,1... | collective-permute-start | bytes 393224 | tf_op jit(solution)/shard_map/ppermute | solution.py:312
  13.4 0.2 collective-permute-done.refs_0_.refs_1_
  13.6 1.2 %forward_fetched_a.1.refs_3_.refs_2_ = bf16[8,64,256]{2,1,0:T(8,128)(2,1)S(1)} custom-call(s32[12,1,16]{2,1,0:T(1,128)S(4)} %get-tuple-element.37.rows_ref, s32[1,16]{1,0:T(1,128)S(4)} %get-tuple-element.38.counts_ref, bf16[32,2048]{1,0:T(8,128)(2,1)S(1)} %collective-permute-done.refs_0_.refs_1_, ...), custom_call_target="tpu_custom_call" | custom-call | flops 402653184 | bytes 6291456 | tf_op jit(solution)/shard_map/forward_fetched_a/pallas_call | solution.py:401
  14.8 1.4 %collective-permute-start.5 = (bf16[8,64,256]{2,1,0:T(8,128)(2,1)S(1)}, bf16[8,64,256]{2,1,0:T(8,128)(2,1)S(1)}, u32[]{:S(2)}, u32[]{:S(2)}) collective-permute-start(bf16[8,64,256]{2,1,0:T(8,128)(2,1)S(1)} %forward_fetched_a.1.refs_3_.refs_2_), channel_id=1, source_target_pairs={{0,2},{2,0},{1,3},{3,1},{4,6},{6,4},{5,7},{7,5},{8,10},{10,8},{9,1... | collective-permute-start | bytes 786440 | tf_op jit(solution)/shard_map/ppermute | solution.py:312
  16.1 1.1 %forward_swapped_a.1.refs_6_.refs_4_ = bf16[8,32,256]{2,1,0:T(8,128)(2,1)S(1)} custom-call(s32[12,1,16]{2,1,0:T(1,128)S(4)} %get-tuple-element.37.rows_ref, s32[1,16]{1,0:T(1,128)S(4)} %get-tuple-element.38.counts_ref, bf16[32,2048]{1,0:T(8,128)(2,1)S(1)} %collective-permute-done.2.refs_0_.refs_3_, ...), custom_call_target="tpu_custom_call" | custom-call | flops 201326592 | bytes 6291456 | tf_op jit(solution)/shard_map/forward_swapped_a/pallas_call | solution.py:401
  17.2 0.8 %collective-permute-start.6 = (bf16[8,32,256]{2,1,0:T(8,128)(2,1)S(1)}, bf16[8,32,256]{2,1,0:T(8,128)(2,1)S(1)}, u32[]{:S(2)}, u32[]{:S(2)}) collective-permute-start(bf16[8,32,256]{2,1,0:T(8,128)(2,1)S(1)} %forward_swapped_a.1.refs_6_.refs_4_), channel_id=1, source_target_pairs={{0,2},{2,0},{1,3},{3,1},{4,6},{6,4},{5,7},{7,5},{8,10},{10,8},{9,1... | collective-permute-start | bytes 393224 | tf_op jit(solution)/shard_map/ppermute | solution.py:312
  18.0 1.1 %collective-permute-done.4.refs_7_.refs_1_ = bf16[8,32,256]{2,1,0:T(8,128)(2,1)S(1)} collective-permute-done((bf16[8,32,256]{2,1,0:T(8,128)(2,1)S(1)}, bf16[8,32,256]{2,1,0:T(8,128)(2,1)S(1)}, u32[]{:S(2)}, u32[]{:S(2)}) %collective-permute-start.4) | collective-permute-done | bytes 131104 | tf_op jit(solution)/shard_map/ppermute | solution.py:312
  19.1 3.4 %forward_b.1 = (bf16[8,64,256]{2,1,0:T(8,128)(2,1)S(1)}, bf16[8,32,256]{2,1,0:T(8,128)(2,1)S(1)}, bf16[8,32,256]{2,1,0:T(8,128)(2,1)S(1)}, bf16[8,1,12,128,128]{...) custom-call(s32[12,1,16]{2,1,0:T(1,128)S(4)} %get-tuple-element.37.rows_ref, ...), custom_call_target="tpu_custom_call" | custom-call | flops 4026531840 | bytes 31457280 | tf_op jit(solution)/shard_map/forward_b/pallas_call | solution.py:417
  22.6 0.4 collective-permute-start.8
  23.0 1.7 %collective-permute-start.7 = (bf16[8,32,256]{2,1,0:T(8,128)(2,1)S(1)}, bf16[8,32,256]{2,1,0:T(8,128)(2,1)S(1)}, u32[]{:S(2)}, u32[]{:S(2)}) collective-permute-start(bf16[8,32,256]{2,1,0:T(8,128)(2,1)S(1)} %get-tuple-element.47.refs_10_.refs_0_), channel_id=1, source_target_pairs={{0,2},{2,0},{1,3},{3,1},{4,6},{6,4},{5,7},{7,5},{8,10},{10,8},{9,1... | collective-permute-start | bytes 393224 | tf_op jit(solution)/shard_map/ppermute | solution.py:312
  24.7 0.3 collective-permute-start.10
  25.0 2.6 %collective-permute-done.6.refs_5_ = bf16[8,32,256]{2,1,0:T(8,128)(2,1)S(1)} collective-permute-done((bf16[8,32,256]{2,1,0:T(8,128)(2,1)S(1)}, bf16[8,32,256]{2,1,0:T(8,128)(2,1)S(1)}, u32[]{:S(2)}, u32[]{:S(2)}) %collective-permute-start.6) | collective-permute-done | bytes 131104 | tf_op jit(solution)/shard_map/ppermute | solution.py:312
  27.6 5.2 %first_half.1 = (bf16[16,1,12,128,128]{4,3,2,1,0:T(8,128)(2,1)}, bf16[16,1,12,128,128]{4,3,2,1,0:T(8,128)(2,1)}, bf16[128,1024]{1,0:T(8,128)(2,1)S(1)}, f32[16,3...) custom-call(s32[12,1,16]{2,1,0:T(1,128)S(4)} %get-tuple-element.37.rows_ref, ...), custom_call_target="tpu_custom_call" | custom-call | flops 1610612736 | bytes 6291456 | tf_op jit(solution)/shard_map/first_half/pallas_call | solution.py:437
  32.8 0.4 collective-permute-done.8.refs_1_
  33.2 2.1 %far_b.1 = (bf16[8,64,256]{2,1,0:T(8,128)(2,1)S(1)}, bf16[64,1024]{1,0:T(8,128)(2,1)S(1)}, bf16[32,2048]{1,0:T(8,128)(2,1)S(1)}, bf16[32,2048]{1,0:T(8,128)(2,1)S(1)}) custom-call(s32[12,1,16]{2,1,0:T(1,128)S(4)} %get-tuple-element.37.rows_ref, s32[1,16]{1,0:T(1,128)S(4)} %get-tuple-element.38.counts_ref, ...), custom_call_target="tpu_custom_call" | custom-call | flops 402653184 | bytes 6291456 | tf_op jit(solution)/shard_map/far_b/pallas_call | solution.py:462
  35.3 0.1 collective-permute-start.9
  35.3 3.0 %collective-permute-done.10.refs_1_ = bf16[8,32,256]{2,1,0:T(8,128)(2,1)S(1)} collective-permute-done((bf16[8,32,256]{2,1,0:T(8,128)(2,1)S(1)}, bf16[8,32,256]{2,1,0:T(8,128)(2,1)S(1)}, u32[]{:S(2)}, u32[]{:S(2)}) %collective-permute-start.10) | collective-permute-done | bytes 131104 | tf_op jit(solution)/shard_map/ppermute | solution.py:312
  38.3 2.0 %next_b.1 = (bf16[8,32,256]{2,1,0:T(8,128)(2,1)S(1)}, bf16[32,1024]{1,0:T(8,128)(2,1)S(1)}, bf16[32,2048]{1,0:T(8,128)(2,1)S(1)}) custom-call(s32[12,1,16]{2,1,0:T(1,128)S(4)} %get-tuple-element.37.rows_ref, s32[1,16]{1,0:T(1,128)S(4)} %get-tuple-element.38.counts_ref, bf16[8,1,12,128,128]{4,3,2,1,0:T(8,128)(2,1)S(1)} %get-tuple-element.43.gate_w, ...), custom_call_target="tpu_custom_call" | custom-call | flops 201326592 | bytes 6291456 | tf_op jit(solution)/shard_map/next_b/pallas_call | solution.py:462
  40.3 0.3 collective-permute-start.11
  40.6 3.3 %collective-permute-start.12 = (bf16[32,2048]{1,0:T(8,128)(2,1)S(1)}, bf16[32,2048]{1,0:T(8,128)(2,1)S(1)}, u32[]{:S(2)}, u32[]{:S(2)}) collective-permute-start(bf16[32,2048]{1,0:T(8,128)(2,1)S(1)} %add_cores.1.refs_4_), channel_id=1, source_target_pairs={{0,8},{1,13},{4,12},{5,9},{8,0},{9,5},{12,4},{13,1},{2,10},{3,15},... | collective-permute-start | bytes 393224 | tf_op jit(solution)/shard_map/ppermute | solution.py:318
  44.0 2.1 %own_b.1 = (bf16[8,32,256]{2,1,0:T(8,128)(2,1)S(1)}, bf16[32,1024]{1,0:T(8,128)(2,1)S(1)}, bf16[32,2048]{1,0:T(8,128)(2,1)S(1)}) custom-call(s32[12,1,16]{2,1,0:T(1,128)S(4)} %get-tuple-element.37.rows_ref, s32[1,16]{1,0:T(1,128)S(4)} %get-tuple-element.38.counts_ref, bf16[8,1,12,128,128]{4,3,2,1,0:T(8,128)(2,1)S(1)} %get-tuple-element.43.gate_w, ...), custom_call_target="tpu_custom_call" | custom-call | flops 201326592 | bytes 6291456 | tf_op jit(solution)/shard_map/own_b/pallas_call | solution.py:462
  46.1 3.5 %last_grads.1 = (bf16[16,1,12,128,128]{4,3,2,1,0:T(8,128)(2,1)}, bf16[16,1,12,128,128]{4,3,2,1,0:T(8,128)(2,1)}, bf16[64,2048]{1,0:T(8,128)(2,1)}, f32[8,128]{1,0:T(8,128)S(1)}) custom-call(s32[12,1,16]{2,1,0:T(1,128)S(4)} %get-tuple-element.37.rows_ref, s32[1,16]{1,0:T(1,128)S(4)} %get-tuple-element.38.counts_ref, ...), custom_call_target="tpu_custom_call", output_to_operand_aliasing={{0}: (10, {}), {1}: (11, {})} | custom-call | flops 8053063680 | bytes 62914560 | tf_op jit(solution)/shard_map/last_grads/pallas_call | solution.py:496
  49.6 0.2 collective-permute-done.12.refs_2_
  49.9 0.1 collective-permute-start.13
  50.0 1.3 %collective-permute-done.13 = bf16[32,2048]{1,0:T(8,128)(2,1)S(1)} collective-permute-done((bf16[32,2048]{1,0:T(8,128)(2,1)S(1)}, bf16[32,2048]{1,0:T(8,128)(2,1)S(1)}, u32[]{:S(2)}, u32[]{:S(2)}) %collective-permute-start.13) | collective-permute-done | bytes 131104 | tf_op jit(solution)/shard_map/ppermute | solution.py:312
  51.3 0.7 %add_convert_fusion = bf16[32,2048]{1,0:T(8,128)(2,1)} fusion(f32[32,2048]{1,0:T(8,128)S(1)} %get-tuple-element.68, bf16[32,2048]{1,0:T(8,128)(2,1)S(1)} %collective-permute-done.13), kind=kLoop, calls=%fused_computation | loop fusion | flops 196608 | bytes 524288 | tf_op jit(solution)/shard_map/convert_element_type | solution.py:533
  (13 shorter events, 0.1 us)
Async XLA Ops:
  0.6 12.9 %collective-permute-start.3 = (bf16[64,2048]{1,0:T(8,128)(2,1)}, bf16[64,2048]{1,0:T(8,128)(2,1)S(1)}, u32[]{:S(2)}, u32[]{:S(2)}) collective-permute-start(bf16[64,2048]{1,0:T(8,128)(2,1)} %refs_2_.5), channel_id=1, source_target_pairs={{0,2},{2,0},{1,3},{3,1},{4,6},{6,4},{5,7},{7,5},{8,10},{10,8},{9,1... | collective-permute-start | bytes 786440 | tf_op jit(solution)/shard_map/ppermute | solution.py:312
  3.6 9.0 %collective-permute-start.1 = (bf16[32,2048]{1,0:T(8,128)(2,1)}, bf16[32,2048]{1,0:T(8,128)(2,1)S(1)}, u32[]{:S(2)}, u32[]{:S(2)}) collective-permute-start(bf16[32,2048]{1,0:T(8,128)(2,1)} %refs_0_.1), channel_id=1, source_target_pairs={{0,8},{1,13},{4,12},{5,9},{8,0},{9,5},{12,4},{13,1},{2,10},{3,15},... | collective-permute-start | bytes 393224 | tf_op jit(solution)/shard_map/ppermute | solution.py:318
  6.2 7.3 %collective-permute-start = (bf16[32,2048]{1,0:T(8,128)(2,1)}, bf16[32,2048]{1,0:T(8,128)(2,1)S(1)}, u32[]{:S(2)}, u32[]{:S(2)}) collective-permute-start(bf16[32,2048]{1,0:T(8,128)(2,1)} %refs_0_.1), channel_id=1, source_target_pairs={{0,4},{4,0},{8,12},{12,8},{1,5},{5,1},{9,13},{13,9},{2,6},{6,2},{1... | collective-permute-start | bytes 393224 | tf_op jit(solution)/shard_map/ppermute | solution.py:312
  12.7 3.4 %collective-permute-start.2 = (bf16[32,2048]{1,0:T(8,128)(2,1)S(1)}, bf16[32,2048]{1,0:T(8,128)(2,1)S(1)}, u32[]{:S(2)}, u32[]{:S(2)}) collective-permute-start(bf16[32,2048]{1,0:T(8,128)(2,1)S(1)} %after_own.1.refs_5_), channel_id=1, source_target_pairs={{0,1},{1,0},{2,3},{3,2},{4,5},{5,4},{6,7},{7,6},{8,9},{9,8},{10,11... | collective-permute-start | bytes 393224 | tf_op jit(solution)/shard_map/ppermute | solution.py:312
  12.8 6.4 %collective-permute-start.4 = (bf16[8,32,256]{2,1,0:T(8,128)(2,1)S(1)}, bf16[8,32,256]{2,1,0:T(8,128)(2,1)S(1)}, u32[]{:S(2)}, u32[]{:S(2)}) collective-permute-start(bf16[8,32,256]{2,1,0:T(8,128)(2,1)S(1)} %get-tuple-element.39._.refs_0_), channel_id=1, source_target_pairs={{0,2},{2,0},{1,3},{3,1},{4,6},{6,4},{5,7},{7,5},{8,10},{10,8},{9,1... | collective-permute-start | bytes 393224 | tf_op jit(solution)/shard_map/ppermute | solution.py:312
  13.6 5.6 %copy-start.1 = (bf16[32,2048]{1,0:T(8,128)(2,1)S(1)}, bf16[32,2048]{1,0:T(8,128)(2,1)}, u32[]{:S(2)}) copy-start(bf16[32,2048]{1,0:T(8,128)(2,1)} %refs_0_.1) | copy-start | bytes 393220
  14.8 12.8 %collective-permute-start.5 = (bf16[8,64,256]{2,1,0:T(8,128)(2,1)S(1)}, bf16[8,64,256]{2,1,0:T(8,128)(2,1)S(1)}, u32[]{:S(2)}, u32[]{:S(2)}) collective-permute-start(bf16[8,64,256]{2,1,0:T(8,128)(2,1)S(1)} %forward_fetched_a.1.refs_3_.refs_2_), channel_id=1, source_target_pairs={{0,2},{2,0},{1,3},{3,1},{4,6},{6,4},{5,7},{7,5},{8,10},{10,8},{9,1... | collective-permute-start | bytes 786440 | tf_op jit(solution)/shard_map/ppermute | solution.py:312
  17.2 10.3 %copy-start = (bf16[64,2048]{1,0:T(8,128)(2,1)S(1)}, bf16[64,2048]{1,0:T(8,128)(2,1)}, u32[]{:S(2)}) copy-start(bf16[64,2048]{1,0:T(8,128)(2,1)} %refs_2_.5) | copy-start | bytes 786436
  17.2 10.3 %collective-permute-start.6 = (bf16[8,32,256]{2,1,0:T(8,128)(2,1)S(1)}, bf16[8,32,256]{2,1,0:T(8,128)(2,1)S(1)}, u32[]{:S(2)}, u32[]{:S(2)}) collective-permute-start(bf16[8,32,256]{2,1,0:T(8,128)(2,1)S(1)} %forward_swapped_a.1.refs_6_.refs_4_), channel_id=1, source_target_pairs={{0,2},{2,0},{1,3},{3,1},{4,6},{6,4},{5,7},{7,5},{8,10},{10,8},{9,1... | collective-permute-start | bytes 393224 | tf_op jit(solution)/shard_map/ppermute | solution.py:312
  22.6 10.6 %collective-permute-start.8 = (bf16[8,64,256]{2,1,0:T(8,128)(2,1)S(1)}, bf16[8,64,256]{2,1,0:T(8,128)(2,1)S(1)}, u32[]{:S(2)}, u32[]{:S(2)}) collective-permute-start(bf16[8,64,256]{2,1,0:T(8,128)(2,1)S(1)} %get-tuple-element.45.refs_8_.refs_0_), channel_id=1, source_target_pairs={{0,2},{2,0},{1,3},{3,1},{4,6},{6,4},{5,7},{7,5},{8,10},{10,8},{9,1... | collective-permute-start | bytes 786440 | tf_op jit(solution)/shard_map/ppermute | solution.py:312
  23.0 17.6 %collective-permute-start.7 = (bf16[8,32,256]{2,1,0:T(8,128)(2,1)S(1)}, bf16[8,32,256]{2,1,0:T(8,128)(2,1)S(1)}, u32[]{:S(2)}, u32[]{:S(2)}) collective-permute-start(bf16[8,32,256]{2,1,0:T(8,128)(2,1)S(1)} %get-tuple-element.47.refs_10_.refs_0_), channel_id=1, source_target_pairs={{0,2},{2,0},{1,3},{3,1},{4,6},{6,4},{5,7},{7,5},{8,10},{10,8},{9,1... | collective-permute-start | bytes 393224 | tf_op jit(solution)/shard_map/ppermute | solution.py:312
  24.7 13.7 %collective-permute-start.10 = (bf16[8,32,256]{2,1,0:T(8,128)(2,1)S(1)}, bf16[8,32,256]{2,1,0:T(8,128)(2,1)S(1)}, u32[]{:S(2)}, u32[]{:S(2)}) collective-permute-start(bf16[8,32,256]{2,1,0:T(8,128)(2,1)S(1)} %get-tuple-element.46.refs_9_.refs_0_), channel_id=1, source_target_pairs={{0,2},{2,0},{1,3},{3,1},{4,6},{6,4},{5,7},{7,5},{8,10},{10,8},{9,1... | collective-permute-start | bytes 393224 | tf_op jit(solution)/shard_map/ppermute | solution.py:312
  35.3 5.4 %collective-permute-start.9 = (bf16[32,2048]{1,0:T(8,128)(2,1)S(1)}, bf16[32,2048]{1,0:T(8,128)(2,1)S(1)}, u32[]{:S(2)}, u32[]{:S(2)}) collective-permute-start(bf16[32,2048]{1,0:T(8,128)(2,1)S(1)} %get-tuple-element.51), channel_id=1, source_target_pairs={{0,1},{1,0},{2,3},{3,2},{4,5},{5,4},{6,7},{7,6},{8,9},{9,8},{10,11... | collective-permute-start | bytes 393224 | tf_op jit(solution)/shard_map/ppermute | solution.py:312
  40.3 9.3 %collective-permute-start.11 = (bf16[32,2048]{1,0:T(8,128)(2,1)S(1)}, bf16[32,2048]{1,0:T(8,128)(2,1)S(1)}, u32[]{:S(2)}, u32[]{:S(2)}) collective-permute-start(bf16[32,2048]{1,0:T(8,128)(2,1)S(1)} %get-tuple-element.66), channel_id=1, source_target_pairs={{0,4},{4,0},{8,12},{12,8},{1,5},{5,1},{9,13},{13,9},{2,6},{6,2},{1... | collective-permute-start | bytes 393224 | tf_op jit(solution)/shard_map/ppermute | solution.py:312
  40.6 9.2 %collective-permute-start.12 = (bf16[32,2048]{1,0:T(8,128)(2,1)S(1)}, bf16[32,2048]{1,0:T(8,128)(2,1)S(1)}, u32[]{:S(2)}, u32[]{:S(2)}) collective-permute-start(bf16[32,2048]{1,0:T(8,128)(2,1)S(1)} %add_cores.1.refs_4_), channel_id=1, source_target_pairs={{0,8},{1,13},{4,12},{5,9},{8,0},{9,5},{12,4},{13,1},{2,10},{3,15},... | collective-permute-start | bytes 393224 | tf_op jit(solution)/shard_map/ppermute | solution.py:318
  49.9 1.4 %collective-permute-start.13 = (bf16[32,2048]{1,0:T(8,128)(2,1)S(1)}, bf16[32,2048]{1,0:T(8,128)(2,1)S(1)}, u32[]{:S(2)}, u32[]{:S(2)}) collective-permute-start(bf16[32,2048]{1,0:T(8,128)(2,1)S(1)} %get-tuple-element.69), channel_id=1, source_target_pairs={{0,1},{1,0},{2,3},{3,2},{4,5},{5,4},{6,7},{7,6},{8,9},{9,8},{10,11... | collective-permute-start | bytes 393224 | tf_op jit(solution)/shard_map/ppermute | solution.py:312

commit v7 on v6

--- a/solution.py
+++ b/solution.py
@@ -227,8 +227,8 @@
 
 
 def first_half_kernel(members, owners, rows_ref, counts_ref, gate_w, up_w, turned_ref, *refs):
-    groups = [refs[start : start + owners] for start in range(0, 3 * owners, owners)]
-    cots = refs[3 * owners : 4 * owners]
+    groups = [refs[start : start + owners] for start in range(0, 2 * owners, owners)]
+    cots = refs[2 * owners : 3 * owners]
     gate_hbm, up_hbm, hidden_ref = refs[-10:-7]
     accs = refs[-7:-4]
     grads_ref, gate_ref, up_ref, sems = refs[-4:]
@@ -272,23 +272,35 @@
             dx[:, r * tile : (r + 1) * tile] = block[m * shard_rows : (m + 1) * shard_rows]
 
 
-def last_grads_kernel(members, first, rows_ref, counts_ref, turned_ref, *refs):
-    all_grads, hidden_a, hiddens = refs[:3], refs[3], refs[4:7]
-    gate_hbm, up_hbm, hidden_hbm, token_ref, gate_ref, up_ref, sems, hidden_sems = refs[-8:]
-    cols, _, _, tile, _ = gate_ref.shape
-    shard_rows = hiddens[0].shape[0]
-    token_ref[...] = jnp.zeros_like(token_ref)
-
-    def parts(member):
+def last_half_kernel(members, owners, first, rows_ref, counts_ref, gate_w, up_w, turned_ref, acc_in, *refs):
+    parts, cots = refs[:owners], refs[owners : 2 * owners]
+    next_grads, far_grads, hidden_a, next_hidden, far_hidden = refs[2 * owners : 2 * owners + 5]
+    gate_hbm, up_hbm, hidden_hbm, dx_ref = refs[-11:-7]
+    acc_ref, grads_ref, hidden_ref, gate_ref, up_ref, sems, hidden_sems = refs[-7:]
+    cols, _, slots, tile, _ = gate_ref.shape
+    shard_rows = hidden_ref.shape[0]
+    lists = (rows_ref, counts_ref)
+
+    def hidden_of(member):
         at = members.index(member)
-        mine = (hiddens[at], 0) if at < 2 else (hiddens[2], (at - 2) * shard_rows)
+        mine = ((hidden_ref, 0), (next_hidden, 0))[at] if at < 2 else (far_hidden, (at - 2) * shard_rows)
         return (hidden_a, at * shard_rows, 0), (*mine, first * tile)
 
-    copies = start_hidden(members, parts, hidden_hbm, shard_rows, hidden_sems)
-    for c in range(cols):
-        grads = jnp.concatenate([part[c] for part in all_grads], axis=0)
-        tile_grads(c, first, (rows_ref, counts_ref), turned_ref, grads, gate_ref, up_ref)
+    acc_ref[...] = acc_in[...]
+    copies = []
+    for c in range(cols):
+        where = slice((first + c) * tile, (first + c + 1) * tile)
+        hidden, grads = nonlinear(total_of(c, parts), cotangent_of(members[:1], cots, shard_rows, where))
+        hidden_ref[:, c * tile : (c + 1) * tile] = hidden
+        grads_ref[c] = grads
+        grads = jnp.concatenate([grads, next_grads[c], far_grads[c]], axis=0)
+        tile_grads(c, first, lists, turned_ref, grads, gate_ref, up_ref)
         copies += store_tiles(first, c, gate_ref, up_ref, gate_hbm, up_hbm, sems)
+    copies += start_hidden(members, hidden_of, hidden_hbm, shard_rows, hidden_sems)
+    for c in range(cols):
+        add_back(first + c, lists, back_terms(c, grads_ref[c], gate_w, up_w), (acc_ref,), slots, tile)
+    for r in range(acc_ref.shape[0]):
+        dx_ref[:, r * tile : (r + 1) * tile] = acc_ref[r].astype(BF16)
     for copy in copies:
         copy.wait()
 
@@ -409,8 +421,7 @@
             )(*lists, *shard_xs, *weights_a, *after)
         )
 
-    fetched_a = forward_a("forward_fetched_a", fetched, [cots[-1], before_swap[-1]])
-    swapped_a = forward_a("forward_swapped_a", swapped, [fetched_a[0]])
+    rest_a = forward_a("forward_rest_a", [*fetched, *swapped], [cots[-1]])
 
     rest = cols - half
     groups = ((near_rows, row_total), (own_rows, near_rows), (0, own_rows))
@@ -428,9 +439,9 @@
         compiler_params=limit(8),
         cost_estimate=cost(row_total, rest, 1, 1, 5),
         name="forward_b",
-    )(*lists, *xs, *from_hbm(gate_tiles, up_tiles), swapped_a[0], near_a[-1])
+    )(*lists, *xs, *from_hbm(gate_tiles, up_tiles), rest_a[0], near_a[-1])
     weights_b = [gate_b, up_b]
-    far_b, next_b, own_b = to_owners(far_b), to_owners(next_b), to_owners(own_b)
+    own_b, next_b, far_b = to_owners(own_b), to_owners(next_b), to_owners(far_b)
 
     out_tiles = shape(*gate_tiles.shape)
     tile_bytes = slots * tile * tile * 2
@@ -442,7 +453,7 @@
             shape(row_total, half * tile),
             *[shape(row_blocks, rows, tile, dtype=F32) for rows in (own_rows, own_rows, far_rows)],
         ),
-        in_specs=[SMEM_SPEC] * 2 + [VMEM_SPEC] * (3 + 4 * owners) + [ANY_SPEC] * 3,
+        in_specs=[SMEM_SPEC] * 2 + [VMEM_SPEC] * (3 + 3 * owners) + [ANY_SPEC] * 3,
         out_specs=(ANY_SPEC,) * 2 + (VMEM_SPEC,) * 4,
         scratch_shapes=[
             pltpu.VMEM((half, row_total, 2 * tile), BF16),
@@ -454,7 +465,7 @@
         cost_estimate=cost(row_total, half, 2, 1, 1),
         name="first_half",
     )(
-        *lists, *weights_a, turned, *near_a, *fetched_a, *swapped_a, *cots, far_b[0], next_b[0], own_b[0]
+        *lists, *weights_a, turned, *near_a, *rest_a, *cots, far_b[0], next_b[0], own_b[0]
     )
 
     def second_half(name, chunk, acc, parts, after, weight):
@@ -491,45 +502,49 @@
         )
     back_far = [swap_far(total, base) for total, base in zip(both_cores, bases)]
     back_next = swap(next_dx, "tok", 1)
-    own_grads, own_hidden, own_dx = second_half("own_b", [0], acc_own, own_b, both_cores[-1], 1)
-
-    gate_out, up_out, hidden_out, token = pl.pallas_call(
-        functools.partial(last_grads_kernel, members, half),
-        out_shape=(out_tiles, out_tiles, shape(*d_hidden.shape), shape(8, tile, dtype=F32)),
-        in_specs=[SMEM_SPEC] * 2 + [VMEM_SPEC] * 8 + [ANY_SPEC] * 2,
+    gate_out, up_out, hidden_out, own_dx = pl.pallas_call(
+        functools.partial(last_half_kernel, members, owners, half),
+        out_shape=(out_tiles, out_tiles, shape(*d_hidden.shape), shape(shard_rows, width)),
+        in_specs=[SMEM_SPEC] * 2 + [VMEM_SPEC] * (9 + 2 * owners) + [ANY_SPEC] * 3,
         out_specs=(ANY_SPEC,) * 3 + (VMEM_SPEC,),
         scratch_shapes=[
+            pltpu.VMEM((row_blocks, shard_rows, tile), F32),
+            pltpu.VMEM((rest, shard_rows, 2 * tile), BF16),
+            pltpu.VMEM((shard_rows, rest * tile), BF16),
             tile_shape(rest),
             tile_shape(rest),
             pltpu.SemaphoreType.DMA((2, rest)),
             pltpu.SemaphoreType.DMA((2, d_hidden.shape[0] // shard_rows)),
         ],
-        input_output_aliases={10: 0, 11: 1},
+        input_output_aliases={11 + 2 * owners: 0, 12 + 2 * owners: 1},
         compiler_params=limit(8 + 2 * rest * tile_bytes // MIB),
         cost_estimate=cost(row_total, rest, 1, 1, 10),
-        name="last_grads",
+        name="last_half",
     )(
         *lists,
+        *weights_b,
         turned,
-        own_grads,
+        acc_own,
+        *own_b,
+        *cots,
         next_grads,
         far_grads,
         hidden_a,
-        own_hidden,
         next_hidden,
         far_hidden,
         gate_out,
         up_out,
+        both_cores[-1],
     )
     arrived = [own_dx, back_next, *back_far]
     mine, mine_sent = pl.pallas_call(
         functools.partial(sum_kernel, len(arrived)),
         out_shape=(shape(shard_rows, width, dtype=F32), shape(shard_rows, width)),
-        in_specs=[VMEM_SPEC] * len(arrived) + [ANY_SPEC],
+        in_specs=[VMEM_SPEC] * len(arrived),
         out_specs=(VMEM_SPEC,) * 2,
         compiler_params=limit(8),
         name="sum_shards",
-    )(*arrived, token)
+    )(*arrived)
     features_grad = (mine + swap(mine_sent, "sub", 1).astype(F32)).astype(BF16)
     return (hidden_out, gate_out, up_out, features_grad)
 

time: 52.1 us -> 49.1 us (0.942)
  Pallas kernels: 24.7 us -> 22.8 us
  waiting for transfers between devices: 9.64 us -> 8.73 us
    pallas_call x3 -> x2, Pallas kernels: 6.17 us -> 4.04 us  [second_half(): pl.pallas_call(functools.partial(second_half_kernel, chunk, owners, half)...]
    ppermute x12 -> x11, waiting for transfers between devices: 8.61 us -> 7.17 us  [swap(): lax.ppermute(x, axis, [(i, i ^ step) for i in range(lax.axis_size(axis))])]
    pallas_call x1, Pallas kernels: 3.46 us -> 4.82 us  [on_device(): pl.pallas_call(functools.partial(last_half_kernel, members, owners, half)...]
    pallas_call x2 -> x1, Pallas kernels: 2.26 us -> 1.13 us  [forward_a(): pl.pallas_call(functools.partial(forward_kernel, len(shard_xs)), out_shap...]
    ppermute x12 -> x11, starting transfers between devices: 10.3 us -> 9.25 us  [swap(): lax.ppermute(x, axis, [(i, i ^ step) for i in range(lax.axis_size(axis))])]
    ppermute x2, starting transfers between devices: 5.93 us -> 6.69 us  [swap_far(): return lax.ppermute(x, ('tok', 'sub'), pairs)]
    ppermute x2, waiting for transfers between devices: 1.03 us -> 1.56 us  [swap_far(): return lax.ppermute(x, ('tok', 'sub'), pairs)]
  transfers between devices with their start and end apart: 14 -> 13, of which waited for: 8 -> 7; matrix products, arithmetic and copies ran while one was open for 0% -> 0% of each run, Pallas kernels for 47% -> 47%
where the time goes in v7:
time: 49.1 us; the launch traced here: 49 us
  Pallas kernels  22.8 us (46%)
  starting transfers between devices  15.9 us (32%)
  waiting for transfers between devices  8.73 us (18%)
  between operations  0.77 us (2%)
  other arithmetic  0.68 us (1%)
    ppermute x11, starting transfers between devices, swap(): lax.ppermute(x, axis, [(i, i ^ step) for i in range(lax.axis_size(axis))])  9.25 us
    ppermute x11, waiting for transfers between devices, swap(): lax.ppermute(x, axis, [(i, i ^ step) for i in range(lax.axis_size(axis))])  7.17 us
    ppermute x2, starting transfers between devices, swap_far(): return lax.ppermute(x, ('tok', 'sub'), pairs)  6.69 us
    pallas_call x1, Pallas kernels, on_device(): pl.pallas_call(functools.partial(first_half_kernel, members, owners), out...  5.23 us
    pallas_call x1, Pallas kernels, on_device(): pl.pallas_call(functools.partial(last_half_kernel, members, owners, half)...  4.82 us
    pallas_call x1, Pallas kernels, on_device(): pl.pallas_call(forward_own_kernel, out_shape=(shape(half, shard_rows, 2 *...  4.07 us
    pallas_call x2, Pallas kernels, second_half(): pl.pallas_call(functools.partial(second_half_kernel, chunk, owners, half)...  4.04 us
    pallas_call x1, Pallas kernels, on_device(): pl.pallas_call(functools.partial(load_forward_kernel, shards, groups, hal...  3.45 us
  transfers between devices with their start and end apart: 13, of which 7 were waited for; matrix products, arithmetic and copies ran while one was open for 0% of the time, Pallas kernels for 47%

profile of v7, /device:TPU:0, one launch (start us, length us, event | category | flops | bytes accessed | tf_op | source)
XLA Modules:
  0.0 49.0 jit_solution(8017845439059940193)
XLA Ops:
  0.6 4.1 %collective-permute-start.1 = (bf16[32,2048]{1,0:T(8,128)(2,1)}, bf16[32,2048]{1,0:T(8,128)(2,1)S(1)}, u32[]{:S(2)}, u32[]{:S(2)}) collective-permute-start(bf16[32,2048]{1,0:T(8,128)(2,1)} %refs_0_.1), channel_id=1, source_target_pairs={{0,8},{1,13},{4,12},{5,9},{8,0},{9,5},{12,4},{13,1},{2,10},{3,15},... | collective-permute-start | bytes 393224 | tf_op jit(solution)/shard_map/ppermute | solution.py:330
  4.7 1.5 %collective-permute-start.3 = (bf16[64,2048]{1,0:T(8,128)(2,1)}, bf16[64,2048]{1,0:T(8,128)(2,1)S(1)}, u32[]{:S(2)}, u32[]{:S(2)}) collective-permute-start(bf16[64,2048]{1,0:T(8,128)(2,1)} %refs_2_.5), channel_id=1, source_target_pairs={{0,2},{2,0},{1,3},{3,1},{4,6},{6,4},{5,7},{7,5},{8,10},{10,8},{9,1... | collective-permute-start | bytes 786440 | tf_op jit(solution)/shard_map/ppermute | solution.py:324
  6.2 1.6 %collective-permute-start = (bf16[32,2048]{1,0:T(8,128)(2,1)}, bf16[32,2048]{1,0:T(8,128)(2,1)S(1)}, u32[]{:S(2)}, u32[]{:S(2)}) collective-permute-start(bf16[32,2048]{1,0:T(8,128)(2,1)} %refs_0_.1), channel_id=1, source_target_pairs={{0,4},{4,0},{8,12},{12,8},{1,5},{5,1},{9,13},{13,9},{2,6},{6,2},{1... | collective-permute-start | bytes 393224 | tf_op jit(solution)/shard_map/ppermute | solution.py:324
  7.8 4.1 %forward_own_a.1 = (bf16[8,32,256]{2,1,0:T(8,128)(2,1)S(1)}, bf16[8,1,12,128,128]{4,3,2,1,0:T(8,128)(2,1)S(1)}, bf16[8,1,12,128,128]{4,3,2,1,0:T(8,128)(2,1)S(1)}, s32[12,1,16]{2,1,0:T(1,128)S(4)}, s32[1,16]{1,0:T(1,128)S(4)}) custom-call(bf16[32,2048]{1,0:T(8,128)(2,1)} %refs_0_.1, s32[12,1,16]{2,1,0:T(1,128)} %bitcast.2, s32[1,16]{1,0:T(1,128)} %bitcast.3, ...), custom_call_target="tpu_custom_call" | custom-call | flops 201326592 | bytes 6291456 | tf_op jit(solution)/shard_map/forward_own_a/pallas_call | solution.py:368
  11.9 0.0 copy-start.1
  11.9 0.0 collective-permute-done.1.x_ref.refs_1_.refs_2_
  11.9 0.1 collective-permute-start.2
  12.0 1.2 %collective-permute-start.4 = (bf16[8,32,256]{2,1,0:T(8,128)(2,1)S(1)}, bf16[8,32,256]{2,1,0:T(8,128)(2,1)S(1)}, u32[]{:S(2)}, u32[]{:S(2)}) collective-permute-start(bf16[8,32,256]{2,1,0:T(8,128)(2,1)S(1)} %get-tuple-element.36._.refs_0_), channel_id=1, source_target_pairs={{0,2},{2,0},{1,3},{3,1},{4,6},{6,4},{5,7},{7,5},{8,10},{10,8},{9,1... | collective-permute-start | bytes 393224 | tf_op jit(solution)/shard_map/ppermute | solution.py:324
  13.2 0.6 %collective-permute-done.3.refs_5_.refs_3_ = bf16[64,2048]{1,0:T(8,128)(2,1)S(1)} collective-permute-done((bf16[64,2048]{1,0:T(8,128)(2,1)}, bf16[64,2048]{1,0:T(8,128)(2,1)S(1)}, u32[]{:S(2)}, u32[]{:S(2)}) %collective-permute-start.3) | collective-permute-done | bytes 262176 | tf_op jit(solution)/shard_map/ppermute | solution.py:324
  13.7 1.1 %forward_rest_a.1.refs_6_.refs_2_ = bf16[8,96,256]{2,1,0:T(8,128)(2,1)S(1)} custom-call(s32[12,1,16]{2,1,0:T(1,128)S(4)} %get-tuple-element.34.rows_ref, s32[1,16]{1,0:T(1,128)S(4)} %get-tuple-element.35.counts_ref, bf16[32,2048]{1,0:T(8,128)(2,1)S(1)} %collective-permute-done.refs_0_.refs_1_, ...), custom_call_target="tpu_custom_call" | custom-call | flops 603979776 | bytes 6291456 | tf_op jit(solution)/shard_map/forward_rest_a/pallas_call | solution.py:413
  14.9 0.0 copy-start
  14.9 1.6 %collective-permute-start.5 = (bf16[8,96,256]{2,1,0:T(8,128)(2,1)S(1)}, bf16[8,96,256]{2,1,0:T(8,128)(2,1)S(1)}, u32[]{:S(2)}, u32[]{:S(2)}) collective-permute-start(bf16[8,96,256]{2,1,0:T(8,128)(2,1)S(1)} %forward_rest_a.1.refs_6_.refs_2_), channel_id=1, source_target_pairs={{0,2},{2,0},{1,3},{3,1},{4,6},{6,4},{5,7},{7,5},{8,10},{10,8},{9,1... | collective-permute-start | bytes 1179656 | tf_op jit(solution)/shard_map/ppermute | solution.py:324
  16.4 1.9 %collective-permute-done.4.refs_7_.refs_1_ = bf16[8,32,256]{2,1,0:T(8,128)(2,1)S(1)} collective-permute-done((bf16[8,32,256]{2,1,0:T(8,128)(2,1)S(1)}, bf16[8,32,256]{2,1,0:T(8,128)(2,1)S(1)}, u32[]{:S(2)}, u32[]{:S(2)}) %collective-permute-start.4) | collective-permute-done | bytes 131104 | tf_op jit(solution)/shard_map/ppermute | solution.py:324
  18.4 3.4 %forward_b.1 = (bf16[8,64,256]{2,1,0:T(8,128)(2,1)S(1)}, bf16[8,32,256]{2,1,0:T(8,128)(2,1)S(1)}, bf16[8,32,256]{2,1,0:T(8,128)(2,1)S(1)}, bf16[8,1,12,128,128]{...) custom-call(s32[12,1,16]{2,1,0:T(1,128)S(4)} %get-tuple-element.34.rows_ref, ...), custom_call_target="tpu_custom_call" | custom-call | flops 4026531840 | bytes 31457280 | tf_op jit(solution)/shard_map/forward_b/pallas_call | solution.py:428
  21.8 0.8 %collective-permute-start.8 = (bf16[8,64,256]{2,1,0:T(8,128)(2,1)S(1)}, bf16[8,64,256]{2,1,0:T(8,128)(2,1)S(1)}, u32[]{:S(2)}, u32[]{:S(2)}) collective-permute-start(bf16[8,64,256]{2,1,0:T(8,128)(2,1)S(1)} %get-tuple-element.42.refs_6_.refs_0_), channel_id=1, source_target_pairs={{0,2},{2,0},{1,3},{3,1},{4,6},{6,4},{5,7},{7,5},{8,10},{10,8},{9,1... | collective-permute-start | bytes 786440 | tf_op jit(solution)/shard_map/ppermute | solution.py:324
  22.6 1.3 %collective-permute-start.7 = (bf16[8,32,256]{2,1,0:T(8,128)(2,1)S(1)}, bf16[8,32,256]{2,1,0:T(8,128)(2,1)S(1)}, u32[]{:S(2)}, u32[]{:S(2)}) collective-permute-start(bf16[8,32,256]{2,1,0:T(8,128)(2,1)S(1)} %get-tuple-element.43.refs_7_.refs_0_), channel_id=1, source_target_pairs={{0,2},{2,0},{1,3},{3,1},{4,6},{6,4},{5,7},{7,5},{8,10},{10,8},{9,1... | collective-permute-start | bytes 393224 | tf_op jit(solution)/shard_map/ppermute | solution.py:324
  23.9 0.8 %collective-permute-start.6 = (bf16[8,32,256]{2,1,0:T(8,128)(2,1)S(1)}, bf16[8,32,256]{2,1,0:T(8,128)(2,1)S(1)}, u32[]{:S(2)}, u32[]{:S(2)}) collective-permute-start(bf16[8,32,256]{2,1,0:T(8,128)(2,1)S(1)} %get-tuple-element.44.refs_8_.refs_0_), channel_id=1, source_target_pairs={{0,2},{2,0},{1,3},{3,1},{4,6},{6,4},{5,7},{7,5},{8,10},{10,8},{9,1... | collective-permute-start | bytes 393224 | tf_op jit(solution)/shard_map/ppermute | solution.py:324
  24.7 2.3 %collective-permute-done.5.refs_3_ = bf16[8,96,256]{2,1,0:T(8,128)(2,1)S(1)} collective-permute-done((bf16[8,96,256]{2,1,0:T(8,128)(2,1)S(1)}, bf16[8,96,256]{2,1,0:T(8,128)(2,1)S(1)}, u32[]{:S(2)}, u32[]{:S(2)}) %collective-permute-start.5) | collective-permute-done | bytes 393248 | tf_op jit(solution)/shard_map/ppermute | solution.py:324
  27.0 5.2 %first_half.1 = (bf16[16,1,12,128,128]{4,3,2,1,0:T(8,128)(2,1)}, bf16[16,1,12,128,128]{4,3,2,1,0:T(8,128)(2,1)}, bf16[128,1024]{1,0:T(8,128)(2,1)S(1)}, f32[16,3...) custom-call(s32[12,1,16]{2,1,0:T(1,128)S(4)} %get-tuple-element.34.rows_ref, ...), custom_call_target="tpu_custom_call" | custom-call | flops 1610612736 | bytes 6291456 | tf_op jit(solution)/shard_map/first_half/pallas_call | solution.py:448
  32.2 0.4 collective-permute-done.8.refs_1_
  32.6 2.1 %far_b.1 = (bf16[8,64,256]{2,1,0:T(8,128)(2,1)S(1)}, bf16[64,1024]{1,0:T(8,128)(2,1)S(1)}, bf16[32,2048]{1,0:T(8,128)(2,1)S(1)}, bf16[32,2048]{1,0:T(8,128)(2,1)S(1)}) custom-call(s32[12,1,16]{2,1,0:T(1,128)S(4)} %get-tuple-element.34.rows_ref, s32[1,16]{1,0:T(1,128)S(4)} %get-tuple-element.35.counts_ref, ...), custom_call_target="tpu_custom_call" | custom-call | flops 402653184 | bytes 6291456 | tf_op jit(solution)/shard_map/far_b/pallas_call | solution.py:473
  34.7 0.1 collective-permute-start.9
  34.8 0.6 %collective-permute-done.7.refs_1_ = bf16[8,32,256]{2,1,0:T(8,128)(2,1)S(1)} collective-permute-done((bf16[8,32,256]{2,1,0:T(8,128)(2,1)S(1)}, bf16[8,32,256]{2,1,0:T(8,128)(2,1)S(1)}, u32[]{:S(2)}, u32[]{:S(2)}) %collective-permute-start.7) | collective-permute-done | bytes 131104 | tf_op jit(solution)/shard_map/ppermute | solution.py:324
  35.4 2.0 %next_b.1 = (bf16[8,32,256]{2,1,0:T(8,128)(2,1)S(1)}, bf16[32,1024]{1,0:T(8,128)(2,1)S(1)}, bf16[32,2048]{1,0:T(8,128)(2,1)S(1)}) custom-call(s32[12,1,16]{2,1,0:T(1,128)S(4)} %get-tuple-element.34.rows_ref, s32[1,16]{1,0:T(1,128)S(4)} %get-tuple-element.35.counts_ref, bf16[8,1,12,128,128]{4,3,2,1,0:T(8,128)(2,1)S(1)} %get-tuple-element.39.gate_w, ...), custom_call_target="tpu_custom_call" | custom-call | flops 201326592 | bytes 6291456 | tf_op jit(solution)/shard_map/next_b/pallas_call | solution.py:473
  37.4 0.4 collective-permute-start.10
  37.8 2.6 %collective-permute-start.11 = (bf16[32,2048]{1,0:T(8,128)(2,1)S(1)}, bf16[32,2048]{1,0:T(8,128)(2,1)S(1)}, u32[]{:S(2)}, u32[]{:S(2)}) collective-permute-start(bf16[32,2048]{1,0:T(8,128)(2,1)S(1)} %add_cores.1.refs_11_), channel_id=1, source_target_pairs={{0,8},{1,13},{4,12},{5,9},{8,0},{9,5},{12,4},{13,1},{2,10},{3,15},... | collective-permute-start | bytes 393224 | tf_op jit(solution)/shard_map/ppermute | solution.py:330
  40.4 4.8 %last_half.1 = (bf16[16,1,12,128,128]{4,3,2,1,0:T(8,128)(2,1)}, bf16[16,1,12,128,128]{4,3,2,1,0:T(8,128)(2,1)}, bf16[64,2048]{1,0:T(8,128)(2,1)}, bf16[32,2048]{1,0:T(8,128)(2,1)S(1)}) custom-call(s32[12,1,16]{2,1,0:T(1,128)S(4)} %get-tuple-element.34.rows_ref, ...), custom_call_target="tpu_custom_call", output_to_operand_aliasing={{0}: (15, {}), {1}: (16, {})} | custom-call | flops 8053063680 | bytes 62914560 | tf_op jit(solution)/shard_map/last_half/pallas_call | solution.py:505
  45.3 1.6 %collective-permute-done.11.refs_2_ = bf16[32,2048]{1,0:T(8,128)(2,1)S(1)} collective-permute-done((bf16[32,2048]{1,0:T(8,128)(2,1)S(1)}, bf16[32,2048]{1,0:T(8,128)(2,1)S(1)}, u32[]{:S(2)}, u32[]{:S(2)}) %collective-permute-start.11) | collective-permute-done | bytes 131104 | tf_op jit(solution)/shard_map/ppermute | solution.py:330
  46.8 0.1 sum_shards.1
  46.9 0.1 collective-permute-start.12
  47.0 1.3 %collective-permute-done.12 = bf16[32,2048]{1,0:T(8,128)(2,1)S(1)} collective-permute-done((bf16[32,2048]{1,0:T(8,128)(2,1)S(1)}, bf16[32,2048]{1,0:T(8,128)(2,1)S(1)}, u32[]{:S(2)}, u32[]{:S(2)}) %collective-permute-start.12) | collective-permute-done | bytes 131104 | tf_op jit(solution)/shard_map/ppermute | solution.py:324
  48.3 0.7 %add_convert_fusion = bf16[32,2048]{1,0:T(8,128)(2,1)} fusion(f32[32,2048]{1,0:T(8,128)S(1)} %get-tuple-element.62, bf16[32,2048]{1,0:T(8,128)(2,1)S(1)} %collective-permute-done.12), kind=kLoop, calls=%fused_computation | loop fusion | flops 196608 | bytes 524288 | tf_op jit(solution)/shard_map/convert_element_type | solution.py:548
  (9 shorter events, 0.1 us)
Async XLA Ops:
  0.6 11.3 %collective-permute-start.1 = (bf16[32,2048]{1,0:T(8,128)(2,1)}, bf16[32,2048]{1,0:T(8,128)(2,1)S(1)}, u32[]{:S(2)}, u32[]{:S(2)}) collective-permute-start(bf16[32,2048]{1,0:T(8,128)(2,1)} %refs_0_.1), channel_id=1, source_target_pairs={{0,8},{1,13},{4,12},{5,9},{8,0},{9,5},{12,4},{13,1},{2,10},{3,15},... | collective-permute-start | bytes 393224 | tf_op jit(solution)/shard_map/ppermute | solution.py:330
  4.7 9.0 %collective-permute-start.3 = (bf16[64,2048]{1,0:T(8,128)(2,1)}, bf16[64,2048]{1,0:T(8,128)(2,1)S(1)}, u32[]{:S(2)}, u32[]{:S(2)}) collective-permute-start(bf16[64,2048]{1,0:T(8,128)(2,1)} %refs_2_.5), channel_id=1, source_target_pairs={{0,2},{2,0},{1,3},{3,1},{4,6},{6,4},{5,7},{7,5},{8,10},{10,8},{9,1... | collective-permute-start | bytes 786440 | tf_op jit(solution)/shard_map/ppermute | solution.py:324
  6.2 6.9 %collective-permute-start = (bf16[32,2048]{1,0:T(8,128)(2,1)}, bf16[32,2048]{1,0:T(8,128)(2,1)S(1)}, u32[]{:S(2)}, u32[]{:S(2)}) collective-permute-start(bf16[32,2048]{1,0:T(8,128)(2,1)} %refs_0_.1), channel_id=1, source_target_pairs={{0,4},{4,0},{8,12},{12,8},{1,5},{5,1},{9,13},{13,9},{2,6},{6,2},{1... | collective-permute-start | bytes 393224 | tf_op jit(solution)/shard_map/ppermute | solution.py:324
  11.9 6.5 %copy-start.1 = (bf16[32,2048]{1,0:T(8,128)(2,1)S(1)}, bf16[32,2048]{1,0:T(8,128)(2,1)}, u32[]{:S(2)}) copy-start(bf16[32,2048]{1,0:T(8,128)(2,1)} %refs_0_.1) | copy-start | bytes 393220
  11.9 1.8 %collective-permute-start.2 = (bf16[32,2048]{1,0:T(8,128)(2,1)S(1)}, bf16[32,2048]{1,0:T(8,128)(2,1)S(1)}, u32[]{:S(2)}, u32[]{:S(2)}) collective-permute-start(bf16[32,2048]{1,0:T(8,128)(2,1)S(1)} %after_own.1), channel_id=1, source_target_pairs={{0,1},{1,0},{2,3},{3,2},{4,5},{5,4},{6,7},{7,6},{8,9},{9,8},{10,11... | collective-permute-start | bytes 393224 | tf_op jit(solution)/shard_map/ppermute | solution.py:324
  12.0 6.4 %collective-permute-start.4 = (bf16[8,32,256]{2,1,0:T(8,128)(2,1)S(1)}, bf16[8,32,256]{2,1,0:T(8,128)(2,1)S(1)}, u32[]{:S(2)}, u32[]{:S(2)}) collective-permute-start(bf16[8,32,256]{2,1,0:T(8,128)(2,1)S(1)} %get-tuple-element.36._.refs_0_), channel_id=1, source_target_pairs={{0,2},{2,0},{1,3},{3,1},{4,6},{6,4},{5,7},{7,5},{8,10},{10,8},{9,1... | collective-permute-start | bytes 393224 | tf_op jit(solution)/shard_map/ppermute | solution.py:324
  14.9 12.1 %copy-start = (bf16[64,2048]{1,0:T(8,128)(2,1)S(1)}, bf16[64,2048]{1,0:T(8,128)(2,1)}, u32[]{:S(2)}) copy-start(bf16[64,2048]{1,0:T(8,128)(2,1)} %refs_2_.5) | copy-start | bytes 786436
  14.9 12.1 %collective-permute-start.5 = (bf16[8,96,256]{2,1,0:T(8,128)(2,1)S(1)}, bf16[8,96,256]{2,1,0:T(8,128)(2,1)S(1)}, u32[]{:S(2)}, u32[]{:S(2)}) collective-permute-start(bf16[8,96,256]{2,1,0:T(8,128)(2,1)S(1)} %forward_rest_a.1.refs_6_.refs_2_), channel_id=1, source_target_pairs={{0,2},{2,0},{1,3},{3,1},{4,6},{6,4},{5,7},{7,5},{8,10},{10,8},{9,1... | collective-permute-start | bytes 1179656 | tf_op jit(solution)/shard_map/ppermute | solution.py:324
  21.8 10.8 %collective-permute-start.8 = (bf16[8,64,256]{2,1,0:T(8,128)(2,1)S(1)}, bf16[8,64,256]{2,1,0:T(8,128)(2,1)S(1)}, u32[]{:S(2)}, u32[]{:S(2)}) collective-permute-start(bf16[8,64,256]{2,1,0:T(8,128)(2,1)S(1)} %get-tuple-element.42.refs_6_.refs_0_), channel_id=1, source_target_pairs={{0,2},{2,0},{1,3},{3,1},{4,6},{6,4},{5,7},{7,5},{8,10},{10,8},{9,1... | collective-permute-start | bytes 786440 | tf_op jit(solution)/shard_map/ppermute | solution.py:324
  22.6 12.8 %collective-permute-start.7 = (bf16[8,32,256]{2,1,0:T(8,128)(2,1)S(1)}, bf16[8,32,256]{2,1,0:T(8,128)(2,1)S(1)}, u32[]{:S(2)}, u32[]{:S(2)}) collective-permute-start(bf16[8,32,256]{2,1,0:T(8,128)(2,1)S(1)} %get-tuple-element.43.refs_7_.refs_0_), channel_id=1, source_target_pairs={{0,2},{2,0},{1,3},{3,1},{4,6},{6,4},{5,7},{7,5},{8,10},{10,8},{9,1... | collective-permute-start | bytes 393224 | tf_op jit(solution)/shard_map/ppermute | solution.py:324
  23.9 13.9 %collective-permute-start.6 = (bf16[8,32,256]{2,1,0:T(8,128)(2,1)S(1)}, bf16[8,32,256]{2,1,0:T(8,128)(2,1)S(1)}, u32[]{:S(2)}, u32[]{:S(2)}) collective-permute-start(bf16[8,32,256]{2,1,0:T(8,128)(2,1)S(1)} %get-tuple-element.44.refs_8_.refs_0_), channel_id=1, source_target_pairs={{0,2},{2,0},{1,3},{3,1},{4,6},{6,4},{5,7},{7,5},{8,10},{10,8},{9,1... | collective-permute-start | bytes 393224 | tf_op jit(solution)/shard_map/ppermute | solution.py:324
  34.7 3.1 %collective-permute-start.9 = (bf16[32,2048]{1,0:T(8,128)(2,1)S(1)}, bf16[32,2048]{1,0:T(8,128)(2,1)S(1)}, u32[]{:S(2)}, u32[]{:S(2)}) collective-permute-start(bf16[32,2048]{1,0:T(8,128)(2,1)S(1)} %get-tuple-element.56), channel_id=1, source_target_pairs={{0,1},{1,0},{2,3},{3,2},{4,5},{5,4},{6,7},{7,6},{8,9},{9,8},{10,11... | collective-permute-start | bytes 393224 | tf_op jit(solution)/shard_map/ppermute | solution.py:324
  37.4 7.9 %collective-permute-start.10 = (bf16[32,2048]{1,0:T(8,128)(2,1)S(1)}, bf16[32,2048]{1,0:T(8,128)(2,1)S(1)}, u32[]{:S(2)}, u32[]{:S(2)}) collective-permute-start(bf16[32,2048]{1,0:T(8,128)(2,1)S(1)} %get-tuple-element.61), channel_id=1, source_target_pairs={{0,4},{4,0},{8,12},{12,8},{1,5},{5,1},{9,13},{13,9},{2,6},{6,2},{1... | collective-permute-start | bytes 393224 | tf_op jit(solution)/shard_map/ppermute | solution.py:324
  37.8 9.0 %collective-permute-start.11 = (bf16[32,2048]{1,0:T(8,128)(2,1)S(1)}, bf16[32,2048]{1,0:T(8,128)(2,1)S(1)}, u32[]{:S(2)}, u32[]{:S(2)}) collective-permute-start(bf16[32,2048]{1,0:T(8,128)(2,1)S(1)} %add_cores.1.refs_11_), channel_id=1, source_target_pairs={{0,8},{1,13},{4,12},{5,9},{8,0},{9,5},{12,4},{13,1},{2,10},{3,15},... | collective-permute-start | bytes 393224 | tf_op jit(solution)/shard_map/ppermute | solution.py:330
  46.9 1.4 %collective-permute-start.12 = (bf16[32,2048]{1,0:T(8,128)(2,1)S(1)}, bf16[32,2048]{1,0:T(8,128)(2,1)S(1)}, u32[]{:S(2)}, u32[]{:S(2)}) collective-permute-start(bf16[32,2048]{1,0:T(8,128)(2,1)S(1)} %get-tuple-element.63), channel_id=1, source_target_pairs={{0,1},{1,0},{2,3},{3,2},{4,5},{5,4},{6,7},{7,6},{8,9},{9,8},{10,11... | collective-permute-start | bytes 393224 | tf_op jit(solution)/shard_map/ppermute | solution.py:324

commit v8 on v5

--- a/solution.py
+++ b/solution.py
@@ -95,17 +95,25 @@
     arrive = load_tiles(0, cols, gate_hbm, up_hbm, gate_ref, up_ref, sems)
     for copy in small:
         copy.wait()
-    for c in range(cols):
-        arrive(c)
-        part_ref[c] = forward_column(c, 0, (rows_ref, counts_ref), [x_ref], gate_ref, up_ref)
+    for start, stop in groups_of(cols):
+        arrive(start)
+        found = [
+            forward_column(c, 0, (rows_ref, counts_ref), [x_ref], gate_ref, up_ref) for c in range(start, stop)
+        ]
+        for c in range(start, stop):
+            part_ref[c] = found[c - start]
 
 
 def forward_kernel(members, rows_ref, counts_ref, *refs):
     xs = refs[:members]
     gate_ref, up_ref = refs[members : members + 2]
     part_ref = refs[-1]
-    for c in range(gate_ref.shape[0]):
-        part_ref[c] = forward_column(c, 0, (rows_ref, counts_ref), xs, gate_ref, up_ref)
+    for start, stop in groups_of(gate_ref.shape[0]):
+        found = [
+            forward_column(c, 0, (rows_ref, counts_ref), xs, gate_ref, up_ref) for c in range(start, stop)
+        ]
+        for c in range(start, stop):
+            part_ref[c] = found[c - start]
 
 
 def load_forward_kernel(members, groups, first, turn, rows_ref, counts_ref, *refs):
@@ -125,11 +133,14 @@
             turned_ref[r] = lax.dot_general(
                 identity, block, (((1,), (1,)), ((), ())), preferred_element_type=F32
             ).astype(BF16)
-    for c in range(cols):
-        arrive(c)
-        part = forward_column(c, first, (rows_ref, counts_ref), xs, gate_ref, up_ref)
-        for (start, stop), part_ref in zip(groups, parts):
-            part_ref[c] = part[start:stop]
+    for begin, end in groups_of(cols):
+        arrive(begin)
+        found = [
+            forward_column(c, first, (rows_ref, counts_ref), xs, gate_ref, up_ref) for c in range(begin, end)
+        ]
+        for c in range(begin, end):
+            for (start, stop), part_ref in zip(groups, parts):
+                part_ref[c] = found[c - begin][start:stop]
 
 
 def shard_of(member):
@@ -170,25 +181,52 @@
     return total
 
 
-def back_terms(c, grads, gate_ref, up_ref):
-    return lax.dot_general(
-        grads, weights_of(c, gate_ref, up_ref), (((1,), (1,)), ((), ())), preferred_element_type=F32
-    )
-
-
-def add_back(c, lists, back, accs, slots, tile):
+def elementwise(members, parts_of, cots, first, shard_rows, hidden_ref, grads_ref):
+    cols, _, width = grads_ref.shape
+    tile = width // 2
+    for start in range(0, cols, 2):
+        found = []
+        for c in range(start, min(start + 2, cols)):
+            where = slice((first + c) * tile, (first + c + 1) * tile)
+            found.append(nonlinear(parts_of(c), cotangent_of(members, cots, shard_rows, where)))
+        for c, (hidden, grads) in enumerate(found, start):
+            hidden_ref[:, c * tile : (c + 1) * tile] = hidden
+            grads_ref[c] = grads
+
+
+def add_back(first, lists, grads_ref, gate_ref, up_ref, accs):
     rows_ref, counts_ref = lists
-    rows = [rows_ref[k, 0, c] for k in range(slots)]
-    start = 0
-    for acc in accs:
-        stop = start + acc.shape[1]
-        sums = [
-            acc[rows[k]] + keep(k, counts_ref[0, c], back[start:stop, k * tile : (k + 1) * tile])
-            for k in range(slots)
-        ]
-        for k in range(slots):
-            acc[rows[k]] = sums[k]
-        start = stop
+    cols, _, slots, tile, _ = gate_ref.shape
+    step = slots // 3 if grads_ref.shape[1] > 64 else slots // 2
+
+    def product(c, k):
+        tiles = [w[c, 0, k : k + step].reshape(step * tile, tile) for w in (gate_ref, up_ref)]
+        return lax.dot_general(
+            grads_ref[c], jnp.concatenate(tiles, axis=1), (((1,), (1,)), ((), ())), preferred_element_type=F32
+        )
+
+    def add(c, k, back):
+        count = counts_ref[0, first + c]
+        rows = [rows_ref[k + i, 0, first + c] for i in range(step)]
+        start = 0
+        for acc in accs:
+            stop = start + acc.shape[1]
+            sums = [
+                acc[row] + keep(k + i, count, back[start:stop, i * tile : (i + 1) * tile])
+                for i, row in enumerate(rows)
+            ]
+            for row, value in zip(rows, sums):
+                acc[row] = value
+            start = stop
+
+    waiting = None
+    for c in range(cols):
+        for k in range(0, slots, step):
+            back = product(c, k)
+            if waiting is not None:
+                add(*waiting)
+            waiting = (c, k, back)
+    add(*waiting)
 
 
 def tile_grads(c, first, lists, turned_ref, grads, gate_ref, up_ref):
@@ -229,22 +267,25 @@
 def first_half_kernel(members, owners, rows_ref, counts_ref, gate_w, up_w, turned_ref, *refs):
     near, rest, cots = refs[:owners], refs[owners : 2 * owners], refs[2 * owners : 3 * owners]
     gate_hbm, up_hbm, hidden_ref, acc_near, acc_far, grads_ref, gate_ref, up_ref, sems = refs[-9:]
-    cols, _, slots, tile, _ = gate_ref.shape
+    cols = gate_ref.shape[0]
     shard_rows = hidden_ref.shape[0] // members
     lists = (rows_ref, counts_ref)
     acc_near[...] = jnp.zeros_like(acc_near)
     acc_far[...] = jnp.zeros_like(acc_far)
+    elementwise(
+        range(members),
+        lambda c: jnp.concatenate([total_of(c, near), total_of(c, rest)], axis=0),
+        cots,
+        0,
+        shard_rows,
+        hidden_ref,
+        grads_ref,
+    )
     copies = []
     for c in range(cols):
-        total = jnp.concatenate([total_of(c, near), total_of(c, rest)], axis=0)
-        where = slice(c * tile, (c + 1) * tile)
-        hidden, grads = nonlinear(total, cotangent_of(range(members), cots, shard_rows, where))
-        hidden_ref[:, where] = hidden
-        grads_ref[c] = grads
-        tile_grads(c, 0, lists, turned_ref, grads, gate_ref, up_ref)
+        tile_grads(c, 0, lists, turned_ref, grads_ref[c], gate_ref, up_ref)
         copies += store_tiles(0, c, gate_ref, up_ref, gate_hbm, up_hbm, sems)
-    for c in range(cols):
-        add_back(c, lists, back_terms(c, grads_ref[c], gate_w, up_w), (acc_near, acc_far), slots, tile)
+    add_back(0, lists, grads_ref, gate_w, up_w, (acc_near, acc_far))
     for copy in copies:
         copy.wait()
 
@@ -254,15 +295,11 @@
     outs = refs[-(2 + len(members) + 1) :]
     grads_ref, hidden_ref = outs[:2]
     dxs, acc_ref = outs[2:-1], outs[-1]
-    cols, _, slots, tile, _ = gate_w.shape
+    tile = gate_w.shape[3]
     shard_rows = hidden_ref.shape[0] // len(members)
     acc_ref[...] = acc_in[...]
-    for c in range(cols):
-        where = slice((first + c) * tile, (first + c + 1) * tile)
-        hidden, grads = nonlinear(total_of(c, parts), cotangent_of(members, cots, shard_rows, where))
-        hidden_ref[:, c * tile : (c + 1) * tile] = hidden
-        grads_ref[c] = grads
-        add_back(first + c, (rows_ref, counts_ref), back_terms(c, grads, gate_w, up_w), (acc_ref,), slots, tile)
+    elementwise(members, lambda c: total_of(c, parts), cots, first, shard_rows, hidden_ref, grads_ref)
+    add_back(first, (rows_ref, counts_ref), grads_ref, gate_w, up_w, (acc_ref,))
     for r in range(acc_ref.shape[0]):
         block = acc_ref[r].astype(BF16)
         for m, dx in enumerate(dxs):

time: 49.8 us -> 49.8 us (level)
  no operation moved by 1% of the time
where the time goes in v8:
time: 49.8 us; the launch traced here: 49.6 us
  Pallas kernels  21.4 us (43%)
  starting transfers between devices  14 us (28%)
  waiting for transfers between devices  12.7 us (26%)
  between operations  0.75 us (2%)
  other arithmetic  0.68 us (1%)
    ppermute x10, waiting for transfers between devices, swap(): lax.ppermute(x, axis, [(i, i ^ step) for i in range(lax.axis_size(axis))])  12.7 us
    ppermute x10, starting transfers between devices, swap(): lax.ppermute(x, axis, [(i, i ^ step) for i in range(lax.axis_size(axis))])  9.75 us
    pallas_call x1, Pallas kernels, on_device(): pl.pallas_call(functools.partial(first_half_kernel, shards, owners), out_...  5.08 us
    ppermute x2, starting transfers between devices, swap_far(): return lax.ppermute(x, ('tok', 'sub'), pairs)  4.27 us
    pallas_call x2, Pallas kernels, second_half(): pl.pallas_call(functools.partial(second_half_kernel, members, owners, hal...  4.12 us
    pallas_call x1, Pallas kernels, on_device(): pl.pallas_call(forward_own_kernel, out_shape=(shape(half, shard_rows, 2 *...  4.07 us
    pallas_call x1, Pallas kernels, on_device(): pl.pallas_call(functools.partial(load_forward_kernel, shards, ((near_rows...  3.46 us
    pallas_call x1, Pallas kernels, on_device(): pl.pallas_call(functools.partial(last_grads_kernel, shards, half), out_sh...  3.45 us
  transfers between devices with their start and end apart: 12, of which 9 were waited for; matrix products, arithmetic and copies ran while one was open for 0% of the time, Pallas kernels for 43%

profile of v8, /device:TPU:0, one launch (start us, length us, event | category | flops | bytes accessed | tf_op | source)
XLA Modules:
  0.0 49.6 jit_solution(1377804945347762216)
XLA Ops:
  0.6 4.1 %collective-permute-start.1 = (bf16[32,2048]{1,0:T(8,128)(2,1)}, bf16[32,2048]{1,0:T(8,128)(2,1)S(1)}, u32[]{:S(2)}, u32[]{:S(2)}) collective-permute-start(bf16[32,2048]{1,0:T(8,128)(2,1)} %refs_0_.1), channel_id=1, source_target_pairs={{0,8},{1,13},{4,12},{5,9},{8,0},{9,5},{12,4},{13,1},{2,10},{3,15},... | collective-permute-start | bytes 393224 | tf_op jit(solution)/shard_map/ppermute | solution.py:350
  4.7 1.5 %collective-permute-start.3 = (bf16[64,2048]{1,0:T(8,128)(2,1)}, bf16[64,2048]{1,0:T(8,128)(2,1)S(1)}, u32[]{:S(2)}, u32[]{:S(2)}) collective-permute-start(bf16[64,2048]{1,0:T(8,128)(2,1)} %refs_2_.3), channel_id=1, source_target_pairs={{0,2},{2,0},{1,3},{3,1},{4,6},{6,4},{5,7},{7,5},{8,10},{10,8},{9,1... | collective-permute-start | bytes 786440 | tf_op jit(solution)/shard_map/ppermute | solution.py:344
  6.2 1.6 %collective-permute-start = (bf16[32,2048]{1,0:T(8,128)(2,1)}, bf16[32,2048]{1,0:T(8,128)(2,1)S(1)}, u32[]{:S(2)}, u32[]{:S(2)}) collective-permute-start(bf16[32,2048]{1,0:T(8,128)(2,1)} %refs_0_.1), channel_id=1, source_target_pairs={{0,4},{4,0},{8,12},{12,8},{1,5},{5,1},{9,13},{13,9},{2,6},{6,2},{1... | collective-permute-start | bytes 393224 | tf_op jit(solution)/shard_map/ppermute | solution.py:344
  7.8 4.1 %forward_own_a.1 = (bf16[8,32,256]{2,1,0:T(8,128)(2,1)S(1)}, bf16[8,1,12,128,128]{4,3,2,1,0:T(8,128)(2,1)S(1)}, bf16[8,1,12,128,128]{4,3,2,1,0:T(8,128)(2,1)S(1)}, s32[12,1,16]{2,1,0:T(1,128)S(4)}, s32[1,16]{1,0:T(1,128)S(4)}) custom-call(bf16[32,2048]{1,0:T(8,128)(2,1)} %refs_0_.1, s32[12,1,16]{2,1,0:T(1,128)} %bitcast.2, s32[1,16]{1,0:T(1,128)} %bitcast.3, ...), custom_call_target="tpu_custom_call" | custom-call | flops 201326592 | bytes 6291456 | tf_op jit(solution)/shard_map/forward_own_a/pallas_call | solution.py:388
  11.9 0.0 copy-start.1
  11.9 0.1 collective-permute-start.2
  12.0 1.2 %collective-permute-start.4 = (bf16[8,32,256]{2,1,0:T(8,128)(2,1)S(1)}, bf16[8,32,256]{2,1,0:T(8,128)(2,1)S(1)}, u32[]{:S(2)}, u32[]{:S(2)}) collective-permute-start(bf16[8,32,256]{2,1,0:T(8,128)(2,1)S(1)} %get-tuple-element.35._.refs_0_), channel_id=1, source_target_pairs={{0,2},{2,0},{1,3},{3,1},{4,6},{6,4},{5,7},{7,5},{8,10},{10,8},{9,1... | collective-permute-start | bytes 393224 | tf_op jit(solution)/shard_map/ppermute | solution.py:344
  13.2 0.2 collective-permute-done.2.refs_2_.refs_3_
  13.3 0.4 collective-permute-done.3.refs_5_.refs_3_
  13.7 1.1 %forward_rest_a.1.refs_6_.refs_2_ = bf16[8,96,256]{2,1,0:T(8,128)(2,1)S(1)} custom-call(s32[12,1,16]{2,1,0:T(1,128)S(4)} %get-tuple-element.33.rows_ref, s32[1,16]{1,0:T(1,128)S(4)} %get-tuple-element.34.counts_ref, bf16[32,2048]{1,0:T(8,128)(2,1)S(1)} %collective-permute-done.refs_0_.refs_1_, ...), custom_call_target="tpu_custom_call" | custom-call | flops 805306368 | bytes 6291456 | tf_op jit(solution)/shard_map/forward_rest_a/pallas_call | solution.py:423
  14.9 0.0 copy-start
  14.9 1.6 %collective-permute-start.5 = (bf16[8,96,256]{2,1,0:T(8,128)(2,1)S(1)}, bf16[8,96,256]{2,1,0:T(8,128)(2,1)S(1)}, u32[]{:S(2)}, u32[]{:S(2)}) collective-permute-start(bf16[8,96,256]{2,1,0:T(8,128)(2,1)S(1)} %forward_rest_a.1.refs_6_.refs_2_), channel_id=1, source_target_pairs={{0,2},{2,0},{1,3},{3,1},{4,6},{6,4},{5,7},{7,5},{8,10},{10,8},{9,1... | collective-permute-start | bytes 1179656 | tf_op jit(solution)/shard_map/ppermute | solution.py:344
  16.5 1.9 %collective-permute-done.4.refs_7_.refs_1_ = bf16[8,32,256]{2,1,0:T(8,128)(2,1)S(1)} collective-permute-done((bf16[8,32,256]{2,1,0:T(8,128)(2,1)S(1)}, bf16[8,32,256]{2,1,0:T(8,128)(2,1)S(1)}, u32[]{:S(2)}, u32[]{:S(2)}) %collective-permute-start.4) | collective-permute-done | bytes 131104 | tf_op jit(solution)/shard_map/ppermute | solution.py:344
  18.4 3.5 %forward_b.1 = (bf16[8,64,256]{2,1,0:T(8,128)(2,1)S(1)}, bf16[8,64,256]{2,1,0:T(8,128)(2,1)S(1)}, bf16[8,1,12,128,128]{4,3,2,1,0:T(8,128)(2,1)S(1)}, bf16[8,1,12...) custom-call(s32[12,1,16]{2,1,0:T(1,128)S(4)} %get-tuple-element.33.rows_ref, ...), custom_call_target="tpu_custom_call" | custom-call | flops 4026531840 | bytes 31457280 | tf_op jit(solution)/shard_map/forward_b/pallas_call | solution.py:435
  21.8 0.8 %collective-permute-start.7 = (bf16[8,64,256]{2,1,0:T(8,128)(2,1)S(1)}, bf16[8,64,256]{2,1,0:T(8,128)(2,1)S(1)}, u32[]{:S(2)}, u32[]{:S(2)}) collective-permute-start(bf16[8,64,256]{2,1,0:T(8,128)(2,1)S(1)} %get-tuple-element.41.refs_6_.refs_0_), channel_id=1, source_target_pairs={{0,2},{2,0},{1,3},{3,1},{4,6},{6,4},{5,7},{7,5},{8,10},{10,8},{9,1... | collective-permute-start | bytes 786440 | tf_op jit(solution)/shard_map/ppermute | solution.py:344
  22.7 1.3 %collective-permute-start.6 = (bf16[8,64,256]{2,1,0:T(8,128)(2,1)S(1)}, bf16[8,64,256]{2,1,0:T(8,128)(2,1)S(1)}, u32[]{:S(2)}, u32[]{:S(2)}) collective-permute-start(bf16[8,64,256]{2,1,0:T(8,128)(2,1)S(1)} %get-tuple-element.42.refs_7_.refs_0_), channel_id=1, source_target_pairs={{0,2},{2,0},{1,3},{3,1},{4,6},{6,4},{5,7},{7,5},{8,10},{10,8},{9,1... | collective-permute-start | bytes 786440 | tf_op jit(solution)/shard_map/ppermute | solution.py:344
  23.9 3.1 %collective-permute-done.5.refs_3_ = bf16[8,96,256]{2,1,0:T(8,128)(2,1)S(1)} collective-permute-done((bf16[8,96,256]{2,1,0:T(8,128)(2,1)S(1)}, bf16[8,96,256]{2,1,0:T(8,128)(2,1)S(1)}, u32[]{:S(2)}, u32[]{:S(2)}) %collective-permute-start.5) | collective-permute-done | bytes 393248 | tf_op jit(solution)/shard_map/ppermute | solution.py:344
  27.0 5.1 %first_half.1 = (bf16[16,1,12,128,128]{4,3,2,1,0:T(8,128)(2,1)}, bf16[16,1,12,128,128]{4,3,2,1,0:T(8,128)(2,1)}, bf16[128,1024]{1,0:T(8,128)(2,1)S(1)}, f32[16,64,128]{2,1,0:T(8,128)S(1)}, f32[16,64,128]{2,1,0:T(8,128)S(1)}) custom-call(s32[12,1,16]{2,1,0:T(1,128)S(4)} %get-tuple-element.33.rows_ref, s32[1,16]{1,0:T(1,128)S(4)} %get-tuple-element.34.counts_ref, ...), custom_call_target="tpu_custom_call" | custom-call | flops 1610612736 | bytes 6291456 | tf_op jit(solution)/shard_map/first_half/pallas_call | solution.py:456
  32.1 0.5 %collective-permute-done.7.refs_1_ = bf16[8,64,256]{2,1,0:T(8,128)(2,1)S(1)} collective-permute-done((bf16[8,64,256]{2,1,0:T(8,128)(2,1)S(1)}, bf16[8,64,256]{2,1,0:T(8,128)(2,1)S(1)}, u32[]{:S(2)}, u32[]{:S(2)}) %collective-permute-start.7) | collective-permute-done | bytes 262176 | tf_op jit(solution)/shard_map/ppermute | solution.py:344
  32.6 2.1 %second_half.2 = (bf16[8,64,256]{2,1,0:T(8,128)(2,1)S(1)}, bf16[64,1024]{1,0:T(8,128)(2,1)S(1)}, bf16[32,2048]{1,0:T(8,128)(2,1)S(1)}, bf16[32,2048]{1,0:T(8,128)(2,1)S(1)}) custom-call(s32[12,1,16]{2,1,0:T(1,128)S(4)} %get-tuple-element.33.rows_ref, s32[1,16]{1,0:T(1,128)S(4)} %get-tuple-element.34.counts_ref, ...), custom_call_target="tpu_custom_call" | custom-call | flops 402653184 | bytes 6291456 | tf_op jit(solution)/shard_map/second_half/pallas_call | solution.py:480
  34.7 0.1 collective-permute-start.8
  34.8 1.3 %collective-permute-done.8.right_ref = bf16[32,2048]{1,0:T(8,128)(2,1)S(1)} collective-permute-done((bf16[32,2048]{1,0:T(8,128)(2,1)S(1)}, bf16[32,2048]{1,0:T(8,128)(2,1)S(1)}, u32[]{:S(2)}, u32[]{:S(2)}) %collective-permute-start.8) | collective-permute-done | bytes 131104 | tf_op jit(solution)/shard_map/ppermute | solution.py:344
  36.1 0.2 collective-permute-start.10
  36.3 1.3 %collective-permute-done.6.refs_1_ = bf16[8,64,256]{2,1,0:T(8,128)(2,1)S(1)} collective-permute-done((bf16[8,64,256]{2,1,0:T(8,128)(2,1)S(1)}, bf16[8,64,256]{2,1,0:T(8,128)(2,1)S(1)}, u32[]{:S(2)}, u32[]{:S(2)}) %collective-permute-start.6) | collective-permute-done | bytes 262176 | tf_op jit(solution)/shard_map/ppermute | solution.py:344
  37.6 2.1 %second_half.3 = (bf16[8,64,256]{2,1,0:T(8,128)(2,1)S(1)}, bf16[64,1024]{1,0:T(8,128)(2,1)S(1)}, bf16[32,2048]{1,0:T(8,128)(2,1)S(1)}, bf16[32,2048]{1,0:T(8,128)(2,1)S(1)}) custom-call(s32[12,1,16]{2,1,0:T(1,128)S(4)} %get-tuple-element.33.rows_ref, s32[1,16]{1,0:T(1,128)S(4)} %get-tuple-element.34.counts_ref, ...), custom_call_target="tpu_custom_call" | custom-call | flops 402653184 | bytes 6291456 | tf_op jit(solution)/shard_map/second_half/pallas_call | solution.py:480
  39.6 1.6 %collective-permute-start.9 = (bf16[32,2048]{1,0:T(8,128)(2,1)S(1)}, bf16[32,2048]{1,0:T(8,128)(2,1)S(1)}, u32[]{:S(2)}, u32[]{:S(2)}) collective-permute-start(bf16[32,2048]{1,0:T(8,128)(2,1)S(1)} %get-tuple-element.58), channel_id=1, source_target_pairs={{0,4},{4,0},{8,12},{12,8},{1,5},{5,1},{9,13},{13,9},{2,6},{6,2},{1... | collective-permute-start | bytes 393224 | tf_op jit(solution)/shard_map/ppermute | solution.py:344
  41.2 3.5 %last_grads.1 = (bf16[16,1,12,128,128]{4,3,2,1,0:T(8,128)(2,1)}, bf16[16,1,12,128,128]{4,3,2,1,0:T(8,128)(2,1)}, bf16[64,2048]{1,0:T(8,128)(2,1)}, f32[8,128]{1,0:T(8,128)S(1)}) custom-call(s32[12,1,16]{2,1,0:T(1,128)S(4)} %get-tuple-element.33.rows_ref, s32[1,16]{1,0:T(1,128)S(4)} %get-tuple-element.34.counts_ref, ...), custom_call_target="tpu_custom_call", output_to_operand_aliasing={{0}: (8, {}), {1}: (9, {})} | custom-call | flops 8053063680 | bytes 62914560 | tf_op jit(solution)/shard_map/last_grads/pallas_call | solution.py:515
  44.7 2.8 %collective-permute-done.9.refs_1_ = bf16[32,2048]{1,0:T(8,128)(2,1)S(1)} collective-permute-done((bf16[32,2048]{1,0:T(8,128)(2,1)S(1)}, bf16[32,2048]{1,0:T(8,128)(2,1)S(1)}, u32[]{:S(2)}, u32[]{:S(2)}) %collective-permute-start.9) | collective-permute-done | bytes 131104 | tf_op jit(solution)/shard_map/ppermute | solution.py:344
  47.4 0.1 sum_shards.1
  47.5 0.2 collective-permute-start.11
  47.7 1.2 %collective-permute-done.11 = bf16[32,2048]{1,0:T(8,128)(2,1)S(1)} collective-permute-done((bf16[32,2048]{1,0:T(8,128)(2,1)S(1)}, bf16[32,2048]{1,0:T(8,128)(2,1)S(1)}, u32[]{:S(2)}, u32[]{:S(2)}) %collective-permute-start.11) | collective-permute-done | bytes 131104 | tf_op jit(solution)/shard_map/ppermute | solution.py:344
  48.9 0.7 %add_convert_fusion = bf16[32,2048]{1,0:T(8,128)(2,1)} fusion(f32[32,2048]{1,0:T(8,128)S(1)} %get-tuple-element.60, bf16[32,2048]{1,0:T(8,128)(2,1)S(1)} %collective-permute-done.11), kind=kLoop, calls=%fused_computation | loop fusion | flops 196608 | bytes 524288 | tf_op jit(solution)/shard_map/convert_element_type | solution.py:540
  (7 shorter events, 0.1 us)
Async XLA Ops:
  0.6 11.3 %collective-permute-start.1 = (bf16[32,2048]{1,0:T(8,128)(2,1)}, bf16[32,2048]{1,0:T(8,128)(2,1)S(1)}, u32[]{:S(2)}, u32[]{:S(2)}) collective-permute-start(bf16[32,2048]{1,0:T(8,128)(2,1)} %refs_0_.1), channel_id=1, source_target_pairs={{0,8},{1,13},{4,12},{5,9},{8,0},{9,5},{12,4},{13,1},{2,10},{3,15},... | collective-permute-start | bytes 393224 | tf_op jit(solution)/shard_map/ppermute | solution.py:350
  4.7 9.0 %collective-permute-start.3 = (bf16[64,2048]{1,0:T(8,128)(2,1)}, bf16[64,2048]{1,0:T(8,128)(2,1)S(1)}, u32[]{:S(2)}, u32[]{:S(2)}) collective-permute-start(bf16[64,2048]{1,0:T(8,128)(2,1)} %refs_2_.3), channel_id=1, source_target_pairs={{0,2},{2,0},{1,3},{3,1},{4,6},{6,4},{5,7},{7,5},{8,10},{10,8},{9,1... | collective-permute-start | bytes 786440 | tf_op jit(solution)/shard_map/ppermute | solution.py:344
  6.2 6.9 %collective-permute-start = (bf16[32,2048]{1,0:T(8,128)(2,1)}, bf16[32,2048]{1,0:T(8,128)(2,1)S(1)}, u32[]{:S(2)}, u32[]{:S(2)}) collective-permute-start(bf16[32,2048]{1,0:T(8,128)(2,1)} %refs_0_.1), channel_id=1, source_target_pairs={{0,4},{4,0},{8,12},{12,8},{1,5},{5,1},{9,13},{13,9},{2,6},{6,2},{1... | collective-permute-start | bytes 393224 | tf_op jit(solution)/shard_map/ppermute | solution.py:344
  11.9 6.5 %copy-start.1 = (bf16[32,2048]{1,0:T(8,128)(2,1)S(1)}, bf16[32,2048]{1,0:T(8,128)(2,1)}, u32[]{:S(2)}) copy-start(bf16[32,2048]{1,0:T(8,128)(2,1)} %refs_0_.1) | copy-start | bytes 393220
  11.9 1.4 %collective-permute-start.2 = (bf16[32,2048]{1,0:T(8,128)(2,1)S(1)}, bf16[32,2048]{1,0:T(8,128)(2,1)S(1)}, u32[]{:S(2)}, u32[]{:S(2)}) collective-permute-start(bf16[32,2048]{1,0:T(8,128)(2,1)S(1)} %after_own.1), channel_id=1, source_target_pairs={{0,1},{1,0},{2,3},{3,2},{4,5},{5,4},{6,7},{7,6},{8,9},{9,8},{10,11... | collective-permute-start | bytes 393224 | tf_op jit(solution)/shard_map/ppermute | solution.py:344
  12.0 6.4 %collective-permute-start.4 = (bf16[8,32,256]{2,1,0:T(8,128)(2,1)S(1)}, bf16[8,32,256]{2,1,0:T(8,128)(2,1)S(1)}, u32[]{:S(2)}, u32[]{:S(2)}) collective-permute-start(bf16[8,32,256]{2,1,0:T(8,128)(2,1)S(1)} %get-tuple-element.35._.refs_0_), channel_id=1, source_target_pairs={{0,2},{2,0},{1,3},{3,1},{4,6},{6,4},{5,7},{7,5},{8,10},{10,8},{9,1... | collective-permute-start | bytes 393224 | tf_op jit(solution)/shard_map/ppermute | solution.py:344
  14.9 12.1 %copy-start = (bf16[64,2048]{1,0:T(8,128)(2,1)S(1)}, bf16[64,2048]{1,0:T(8,128)(2,1)}, u32[]{:S(2)}) copy-start(bf16[64,2048]{1,0:T(8,128)(2,1)} %refs_2_.3) | copy-start | bytes 786436
  14.9 12.1 %collective-permute-start.5 = (bf16[8,96,256]{2,1,0:T(8,128)(2,1)S(1)}, bf16[8,96,256]{2,1,0:T(8,128)(2,1)S(1)}, u32[]{:S(2)}, u32[]{:S(2)}) collective-permute-start(bf16[8,96,256]{2,1,0:T(8,128)(2,1)S(1)} %forward_rest_a.1.refs_6_.refs_2_), channel_id=1, source_target_pairs={{0,2},{2,0},{1,3},{3,1},{4,6},{6,4},{5,7},{7,5},{8,10},{10,8},{9,1... | collective-permute-start | bytes 1179656 | tf_op jit(solution)/shard_map/ppermute | solution.py:344
  21.8 10.8 %collective-permute-start.7 = (bf16[8,64,256]{2,1,0:T(8,128)(2,1)S(1)}, bf16[8,64,256]{2,1,0:T(8,128)(2,1)S(1)}, u32[]{:S(2)}, u32[]{:S(2)}) collective-permute-start(bf16[8,64,256]{2,1,0:T(8,128)(2,1)S(1)} %get-tuple-element.41.refs_6_.refs_0_), channel_id=1, source_target_pairs={{0,2},{2,0},{1,3},{3,1},{4,6},{6,4},{5,7},{7,5},{8,10},{10,8},{9,1... | collective-permute-start | bytes 786440 | tf_op jit(solution)/shard_map/ppermute | solution.py:344
  22.7 14.9 %collective-permute-start.6 = (bf16[8,64,256]{2,1,0:T(8,128)(2,1)S(1)}, bf16[8,64,256]{2,1,0:T(8,128)(2,1)S(1)}, u32[]{:S(2)}, u32[]{:S(2)}) collective-permute-start(bf16[8,64,256]{2,1,0:T(8,128)(2,1)S(1)} %get-tuple-element.42.refs_7_.refs_0_), channel_id=1, source_target_pairs={{0,2},{2,0},{1,3},{3,1},{4,6},{6,4},{5,7},{7,5},{8,10},{10,8},{9,1... | collective-permute-start | bytes 786440 | tf_op jit(solution)/shard_map/ppermute | solution.py:344
  34.7 1.4 %collective-permute-start.8 = (bf16[32,2048]{1,0:T(8,128)(2,1)S(1)}, bf16[32,2048]{1,0:T(8,128)(2,1)S(1)}, u32[]{:S(2)}, u32[]{:S(2)}) collective-permute-start(bf16[32,2048]{1,0:T(8,128)(2,1)S(1)} %get-tuple-element.46), channel_id=1, source_target_pairs={{0,1},{1,0},{2,3},{3,2},{4,5},{5,4},{6,7},{7,6},{8,9},{9,8},{10,11... | collective-permute-start | bytes 393224 | tf_op jit(solution)/shard_map/ppermute | solution.py:344
  36.1 11.3 %collective-permute-start.10 = (bf16[32,2048]{1,0:T(8,128)(2,1)S(1)}, bf16[32,2048]{1,0:T(8,128)(2,1)S(1)}, u32[]{:S(2)}, u32[]{:S(2)}) collective-permute-start(bf16[32,2048]{1,0:T(8,128)(2,1)S(1)} %add_cores.1.refs_4_), channel_id=1, source_target_pairs={{0,8},{1,13},{4,12},{5,9},{8,0},{9,5},{12,4},{13,1},{2,10},{3,15},... | collective-permute-start | bytes 393224 | tf_op jit(solution)/shard_map/ppermute | solution.py:350
  39.6 7.8 %collective-permute-start.9 = (bf16[32,2048]{1,0:T(8,128)(2,1)S(1)}, bf16[32,2048]{1,0:T(8,128)(2,1)S(1)}, u32[]{:S(2)}, u32[]{:S(2)}) collective-permute-start(bf16[32,2048]{1,0:T(8,128)(2,1)S(1)} %get-tuple-element.58), channel_id=1, source_target_pairs={{0,4},{4,0},{8,12},{12,8},{1,5},{5,1},{9,13},{13,9},{2,6},{6,2},{1... | collective-permute-start | bytes 393224 | tf_op jit(solution)/shard_map/ppermute | solution.py:344
  47.5 1.4 %collective-permute-start.11 = (bf16[32,2048]{1,0:T(8,128)(2,1)S(1)}, bf16[32,2048]{1,0:T(8,128)(2,1)S(1)}, u32[]{:S(2)}, u32[]{:S(2)}) collective-permute-start(bf16[32,2048]{1,0:T(8,128)(2,1)S(1)} %get-tuple-element.61), channel_id=1, source_target_pairs={{0,1},{1,0},{2,3},{3,2},{4,5},{5,4},{6,7},{7,6},{8,9},{9,8},{10,11... | collective-permute-start | bytes 393224 | tf_op jit(solution)/shard_map/ppermute | solution.py:344

commit v9 on v7

--- a/solution.py
+++ b/solution.py
@@ -108,6 +108,11 @@
         part_ref[c] = forward_column(c, 0, (rows_ref, counts_ref), xs, gate_ref, up_ref)
 
 
+def unit(size):
+    row, column = (lax.broadcasted_iota(jnp.int32, (size, size), axis) for axis in (0, 1))
+    return (row == column).astype(F32).astype(BF16)
+
+
 def load_forward_kernel(members, groups, first, turn, rows_ref, counts_ref, *refs):
     xs = refs[:members]
     gate_hbm, up_hbm = refs[members : members + 2]
@@ -117,9 +122,7 @@
     arrive = load_tiles(first, cols, gate_hbm, up_hbm, gate_ref, up_ref, sems)
     if turn:
         turned_ref = outs[-2]
-        identity = (
-            lax.broadcasted_iota(jnp.int32, (tile, tile), 0) == lax.broadcasted_iota(jnp.int32, (tile, tile), 1)
-        ).astype(F32).astype(BF16)
+        identity = unit(tile)
         for r in range(turned_ref.shape[0]):
             block = jnp.concatenate([x[:, r * tile : (r + 1) * tile] for x in xs], axis=0)
             turned_ref[r] = lax.dot_general(
@@ -174,6 +177,19 @@
     return lax.dot_general(
         grads, weights_of(c, gate_ref, up_ref), (((1,), (1,)), ((), ())), preferred_element_type=F32
     )
+
+
+def turn_kernel(gate_ref, up_ref, _, turned_ref):
+    cols, _, slots, rows, tile = gate_ref.shape
+    identity = unit(tile)
+    for c in range(cols):
+        for i, tiles in enumerate((gate_ref, up_ref)):
+            turned_ref[c, i * tile : (i + 1) * tile] = lax.dot_general(
+                identity,
+                tiles[c, 0].reshape(slots * rows, tile),
+                (((1,), (1,)), ((), ())),
+                preferred_element_type=F32,
+            ).astype(BF16)
 
 
 def add_back(c, lists, back, accs, slots, tile):
@@ -252,12 +268,12 @@
         copy.wait()
 
 
-def second_half_kernel(members, owners, first, rows_ref, counts_ref, gate_w, up_w, acc_in, *refs):
+def second_half_kernel(members, owners, first, slots, rows_ref, counts_ref, turned_w, acc_in, *refs):
     parts, cots = refs[:owners], refs[owners : 2 * owners]
     outs = refs[-(2 + len(members) + 1) :]
     grads_ref, hidden_ref = outs[:2]
     dxs, acc_ref = outs[2:-1], outs[-1]
-    cols, _, slots, tile, _ = gate_w.shape
+    cols, tile = turned_w.shape[0], turned_w.shape[1] // 2
     shard_rows = hidden_ref.shape[0] // len(members)
     acc_ref[...] = acc_in[...]
     for c in range(cols):
@@ -265,14 +281,15 @@
         hidden, grads = nonlinear(total_of(c, parts), cotangent_of(members, cots, shard_rows, where))
         hidden_ref[:, c * tile : (c + 1) * tile] = hidden
         grads_ref[c] = grads
-        add_back(first + c, (rows_ref, counts_ref), back_terms(c, grads, gate_w, up_w), (acc_ref,), slots, tile)
+        back = jnp.dot(grads, turned_w[c], preferred_element_type=F32)
+        add_back(first + c, (rows_ref, counts_ref), back, (acc_ref,), slots, tile)
     for r in range(acc_ref.shape[0]):
         block = acc_ref[r].astype(BF16)
         for m, dx in enumerate(dxs):
             dx[:, r * tile : (r + 1) * tile] = block[m * shard_rows : (m + 1) * shard_rows]
 
 
-def last_half_kernel(members, owners, first, rows_ref, counts_ref, gate_w, up_w, turned_ref, acc_in, *refs):
+def last_half_kernel(members, owners, first, rows_ref, counts_ref, turned_w, turned_ref, acc_in, *refs):
     parts, cots = refs[:owners], refs[owners : 2 * owners]
     next_grads, far_grads, hidden_a, next_hidden, far_hidden = refs[2 * owners : 2 * owners + 5]
     gate_hbm, up_hbm, hidden_hbm, dx_ref = refs[-11:-7]
@@ -298,7 +315,8 @@
         copies += store_tiles(first, c, gate_ref, up_ref, gate_hbm, up_hbm, sems)
     copies += start_hidden(members, hidden_of, hidden_hbm, shard_rows, hidden_sems)
     for c in range(cols):
-        add_back(first + c, lists, back_terms(c, grads_ref[c], gate_w, up_w), (acc_ref,), slots, tile)
+        back = jnp.dot(grads_ref[c], turned_w[c], preferred_element_type=F32)
+        add_back(first + c, lists, back, (acc_ref,), slots, tile)
     for r in range(acc_ref.shape[0]):
         dx_ref[:, r * tile : (r + 1) * tile] = acc_ref[r].astype(BF16)
     for copy in copies:
@@ -309,8 +327,7 @@
     out_ref[...] = x_ref[...]
 
 
-def add_kernel(left_ref, right_ref, *refs):
-    out_ref = refs[-1]
+def add_kernel(left_ref, right_ref, _, out_ref):
     out_ref[...] = (left_ref[...].astype(F32) + right_ref[...].astype(F32)).astype(BF16)
 
 
@@ -440,8 +457,17 @@
         cost_estimate=cost(row_total, rest, 1, 1, 5),
         name="forward_b",
     )(*lists, *xs, *from_hbm(gate_tiles, up_tiles), rest_a[0], near_a[-1])
-    weights_b = [gate_b, up_b]
     own_b, next_b, far_b = to_owners(own_b), to_owners(next_b), to_owners(far_b)
+
+    turned_b = pl.pallas_call(
+        turn_kernel,
+        out_shape=shape(rest, 2 * tile, slots * tile),
+        in_specs=[VMEM_SPEC] * 2 + [ANY_SPEC],
+        out_specs=VMEM_SPEC,
+        compiler_params=limit(8),
+        cost_estimate=cost(2 * tile, rest, 1, 1, 0),
+        name="turn_b",
+    )(gate_b, up_b, far_b[0])
 
     out_tiles = shape(*gate_tiles.shape)
     tile_bytes = slots * tile * tile * 2
@@ -465,47 +491,47 @@
         cost_estimate=cost(row_total, half, 2, 1, 1),
         name="first_half",
     )(
-        *lists, *weights_a, turned, *near_a, *rest_a, *cots, far_b[0], next_b[0], own_b[0]
+        *lists, *weights_a, turned, *near_a, *rest_a, *cots, far_b[0], next_b[0], turned_b
     )
 
     def second_half(name, chunk, acc, parts, after, weight):
         rows_here = len(chunk) * shard_rows
         return pl.pallas_call(
-            functools.partial(second_half_kernel, chunk, owners, half),
+            functools.partial(second_half_kernel, chunk, owners, half, slots),
             out_shape=(
                 shape(rest, rows_here, 2 * tile),
                 shape(rows_here, rest * tile),
                 *[shape(shard_rows, width) for _ in chunk],
             ),
-            in_specs=[SMEM_SPEC] * 2 + [VMEM_SPEC] * (3 + 2 * owners) + [ANY_SPEC],
+            in_specs=[SMEM_SPEC] * 2 + [VMEM_SPEC] * (2 + 2 * owners) + [ANY_SPEC],
             out_specs=(VMEM_SPEC,) * (2 + len(chunk)),
             scratch_shapes=[pltpu.VMEM((row_blocks, rows_here, tile), F32)],
             compiler_params=limit(8),
             cost_estimate=cost(rows_here, rest, 1, 1, weight),
             name=name,
-        )(*lists, *weights_b, acc, *parts, *cots, after)
+        )(*lists, turned_b, acc, *parts, *cots, after)
 
     far_grads, far_hidden, *far_dxs = second_half("far_b", far_members, acc_far, far_b, acc_own, 1)
-    next_grads, next_hidden, next_dx = second_half("next_b", [1], acc_next, next_b, far_grads, 1)
     both_cores = []
     for mine, others in zip(far_dxs[: len(bases)], far_dxs[len(bases) :]):
         both_cores.append(
             pl.pallas_call(
                 add_kernel,
                 out_shape=shape(shard_rows, width),
-                in_specs=[VMEM_SPEC] * 2 + [ANY_SPEC] * 2,
+                in_specs=[VMEM_SPEC] * 2 + [ANY_SPEC],
                 out_specs=VMEM_SPEC,
                 compiler_params=limit(8),
                 cost_estimate=pl.CostEstimate(flops=0, bytes_accessed=0, transcendentals=0),
                 name="add_cores",
-            )(mine, swap(others, "sub", 1), next_grads, own_b[-1])
+            )(mine, swap(others, "sub", 1), next_b[-1])
         )
     back_far = [swap_far(total, base) for total, base in zip(both_cores, bases)]
+    next_grads, next_hidden, next_dx = second_half("next_b", [1], acc_next, next_b, both_cores[-1], 1)
     back_next = swap(next_dx, "tok", 1)
     gate_out, up_out, hidden_out, own_dx = pl.pallas_call(
         functools.partial(last_half_kernel, members, owners, half),
         out_shape=(out_tiles, out_tiles, shape(*d_hidden.shape), shape(shard_rows, width)),
-        in_specs=[SMEM_SPEC] * 2 + [VMEM_SPEC] * (9 + 2 * owners) + [ANY_SPEC] * 3,
+        in_specs=[SMEM_SPEC] * 2 + [VMEM_SPEC] * (8 + 2 * owners) + [ANY_SPEC] * 3,
         out_specs=(ANY_SPEC,) * 3 + (VMEM_SPEC,),
         scratch_shapes=[
             pltpu.VMEM((row_blocks, shard_rows, tile), F32),
@@ -516,13 +542,13 @@
             pltpu.SemaphoreType.DMA((2, rest)),
             pltpu.SemaphoreType.DMA((2, d_hidden.shape[0] // shard_rows)),
         ],
-        input_output_aliases={11 + 2 * owners: 0, 12 + 2 * owners: 1},
+        input_output_aliases={10 + 2 * owners: 0, 11 + 2 * owners: 1},
         compiler_params=limit(8 + 2 * rest * tile_bytes // MIB),
         cost_estimate=cost(row_total, rest, 1, 1, 10),
         name="last_half",
     )(
         *lists,
-        *weights_b,
+        turned_b,
         turned,
         acc_own,
         *own_b,

time: 49.1 us -> 48.5 us (0.988)
  waiting for transfers between devices: 8.73 us -> 7.46 us
  starting transfers between devices: 15.9 us -> 16.9 us
    ppermute x11, starting transfers between devices: 9.25 us -> 12.5 us  [swap(): lax.ppermute(x, axis, [(i, i ^ step) for i in range(lax.axis_size(axis))])]
    ppermute x2, starting transfers between devices: 6.69 us -> 4.36 us  [swap_far(): return lax.ppermute(x, ('tok', 'sub'), pairs)]
    ppermute x2, waiting for transfers between devices: 1.56 us -> 0.01 us  [swap_far(): return lax.ppermute(x, ('tok', 'sub'), pairs)]
    pallas_call x1, Pallas kernels: 4.82 us -> 4.18 us  [on_device(): pl.pallas_call(functools.partial(last_half_kernel, members, owners, half)...]
    pallas_call x2 -> x3, Pallas kernels: 4.04 us -> 4.36 us  [the longest x2 2.56 us: second_half(): pl.pallas_call(functools.partial(second_half_kernel, chunk, owners, half,...]
where the time goes in v9:
time: 48.5 us; the launch traced here: 48.3 us
  Pallas kernels  22.5 us (46%)
  starting transfers between devices  16.9 us (35%)
  waiting for transfers between devices  7.46 us (15%)
  between operations  0.76 us (2%)
  other arithmetic  0.68 us (1%)
    ppermute x11, starting transfers between devices, swap(): lax.ppermute(x, axis, [(i, i ^ step) for i in range(lax.axis_size(axis))])  12.5 us
    ppermute x11, waiting for transfers between devices, swap(): lax.ppermute(x, axis, [(i, i ^ step) for i in range(lax.axis_size(axis))])  7.46 us
    pallas_call x1, Pallas kernels, on_device(): pl.pallas_call(functools.partial(first_half_kernel, members, owners), out...  5.21 us
    ppermute x2, starting transfers between devices, swap_far(): return lax.ppermute(x, ('tok', 'sub'), pairs)  4.36 us
    pallas_call x1, Pallas kernels, on_device(): pl.pallas_call(functools.partial(last_half_kernel, members, owners, half)...  4.18 us
    pallas_call x1, Pallas kernels, on_device(): pl.pallas_call(forward_own_kernel, out_shape=(shape(half, shard_rows, 2 *...  4.07 us
    pallas_call x1, Pallas kernels, on_device(): pl.pallas_call(functools.partial(load_forward_kernel, shards, groups, hal...  3.46 us
    pallas_call x2, Pallas kernels, second_half(): pl.pallas_call(functools.partial(second_half_kernel, chunk, owners, half,...  2.56 us
  transfers between devices with their start and end apart: 13, of which 7 were waited for; matrix products, arithmetic and copies ran while one was open for 0% of the time, Pallas kernels for 47%

profile of v9, /device:TPU:0, one launch (start us, length us, event | category | flops | bytes accessed | tf_op | source)
XLA Modules:
  0.0 48.3 jit_solution(5154996185425188845)
XLA Ops:
  0.6 4.1 %collective-permute-start.1 = (bf16[32,2048]{1,0:T(8,128)(2,1)}, bf16[32,2048]{1,0:T(8,128)(2,1)S(1)}, u32[]{:S(2)}, u32[]{:S(2)}) collective-permute-start(bf16[32,2048]{1,0:T(8,128)(2,1)} %refs_0_.1), channel_id=1, source_target_pairs={{0,8},{1,13},{4,12},{5,9},{8,0},{9,5},{12,4},{13,1},{2,10},{3,15},... | collective-permute-start | bytes 393224 | tf_op jit(solution)/shard_map/ppermute | solution.py:347
  4.7 1.5 %collective-permute-start.3 = (bf16[64,2048]{1,0:T(8,128)(2,1)}, bf16[64,2048]{1,0:T(8,128)(2,1)S(1)}, u32[]{:S(2)}, u32[]{:S(2)}) collective-permute-start(bf16[64,2048]{1,0:T(8,128)(2,1)} %refs_2_.5), channel_id=1, source_target_pairs={{0,2},{2,0},{1,3},{3,1},{4,6},{6,4},{5,7},{7,5},{8,10},{10,8},{9,1... | collective-permute-start | bytes 786440 | tf_op jit(solution)/shard_map/ppermute | solution.py:341
  6.2 1.6 %collective-permute-start = (bf16[32,2048]{1,0:T(8,128)(2,1)}, bf16[32,2048]{1,0:T(8,128)(2,1)S(1)}, u32[]{:S(2)}, u32[]{:S(2)}) collective-permute-start(bf16[32,2048]{1,0:T(8,128)(2,1)} %refs_0_.1), channel_id=1, source_target_pairs={{0,4},{4,0},{8,12},{12,8},{1,5},{5,1},{9,13},{13,9},{2,6},{6,2},{1... | collective-permute-start | bytes 393224 | tf_op jit(solution)/shard_map/ppermute | solution.py:341
  7.8 4.1 %forward_own_a.1 = (bf16[8,32,256]{2,1,0:T(8,128)(2,1)S(1)}, bf16[8,1,12,128,128]{4,3,2,1,0:T(8,128)(2,1)S(1)}, bf16[8,1,12,128,128]{4,3,2,1,0:T(8,128)(2,1)S(1)}, s32[12,1,16]{2,1,0:T(1,128)S(4)}, s32[1,16]{1,0:T(1,128)S(4)}) custom-call(bf16[32,2048]{1,0:T(8,128)(2,1)} %refs_0_.1, s32[12,1,16]{2,1,0:T(1,128)} %bitcast.2, s32[1,16]{1,0:T(1,128)} %bitcast.3, ...), custom_call_target="tpu_custom_call" | custom-call | flops 201326592 | bytes 6291456 | tf_op jit(solution)/shard_map/forward_own_a/pallas_call | solution.py:385
  11.9 0.0 copy-start.1
  11.9 0.1 collective-permute-start.2
  12.0 1.2 %collective-permute-start.4 = (bf16[8,32,256]{2,1,0:T(8,128)(2,1)S(1)}, bf16[8,32,256]{2,1,0:T(8,128)(2,1)S(1)}, u32[]{:S(2)}, u32[]{:S(2)}) collective-permute-start(bf16[8,32,256]{2,1,0:T(8,128)(2,1)S(1)} %get-tuple-element.36._.refs_0_), channel_id=1, source_target_pairs={{0,2},{2,0},{1,3},{3,1},{4,6},{6,4},{5,7},{7,5},{8,10},{10,8},{9,1... | collective-permute-start | bytes 393224 | tf_op jit(solution)/shard_map/ppermute | solution.py:341
  13.2 0.6 %collective-permute-done.3.refs_5_.refs_3_ = bf16[64,2048]{1,0:T(8,128)(2,1)S(1)} collective-permute-done((bf16[64,2048]{1,0:T(8,128)(2,1)}, bf16[64,2048]{1,0:T(8,128)(2,1)S(1)}, u32[]{:S(2)}, u32[]{:S(2)}) %collective-permute-start.3) | collective-permute-done | bytes 262176 | tf_op jit(solution)/shard_map/ppermute | solution.py:341
  13.7 1.1 %forward_rest_a.1.refs_6_.refs_2_ = bf16[8,96,256]{2,1,0:T(8,128)(2,1)S(1)} custom-call(s32[12,1,16]{2,1,0:T(1,128)S(4)} %get-tuple-element.34.rows_ref, s32[1,16]{1,0:T(1,128)S(4)} %get-tuple-element.35.counts_ref, bf16[32,2048]{1,0:T(8,128)(2,1)S(1)} %collective-permute-done.refs_0_.refs_1_, ...), custom_call_target="tpu_custom_call" | custom-call | flops 603979776 | bytes 6291456 | tf_op jit(solution)/shard_map/forward_rest_a/pallas_call | solution.py:430
  14.9 1.6 %collective-permute-start.5 = (bf16[8,96,256]{2,1,0:T(8,128)(2,1)S(1)}, bf16[8,96,256]{2,1,0:T(8,128)(2,1)S(1)}, u32[]{:S(2)}, u32[]{:S(2)}) collective-permute-start(bf16[8,96,256]{2,1,0:T(8,128)(2,1)S(1)} %forward_rest_a.1.refs_6_.refs_2_), channel_id=1, source_target_pairs={{0,2},{2,0},{1,3},{3,1},{4,6},{6,4},{5,7},{7,5},{8,10},{10,8},{9,1... | collective-permute-start | bytes 1179656 | tf_op jit(solution)/shard_map/ppermute | solution.py:341
  16.4 1.9 %collective-permute-done.4.refs_7_.refs_1_ = bf16[8,32,256]{2,1,0:T(8,128)(2,1)S(1)} collective-permute-done((bf16[8,32,256]{2,1,0:T(8,128)(2,1)S(1)}, bf16[8,32,256]{2,1,0:T(8,128)(2,1)S(1)}, u32[]{:S(2)}, u32[]{:S(2)}) %collective-permute-start.4) | collective-permute-done | bytes 131104 | tf_op jit(solution)/shard_map/ppermute | solution.py:341
  18.4 3.5 %forward_b.1 = (bf16[8,64,256]{2,1,0:T(8,128)(2,1)S(1)}, bf16[8,32,256]{2,1,0:T(8,128)(2,1)S(1)}, bf16[8,32,256]{2,1,0:T(8,128)(2,1)S(1)}, bf16[8,1,12,128,128]{...) custom-call(s32[12,1,16]{2,1,0:T(1,128)S(4)} %get-tuple-element.34.rows_ref, ...), custom_call_target="tpu_custom_call" | custom-call | flops 4026531840 | bytes 31457280 | tf_op jit(solution)/shard_map/forward_b/pallas_call | solution.py:445
  21.8 0.8 %collective-permute-start.8 = (bf16[8,64,256]{2,1,0:T(8,128)(2,1)S(1)}, bf16[8,64,256]{2,1,0:T(8,128)(2,1)S(1)}, u32[]{:S(2)}, u32[]{:S(2)}) collective-permute-start(bf16[8,64,256]{2,1,0:T(8,128)(2,1)S(1)} %get-tuple-element.41._.refs_6_.refs_0_), channel_id=1, source_target_pairs={{0,2},{2,0},{1,3},{3,1},{4,6},{6,4},{5,7},{7,5},{8,10},{10,8},{9,1... | collective-permute-start | bytes 786440 | tf_op jit(solution)/shard_map/ppermute | solution.py:341
  22.6 1.3 %collective-permute-start.7 = (bf16[8,32,256]{2,1,0:T(8,128)(2,1)S(1)}, bf16[8,32,256]{2,1,0:T(8,128)(2,1)S(1)}, u32[]{:S(2)}, u32[]{:S(2)}) collective-permute-start(bf16[8,32,256]{2,1,0:T(8,128)(2,1)S(1)} %get-tuple-element.43.refs_7_.refs_0_), channel_id=1, source_target_pairs={{0,2},{2,0},{1,3},{3,1},{4,6},{6,4},{5,7},{7,5},{8,10},{10,8},{9,1... | collective-permute-start | bytes 393224 | tf_op jit(solution)/shard_map/ppermute | solution.py:341
  23.9 1.8 %turn_b.1.refs_8_.turned_w = bf16[8,256,1536]{2,1,0:T(8,128)(2,1)S(1)} custom-call(bf16[8,1,12,128,128]{4,3,2,1,0:T(8,128)(2,1)S(1)} %get-tuple-element.39.gate_ref, bf16[8,1,12,128,128]{4,3,2,1,0:T(8,128)(2,1)S(1)} %get-tuple-element.40.up_ref, bf16[8,64,256]{2,1,0:T(8,128)(2,1)S(1)} %get-tuple-element.41._.refs_6_.refs_0_), custom_call_target="tpu_custom_call" | custom-call | tf_op jit(solution)/shard_map/turn_b/pallas_call | solution.py:462
  25.7 1.2 %collective-permute-done.5.refs_3_ = bf16[8,96,256]{2,1,0:T(8,128)(2,1)S(1)} collective-permute-done((bf16[8,96,256]{2,1,0:T(8,128)(2,1)S(1)}, bf16[8,96,256]{2,1,0:T(8,128)(2,1)S(1)}, u32[]{:S(2)}, u32[]{:S(2)}) %collective-permute-start.5) | collective-permute-done | bytes 393248 | tf_op jit(solution)/shard_map/ppermute | solution.py:341
  27.0 5.2 %first_half.1 = (bf16[16,1,12,128,128]{4,3,2,1,0:T(8,128)(2,1)}, bf16[16,1,12,128,128]{4,3,2,1,0:T(8,128)(2,1)}, bf16[128,1024]{1,0:T(8,128)(2,1)S(1)}, f32[16,3...) custom-call(s32[12,1,16]{2,1,0:T(1,128)S(4)} %get-tuple-element.34.rows_ref, ...), custom_call_target="tpu_custom_call" | custom-call | flops 1610612736 | bytes 6291456 | tf_op jit(solution)/shard_map/first_half/pallas_call | solution.py:474
  32.2 0.4 collective-permute-done.8.refs_1_
  32.6 1.3 %far_b.1 = (bf16[8,64,256]{2,1,0:T(8,128)(2,1)S(1)}, bf16[64,1024]{1,0:T(8,128)(2,1)S(1)}, bf16[32,2048]{1,0:T(8,128)(2,1)S(1)}, bf16[32,2048]{1,0:T(8,128)(2,1)S(1)}) custom-call(s32[12,1,16]{2,1,0:T(1,128)S(4)} %get-tuple-element.34.rows_ref, s32[1,16]{1,0:T(1,128)S(4)} %get-tuple-element.35.counts_ref, bf16[8,256,1536]{2,1,0:T(8,128)(2,1)S(1)} %turn_b.1.refs_8_.turned_w, ...), custom_call_target="tpu_custom_call" | custom-call | flops 402653184 | bytes 6291456 | tf_op jit(solution)/shard_map/far_b/pallas_call | solution.py:499
  34.0 0.1 collective-permute-start.9
  34.0 1.5 %collective-permute-start.6 = (bf16[8,32,256]{2,1,0:T(8,128)(2,1)S(1)}, bf16[8,32,256]{2,1,0:T(8,128)(2,1)S(1)}, u32[]{:S(2)}, u32[]{:S(2)}) collective-permute-start(bf16[8,32,256]{2,1,0:T(8,128)(2,1)S(1)} %get-tuple-element.45.refs_0_), channel_id=1, source_target_pairs={{0,2},{2,0},{1,3},{3,1},{4,6},{6,4},{5,7},{7,5},{8,10},{10,8},{9,1... | collective-permute-start | bytes 393224 | tf_op jit(solution)/shard_map/ppermute | solution.py:341
  35.6 0.3 collective-permute-start.11
  35.9 1.2 %next_b.1 = (bf16[8,32,256]{2,1,0:T(8,128)(2,1)S(1)}, bf16[32,1024]{1,0:T(8,128)(2,1)S(1)}, bf16[32,2048]{1,0:T(8,128)(2,1)S(1)}) custom-call(s32[12,1,16]{2,1,0:T(1,128)S(4)} %get-tuple-element.34.rows_ref, s32[1,16]{1,0:T(1,128)S(4)} %get-tuple-element.35.counts_ref, bf16[8,256,1536]{2,1,0:T(8,128)(2,1)S(1)} %turn_b.1.refs_8_.turned_w, ...), custom_call_target="tpu_custom_call" | custom-call | flops 201326592 | bytes 6291456 | tf_op jit(solution)/shard_map/next_b/pallas_call | solution.py:499
  37.1 2.8 %collective-permute-start.10 = (bf16[32,2048]{1,0:T(8,128)(2,1)S(1)}, bf16[32,2048]{1,0:T(8,128)(2,1)S(1)}, u32[]{:S(2)}, u32[]{:S(2)}) collective-permute-start(bf16[32,2048]{1,0:T(8,128)(2,1)S(1)} %get-tuple-element.61), channel_id=1, source_target_pairs={{0,4},{4,0},{8,12},{12,8},{1,5},{5,1},{9,13},{13,9},{2,6},{6,2},{1... | collective-permute-start | bytes 393224 | tf_op jit(solution)/shard_map/ppermute | solution.py:341
  39.9 0.1 collective-permute-done.6.refs_1_
  40.0 4.2 %last_half.1 = (bf16[16,1,12,128,128]{4,3,2,1,0:T(8,128)(2,1)}, bf16[16,1,12,128,128]{4,3,2,1,0:T(8,128)(2,1)}, bf16[64,2048]{1,0:T(8,128)(2,1)}, bf16[32,2048]{1,0:T(8,128)(2,1)S(1)}) custom-call(s32[12,1,16]{2,1,0:T(1,128)S(4)} %get-tuple-element.34.rows_ref, ...), custom_call_target="tpu_custom_call", output_to_operand_aliasing={{0}: (14, {}), {1}: (15, {})} | custom-call | flops 8053063680 | bytes 62914560 | tf_op jit(solution)/shard_map/last_half/pallas_call | solution.py:531
  44.1 2.0 %collective-permute-done.10.refs_1_ = bf16[32,2048]{1,0:T(8,128)(2,1)S(1)} collective-permute-done((bf16[32,2048]{1,0:T(8,128)(2,1)S(1)}, bf16[32,2048]{1,0:T(8,128)(2,1)S(1)}, u32[]{:S(2)}, u32[]{:S(2)}) %collective-permute-start.10) | collective-permute-done | bytes 131104 | tf_op jit(solution)/shard_map/ppermute | solution.py:341
  46.2 0.0 collective-permute-done.11.refs_2_
  46.2 0.1 sum_shards.1
  46.2 0.2 collective-permute-start.12
  46.4 1.2 %collective-permute-done.12 = bf16[32,2048]{1,0:T(8,128)(2,1)S(1)} collective-permute-done((bf16[32,2048]{1,0:T(8,128)(2,1)S(1)}, bf16[32,2048]{1,0:T(8,128)(2,1)S(1)}, u32[]{:S(2)}, u32[]{:S(2)}) %collective-permute-start.12) | collective-permute-done | bytes 131104 | tf_op jit(solution)/shard_map/ppermute | solution.py:341
  47.6 0.7 %add_convert_fusion = bf16[32,2048]{1,0:T(8,128)(2,1)} fusion(f32[32,2048]{1,0:T(8,128)S(1)} %get-tuple-element.62, bf16[32,2048]{1,0:T(8,128)(2,1)S(1)} %collective-permute-done.12), kind=kLoop, calls=%fused_computation | loop fusion | flops 196608 | bytes 524288 | tf_op jit(solution)/shard_map/convert_element_type | solution.py:574
  (10 shorter events, 0.1 us)
Async XLA Ops:
  0.6 11.3 %collective-permute-start.1 = (bf16[32,2048]{1,0:T(8,128)(2,1)}, bf16[32,2048]{1,0:T(8,128)(2,1)S(1)}, u32[]{:S(2)}, u32[]{:S(2)}) collective-permute-start(bf16[32,2048]{1,0:T(8,128)(2,1)} %refs_0_.1), channel_id=1, source_target_pairs={{0,8},{1,13},{4,12},{5,9},{8,0},{9,5},{12,4},{13,1},{2,10},{3,15},... | collective-permute-start | bytes 393224 | tf_op jit(solution)/shard_map/ppermute | solution.py:347
  4.7 9.0 %collective-permute-start.3 = (bf16[64,2048]{1,0:T(8,128)(2,1)}, bf16[64,2048]{1,0:T(8,128)(2,1)S(1)}, u32[]{:S(2)}, u32[]{:S(2)}) collective-permute-start(bf16[64,2048]{1,0:T(8,128)(2,1)} %refs_2_.5), channel_id=1, source_target_pairs={{0,2},{2,0},{1,3},{3,1},{4,6},{6,4},{5,7},{7,5},{8,10},{10,8},{9,1... | collective-permute-start | bytes 786440 | tf_op jit(solution)/shard_map/ppermute | solution.py:341
  6.2 6.9 %collective-permute-start = (bf16[32,2048]{1,0:T(8,128)(2,1)}, bf16[32,2048]{1,0:T(8,128)(2,1)S(1)}, u32[]{:S(2)}, u32[]{:S(2)}) collective-permute-start(bf16[32,2048]{1,0:T(8,128)(2,1)} %refs_0_.1), channel_id=1, source_target_pairs={{0,4},{4,0},{8,12},{12,8},{1,5},{5,1},{9,13},{13,9},{2,6},{6,2},{1... | collective-permute-start | bytes 393224 | tf_op jit(solution)/shard_map/ppermute | solution.py:341
  11.9 6.5 %copy-start.1 = (bf16[32,2048]{1,0:T(8,128)(2,1)S(1)}, bf16[32,2048]{1,0:T(8,128)(2,1)}, u32[]{:S(2)}) copy-start(bf16[32,2048]{1,0:T(8,128)(2,1)} %refs_0_.1) | copy-start | bytes 393220
  11.9 1.8 %collective-permute-start.2 = (bf16[32,2048]{1,0:T(8,128)(2,1)S(1)}, bf16[32,2048]{1,0:T(8,128)(2,1)S(1)}, u32[]{:S(2)}, u32[]{:S(2)}) collective-permute-start(bf16[32,2048]{1,0:T(8,128)(2,1)S(1)} %after_own.1), channel_id=1, source_target_pairs={{0,1},{1,0},{2,3},{3,2},{4,5},{5,4},{6,7},{7,6},{8,9},{9,8},{10,11... | collective-permute-start | bytes 393224 | tf_op jit(solution)/shard_map/ppermute | solution.py:341
  12.0 6.4 %collective-permute-start.4 = (bf16[8,32,256]{2,1,0:T(8,128)(2,1)S(1)}, bf16[8,32,256]{2,1,0:T(8,128)(2,1)S(1)}, u32[]{:S(2)}, u32[]{:S(2)}) collective-permute-start(bf16[8,32,256]{2,1,0:T(8,128)(2,1)S(1)} %get-tuple-element.36._.refs_0_), channel_id=1, source_target_pairs={{0,2},{2,0},{1,3},{3,1},{4,6},{6,4},{5,7},{7,5},{8,10},{10,8},{9,1... | collective-permute-start | bytes 393224 | tf_op jit(solution)/shard_map/ppermute | solution.py:341
  14.9 12.1 %collective-permute-start.5 = (bf16[8,96,256]{2,1,0:T(8,128)(2,1)S(1)}, bf16[8,96,256]{2,1,0:T(8,128)(2,1)S(1)}, u32[]{:S(2)}, u32[]{:S(2)}) collective-permute-start(bf16[8,96,256]{2,1,0:T(8,128)(2,1)S(1)} %forward_rest_a.1.refs_6_.refs_2_), channel_id=1, source_target_pairs={{0,2},{2,0},{1,3},{3,1},{4,6},{6,4},{5,7},{7,5},{8,10},{10,8},{9,1... | collective-permute-start | bytes 1179656 | tf_op jit(solution)/shard_map/ppermute | solution.py:341
  21.8 10.8 %collective-permute-start.8 = (bf16[8,64,256]{2,1,0:T(8,128)(2,1)S(1)}, bf16[8,64,256]{2,1,0:T(8,128)(2,1)S(1)}, u32[]{:S(2)}, u32[]{:S(2)}) collective-permute-start(bf16[8,64,256]{2,1,0:T(8,128)(2,1)S(1)} %get-tuple-element.41._.refs_6_.refs_0_), channel_id=1, source_target_pairs={{0,2},{2,0},{1,3},{3,1},{4,6},{6,4},{5,7},{7,5},{8,10},{10,8},{9,1... | collective-permute-start | bytes 786440 | tf_op jit(solution)/shard_map/ppermute | solution.py:341
  22.6 12.9 %collective-permute-start.7 = (bf16[8,32,256]{2,1,0:T(8,128)(2,1)S(1)}, bf16[8,32,256]{2,1,0:T(8,128)(2,1)S(1)}, u32[]{:S(2)}, u32[]{:S(2)}) collective-permute-start(bf16[8,32,256]{2,1,0:T(8,128)(2,1)S(1)} %get-tuple-element.43.refs_7_.refs_0_), channel_id=1, source_target_pairs={{0,2},{2,0},{1,3},{3,1},{4,6},{6,4},{5,7},{7,5},{8,10},{10,8},{9,1... | collective-permute-start | bytes 393224 | tf_op jit(solution)/shard_map/ppermute | solution.py:341
  23.9 3.1 %copy-start = (bf16[64,2048]{1,0:T(8,128)(2,1)S(1)}, bf16[64,2048]{1,0:T(8,128)(2,1)}, u32[]{:S(2)}) copy-start(bf16[64,2048]{1,0:T(8,128)(2,1)} %refs_2_.5) | copy-start | bytes 786436
  34.0 1.6 %collective-permute-start.9 = (bf16[32,2048]{1,0:T(8,128)(2,1)S(1)}, bf16[32,2048]{1,0:T(8,128)(2,1)S(1)}, u32[]{:S(2)}, u32[]{:S(2)}) collective-permute-start(bf16[32,2048]{1,0:T(8,128)(2,1)S(1)} %get-tuple-element.49), channel_id=1, source_target_pairs={{0,1},{1,0},{2,3},{3,2},{4,5},{5,4},{6,7},{7,6},{8,9},{9,8},{10,11... | collective-permute-start | bytes 393224 | tf_op jit(solution)/shard_map/ppermute | solution.py:341
  34.0 5.9 %collective-permute-start.6 = (bf16[8,32,256]{2,1,0:T(8,128)(2,1)S(1)}, bf16[8,32,256]{2,1,0:T(8,128)(2,1)S(1)}, u32[]{:S(2)}, u32[]{:S(2)}) collective-permute-start(bf16[8,32,256]{2,1,0:T(8,128)(2,1)S(1)} %get-tuple-element.45.refs_0_), channel_id=1, source_target_pairs={{0,2},{2,0},{1,3},{3,1},{4,6},{6,4},{5,7},{7,5},{8,10},{10,8},{9,1... | collective-permute-start | bytes 393224 | tf_op jit(solution)/shard_map/ppermute | solution.py:341
  35.6 10.6 %collective-permute-start.11 = (bf16[32,2048]{1,0:T(8,128)(2,1)S(1)}, bf16[32,2048]{1,0:T(8,128)(2,1)S(1)}, u32[]{:S(2)}, u32[]{:S(2)}) collective-permute-start(bf16[32,2048]{1,0:T(8,128)(2,1)S(1)} %add_cores.1.refs_4_.refs_11_), channel_id=1, source_target_pairs={{0,8},{1,13},{4,12},{5,9},{8,0},{9,5},{12,4},{13,1},{2,10},{3,15},... | collective-permute-start | bytes 393224 | tf_op jit(solution)/shard_map/ppermute | solution.py:347
  37.1 9.1 %collective-permute-start.10 = (bf16[32,2048]{1,0:T(8,128)(2,1)S(1)}, bf16[32,2048]{1,0:T(8,128)(2,1)S(1)}, u32[]{:S(2)}, u32[]{:S(2)}) collective-permute-start(bf16[32,2048]{1,0:T(8,128)(2,1)S(1)} %get-tuple-element.61), channel_id=1, source_target_pairs={{0,4},{4,0},{8,12},{12,8},{1,5},{5,1},{9,13},{13,9},{2,6},{6,2},{1... | collective-permute-start | bytes 393224 | tf_op jit(solution)/shard_map/ppermute | solution.py:341
  46.2 1.4 %collective-permute-start.12 = (bf16[32,2048]{1,0:T(8,128)(2,1)S(1)}, bf16[32,2048]{1,0:T(8,128)(2,1)S(1)}, u32[]{:S(2)}, u32[]{:S(2)}) collective-permute-start(bf16[32,2048]{1,0:T(8,128)(2,1)S(1)} %get-tuple-element.63), channel_id=1, source_target_pairs={{0,1},{1,0},{2,3},{3,2},{4,5},{5,4},{6,7},{7,6},{8,9},{9,8},{10,11... | collective-permute-start | bytes 393224 | tf_op jit(solution)/shard_map/ppermute | solution.py:341

commit v10 on v9

--- a/solution.py
+++ b/solution.py
@@ -287,6 +287,10 @@
         block = acc_ref[r].astype(BF16)
         for m, dx in enumerate(dxs):
             dx[:, r * tile : (r + 1) * tile] = block[m * shard_rows : (m + 1) * shard_rows]
+    width = acc_ref.shape[0] * tile
+    for dx in dxs:
+        if dx.shape[1] > width:
+            dx[:, width:] = jnp.zeros_like(dx[:, width:])
 
 
 def last_half_kernel(members, owners, first, rows_ref, counts_ref, turned_w, turned_ref, acc_in, *refs):
@@ -328,7 +332,8 @@
 
 
 def add_kernel(left_ref, right_ref, _, out_ref):
-    out_ref[...] = (left_ref[...].astype(F32) + right_ref[...].astype(F32)).astype(BF16)
+    right = right_ref[:, : left_ref.shape[1]]
+    out_ref[...] = (left_ref[...].astype(F32) + right.astype(F32)).astype(BF16)
 
 
 def sum_kernel(count, *refs):
@@ -354,7 +359,7 @@
     row_blocks = width // tile
     row_total = shards * shard_rows
     near_rows = 2 * shard_rows
-    half = max(1, cols // 2)
+    half = max(1, cols * 6 // 16)
     bases = range(2, shards, 2)
     lists = (jnp.transpose(block_rows, (2, 1, 0)), jnp.transpose(block_counts, (1, 0)))
 
@@ -501,7 +506,7 @@
             out_shape=(
                 shape(rest, rows_here, 2 * tile),
                 shape(rows_here, rest * tile),
-                *[shape(shard_rows, width) for _ in chunk],
+                *[shape(shard_rows, max(width, 2 * rest * tile) if m >= 2 and m % 2 else width) for m in chunk],
             ),
             in_specs=[SMEM_SPEC] * 2 + [VMEM_SPEC] * (2 + 2 * owners) + [ANY_SPEC],
             out_specs=(VMEM_SPEC,) * (2 + len(chunk)),

time: 48.5 us -> 48.1 us (level)
  waiting for transfers between devices: 7.46 us -> 5.35 us
  starting transfers between devices: 16.9 us -> 18 us
  Pallas kernels: 22.5 us -> 23.2 us
    ppermute x11, waiting for transfers between devices: 7.46 us -> 5.19 us  [swap(): lax.ppermute(x, axis, [(i, i ^ step) for i in range(lax.axis_size(axis))])]
    pallas_call x1, Pallas kernels: 5.21 us -> 4.17 us  [on_device(): pl.pallas_call(functools.partial(first_half_kernel, members, owners), out...]
    pallas_call x1, Pallas kernels: 4.18 us -> 5.16 us  [on_device(): pl.pallas_call(functools.partial(last_half_kernel, members, owners, half)...]
    ppermute x2, starting transfers between devices: 4.36 us -> 4.99 us  [swap_far(): return lax.ppermute(x, ('tok', 'sub'), pairs)]
    pallas_call x1, Pallas kernels: 3.46 us -> 4.02 us  [on_device(): pl.pallas_call(functools.partial(load_forward_kernel, shards, groups, hal...]
    pallas_call x2, Pallas kernels: 2.56 us -> 3.12 us  [second_half(): pl.pallas_call(functools.partial(second_half_kernel, chunk, owners, half,...]
    pallas_call x1, Pallas kernels: 4.07 us -> 3.55 us  [on_device(): pl.pallas_call(forward_own_kernel, out_shape=(shape(half, shard_rows, 2 *...]
  transfers between devices with their start and end apart: 13 -> 13, of which waited for: 7 -> 6; matrix products, arithmetic and copies ran while one was open for 0% -> 0% of each run, Pallas kernels for 47% -> 48%
where the time goes in v10:
time: 48.1 us; the launch traced here: 48 us
  Pallas kernels  23.2 us (48%)
  starting transfers between devices  18 us (37%)
  waiting for transfers between devices  5.35 us (11%)
  between operations  0.75 us (2%)
  other arithmetic  0.68 us (1%)
    ppermute x11, starting transfers between devices, swap(): lax.ppermute(x, axis, [(i, i ^ step) for i in range(lax.axis_size(axis))])  13 us
    ppermute x11, waiting for transfers between devices, swap(): lax.ppermute(x, axis, [(i, i ^ step) for i in range(lax.axis_size(axis))])  5.19 us
    pallas_call x1, Pallas kernels, on_device(): pl.pallas_call(functools.partial(last_half_kernel, members, owners, half)...  5.16 us
    ppermute x2, starting transfers between devices, swap_far(): return lax.ppermute(x, ('tok', 'sub'), pairs)  4.99 us
    pallas_call x1, Pallas kernels, on_device(): pl.pallas_call(functools.partial(first_half_kernel, members, owners), out...  4.17 us
    pallas_call x1, Pallas kernels, on_device(): pl.pallas_call(functools.partial(load_forward_kernel, shards, groups, hal...  4.02 us
    pallas_call x1, Pallas kernels, on_device(): pl.pallas_call(forward_own_kernel, out_shape=(shape(half, shard_rows, 2 *...  3.55 us
    pallas_call x2, Pallas kernels, second_half(): pl.pallas_call(functools.partial(second_half_kernel, chunk, owners, half,...  3.12 us
  transfers between devices with their start and end apart: 13, of which 6 were waited for; matrix products, arithmetic and copies ran while one was open for 0% of the time, Pallas kernels for 48%

profile of v10, /device:TPU:0, one launch (start us, length us, event | category | flops | bytes accessed | tf_op | source)
XLA Modules:
  0.0 48.0 jit_solution(9393669748056667603)
XLA Ops:
  0.6 4.1 %collective-permute-start.1 = (bf16[32,2048]{1,0:T(8,128)(2,1)}, bf16[32,2048]{1,0:T(8,128)(2,1)S(1)}, u32[]{:S(2)}, u32[]{:S(2)}) collective-permute-start(bf16[32,2048]{1,0:T(8,128)(2,1)} %refs_0_.1), channel_id=1, source_target_pairs={{0,8},{1,13},{4,12},{5,9},{8,0},{9,5},{12,4},{13,1},{2,10},{3,15},... | collective-permute-start | bytes 393224 | tf_op jit(solution)/shard_map/ppermute | solution.py:352
  4.7 1.5 %collective-permute-start.3 = (bf16[64,2048]{1,0:T(8,128)(2,1)}, bf16[64,2048]{1,0:T(8,128)(2,1)S(1)}, u32[]{:S(2)}, u32[]{:S(2)}) collective-permute-start(bf16[64,2048]{1,0:T(8,128)(2,1)} %refs_2_.5), channel_id=1, source_target_pairs={{0,2},{2,0},{1,3},{3,1},{4,6},{6,4},{5,7},{7,5},{8,10},{10,8},{9,1... | collective-permute-start | bytes 786440 | tf_op jit(solution)/shard_map/ppermute | solution.py:346
  6.2 1.6 %collective-permute-start = (bf16[32,2048]{1,0:T(8,128)(2,1)}, bf16[32,2048]{1,0:T(8,128)(2,1)S(1)}, u32[]{:S(2)}, u32[]{:S(2)}) collective-permute-start(bf16[32,2048]{1,0:T(8,128)(2,1)} %refs_0_.1), channel_id=1, source_target_pairs={{0,4},{4,0},{8,12},{12,8},{1,5},{5,1},{9,13},{13,9},{2,6},{6,2},{1... | collective-permute-start | bytes 393224 | tf_op jit(solution)/shard_map/ppermute | solution.py:346
  7.8 3.5 %forward_own_a.1 = (bf16[6,32,256]{2,1,0:T(8,128)(2,1)S(1)}, bf16[6,1,12,128,128]{4,3,2,1,0:T(8,128)(2,1)S(1)}, bf16[6,1,12,128,128]{4,3,2,1,0:T(8,128)(2,1)S(1)}, s32[12,1,16]{2,1,0:T(1,128)S(4)}, s32[1,16]{1,0:T(1,128)S(4)}) custom-call(bf16[32,2048]{1,0:T(8,128)(2,1)} %refs_0_.1, s32[12,1,16]{2,1,0:T(1,128)} %bitcast.2, s32[1,16]{1,0:T(1,128)} %bitcast.3, ...), custom_call_target="tpu_custom_call" | custom-call | flops 150994944 | bytes 4718592 | tf_op jit(solution)/shard_map/forward_own_a/pallas_call | solution.py:390
  11.4 0.2 collective-permute-done.1.x_ref.refs_1_.refs_2_
  11.5 0.1 collective-permute-start.2
  11.6 1.6 %collective-permute-start.4 = (bf16[6,32,256]{2,1,0:T(8,128)(2,1)S(1)}, bf16[6,32,256]{2,1,0:T(8,128)(2,1)S(1)}, u32[]{:S(2)}, u32[]{:S(2)}) collective-permute-start(bf16[6,32,256]{2,1,0:T(8,128)(2,1)S(1)} %get-tuple-element.36._.refs_0_), channel_id=1, source_target_pairs={{0,2},{2,0},{1,3},{3,1},{4,6},{6,4},{5,7},{7,5},{8,10},{10,8},{9,1... | collective-permute-start | bytes 294920 | tf_op jit(solution)/shard_map/ppermute | solution.py:346
  13.2 0.6 %collective-permute-done.3.refs_5_.refs_3_ = bf16[64,2048]{1,0:T(8,128)(2,1)S(1)} collective-permute-done((bf16[64,2048]{1,0:T(8,128)(2,1)}, bf16[64,2048]{1,0:T(8,128)(2,1)S(1)}, u32[]{:S(2)}, u32[]{:S(2)}) %collective-permute-start.3) | collective-permute-done | bytes 262176 | tf_op jit(solution)/shard_map/ppermute | solution.py:346
  13.7 0.0 collective-permute-done.2.refs_2_.refs_3_
  13.7 0.9 %forward_rest_a.1.refs_6_.refs_2_ = bf16[6,96,256]{2,1,0:T(8,128)(2,1)S(1)} custom-call(s32[12,1,16]{2,1,0:T(1,128)S(4)} %get-tuple-element.34.rows_ref, s32[1,16]{1,0:T(1,128)S(4)} %get-tuple-element.35.counts_ref, bf16[32,2048]{1,0:T(8,128)(2,1)S(1)} %collective-permute-done.refs_0_.refs_1_, ...), custom_call_target="tpu_custom_call" | custom-call | flops 452984832 | bytes 4718592 | tf_op jit(solution)/shard_map/forward_rest_a/pallas_call | solution.py:435
  14.6 1.6 %collective-permute-start.5 = (bf16[6,96,256]{2,1,0:T(8,128)(2,1)S(1)}, bf16[6,96,256]{2,1,0:T(8,128)(2,1)S(1)}, u32[]{:S(2)}, u32[]{:S(2)}) collective-permute-start(bf16[6,96,256]{2,1,0:T(8,128)(2,1)S(1)} %forward_rest_a.1.refs_6_.refs_2_), channel_id=1, source_target_pairs={{0,2},{2,0},{1,3},{3,1},{4,6},{6,4},{5,7},{7,5},{8,10},{10,8},{9,1... | collective-permute-start | bytes 884744 | tf_op jit(solution)/shard_map/ppermute | solution.py:346
  16.2 0.6 %collective-permute-done.4.refs_7_.refs_1_ = bf16[6,32,256]{2,1,0:T(8,128)(2,1)S(1)} collective-permute-done((bf16[6,32,256]{2,1,0:T(8,128)(2,1)S(1)}, bf16[6,32,256]{2,1,0:T(8,128)(2,1)S(1)}, u32[]{:S(2)}, u32[]{:S(2)}) %collective-permute-start.4) | collective-permute-done | bytes 98336 | tf_op jit(solution)/shard_map/ppermute | solution.py:346
  16.8 4.0 %forward_b.1 = (bf16[10,64,256]{2,1,0:T(8,128)(2,1)S(1)}, bf16[10,32,256]{2,1,0:T(8,128)(2,1)S(1)}, bf16[10,32,256]{2,1,0:T(8,128)(2,1)S(1)}, bf16[10,1,12,128,1...) custom-call(s32[12,1,16]{2,1,0:T(1,128)S(4)} %get-tuple-element.34.rows_ref, ...), custom_call_target="tpu_custom_call" | custom-call | flops 5033164800 | bytes 39321600 | tf_op jit(solution)/shard_map/forward_b/pallas_call | solution.py:450
  20.9 1.6 %collective-permute-start.8 = (bf16[10,64,256]{2,1,0:T(8,128)(2,1)S(1)}, bf16[10,64,256]{2,1,0:T(8,128)(2,1)S(1)}, u32[]{:S(2)}, u32[]{:S(2)}) collective-permute-start(bf16[10,64,256]{2,1,0:T(8,128)(2,1)S(1)} %get-tuple-element.41._.refs_6_.refs_0_), channel_id=1, source_target_pairs={{0,2},{2,0},{1,3},{3,1},{4,6},{6,4},{5,7},{7,5},{8,10},{10,8},{9,1... | collective-permute-start | bytes 983048 | tf_op jit(solution)/shard_map/ppermute | solution.py:346
  22.4 0.5 %collective-permute-start.7 = (bf16[10,32,256]{2,1,0:T(8,128)(2,1)S(1)}, bf16[10,32,256]{2,1,0:T(8,128)(2,1)S(1)}, u32[]{:S(2)}, u32[]{:S(2)}) collective-permute-start(bf16[10,32,256]{2,1,0:T(8,128)(2,1)S(1)} %get-tuple-element.43.refs_7_.refs_0_), channel_id=1, source_target_pairs={{0,2},{2,0},{1,3},{3,1},{4,6},{6,4},{5,7},{7,5},{8,10},{10,8},{9,1... | collective-permute-start | bytes 491528 | tf_op jit(solution)/shard_map/ppermute | solution.py:346
  23.0 2.2 %turn_b.1.refs_8_.turned_w = bf16[10,256,1536]{2,1,0:T(8,128)(2,1)S(1)} custom-call(bf16[10,1,12,128,128]{4,3,2,1,0:T(8,128)(2,1)S(1)} %get-tuple-element.39.gate_ref, bf16[10,1,12,128,128]{4,3,2,1,0:T(8,128)(2,1)S(1)} %get-tuple-element.40.up_ref, bf16[10,64,256]{2,1,0:T(8,128)(2,1)S(1)} %get-tuple-element.41._.refs_6_.refs_0_), custom_call_target="tpu_custom_call" | custom-call | tf_op jit(solution)/shard_map/turn_b/pallas_call | solution.py:467
  25.2 4.2 %first_half.1 = (bf16[16,1,12,128,128]{4,3,2,1,0:T(8,128)(2,1)}, bf16[16,1,12,128,128]{4,3,2,1,0:T(8,128)(2,1)}, bf16[128,768]{1,0:T(8,128)(2,1)S(1)}, f32[16,32...) custom-call(s32[12,1,16]{2,1,0:T(1,128)S(4)} %get-tuple-element.34.rows_ref, ...), custom_call_target="tpu_custom_call" | custom-call | flops 1207959552 | bytes 4718592 | tf_op jit(solution)/shard_map/first_half/pallas_call | solution.py:479
  29.4 2.2 %collective-permute-done.8.refs_1_ = bf16[10,64,256]{2,1,0:T(8,128)(2,1)S(1)} collective-permute-done((bf16[10,64,256]{2,1,0:T(8,128)(2,1)S(1)}, bf16[10,64,256]{2,1,0:T(8,128)(2,1)S(1)}, u32[]{:S(2)}, u32[]{:S(2)}) %collective-permute-start.8) | collective-permute-done | bytes 327712 | tf_op jit(solution)/shard_map/ppermute | solution.py:346
  31.6 1.6 %far_b.1 = (bf16[10,64,256]{2,1,0:T(8,128)(2,1)S(1)}, bf16[64,1280]{1,0:T(8,128)(2,1)S(1)}, bf16[32,2048]{1,0:T(8,128)(2,1)S(1)}, bf16[32,2560]{1,0:T(8,128)(2,1)S(1)}) custom-call(s32[12,1,16]{2,1,0:T(1,128)S(4)} %get-tuple-element.34.rows_ref, s32[1,16]{1,0:T(1,128)S(4)} %get-tuple-element.35.counts_ref, ...), custom_call_target="tpu_custom_call" | custom-call | flops 503316480 | bytes 7864320 | tf_op jit(solution)/shard_map/far_b/pallas_call | solution.py:504
  33.2 0.1 collective-permute-start.9
  33.3 1.6 %collective-permute-start.6 = (bf16[10,32,256]{2,1,0:T(8,128)(2,1)S(1)}, bf16[10,32,256]{2,1,0:T(8,128)(2,1)S(1)}, u32[]{:S(2)}, u32[]{:S(2)}) collective-permute-start(bf16[10,32,256]{2,1,0:T(8,128)(2,1)S(1)} %get-tuple-element.45.refs_0_), channel_id=1, source_target_pairs={{0,2},{2,0},{1,3},{3,1},{4,6},{6,4},{5,7},{7,5},{8,10},{10,8},{9,1... | collective-permute-start | bytes 491528 | tf_op jit(solution)/shard_map/ppermute | solution.py:346
  34.8 0.0 collective-permute-done.7._.refs_1_
  34.9 0.9 %collective-permute-start.11 = (bf16[32,2048]{1,0:T(8,128)(2,1)S(1)}, bf16[32,2048]{1,0:T(8,128)(2,1)S(1)}, u32[]{:S(2)}, u32[]{:S(2)}) collective-permute-start(bf16[32,2048]{1,0:T(8,128)(2,1)S(1)} %add_cores.1.refs_4_.refs_11_), channel_id=1, source_target_pairs={{0,8},{1,13},{4,12},{5,9},{8,0},{9,5},{12,4},{13,1},{2,10},{3,15},... | collective-permute-start | bytes 393224 | tf_op jit(solution)/shard_map/ppermute | solution.py:352
  35.8 1.5 %next_b.1 = (bf16[10,32,256]{2,1,0:T(8,128)(2,1)S(1)}, bf16[32,1280]{1,0:T(8,128)(2,1)S(1)}, bf16[32,2048]{1,0:T(8,128)(2,1)S(1)}) custom-call(s32[12,1,16]{2,1,0:T(1,128)S(4)} %get-tuple-element.34.rows_ref, s32[1,16]{1,0:T(1,128)S(4)} %get-tuple-element.35.counts_ref, bf16[10,256,1536]{2,1,0:T(8,128)(2,1)S(1)} %turn_b.1.refs_8_.turned_w, ...), custom_call_target="tpu_custom_call" | custom-call | flops 251658240 | bytes 7864320 | tf_op jit(solution)/shard_map/next_b/pallas_call | solution.py:504
  37.3 2.8 %collective-permute-start.10 = (bf16[32,2048]{1,0:T(8,128)(2,1)S(1)}, bf16[32,2048]{1,0:T(8,128)(2,1)S(1)}, u32[]{:S(2)}, u32[]{:S(2)}) collective-permute-start(bf16[32,2048]{1,0:T(8,128)(2,1)S(1)} %get-tuple-element.61), channel_id=1, source_target_pairs={{0,4},{4,0},{8,12},{12,8},{1,5},{5,1},{9,13},{13,9},{2,6},{6,2},{1... | collective-permute-start | bytes 393224 | tf_op jit(solution)/shard_map/ppermute | solution.py:346
  40.1 0.0 collective-permute-done.6.refs_1_
  40.1 5.2 %last_half.1 = (bf16[16,1,12,128,128]{4,3,2,1,0:T(8,128)(2,1)}, bf16[16,1,12,128,128]{4,3,2,1,0:T(8,128)(2,1)}, bf16[64,2048]{1,0:T(8,128)(2,1)}, bf16[32,2048]{1,0:T(8,128)(2,1)S(1)}) custom-call(s32[12,1,16]{2,1,0:T(1,128)S(4)} %get-tuple-element.34.rows_ref, ...), custom_call_target="tpu_custom_call", output_to_operand_aliasing={{0}: (14, {}), {1}: (15, {})} | custom-call | flops 10066329600 | bytes 78643200 | tf_op jit(solution)/shard_map/last_half/pallas_call | solution.py:536
  45.3 0.6 %collective-permute-done.10.refs_1_ = bf16[32,2048]{1,0:T(8,128)(2,1)S(1)} collective-permute-done((bf16[32,2048]{1,0:T(8,128)(2,1)S(1)}, bf16[32,2048]{1,0:T(8,128)(2,1)S(1)}, u32[]{:S(2)}, u32[]{:S(2)}) %collective-permute-start.10) | collective-permute-done | bytes 131104 | tf_op jit(solution)/shard_map/ppermute | solution.py:346
  45.8 0.1 sum_shards.1
  45.9 0.2 collective-permute-start.12
  46.1 1.2 %collective-permute-done.12 = bf16[32,2048]{1,0:T(8,128)(2,1)S(1)} collective-permute-done((bf16[32,2048]{1,0:T(8,128)(2,1)S(1)}, bf16[32,2048]{1,0:T(8,128)(2,1)S(1)}, u32[]{:S(2)}, u32[]{:S(2)}) %collective-permute-start.12) | collective-permute-done | bytes 131104 | tf_op jit(solution)/shard_map/ppermute | solution.py:346
  47.3 0.7 %add_convert_fusion = bf16[32,2048]{1,0:T(8,128)(2,1)} fusion(f32[32,2048]{1,0:T(8,128)S(1)} %get-tuple-element.62, bf16[32,2048]{1,0:T(8,128)(2,1)S(1)} %collective-permute-done.12), kind=kLoop, calls=%fused_computation | loop fusion | flops 196608 | bytes 524288 | tf_op jit(solution)/shard_map/convert_element_type | solution.py:579
  (10 shorter events, 0.1 us)
Async XLA Ops:
  0.6 10.9 %collective-permute-start.1 = (bf16[32,2048]{1,0:T(8,128)(2,1)}, bf16[32,2048]{1,0:T(8,128)(2,1)S(1)}, u32[]{:S(2)}, u32[]{:S(2)}) collective-permute-start(bf16[32,2048]{1,0:T(8,128)(2,1)} %refs_0_.1), channel_id=1, source_target_pairs={{0,8},{1,13},{4,12},{5,9},{8,0},{9,5},{12,4},{13,1},{2,10},{3,15},... | collective-permute-start | bytes 393224 | tf_op jit(solution)/shard_map/ppermute | solution.py:352
  4.7 9.0 %collective-permute-start.3 = (bf16[64,2048]{1,0:T(8,128)(2,1)}, bf16[64,2048]{1,0:T(8,128)(2,1)S(1)}, u32[]{:S(2)}, u32[]{:S(2)}) collective-permute-start(bf16[64,2048]{1,0:T(8,128)(2,1)} %refs_2_.5), channel_id=1, source_target_pairs={{0,2},{2,0},{1,3},{3,1},{4,6},{6,4},{5,7},{7,5},{8,10},{10,8},{9,1... | collective-permute-start | bytes 786440 | tf_op jit(solution)/shard_map/ppermute | solution.py:346
  6.2 6.9 %collective-permute-start = (bf16[32,2048]{1,0:T(8,128)(2,1)}, bf16[32,2048]{1,0:T(8,128)(2,1)S(1)}, u32[]{:S(2)}, u32[]{:S(2)}) collective-permute-start(bf16[32,2048]{1,0:T(8,128)(2,1)} %refs_0_.1), channel_id=1, source_target_pairs={{0,4},{4,0},{8,12},{12,8},{1,5},{5,1},{9,13},{13,9},{2,6},{6,2},{1... | collective-permute-start | bytes 393224 | tf_op jit(solution)/shard_map/ppermute | solution.py:346
  7.8 9.0 %copy-start.1 = (bf16[32,2048]{1,0:T(8,128)(2,1)S(1)}, bf16[32,2048]{1,0:T(8,128)(2,1)}, u32[]{:S(2)}) copy-start(bf16[32,2048]{1,0:T(8,128)(2,1)} %refs_0_.1) | copy-start | bytes 393220
  11.5 2.2 %collective-permute-start.2 = (bf16[32,2048]{1,0:T(8,128)(2,1)S(1)}, bf16[32,2048]{1,0:T(8,128)(2,1)S(1)}, u32[]{:S(2)}, u32[]{:S(2)}) collective-permute-start(bf16[32,2048]{1,0:T(8,128)(2,1)S(1)} %after_own.1), channel_id=1, source_target_pairs={{0,1},{1,0},{2,3},{3,2},{4,5},{5,4},{6,7},{7,6},{8,9},{9,8},{10,11... | collective-permute-start | bytes 393224 | tf_op jit(solution)/shard_map/ppermute | solution.py:346
  11.6 5.2 %collective-permute-start.4 = (bf16[6,32,256]{2,1,0:T(8,128)(2,1)S(1)}, bf16[6,32,256]{2,1,0:T(8,128)(2,1)S(1)}, u32[]{:S(2)}, u32[]{:S(2)}) collective-permute-start(bf16[6,32,256]{2,1,0:T(8,128)(2,1)S(1)} %get-tuple-element.36._.refs_0_), channel_id=1, source_target_pairs={{0,2},{2,0},{1,3},{3,1},{4,6},{6,4},{5,7},{7,5},{8,10},{10,8},{9,1... | collective-permute-start | bytes 294920 | tf_op jit(solution)/shard_map/ppermute | solution.py:346
  14.6 10.5 %collective-permute-start.5 = (bf16[6,96,256]{2,1,0:T(8,128)(2,1)S(1)}, bf16[6,96,256]{2,1,0:T(8,128)(2,1)S(1)}, u32[]{:S(2)}, u32[]{:S(2)}) collective-permute-start(bf16[6,96,256]{2,1,0:T(8,128)(2,1)S(1)} %forward_rest_a.1.refs_6_.refs_2_), channel_id=1, source_target_pairs={{0,2},{2,0},{1,3},{3,1},{4,6},{6,4},{5,7},{7,5},{8,10},{10,8},{9,1... | collective-permute-start | bytes 884744 | tf_op jit(solution)/shard_map/ppermute | solution.py:346
  20.9 10.7 %collective-permute-start.8 = (bf16[10,64,256]{2,1,0:T(8,128)(2,1)S(1)}, bf16[10,64,256]{2,1,0:T(8,128)(2,1)S(1)}, u32[]{:S(2)}, u32[]{:S(2)}) collective-permute-start(bf16[10,64,256]{2,1,0:T(8,128)(2,1)S(1)} %get-tuple-element.41._.refs_6_.refs_0_), channel_id=1, source_target_pairs={{0,2},{2,0},{1,3},{3,1},{4,6},{6,4},{5,7},{7,5},{8,10},{10,8},{9,1... | collective-permute-start | bytes 983048 | tf_op jit(solution)/shard_map/ppermute | solution.py:346
  22.4 12.4 %collective-permute-start.7 = (bf16[10,32,256]{2,1,0:T(8,128)(2,1)S(1)}, bf16[10,32,256]{2,1,0:T(8,128)(2,1)S(1)}, u32[]{:S(2)}, u32[]{:S(2)}) collective-permute-start(bf16[10,32,256]{2,1,0:T(8,128)(2,1)S(1)} %get-tuple-element.43.refs_7_.refs_0_), channel_id=1, source_target_pairs={{0,2},{2,0},{1,3},{3,1},{4,6},{6,4},{5,7},{7,5},{8,10},{10,8},{9,1... | collective-permute-start | bytes 491528 | tf_op jit(solution)/shard_map/ppermute | solution.py:346
  23.0 2.2 %copy-start = (bf16[64,2048]{1,0:T(8,128)(2,1)S(1)}, bf16[64,2048]{1,0:T(8,128)(2,1)}, u32[]{:S(2)}) copy-start(bf16[64,2048]{1,0:T(8,128)(2,1)} %refs_2_.5) | copy-start | bytes 786436
  33.2 1.6 %collective-permute-start.9 = (bf16[32,2560]{1,0:T(8,128)(2,1)S(1)}, bf16[32,2560]{1,0:T(8,128)(2,1)S(1)}, u32[]{:S(2)}, u32[]{:S(2)}) collective-permute-start(bf16[32,2560]{1,0:T(8,128)(2,1)S(1)} %get-tuple-element.49), channel_id=1, source_target_pairs={{0,1},{1,0},{2,3},{3,2},{4,5},{5,4},{6,7},{7,6},{8,9},{9,8},{10,11... | collective-permute-start | bytes 491528 | tf_op jit(solution)/shard_map/ppermute | solution.py:346
  33.3 6.8 %collective-permute-start.6 = (bf16[10,32,256]{2,1,0:T(8,128)(2,1)S(1)}, bf16[10,32,256]{2,1,0:T(8,128)(2,1)S(1)}, u32[]{:S(2)}, u32[]{:S(2)}) collective-permute-start(bf16[10,32,256]{2,1,0:T(8,128)(2,1)S(1)} %get-tuple-element.45.refs_0_), channel_id=1, source_target_pairs={{0,2},{2,0},{1,3},{3,1},{4,6},{6,4},{5,7},{7,5},{8,10},{10,8},{9,1... | collective-permute-start | bytes 491528 | tf_op jit(solution)/shard_map/ppermute | solution.py:346
  34.9 11.0 %collective-permute-start.11 = (bf16[32,2048]{1,0:T(8,128)(2,1)S(1)}, bf16[32,2048]{1,0:T(8,128)(2,1)S(1)}, u32[]{:S(2)}, u32[]{:S(2)}) collective-permute-start(bf16[32,2048]{1,0:T(8,128)(2,1)S(1)} %add_cores.1.refs_4_.refs_11_), channel_id=1, source_target_pairs={{0,8},{1,13},{4,12},{5,9},{8,0},{9,5},{12,4},{13,1},{2,10},{3,15},... | collective-permute-start | bytes 393224 | tf_op jit(solution)/shard_map/ppermute | solution.py:352
  37.3 8.6 %collective-permute-start.10 = (bf16[32,2048]{1,0:T(8,128)(2,1)S(1)}, bf16[32,2048]{1,0:T(8,128)(2,1)S(1)}, u32[]{:S(2)}, u32[]{:S(2)}) collective-permute-start(bf16[32,2048]{1,0:T(8,128)(2,1)S(1)} %get-tuple-element.61), channel_id=1, source_target_pairs={{0,4},{4,0},{8,12},{12,8},{1,5},{5,1},{9,13},{13,9},{2,6},{6,2},{1... | collective-permute-start | bytes 393224 | tf_op jit(solution)/shard_map/ppermute | solution.py:346
  45.9 1.4 %collective-permute-start.12 = (bf16[32,2048]{1,0:T(8,128)(2,1)S(1)}, bf16[32,2048]{1,0:T(8,128)(2,1)S(1)}, u32[]{:S(2)}, u32[]{:S(2)}) collective-permute-start(bf16[32,2048]{1,0:T(8,128)(2,1)S(1)} %get-tuple-element.63), channel_id=1, source_target_pairs={{0,1},{1,0},{2,3},{3,2},{4,5},{5,4},{6,7},{7,6},{8,9},{9,8},{10,11... | collective-permute-start | bytes 393224 | tf_op jit(solution)/shard_map/ppermute | solution.py:346

commit v11 on v10

--- a/solution.py
+++ b/solution.py
@@ -359,7 +359,7 @@
     row_blocks = width // tile
     row_total = shards * shard_rows
     near_rows = 2 * shard_rows
-    half = max(1, cols * 6 // 16)
+    half = max(1, cols * 7 // 16)
     bases = range(2, shards, 2)
     lists = (jnp.transpose(block_rows, (2, 1, 0)), jnp.transpose(block_counts, (1, 0)))
 

time: 48.1 us -> 48.1 us (level)
  waiting for transfers between devices: 5.35 us -> 6.81 us
  starting transfers between devices: 18 us -> 16.9 us
    ppermute x11, waiting for transfers between devices: 5.19 us -> 6.8 us  [swap(): lax.ppermute(x, axis, [(i, i ^ step) for i in range(lax.axis_size(axis))])]
    ppermute x2, starting transfers between devices: 4.99 us -> 4.17 us  [swap_far(): return lax.ppermute(x, ('tok', 'sub'), pairs)]
    pallas_call x1, Pallas kernels: 5.16 us -> 4.63 us  [on_device(): pl.pallas_call(functools.partial(last_half_kernel, members, owners, half)...]
    pallas_call x1, Pallas kernels: 4.17 us -> 4.66 us  [on_device(): pl.pallas_call(functools.partial(first_half_kernel, members, owners), out...]
  transfers between devices with their start and end apart: 13 -> 13, of which waited for: 6 -> 7; matrix products, arithmetic and copies ran while one was open for 0% -> 0% of each run, Pallas kernels for 48% -> 48%
where the time goes in v11:
time: 48.1 us; the launch traced here: 47.9 us
  Pallas kernels  22.8 us (47%)
  starting transfers between devices  16.9 us (35%)
  waiting for transfers between devices  6.81 us (14%)
  between operations  0.76 us (2%)
  other arithmetic  0.68 us (1%)
    ppermute x11, starting transfers between devices, swap(): lax.ppermute(x, axis, [(i, i ^ step) for i in range(lax.axis_size(axis))])  12.7 us
    ppermute x11, waiting for transfers between devices, swap(): lax.ppermute(x, axis, [(i, i ^ step) for i in range(lax.axis_size(axis))])  6.8 us
    pallas_call x1, Pallas kernels, on_device(): pl.pallas_call(functools.partial(first_half_kernel, members, owners), out...  4.66 us
    pallas_call x1, Pallas kernels, on_device(): pl.pallas_call(functools.partial(last_half_kernel, members, owners, half)...  4.63 us
    ppermute x2, starting transfers between devices, swap_far(): return lax.ppermute(x, ('tok', 'sub'), pairs)  4.17 us
    pallas_call x1, Pallas kernels, on_device(): pl.pallas_call(forward_own_kernel, out_shape=(shape(half, shard_rows, 2 *...  3.87 us
    pallas_call x1, Pallas kernels, on_device(): pl.pallas_call(functools.partial(load_forward_kernel, shards, groups, hal...  3.7 us
    pallas_call x2, Pallas kernels, second_half(): pl.pallas_call(functools.partial(second_half_kernel, chunk, owners, half,...  2.85 us
  transfers between devices with their start and end apart: 13, of which 7 were waited for; matrix products, arithmetic and copies ran while one was open for 0% of the time, Pallas kernels for 48%

profile of v11, /device:TPU:0, one launch (start us, length us, event | category | flops | bytes accessed | tf_op | source)
XLA Modules:
  0.0 47.9 jit_solution(9196991129577269906)
XLA Ops:
  0.6 4.1 %collective-permute-start.1 = (bf16[32,2048]{1,0:T(8,128)(2,1)}, bf16[32,2048]{1,0:T(8,128)(2,1)S(1)}, u32[]{:S(2)}, u32[]{:S(2)}) collective-permute-start(bf16[32,2048]{1,0:T(8,128)(2,1)} %refs_0_.1), channel_id=1, source_target_pairs={{0,8},{1,13},{4,12},{5,9},{8,0},{9,5},{12,4},{13,1},{2,10},{3,15},... | collective-permute-start | bytes 393224 | tf_op jit(solution)/shard_map/ppermute | solution.py:352
  4.7 1.5 %collective-permute-start.3 = (bf16[64,2048]{1,0:T(8,128)(2,1)}, bf16[64,2048]{1,0:T(8,128)(2,1)S(1)}, u32[]{:S(2)}, u32[]{:S(2)}) collective-permute-start(bf16[64,2048]{1,0:T(8,128)(2,1)} %refs_2_.5), channel_id=1, source_target_pairs={{0,2},{2,0},{1,3},{3,1},{4,6},{6,4},{5,7},{7,5},{8,10},{10,8},{9,1... | collective-permute-start | bytes 786440 | tf_op jit(solution)/shard_map/ppermute | solution.py:346
  6.2 1.6 %collective-permute-start = (bf16[32,2048]{1,0:T(8,128)(2,1)}, bf16[32,2048]{1,0:T(8,128)(2,1)S(1)}, u32[]{:S(2)}, u32[]{:S(2)}) collective-permute-start(bf16[32,2048]{1,0:T(8,128)(2,1)} %refs_0_.1), channel_id=1, source_target_pairs={{0,4},{4,0},{8,12},{12,8},{1,5},{5,1},{9,13},{13,9},{2,6},{6,2},{1... | collective-permute-start | bytes 393224 | tf_op jit(solution)/shard_map/ppermute | solution.py:346
  7.8 3.9 %forward_own_a.1 = (bf16[7,32,256]{2,1,0:T(8,128)(2,1)S(1)}, bf16[7,1,12,128,128]{4,3,2,1,0:T(8,128)(2,1)S(1)}, bf16[7,1,12,128,128]{4,3,2,1,0:T(8,128)(2,1)S(1)}, s32[12,1,16]{2,1,0:T(1,128)S(4)}, s32[1,16]{1,0:T(1,128)S(4)}) custom-call(bf16[32,2048]{1,0:T(8,128)(2,1)} %refs_0_.1, s32[12,1,16]{2,1,0:T(1,128)} %bitcast.2, s32[1,16]{1,0:T(1,128)} %bitcast.3, ...), custom_call_target="tpu_custom_call" | custom-call | flops 176160768 | bytes 5505024 | tf_op jit(solution)/shard_map/forward_own_a/pallas_call | solution.py:390
  11.7 0.0 copy-start.1
  11.7 0.1 collective-permute-start.2
  11.8 1.4 %collective-permute-start.4 = (bf16[7,32,256]{2,1,0:T(8,128)(2,1)S(1)}, bf16[7,32,256]{2,1,0:T(8,128)(2,1)S(1)}, u32[]{:S(2)}, u32[]{:S(2)}) collective-permute-start(bf16[7,32,256]{2,1,0:T(8,128)(2,1)S(1)} %get-tuple-element.36._.refs_0_), channel_id=1, source_target_pairs={{0,2},{2,0},{1,3},{3,1},{4,6},{6,4},{5,7},{7,5},{8,10},{10,8},{9,1... | collective-permute-start | bytes 344072 | tf_op jit(solution)/shard_map/ppermute | solution.py:346
  13.2 0.6 %collective-permute-done.3.refs_5_.refs_3_ = bf16[64,2048]{1,0:T(8,128)(2,1)S(1)} collective-permute-done((bf16[64,2048]{1,0:T(8,128)(2,1)}, bf16[64,2048]{1,0:T(8,128)(2,1)S(1)}, u32[]{:S(2)}, u32[]{:S(2)}) %collective-permute-start.3) | collective-permute-done | bytes 262176 | tf_op jit(solution)/shard_map/ppermute | solution.py:346
  13.7 0.0 collective-permute-done.2.refs_2_.refs_3_
  13.7 1.0 %forward_rest_a.1.refs_6_.refs_2_ = bf16[7,96,256]{2,1,0:T(8,128)(2,1)S(1)} custom-call(s32[12,1,16]{2,1,0:T(1,128)S(4)} %get-tuple-element.34.rows_ref, s32[1,16]{1,0:T(1,128)S(4)} %get-tuple-element.35.counts_ref, bf16[32,2048]{1,0:T(8,128)(2,1)S(1)} %collective-permute-done.refs_0_.refs_1_, ...), custom_call_target="tpu_custom_call" | custom-call | flops 528482304 | bytes 5505024 | tf_op jit(solution)/shard_map/forward_rest_a/pallas_call | solution.py:435
  14.8 1.6 %collective-permute-start.5 = (bf16[7,96,256]{2,1,0:T(8,128)(2,1)S(1)}, bf16[7,96,256]{2,1,0:T(8,128)(2,1)S(1)}, u32[]{:S(2)}, u32[]{:S(2)}) collective-permute-start(bf16[7,96,256]{2,1,0:T(8,128)(2,1)S(1)} %forward_rest_a.1.refs_6_.refs_2_), channel_id=1, source_target_pairs={{0,2},{2,0},{1,3},{3,1},{4,6},{6,4},{5,7},{7,5},{8,10},{10,8},{9,1... | collective-permute-start | bytes 1032200 | tf_op jit(solution)/shard_map/ppermute | solution.py:346
  16.3 1.2 %collective-permute-done.4.refs_7_.refs_1_ = bf16[7,32,256]{2,1,0:T(8,128)(2,1)S(1)} collective-permute-done((bf16[7,32,256]{2,1,0:T(8,128)(2,1)S(1)}, bf16[7,32,256]{2,1,0:T(8,128)(2,1)S(1)}, u32[]{:S(2)}, u32[]{:S(2)}) %collective-permute-start.4) | collective-permute-done | bytes 114720 | tf_op jit(solution)/shard_map/ppermute | solution.py:346
  17.5 3.7 %forward_b.1 = (bf16[9,64,256]{2,1,0:T(8,128)(2,1)S(1)}, bf16[9,32,256]{2,1,0:T(8,128)(2,1)S(1)}, bf16[9,32,256]{2,1,0:T(8,128)(2,1)S(1)}, bf16[9,1,12,128,128]{...) custom-call(s32[12,1,16]{2,1,0:T(1,128)S(4)} %get-tuple-element.34.rows_ref, ...), custom_call_target="tpu_custom_call" | custom-call | flops 4529848320 | bytes 35389440 | tf_op jit(solution)/shard_map/forward_b/pallas_call | solution.py:450
  21.2 1.3 %collective-permute-start.8 = (bf16[9,64,256]{2,1,0:T(8,128)(2,1)S(1)}, bf16[9,64,256]{2,1,0:T(8,128)(2,1)S(1)}, u32[]{:S(2)}, u32[]{:S(2)}) collective-permute-start(bf16[9,64,256]{2,1,0:T(8,128)(2,1)S(1)} %get-tuple-element.41._.refs_6_.refs_0_), channel_id=1, source_target_pairs={{0,2},{2,0},{1,3},{3,1},{4,6},{6,4},{5,7},{7,5},{8,10},{10,8},{9,1... | collective-permute-start | bytes 884744 | tf_op jit(solution)/shard_map/ppermute | solution.py:346
  22.4 0.8 %collective-permute-start.7 = (bf16[9,32,256]{2,1,0:T(8,128)(2,1)S(1)}, bf16[9,32,256]{2,1,0:T(8,128)(2,1)S(1)}, u32[]{:S(2)}, u32[]{:S(2)}) collective-permute-start(bf16[9,32,256]{2,1,0:T(8,128)(2,1)S(1)} %get-tuple-element.43.refs_7_.refs_0_), channel_id=1, source_target_pairs={{0,2},{2,0},{1,3},{3,1},{4,6},{6,4},{5,7},{7,5},{8,10},{10,8},{9,1... | collective-permute-start | bytes 442376 | tf_op jit(solution)/shard_map/ppermute | solution.py:346
  23.3 2.0 %turn_b.1.refs_8_.turned_w = bf16[9,256,1536]{2,1,0:T(8,128)(2,1)S(1)} custom-call(bf16[9,1,12,128,128]{4,3,2,1,0:T(8,128)(2,1)S(1)} %get-tuple-element.39.gate_ref, bf16[9,1,12,128,128]{4,3,2,1,0:T(8,128)(2,1)S(1)} %get-tuple-element.40.up_ref, bf16[9,64,256]{2,1,0:T(8,128)(2,1)S(1)} %get-tuple-element.41._.refs_6_.refs_0_), custom_call_target="tpu_custom_call" | custom-call | tf_op jit(solution)/shard_map/turn_b/pallas_call | solution.py:467
  25.3 0.5 %collective-permute-done.5.refs_3_ = bf16[7,96,256]{2,1,0:T(8,128)(2,1)S(1)} collective-permute-done((bf16[7,96,256]{2,1,0:T(8,128)(2,1)S(1)}, bf16[7,96,256]{2,1,0:T(8,128)(2,1)S(1)}, u32[]{:S(2)}, u32[]{:S(2)}) %collective-permute-start.5) | collective-permute-done | bytes 344096 | tf_op jit(solution)/shard_map/ppermute | solution.py:346
  25.8 4.7 %first_half.1 = (bf16[16,1,12,128,128]{4,3,2,1,0:T(8,128)(2,1)}, bf16[16,1,12,128,128]{4,3,2,1,0:T(8,128)(2,1)}, bf16[128,896]{1,0:T(8,128)(2,1)S(1)}, f32[16,32...) custom-call(s32[12,1,16]{2,1,0:T(1,128)S(4)} %get-tuple-element.34.rows_ref, ...), custom_call_target="tpu_custom_call" | custom-call | flops 1409286144 | bytes 5505024 | tf_op jit(solution)/shard_map/first_half/pallas_call | solution.py:479
  30.4 1.6 %collective-permute-done.8.refs_1_ = bf16[9,64,256]{2,1,0:T(8,128)(2,1)S(1)} collective-permute-done((bf16[9,64,256]{2,1,0:T(8,128)(2,1)S(1)}, bf16[9,64,256]{2,1,0:T(8,128)(2,1)S(1)}, u32[]{:S(2)}, u32[]{:S(2)}) %collective-permute-start.8) | collective-permute-done | bytes 294944 | tf_op jit(solution)/shard_map/ppermute | solution.py:346
  32.1 1.5 %far_b.1 = (bf16[9,64,256]{2,1,0:T(8,128)(2,1)S(1)}, bf16[64,1152]{1,0:T(8,128)(2,1)S(1)}, bf16[32,2048]{1,0:T(8,128)(2,1)S(1)}, bf16[32,2304]{1,0:T(8,128)(2,1)S(1)}) custom-call(s32[12,1,16]{2,1,0:T(1,128)S(4)} %get-tuple-element.34.rows_ref, s32[1,16]{1,0:T(1,128)S(4)} %get-tuple-element.35.counts_ref, bf16[9,256,1536]{2,1,0:T(8,128)(2,1)S(1)} %turn_b.1.refs_8_.turned_w, ...), custom_call_target="tpu_custom_call" | custom-call | flops 452984832 | bytes 7077888 | tf_op jit(solution)/shard_map/far_b/pallas_call | solution.py:504
  33.6 0.1 collective-permute-start.9
  33.7 1.6 %collective-permute-start.6 = (bf16[9,32,256]{2,1,0:T(8,128)(2,1)S(1)}, bf16[9,32,256]{2,1,0:T(8,128)(2,1)S(1)}, u32[]{:S(2)}, u32[]{:S(2)}) collective-permute-start(bf16[9,32,256]{2,1,0:T(8,128)(2,1)S(1)} %get-tuple-element.45.refs_0_), channel_id=1, source_target_pairs={{0,2},{2,0},{1,3},{3,1},{4,6},{6,4},{5,7},{7,5},{8,10},{10,8},{9,1... | collective-permute-start | bytes 442376 | tf_op jit(solution)/shard_map/ppermute | solution.py:346
  35.3 0.1 collective-permute-start.11
  35.4 1.4 %next_b.1 = (bf16[9,32,256]{2,1,0:T(8,128)(2,1)S(1)}, bf16[32,1152]{1,0:T(8,128)(2,1)S(1)}, bf16[32,2048]{1,0:T(8,128)(2,1)S(1)}) custom-call(s32[12,1,16]{2,1,0:T(1,128)S(4)} %get-tuple-element.34.rows_ref, s32[1,16]{1,0:T(1,128)S(4)} %get-tuple-element.35.counts_ref, bf16[9,256,1536]{2,1,0:T(8,128)(2,1)S(1)} %turn_b.1.refs_8_.turned_w, ...), custom_call_target="tpu_custom_call" | custom-call | flops 226492416 | bytes 7077888 | tf_op jit(solution)/shard_map/next_b/pallas_call | solution.py:504
  36.7 2.7 %collective-permute-start.10 = (bf16[32,2048]{1,0:T(8,128)(2,1)S(1)}, bf16[32,2048]{1,0:T(8,128)(2,1)S(1)}, u32[]{:S(2)}, u32[]{:S(2)}) collective-permute-start(bf16[32,2048]{1,0:T(8,128)(2,1)S(1)} %get-tuple-element.61), channel_id=1, source_target_pairs={{0,4},{4,0},{8,12},{12,8},{1,5},{5,1},{9,13},{13,9},{2,6},{6,2},{1... | collective-permute-start | bytes 393224 | tf_op jit(solution)/shard_map/ppermute | solution.py:346
  39.4 0.5 %collective-permute-done.6.refs_1_ = bf16[9,32,256]{2,1,0:T(8,128)(2,1)S(1)} collective-permute-done((bf16[9,32,256]{2,1,0:T(8,128)(2,1)S(1)}, bf16[9,32,256]{2,1,0:T(8,128)(2,1)S(1)}, u32[]{:S(2)}, u32[]{:S(2)}) %collective-permute-start.6) | collective-permute-done | bytes 147488 | tf_op jit(solution)/shard_map/ppermute | solution.py:346
  39.9 4.6 %last_half.1 = (bf16[16,1,12,128,128]{4,3,2,1,0:T(8,128)(2,1)}, bf16[16,1,12,128,128]{4,3,2,1,0:T(8,128)(2,1)}, bf16[64,2048]{1,0:T(8,128)(2,1)}, bf16[32,2048]{1,0:T(8,128)(2,1)S(1)}) custom-call(s32[12,1,16]{2,1,0:T(1,128)S(4)} %get-tuple-element.34.rows_ref, ...), custom_call_target="tpu_custom_call", output_to_operand_aliasing={{0}: (14, {}), {1}: (15, {})} | custom-call | flops 9059696640 | bytes 70778880 | tf_op jit(solution)/shard_map/last_half/pallas_call | solution.py:536
  44.6 1.2 %collective-permute-done.10.refs_1_ = bf16[32,2048]{1,0:T(8,128)(2,1)S(1)} collective-permute-done((bf16[32,2048]{1,0:T(8,128)(2,1)S(1)}, bf16[32,2048]{1,0:T(8,128)(2,1)S(1)}, u32[]{:S(2)}, u32[]{:S(2)}) %collective-permute-start.10) | collective-permute-done | bytes 131104 | tf_op jit(solution)/shard_map/ppermute | solution.py:346
  45.8 0.1 sum_shards.1
  45.8 0.2 collective-permute-start.12
  46.0 1.2 %collective-permute-done.12 = bf16[32,2048]{1,0:T(8,128)(2,1)S(1)} collective-permute-done((bf16[32,2048]{1,0:T(8,128)(2,1)S(1)}, bf16[32,2048]{1,0:T(8,128)(2,1)S(1)}, u32[]{:S(2)}, u32[]{:S(2)}) %collective-permute-start.12) | collective-permute-done | bytes 131104 | tf_op jit(solution)/shard_map/ppermute | solution.py:346
  47.3 0.7 %add_convert_fusion = bf16[32,2048]{1,0:T(8,128)(2,1)} fusion(f32[32,2048]{1,0:T(8,128)S(1)} %get-tuple-element.62, bf16[32,2048]{1,0:T(8,128)(2,1)S(1)} %collective-permute-done.12), kind=kLoop, calls=%fused_computation | loop fusion | flops 196608 | bytes 524288 | tf_op jit(solution)/shard_map/convert_element_type | solution.py:579
  (10 shorter events, 0.1 us)
Async XLA Ops:
  0.6 11.1 %collective-permute-start.1 = (bf16[32,2048]{1,0:T(8,128)(2,1)}, bf16[32,2048]{1,0:T(8,128)(2,1)S(1)}, u32[]{:S(2)}, u32[]{:S(2)}) collective-permute-start(bf16[32,2048]{1,0:T(8,128)(2,1)} %refs_0_.1), channel_id=1, source_target_pairs={{0,8},{1,13},{4,12},{5,9},{8,0},{9,5},{12,4},{13,1},{2,10},{3,15},... | collective-permute-start | bytes 393224 | tf_op jit(solution)/shard_map/ppermute | solution.py:352
  4.7 9.0 %collective-permute-start.3 = (bf16[64,2048]{1,0:T(8,128)(2,1)}, bf16[64,2048]{1,0:T(8,128)(2,1)S(1)}, u32[]{:S(2)}, u32[]{:S(2)}) collective-permute-start(bf16[64,2048]{1,0:T(8,128)(2,1)} %refs_2_.5), channel_id=1, source_target_pairs={{0,2},{2,0},{1,3},{3,1},{4,6},{6,4},{5,7},{7,5},{8,10},{10,8},{9,1... | collective-permute-start | bytes 786440 | tf_op jit(solution)/shard_map/ppermute | solution.py:346
  6.2 6.9 %collective-permute-start = (bf16[32,2048]{1,0:T(8,128)(2,1)}, bf16[32,2048]{1,0:T(8,128)(2,1)S(1)}, u32[]{:S(2)}, u32[]{:S(2)}) collective-permute-start(bf16[32,2048]{1,0:T(8,128)(2,1)} %refs_0_.1), channel_id=1, source_target_pairs={{0,4},{4,0},{8,12},{12,8},{1,5},{5,1},{9,13},{13,9},{2,6},{6,2},{1... | collective-permute-start | bytes 393224 | tf_op jit(solution)/shard_map/ppermute | solution.py:346
  11.7 5.8 %copy-start.1 = (bf16[32,2048]{1,0:T(8,128)(2,1)S(1)}, bf16[32,2048]{1,0:T(8,128)(2,1)}, u32[]{:S(2)}) copy-start(bf16[32,2048]{1,0:T(8,128)(2,1)} %refs_0_.1) | copy-start | bytes 393220
  11.7 2.0 %collective-permute-start.2 = (bf16[32,2048]{1,0:T(8,128)(2,1)S(1)}, bf16[32,2048]{1,0:T(8,128)(2,1)S(1)}, u32[]{:S(2)}, u32[]{:S(2)}) collective-permute-start(bf16[32,2048]{1,0:T(8,128)(2,1)S(1)} %after_own.1), channel_id=1, source_target_pairs={{0,1},{1,0},{2,3},{3,2},{4,5},{5,4},{6,7},{7,6},{8,9},{9,8},{10,11... | collective-permute-start | bytes 393224 | tf_op jit(solution)/shard_map/ppermute | solution.py:346
  11.8 5.7 %collective-permute-start.4 = (bf16[7,32,256]{2,1,0:T(8,128)(2,1)S(1)}, bf16[7,32,256]{2,1,0:T(8,128)(2,1)S(1)}, u32[]{:S(2)}, u32[]{:S(2)}) collective-permute-start(bf16[7,32,256]{2,1,0:T(8,128)(2,1)S(1)} %get-tuple-element.36._.refs_0_), channel_id=1, source_target_pairs={{0,2},{2,0},{1,3},{3,1},{4,6},{6,4},{5,7},{7,5},{8,10},{10,8},{9,1... | collective-permute-start | bytes 344072 | tf_op jit(solution)/shard_map/ppermute | solution.py:346
  14.8 11.0 %collective-permute-start.5 = (bf16[7,96,256]{2,1,0:T(8,128)(2,1)S(1)}, bf16[7,96,256]{2,1,0:T(8,128)(2,1)S(1)}, u32[]{:S(2)}, u32[]{:S(2)}) collective-permute-start(bf16[7,96,256]{2,1,0:T(8,128)(2,1)S(1)} %forward_rest_a.1.refs_6_.refs_2_), channel_id=1, source_target_pairs={{0,2},{2,0},{1,3},{3,1},{4,6},{6,4},{5,7},{7,5},{8,10},{10,8},{9,1... | collective-permute-start | bytes 1032200 | tf_op jit(solution)/shard_map/ppermute | solution.py:346
  21.2 10.9 %collective-permute-start.8 = (bf16[9,64,256]{2,1,0:T(8,128)(2,1)S(1)}, bf16[9,64,256]{2,1,0:T(8,128)(2,1)S(1)}, u32[]{:S(2)}, u32[]{:S(2)}) collective-permute-start(bf16[9,64,256]{2,1,0:T(8,128)(2,1)S(1)} %get-tuple-element.41._.refs_6_.refs_0_), channel_id=1, source_target_pairs={{0,2},{2,0},{1,3},{3,1},{4,6},{6,4},{5,7},{7,5},{8,10},{10,8},{9,1... | collective-permute-start | bytes 884744 | tf_op jit(solution)/shard_map/ppermute | solution.py:346
  22.4 12.8 %collective-permute-start.7 = (bf16[9,32,256]{2,1,0:T(8,128)(2,1)S(1)}, bf16[9,32,256]{2,1,0:T(8,128)(2,1)S(1)}, u32[]{:S(2)}, u32[]{:S(2)}) collective-permute-start(bf16[9,32,256]{2,1,0:T(8,128)(2,1)S(1)} %get-tuple-element.43.refs_7_.refs_0_), channel_id=1, source_target_pairs={{0,2},{2,0},{1,3},{3,1},{4,6},{6,4},{5,7},{7,5},{8,10},{10,8},{9,1... | collective-permute-start | bytes 442376 | tf_op jit(solution)/shard_map/ppermute | solution.py:346
  23.3 2.5 %copy-start = (bf16[64,2048]{1,0:T(8,128)(2,1)S(1)}, bf16[64,2048]{1,0:T(8,128)(2,1)}, u32[]{:S(2)}) copy-start(bf16[64,2048]{1,0:T(8,128)(2,1)} %refs_2_.5) | copy-start | bytes 786436
  33.6 1.6 %collective-permute-start.9 = (bf16[32,2304]{1,0:T(8,128)(2,1)S(1)}, bf16[32,2304]{1,0:T(8,128)(2,1)S(1)}, u32[]{:S(2)}, u32[]{:S(2)}) collective-permute-start(bf16[32,2304]{1,0:T(8,128)(2,1)S(1)} %get-tuple-element.49), channel_id=1, source_target_pairs={{0,1},{1,0},{2,3},{3,2},{4,5},{5,4},{6,7},{7,6},{8,9},{9,8},{10,11... | collective-permute-start | bytes 442376 | tf_op jit(solution)/shard_map/ppermute | solution.py:346
  33.7 6.3 %collective-permute-start.6 = (bf16[9,32,256]{2,1,0:T(8,128)(2,1)S(1)}, bf16[9,32,256]{2,1,0:T(8,128)(2,1)S(1)}, u32[]{:S(2)}, u32[]{:S(2)}) collective-permute-start(bf16[9,32,256]{2,1,0:T(8,128)(2,1)S(1)} %get-tuple-element.45.refs_0_), channel_id=1, source_target_pairs={{0,2},{2,0},{1,3},{3,1},{4,6},{6,4},{5,7},{7,5},{8,10},{10,8},{9,1... | collective-permute-start | bytes 442376 | tf_op jit(solution)/shard_map/ppermute | solution.py:346
  35.3 10.5 %collective-permute-start.11 = (bf16[32,2048]{1,0:T(8,128)(2,1)S(1)}, bf16[32,2048]{1,0:T(8,128)(2,1)S(1)}, u32[]{:S(2)}, u32[]{:S(2)}) collective-permute-start(bf16[32,2048]{1,0:T(8,128)(2,1)S(1)} %add_cores.1.refs_4_.refs_11_), channel_id=1, source_target_pairs={{0,8},{1,13},{4,12},{5,9},{8,0},{9,5},{12,4},{13,1},{2,10},{3,15},... | collective-permute-start | bytes 393224 | tf_op jit(solution)/shard_map/ppermute | solution.py:352
  36.7 9.1 %collective-permute-start.10 = (bf16[32,2048]{1,0:T(8,128)(2,1)S(1)}, bf16[32,2048]{1,0:T(8,128)(2,1)S(1)}, u32[]{:S(2)}, u32[]{:S(2)}) collective-permute-start(bf16[32,2048]{1,0:T(8,128)(2,1)S(1)} %get-tuple-element.61), channel_id=1, source_target_pairs={{0,4},{4,0},{8,12},{12,8},{1,5},{5,1},{9,13},{13,9},{2,6},{6,2},{1... | collective-permute-start | bytes 393224 | tf_op jit(solution)/shard_map/ppermute | solution.py:346
  45.8 1.4 %collective-permute-start.12 = (bf16[32,2048]{1,0:T(8,128)(2,1)S(1)}, bf16[32,2048]{1,0:T(8,128)(2,1)S(1)}, u32[]{:S(2)}, u32[]{:S(2)}) collective-permute-start(bf16[32,2048]{1,0:T(8,128)(2,1)S(1)} %get-tuple-element.63), channel_id=1, source_target_pairs={{0,1},{1,0},{2,3},{3,2},{4,5},{5,4},{6,7},{7,6},{8,9},{9,8},{10,11... | collective-permute-start | bytes 393224 | tf_op jit(solution)/shard_map/ppermute | solution.py:346

commit v12 on v10

--- a/solution.py
+++ b/solution.py
@@ -314,10 +314,11 @@
         hidden, grads = nonlinear(total_of(c, parts), cotangent_of(members[:1], cots, shard_rows, where))
         hidden_ref[:, c * tile : (c + 1) * tile] = hidden
         grads_ref[c] = grads
-        grads = jnp.concatenate([grads, next_grads[c], far_grads[c]], axis=0)
+    copies += start_hidden(members, hidden_of, hidden_hbm, shard_rows, hidden_sems)
+    for c in range(cols):
+        grads = jnp.concatenate([grads_ref[c], next_grads[c], far_grads[c]], axis=0)
         tile_grads(c, first, lists, turned_ref, grads, gate_ref, up_ref)
         copies += store_tiles(first, c, gate_ref, up_ref, gate_hbm, up_hbm, sems)
-    copies += start_hidden(members, hidden_of, hidden_hbm, shard_rows, hidden_sems)
     for c in range(cols):
         back = jnp.dot(grads_ref[c], turned_w[c], preferred_element_type=F32)
         add_back(first + c, lists, back, (acc_ref,), slots, tile)

time: 48.1 us -> 48.2 us (level)
  no operation moved by 1% of the time
where the time goes in v12:
time: 48.2 us; the launch traced here: 48 us
  Pallas kernels  23.2 us (48%)
  starting transfers between devices  18 us (37%)
  waiting for transfers between devices  5.4 us (11%)
  between operations  0.75 us (2%)
  other arithmetic  0.68 us (1%)
    ppermute x11, starting transfers between devices, swap(): lax.ppermute(x, axis, [(i, i ^ step) for i in range(lax.axis_size(axis))])  13 us
    ppermute x11, waiting for transfers between devices, swap(): lax.ppermute(x, axis, [(i, i ^ step) for i in range(lax.axis_size(axis))])  5.23 us
    pallas_call x1, Pallas kernels, on_device(): pl.pallas_call(functools.partial(last_half_kernel, members, owners, half)...  5.12 us
    ppermute x2, starting transfers between devices, swap_far(): return lax.ppermute(x, ('tok', 'sub'), pairs)  5 us
    pallas_call x1, Pallas kernels, on_device(): pl.pallas_call(functools.partial(first_half_kernel, members, owners), out...  4.18 us
    pallas_call x1, Pallas kernels, on_device(): pl.pallas_call(functools.partial(load_forward_kernel, shards, groups, hal...  4.04 us
    pallas_call x1, Pallas kernels, on_device(): pl.pallas_call(forward_own_kernel, out_shape=(shape(half, shard_rows, 2 *...  3.55 us
    pallas_call x2, Pallas kernels, second_half(): pl.pallas_call(functools.partial(second_half_kernel, chunk, owners, half,...  3.12 us
  transfers between devices with their start and end apart: 13, of which 6 were waited for; matrix products, arithmetic and copies ran while one was open for 0% of the time, Pallas kernels for 48%

profile of v12, /device:TPU:0, one launch (start us, length us, event | category | flops | bytes accessed | tf_op | source)
XLA Modules:
  0.0 48.0 jit_solution(16531471347022661925)
XLA Ops:
  0.6 4.1 %collective-permute-start.1 = (bf16[32,2048]{1,0:T(8,128)(2,1)}, bf16[32,2048]{1,0:T(8,128)(2,1)S(1)}, u32[]{:S(2)}, u32[]{:S(2)}) collective-permute-start(bf16[32,2048]{1,0:T(8,128)(2,1)} %refs_0_.1), channel_id=1, source_target_pairs={{0,8},{1,13},{4,12},{5,9},{8,0},{9,5},{12,4},{13,1},{2,10},{3,15},... | collective-permute-start | bytes 393224 | tf_op jit(solution)/shard_map/ppermute | solution.py:353
  4.7 1.5 %collective-permute-start.3 = (bf16[64,2048]{1,0:T(8,128)(2,1)}, bf16[64,2048]{1,0:T(8,128)(2,1)S(1)}, u32[]{:S(2)}, u32[]{:S(2)}) collective-permute-start(bf16[64,2048]{1,0:T(8,128)(2,1)} %refs_2_.5), channel_id=1, source_target_pairs={{0,2},{2,0},{1,3},{3,1},{4,6},{6,4},{5,7},{7,5},{8,10},{10,8},{9,1... | collective-permute-start | bytes 786440 | tf_op jit(solution)/shard_map/ppermute | solution.py:347
  6.2 1.6 %collective-permute-start = (bf16[32,2048]{1,0:T(8,128)(2,1)}, bf16[32,2048]{1,0:T(8,128)(2,1)S(1)}, u32[]{:S(2)}, u32[]{:S(2)}) collective-permute-start(bf16[32,2048]{1,0:T(8,128)(2,1)} %refs_0_.1), channel_id=1, source_target_pairs={{0,4},{4,0},{8,12},{12,8},{1,5},{5,1},{9,13},{13,9},{2,6},{6,2},{1... | collective-permute-start | bytes 393224 | tf_op jit(solution)/shard_map/ppermute | solution.py:347
  7.8 3.5 %forward_own_a.1 = (bf16[6,32,256]{2,1,0:T(8,128)(2,1)S(1)}, bf16[6,1,12,128,128]{4,3,2,1,0:T(8,128)(2,1)S(1)}, bf16[6,1,12,128,128]{4,3,2,1,0:T(8,128)(2,1)S(1)}, s32[12,1,16]{2,1,0:T(1,128)S(4)}, s32[1,16]{1,0:T(1,128)S(4)}) custom-call(bf16[32,2048]{1,0:T(8,128)(2,1)} %refs_0_.1, s32[12,1,16]{2,1,0:T(1,128)} %bitcast.2, s32[1,16]{1,0:T(1,128)} %bitcast.3, ...), custom_call_target="tpu_custom_call" | custom-call | flops 150994944 | bytes 4718592 | tf_op jit(solution)/shard_map/forward_own_a/pallas_call | solution.py:391
  11.4 0.2 collective-permute-done.1.x_ref.refs_1_.refs_2_
  11.5 0.1 collective-permute-start.2
  11.6 1.6 %collective-permute-start.4 = (bf16[6,32,256]{2,1,0:T(8,128)(2,1)S(1)}, bf16[6,32,256]{2,1,0:T(8,128)(2,1)S(1)}, u32[]{:S(2)}, u32[]{:S(2)}) collective-permute-start(bf16[6,32,256]{2,1,0:T(8,128)(2,1)S(1)} %get-tuple-element.36._.refs_0_), channel_id=1, source_target_pairs={{0,2},{2,0},{1,3},{3,1},{4,6},{6,4},{5,7},{7,5},{8,10},{10,8},{9,1... | collective-permute-start | bytes 294920 | tf_op jit(solution)/shard_map/ppermute | solution.py:347
  13.2 0.6 %collective-permute-done.3.refs_5_.refs_3_ = bf16[64,2048]{1,0:T(8,128)(2,1)S(1)} collective-permute-done((bf16[64,2048]{1,0:T(8,128)(2,1)}, bf16[64,2048]{1,0:T(8,128)(2,1)S(1)}, u32[]{:S(2)}, u32[]{:S(2)}) %collective-permute-start.3) | collective-permute-done | bytes 262176 | tf_op jit(solution)/shard_map/ppermute | solution.py:347
  13.7 0.9 %forward_rest_a.1.refs_6_.refs_2_ = bf16[6,96,256]{2,1,0:T(8,128)(2,1)S(1)} custom-call(s32[12,1,16]{2,1,0:T(1,128)S(4)} %get-tuple-element.34.rows_ref, s32[1,16]{1,0:T(1,128)S(4)} %get-tuple-element.35.counts_ref, bf16[32,2048]{1,0:T(8,128)(2,1)S(1)} %collective-permute-done.refs_0_.refs_1_, ...), custom_call_target="tpu_custom_call" | custom-call | flops 452984832 | bytes 4718592 | tf_op jit(solution)/shard_map/forward_rest_a/pallas_call | solution.py:436
  14.6 1.6 %collective-permute-start.5 = (bf16[6,96,256]{2,1,0:T(8,128)(2,1)S(1)}, bf16[6,96,256]{2,1,0:T(8,128)(2,1)S(1)}, u32[]{:S(2)}, u32[]{:S(2)}) collective-permute-start(bf16[6,96,256]{2,1,0:T(8,128)(2,1)S(1)} %forward_rest_a.1.refs_6_.refs_2_), channel_id=1, source_target_pairs={{0,2},{2,0},{1,3},{3,1},{4,6},{6,4},{5,7},{7,5},{8,10},{10,8},{9,1... | collective-permute-start | bytes 884744 | tf_op jit(solution)/shard_map/ppermute | solution.py:347
  16.2 0.6 %collective-permute-done.4.refs_7_.refs_1_ = bf16[6,32,256]{2,1,0:T(8,128)(2,1)S(1)} collective-permute-done((bf16[6,32,256]{2,1,0:T(8,128)(2,1)S(1)}, bf16[6,32,256]{2,1,0:T(8,128)(2,1)S(1)}, u32[]{:S(2)}, u32[]{:S(2)}) %collective-permute-start.4) | collective-permute-done | bytes 98336 | tf_op jit(solution)/shard_map/ppermute | solution.py:347
  16.8 4.0 %forward_b.1 = (bf16[10,64,256]{2,1,0:T(8,128)(2,1)S(1)}, bf16[10,32,256]{2,1,0:T(8,128)(2,1)S(1)}, bf16[10,32,256]{2,1,0:T(8,128)(2,1)S(1)}, bf16[10,1,12,128,1...) custom-call(s32[12,1,16]{2,1,0:T(1,128)S(4)} %get-tuple-element.34.rows_ref, ...), custom_call_target="tpu_custom_call" | custom-call | flops 5033164800 | bytes 39321600 | tf_op jit(solution)/shard_map/forward_b/pallas_call | solution.py:451
  20.9 1.6 %collective-permute-start.8 = (bf16[10,64,256]{2,1,0:T(8,128)(2,1)S(1)}, bf16[10,64,256]{2,1,0:T(8,128)(2,1)S(1)}, u32[]{:S(2)}, u32[]{:S(2)}) collective-permute-start(bf16[10,64,256]{2,1,0:T(8,128)(2,1)S(1)} %get-tuple-element.41._.refs_6_.refs_0_), channel_id=1, source_target_pairs={{0,2},{2,0},{1,3},{3,1},{4,6},{6,4},{5,7},{7,5},{8,10},{10,8},{9,1... | collective-permute-start | bytes 983048 | tf_op jit(solution)/shard_map/ppermute | solution.py:347
  22.4 0.5 %collective-permute-start.7 = (bf16[10,32,256]{2,1,0:T(8,128)(2,1)S(1)}, bf16[10,32,256]{2,1,0:T(8,128)(2,1)S(1)}, u32[]{:S(2)}, u32[]{:S(2)}) collective-permute-start(bf16[10,32,256]{2,1,0:T(8,128)(2,1)S(1)} %get-tuple-element.43.refs_7_.refs_0_), channel_id=1, source_target_pairs={{0,2},{2,0},{1,3},{3,1},{4,6},{6,4},{5,7},{7,5},{8,10},{10,8},{9,1... | collective-permute-start | bytes 491528 | tf_op jit(solution)/shard_map/ppermute | solution.py:347
  23.0 2.2 %turn_b.1.refs_8_.turned_w = bf16[10,256,1536]{2,1,0:T(8,128)(2,1)S(1)} custom-call(bf16[10,1,12,128,128]{4,3,2,1,0:T(8,128)(2,1)S(1)} %get-tuple-element.39.gate_ref, bf16[10,1,12,128,128]{4,3,2,1,0:T(8,128)(2,1)S(1)} %get-tuple-element.40.up_ref, bf16[10,64,256]{2,1,0:T(8,128)(2,1)S(1)} %get-tuple-element.41._.refs_6_.refs_0_), custom_call_target="tpu_custom_call" | custom-call | tf_op jit(solution)/shard_map/turn_b/pallas_call | solution.py:468
  25.2 0.0 collective-permute-done.5.refs_3_
  25.2 4.2 %first_half.1 = (bf16[16,1,12,128,128]{4,3,2,1,0:T(8,128)(2,1)}, bf16[16,1,12,128,128]{4,3,2,1,0:T(8,128)(2,1)}, bf16[128,768]{1,0:T(8,128)(2,1)S(1)}, f32[16,32...) custom-call(s32[12,1,16]{2,1,0:T(1,128)S(4)} %get-tuple-element.34.rows_ref, ...), custom_call_target="tpu_custom_call" | custom-call | flops 1207959552 | bytes 4718592 | tf_op jit(solution)/shard_map/first_half/pallas_call | solution.py:480
  29.4 2.2 %collective-permute-done.8.refs_1_ = bf16[10,64,256]{2,1,0:T(8,128)(2,1)S(1)} collective-permute-done((bf16[10,64,256]{2,1,0:T(8,128)(2,1)S(1)}, bf16[10,64,256]{2,1,0:T(8,128)(2,1)S(1)}, u32[]{:S(2)}, u32[]{:S(2)}) %collective-permute-start.8) | collective-permute-done | bytes 327712 | tf_op jit(solution)/shard_map/ppermute | solution.py:347
  31.6 1.6 %far_b.1 = (bf16[10,64,256]{2,1,0:T(8,128)(2,1)S(1)}, bf16[64,1280]{1,0:T(8,128)(2,1)S(1)}, bf16[32,2048]{1,0:T(8,128)(2,1)S(1)}, bf16[32,2560]{1,0:T(8,128)(2,1)S(1)}) custom-call(s32[12,1,16]{2,1,0:T(1,128)S(4)} %get-tuple-element.34.rows_ref, s32[1,16]{1,0:T(1,128)S(4)} %get-tuple-element.35.counts_ref, ...), custom_call_target="tpu_custom_call" | custom-call | flops 503316480 | bytes 7864320 | tf_op jit(solution)/shard_map/far_b/pallas_call | solution.py:505
  33.2 0.1 collective-permute-start.9
  33.3 1.6 %collective-permute-start.6 = (bf16[10,32,256]{2,1,0:T(8,128)(2,1)S(1)}, bf16[10,32,256]{2,1,0:T(8,128)(2,1)S(1)}, u32[]{:S(2)}, u32[]{:S(2)}) collective-permute-start(bf16[10,32,256]{2,1,0:T(8,128)(2,1)S(1)} %get-tuple-element.45.refs_0_), channel_id=1, source_target_pairs={{0,2},{2,0},{1,3},{3,1},{4,6},{6,4},{5,7},{7,5},{8,10},{10,8},{9,1... | collective-permute-start | bytes 491528 | tf_op jit(solution)/shard_map/ppermute | solution.py:347
  34.8 0.0 collective-permute-done.7._.refs_1_
  34.8 0.0 collective-permute-done.9.right_ref
  34.9 0.9 %collective-permute-start.11 = (bf16[32,2048]{1,0:T(8,128)(2,1)S(1)}, bf16[32,2048]{1,0:T(8,128)(2,1)S(1)}, u32[]{:S(2)}, u32[]{:S(2)}) collective-permute-start(bf16[32,2048]{1,0:T(8,128)(2,1)S(1)} %add_cores.1.refs_4_.refs_11_), channel_id=1, source_target_pairs={{0,8},{1,13},{4,12},{5,9},{8,0},{9,5},{12,4},{13,1},{2,10},{3,15},... | collective-permute-start | bytes 393224 | tf_op jit(solution)/shard_map/ppermute | solution.py:353
  35.8 1.5 %next_b.1 = (bf16[10,32,256]{2,1,0:T(8,128)(2,1)S(1)}, bf16[32,1280]{1,0:T(8,128)(2,1)S(1)}, bf16[32,2048]{1,0:T(8,128)(2,1)S(1)}) custom-call(s32[12,1,16]{2,1,0:T(1,128)S(4)} %get-tuple-element.34.rows_ref, s32[1,16]{1,0:T(1,128)S(4)} %get-tuple-element.35.counts_ref, bf16[10,256,1536]{2,1,0:T(8,128)(2,1)S(1)} %turn_b.1.refs_8_.turned_w, ...), custom_call_target="tpu_custom_call" | custom-call | flops 251658240 | bytes 7864320 | tf_op jit(solution)/shard_map/next_b/pallas_call | solution.py:505
  37.3 2.8 %collective-permute-start.10 = (bf16[32,2048]{1,0:T(8,128)(2,1)S(1)}, bf16[32,2048]{1,0:T(8,128)(2,1)S(1)}, u32[]{:S(2)}, u32[]{:S(2)}) collective-permute-start(bf16[32,2048]{1,0:T(8,128)(2,1)S(1)} %get-tuple-element.61), channel_id=1, source_target_pairs={{0,4},{4,0},{8,12},{12,8},{1,5},{5,1},{9,13},{13,9},{2,6},{6,2},{1... | collective-permute-start | bytes 393224 | tf_op jit(solution)/shard_map/ppermute | solution.py:347
  40.1 5.1 %last_half.1 = (bf16[16,1,12,128,128]{4,3,2,1,0:T(8,128)(2,1)}, bf16[16,1,12,128,128]{4,3,2,1,0:T(8,128)(2,1)}, bf16[64,2048]{1,0:T(8,128)(2,1)}, bf16[32,2048]{1,0:T(8,128)(2,1)S(1)}) custom-call(s32[12,1,16]{2,1,0:T(1,128)S(4)} %get-tuple-element.34.rows_ref, ...), custom_call_target="tpu_custom_call", output_to_operand_aliasing={{0}: (14, {}), {1}: (15, {})} | custom-call | flops 10066329600 | bytes 78643200 | tf_op jit(solution)/shard_map/last_half/pallas_call | solution.py:537
  45.2 0.6 %collective-permute-done.10.refs_1_ = bf16[32,2048]{1,0:T(8,128)(2,1)S(1)} collective-permute-done((bf16[32,2048]{1,0:T(8,128)(2,1)S(1)}, bf16[32,2048]{1,0:T(8,128)(2,1)S(1)}, u32[]{:S(2)}, u32[]{:S(2)}) %collective-permute-start.10) | collective-permute-done | bytes 131104 | tf_op jit(solution)/shard_map/ppermute | solution.py:347
  45.9 0.1 sum_shards.1
  45.9 0.2 collective-permute-start.12
  46.1 1.2 %collective-permute-done.12 = bf16[32,2048]{1,0:T(8,128)(2,1)S(1)} collective-permute-done((bf16[32,2048]{1,0:T(8,128)(2,1)S(1)}, bf16[32,2048]{1,0:T(8,128)(2,1)S(1)}, u32[]{:S(2)}, u32[]{:S(2)}) %collective-permute-start.12) | collective-permute-done | bytes 131104 | tf_op jit(solution)/shard_map/ppermute | solution.py:347
  47.3 0.7 %add_convert_fusion = bf16[32,2048]{1,0:T(8,128)(2,1)} fusion(f32[32,2048]{1,0:T(8,128)S(1)} %get-tuple-element.62, bf16[32,2048]{1,0:T(8,128)(2,1)S(1)} %collective-permute-done.12), kind=kLoop, calls=%fused_computation | loop fusion | flops 196608 | bytes 524288 | tf_op jit(solution)/shard_map/convert_element_type | solution.py:580
  (10 shorter events, 0.1 us)
Async XLA Ops:
  0.6 10.9 %collective-permute-start.1 = (bf16[32,2048]{1,0:T(8,128)(2,1)}, bf16[32,2048]{1,0:T(8,128)(2,1)S(1)}, u32[]{:S(2)}, u32[]{:S(2)}) collective-permute-start(bf16[32,2048]{1,0:T(8,128)(2,1)} %refs_0_.1), channel_id=1, source_target_pairs={{0,8},{1,13},{4,12},{5,9},{8,0},{9,5},{12,4},{13,1},{2,10},{3,15},... | collective-permute-start | bytes 393224 | tf_op jit(solution)/shard_map/ppermute | solution.py:353
  4.7 9.0 %collective-permute-start.3 = (bf16[64,2048]{1,0:T(8,128)(2,1)}, bf16[64,2048]{1,0:T(8,128)(2,1)S(1)}, u32[]{:S(2)}, u32[]{:S(2)}) collective-permute-start(bf16[64,2048]{1,0:T(8,128)(2,1)} %refs_2_.5), channel_id=1, source_target_pairs={{0,2},{2,0},{1,3},{3,1},{4,6},{6,4},{5,7},{7,5},{8,10},{10,8},{9,1... | collective-permute-start | bytes 786440 | tf_op jit(solution)/shard_map/ppermute | solution.py:347
  6.2 6.9 %collective-permute-start = (bf16[32,2048]{1,0:T(8,128)(2,1)}, bf16[32,2048]{1,0:T(8,128)(2,1)S(1)}, u32[]{:S(2)}, u32[]{:S(2)}) collective-permute-start(bf16[32,2048]{1,0:T(8,128)(2,1)} %refs_0_.1), channel_id=1, source_target_pairs={{0,4},{4,0},{8,12},{12,8},{1,5},{5,1},{9,13},{13,9},{2,6},{6,2},{1... | collective-permute-start | bytes 393224 | tf_op jit(solution)/shard_map/ppermute | solution.py:347
  7.8 9.0 %copy-start.1 = (bf16[32,2048]{1,0:T(8,128)(2,1)S(1)}, bf16[32,2048]{1,0:T(8,128)(2,1)}, u32[]{:S(2)}) copy-start(bf16[32,2048]{1,0:T(8,128)(2,1)} %refs_0_.1) | copy-start | bytes 393220
  11.5 2.2 %collective-permute-start.2 = (bf16[32,2048]{1,0:T(8,128)(2,1)S(1)}, bf16[32,2048]{1,0:T(8,128)(2,1)S(1)}, u32[]{:S(2)}, u32[]{:S(2)}) collective-permute-start(bf16[32,2048]{1,0:T(8,128)(2,1)S(1)} %after_own.1), channel_id=1, source_target_pairs={{0,1},{1,0},{2,3},{3,2},{4,5},{5,4},{6,7},{7,6},{8,9},{9,8},{10,11... | collective-permute-start | bytes 393224 | tf_op jit(solution)/shard_map/ppermute | solution.py:347
  11.6 5.2 %collective-permute-start.4 = (bf16[6,32,256]{2,1,0:T(8,128)(2,1)S(1)}, bf16[6,32,256]{2,1,0:T(8,128)(2,1)S(1)}, u32[]{:S(2)}, u32[]{:S(2)}) collective-permute-start(bf16[6,32,256]{2,1,0:T(8,128)(2,1)S(1)} %get-tuple-element.36._.refs_0_), channel_id=1, source_target_pairs={{0,2},{2,0},{1,3},{3,1},{4,6},{6,4},{5,7},{7,5},{8,10},{10,8},{9,1... | collective-permute-start | bytes 294920 | tf_op jit(solution)/shard_map/ppermute | solution.py:347
  14.6 10.6 %collective-permute-start.5 = (bf16[6,96,256]{2,1,0:T(8,128)(2,1)S(1)}, bf16[6,96,256]{2,1,0:T(8,128)(2,1)S(1)}, u32[]{:S(2)}, u32[]{:S(2)}) collective-permute-start(bf16[6,96,256]{2,1,0:T(8,128)(2,1)S(1)} %forward_rest_a.1.refs_6_.refs_2_), channel_id=1, source_target_pairs={{0,2},{2,0},{1,3},{3,1},{4,6},{6,4},{5,7},{7,5},{8,10},{10,8},{9,1... | collective-permute-start | bytes 884744 | tf_op jit(solution)/shard_map/ppermute | solution.py:347
  20.9 10.7 %collective-permute-start.8 = (bf16[10,64,256]{2,1,0:T(8,128)(2,1)S(1)}, bf16[10,64,256]{2,1,0:T(8,128)(2,1)S(1)}, u32[]{:S(2)}, u32[]{:S(2)}) collective-permute-start(bf16[10,64,256]{2,1,0:T(8,128)(2,1)S(1)} %get-tuple-element.41._.refs_6_.refs_0_), channel_id=1, source_target_pairs={{0,2},{2,0},{1,3},{3,1},{4,6},{6,4},{5,7},{7,5},{8,10},{10,8},{9,1... | collective-permute-start | bytes 983048 | tf_op jit(solution)/shard_map/ppermute | solution.py:347
  22.4 12.4 %collective-permute-start.7 = (bf16[10,32,256]{2,1,0:T(8,128)(2,1)S(1)}, bf16[10,32,256]{2,1,0:T(8,128)(2,1)S(1)}, u32[]{:S(2)}, u32[]{:S(2)}) collective-permute-start(bf16[10,32,256]{2,1,0:T(8,128)(2,1)S(1)} %get-tuple-element.43.refs_7_.refs_0_), channel_id=1, source_target_pairs={{0,2},{2,0},{1,3},{3,1},{4,6},{6,4},{5,7},{7,5},{8,10},{10,8},{9,1... | collective-permute-start | bytes 491528 | tf_op jit(solution)/shard_map/ppermute | solution.py:347
  23.0 2.2 %copy-start = (bf16[64,2048]{1,0:T(8,128)(2,1)S(1)}, bf16[64,2048]{1,0:T(8,128)(2,1)}, u32[]{:S(2)}) copy-start(bf16[64,2048]{1,0:T(8,128)(2,1)} %refs_2_.5) | copy-start | bytes 786436
  33.2 1.6 %collective-permute-start.9 = (bf16[32,2560]{1,0:T(8,128)(2,1)S(1)}, bf16[32,2560]{1,0:T(8,128)(2,1)S(1)}, u32[]{:S(2)}, u32[]{:S(2)}) collective-permute-start(bf16[32,2560]{1,0:T(8,128)(2,1)S(1)} %get-tuple-element.49), channel_id=1, source_target_pairs={{0,1},{1,0},{2,3},{3,2},{4,5},{5,4},{6,7},{7,6},{8,9},{9,8},{10,11... | collective-permute-start | bytes 491528 | tf_op jit(solution)/shard_map/ppermute | solution.py:347
  33.3 6.8 %collective-permute-start.6 = (bf16[10,32,256]{2,1,0:T(8,128)(2,1)S(1)}, bf16[10,32,256]{2,1,0:T(8,128)(2,1)S(1)}, u32[]{:S(2)}, u32[]{:S(2)}) collective-permute-start(bf16[10,32,256]{2,1,0:T(8,128)(2,1)S(1)} %get-tuple-element.45.refs_0_), channel_id=1, source_target_pairs={{0,2},{2,0},{1,3},{3,1},{4,6},{6,4},{5,7},{7,5},{8,10},{10,8},{9,1... | collective-permute-start | bytes 491528 | tf_op jit(solution)/shard_map/ppermute | solution.py:347
  34.9 11.0 %collective-permute-start.11 = (bf16[32,2048]{1,0:T(8,128)(2,1)S(1)}, bf16[32,2048]{1,0:T(8,128)(2,1)S(1)}, u32[]{:S(2)}, u32[]{:S(2)}) collective-permute-start(bf16[32,2048]{1,0:T(8,128)(2,1)S(1)} %add_cores.1.refs_4_.refs_11_), channel_id=1, source_target_pairs={{0,8},{1,13},{4,12},{5,9},{8,0},{9,5},{12,4},{13,1},{2,10},{3,15},... | collective-permute-start | bytes 393224 | tf_op jit(solution)/shard_map/ppermute | solution.py:353
  37.3 8.6 %collective-permute-start.10 = (bf16[32,2048]{1,0:T(8,128)(2,1)S(1)}, bf16[32,2048]{1,0:T(8,128)(2,1)S(1)}, u32[]{:S(2)}, u32[]{:S(2)}) collective-permute-start(bf16[32,2048]{1,0:T(8,128)(2,1)S(1)} %get-tuple-element.61), channel_id=1, source_target_pairs={{0,4},{4,0},{8,12},{12,8},{1,5},{5,1},{9,13},{13,9},{2,6},{6,2},{1... | collective-permute-start | bytes 393224 | tf_op jit(solution)/shard_map/ppermute | solution.py:347
  45.9 1.4 %collective-permute-start.12 = (bf16[32,2048]{1,0:T(8,128)(2,1)S(1)}, bf16[32,2048]{1,0:T(8,128)(2,1)S(1)}, u32[]{:S(2)}, u32[]{:S(2)}) collective-permute-start(bf16[32,2048]{1,0:T(8,128)(2,1)S(1)} %get-tuple-element.63), channel_id=1, source_target_pairs={{0,1},{1,0},{2,3},{3,2},{4,5},{5,4},{6,7},{7,6},{8,9},{9,8},{10,11... | collective-permute-start | bytes 393224 | tf_op jit(solution)/shard_map/ppermute | solution.py:347
